TPU v7x, 32 devices: a whole 2x2x4 slice. The times are simulated.
32 devices in a mesh: dp: 4 (over y, x), seq: 4 (over z), head: 2 (over core).
Axes of the slice: x: 2, y: 2, z: 4, core: 2. Of those that a mesh axis runs over, the one named last changes fastest.
Arguments:
- states: bfloat16 [4, 512, 2432], P('dp', 'seq'), may hold values from -6 to 6
- adjoint: float32 [4, 512, 2432], P('dp', 'seq'), may hold values from -16 to 16
- text_kv: bfloat16 [4, 32, 2, 1280], P('dp', 'seq', None, 'head'), may hold values from -125 to 125
- text_len: int32 [4], P('dp'), may hold values from 8 to 32, as said below
- step_index: int32 [4], P('dp'), may hold values from 0 to 27
- modulation: float32 [28, 3, 2432], replicated, may hold values from -3 to 3
- w_qkv: bfloat16 [2432, 3, 1280], P('dp', None, 'head'), may hold values from -0.125 to 0.125
- qk_gain: float32 [2, 64], replicated, may hold values from 0.1 to 1.9
- w_out: bfloat16 [1280, 2432], P('head', 'dp'), may hold values from -0.15625 to 0.15625
Outputs:
- pulled: float32 [4, 512, 2432], P('dp', 'seq', 'head')
Inputs may be any that keep to these rules, and one draw needn't show every extreme that they name: `text_len`: some trajectory has all 32 text tokens and some has 8.
All inputs are finite; a program needn't handle non-finite values.
Results may differ from a plain program's by a relative error of at most 0.02.
The roundings to bfloat16 on the way count: a program that leaves them out, or rounds other values in their place, can miss the bound.
Values may be sent and summed in bfloat16 or wider, within the bound.
No kernel may reach another device: no remote copies, remote signals or barrier semaphores. Data moves between devices by JAX's collectives and lax.ppermute only.
A program may use at most 192 MiB of HBM per device.

v0:
```python
import functools

import jax
import jax.numpy as jnp
from jax import lax
from jax.experimental import pallas as pl
from jax.experimental.pallas import tpu as pltpu
from jax.sharding import PartitionSpec as P

HD = 64
GRANT = 60 * 1024 * 1024
SMALL_GRANT = 24 * 1024 * 1024
EXTRA = 128
NT = (((1,), (1,)), ((), ()))
NN = (((1,), (0,)), ((), ()))


def line_ring(count):
    return [0] + list(range(1, count, 2)) + [i for i in range(count - 1, 0, -1) if i % 2 == 0]


def ring_pairs(order):
    return [(order[i], order[(i + 1) % len(order)]) for i in range(len(order))]


def ring_place(order, index):
    place = jnp.int32(0)
    for position, member in enumerate(order):
        place = jnp.where(index == member, jnp.int32(position), place)
    return place


def ring_member(order, place):
    member = jnp.int32(order[0])
    for position, value in enumerate(order):
        member = jnp.where(place == position, jnp.int32(value), member)
    return member


def dot(a, b, dims):
    return lax.dot_general(a, b, dims, preferred_element_type=jnp.float32)


def equal_blocks(columns, block):
    row = lax.broadcasted_iota(jnp.int32, (columns, columns), 0)
    column = lax.broadcasted_iota(jnp.int32, (columns, columns), 1)
    return jnp.where(row // block == column // block, 1.0, 0.0).astype(jnp.bfloat16)


def head_means(values):
    parts = []
    for first in range(0, values.shape[1], 256):
        part = values[:, first : first + 256]
        ones = equal_blocks(part.shape[1], HD)
        high = part.astype(jnp.bfloat16)
        low = (part - high.astype(jnp.float32)).astype(jnp.bfloat16)
        parts.append(dot(high, ones, NN) + dot(low, ones, NN))
    return jnp.concatenate(parts, axis=1) * (1.0 / HD)


def head_gains(gain, slots):
    return jnp.concatenate([gain[0:1, :]] * slots + [gain[1:2, :]] * slots, axis=1)


def whole_tiles(columns):
    return -(-columns // 128) * 128


def spec(space):
    return pl.BlockSpec(memory_space=space)


def text_columns(text, part):
    rows = text[...].astype(jnp.float32)[:, part, :]
    return [rows[:, c * EXTRA : (c + 1) * EXTRA] for c in range(rows.shape[1] // EXTRA)]


def extra_columns(blocks, rows):
    filled = sum(one.shape[0] for one in blocks)
    blocks = blocks + [jnp.zeros((rows - filled, EXTRA), jnp.float32)]
    return jnp.concatenate(blocks, axis=0).astype(jnp.bfloat16)


def first_kernel(step, core, states, table, adjoint, text, out, rows_out, extra_out):
    rows = [table[c, pl.ds(step[0], 1), :] for c in range(3)]
    widened = states[...].astype(jnp.float32)
    centered = widened - jnp.mean(widened, axis=-1, keepdims=True)
    inv_std = lax.rsqrt(jnp.mean(centered * centered, axis=-1, keepdims=True) + 1e-06)
    half, width = states.shape
    out[:, :width] = (centered * inv_std * (1.0 + rows[1]) + rows[0]).astype(jnp.bfloat16)
    for c in range(3):
        rows_out[c : c + 1, :] = rows[c]
    squares = jnp.sum(adjoint[...] * adjoint[...], axis=0, keepdims=True)
    squares = jnp.sum(squares, axis=1, keepdims=True)
    terms = []
    for n in range(3):
        terms.append(squares.astype(jnp.bfloat16).astype(jnp.float32))
        squares = squares - terms[-1]
    lane = lax.broadcasted_iota(jnp.int32, (8, EXTRA), 1)
    sums = jnp.where(lane == 0, terms[0], jnp.where(lane == 1, terms[1], jnp.where(lane == 2, terms[2], 0.0)))
    extra = extra_columns(text_columns(text, 0) + [sums], half)
    out[:, width:] = extra
    extra_out[...] = extra


def first_call(step, core, states, table, adjoint, text):
    rows, width = states.shape
    half = rows // 2
    whole = lambda *shape: pl.BlockSpec(shape, lambda i, step, core: (0,) * len(shape))
    return pl.pallas_call(
        first_kernel,
        out_shape=(
            jax.ShapeDtypeStruct((half, width + EXTRA), jnp.bfloat16),
            jax.ShapeDtypeStruct((8, width), jnp.float32),
            jax.ShapeDtypeStruct((half, EXTRA), jnp.bfloat16),
        ),
        grid_spec=pltpu.PrefetchScalarGridSpec(
            num_scalar_prefetch=2,
            grid=(1,),
            in_specs=[
                pl.BlockSpec((half, width), lambda i, step, core: (core[0], 0)),
                whole(*table.shape),
                whole(*adjoint.shape),
                whole(*text.shape),
            ],
            out_specs=(whole(half, width + EXTRA), whole(8, width), whole(half, EXTRA)),
        ),
        compiler_params=pltpu.CompilerParams(vmem_limit_bytes=GRANT),
        cost_estimate=pl.CostEstimate(flops=8 * half * width, bytes_accessed=16 * half * width, transcendentals=0),
    )(step, core, states, table, adjoint, text)


def pick_half(core, rows):
    half = rows.shape[1] // 2
    return jnp.where(core == 0, rows[:, :half], rows[:, half:])


def cotangent_kernel(limit, core, adjoint, table_rows, text, extra, previous, following, opposite, out, clip_out):
    first = previous.shape[0] - opposite.shape[0]
    row = 8 * (text.shape[2] // EXTRA)
    squares = opposite[...].astype(jnp.float32)[row - first : row - first + 1, :]
    for terms in (extra, previous, following):
        squares = squares + terms[...].astype(jnp.float32)[row : row + 1, :]
    squares = jnp.sum(squares, axis=1, keepdims=True)
    clip_scale = jnp.minimum(1.0, limit / jnp.sqrt(squares + 1e-06))
    half, width = adjoint.shape
    out[:, :width] = (table_rows[2:3, :] * (clip_scale * adjoint[...])).astype(jnp.bfloat16)
    out[:, width:] = extra_columns(text_columns(text, 1), half)
    clip_out[...] = jnp.broadcast_to(clip_scale, clip_out.shape)


def cotangent_call(limit, core, adjoint, table_rows, text, extra, previous, following, opposite):
    rows, width = adjoint.shape
    half = rows // 2
    block = width // EXTRA
    whole = lambda one: pl.BlockSpec(one.shape, lambda i, core: (0,) * one.ndim)
    tail = lambda one: pl.BlockSpec((one.shape[0], EXTRA), lambda i, core: (0, block))
    outs = (
        jax.ShapeDtypeStruct((half, width + EXTRA), jnp.bfloat16),
        jax.ShapeDtypeStruct((8, EXTRA), jnp.float32),
    )
    return pl.pallas_call(
        functools.partial(cotangent_kernel, limit),
        out_shape=outs,
        grid_spec=pltpu.PrefetchScalarGridSpec(
            num_scalar_prefetch=1,
            grid=(1,),
            in_specs=[pl.BlockSpec((half, width), lambda i, core: (core[0], 0))]
            + [whole(table_rows), whole(text), whole(extra)]
            + [tail(one) for one in (previous, following, opposite)],
            out_specs=tuple(whole(one) for one in outs),
        ),
        compiler_params=pltpu.CompilerParams(vmem_limit_bytes=GRANT),
        cost_estimate=pl.CostEstimate(flops=4 * half * width, bytes_accessed=6 * half * width, transcendentals=0),
    )(core, adjoint, table_rows, text, extra, previous, following, opposite)


def own_kernel(
    core, states, adjoint, table_rows, text, extra, clip, out, cot_out, normed_out, stretch_out, inv_out, base_out
):
    rows, width = states.shape
    half = rows // 2
    widened = states[...].astype(jnp.float32)
    centered = widened - jnp.mean(widened, axis=-1, keepdims=True)
    inv_std = lax.rsqrt(jnp.mean(centered * centered, axis=-1, keepdims=True) + 1e-06)
    normed = centered * inv_std
    scale = 1.0 + table_rows[1:2, :]
    out[:, :width] = (normed * scale + table_rows[0:1, :]).astype(jnp.bfloat16)
    normed_out[...] = pick_half(core[0], normed)
    stretch_out[...] = pick_half(core[0], scale)
    inv_out[...] = jnp.broadcast_to(inv_std, inv_out.shape)
    clipped = clip[0:1, 0:1] * adjoint[...]
    cot_out[:, :width] = (table_rows[2:3, :] * clipped).astype(jnp.bfloat16)
    base_out[...] = pick_half(core[0], clipped)
    columns = extra_columns(text_columns(text, 1), half)
    for n in range(2):
        out[n * half : (n + 1) * half, width:] = extra[...]
        cot_out[n * half : (n + 1) * half, width:] = columns


class Copies:
    def __init__(self, sems):
        self.sems = sems
        self.count = 0

    def start(self, source, target):
        copy = pltpu.make_async_copy(source, target, self.sems.at[self.count])
        copy.start()
        self.count += 1
        return copy

    def weights(self, scalars, w_in, w_all, shard, first=0):
        columns = w_in[0].shape[1] - first
        return [
            self.start(
                piece.at[:, pl.ds(first, columns)],
                w_all.at[
                    pl.ds(pl.multiple_of(scalars[1 + n % 4] * shard, 16), shard),
                    pl.ds(n // 4 * columns, columns),
                ],
            )
            for n, piece in enumerate(w_in)
        ]

    def rows(self, core, pieces, target, rows):
        half = rows // 2
        copies = [self.start(pieces[0], target.at[pl.ds(0, rows)])]
        places = [(rows, half), (3 * rows, half)]
        parts = (len(pieces) - 5) // 2
        places += [(2 * rows + n * half // parts, half // parts) for n in range(parts)]
        for n, (first, size) in enumerate(places):
            for m, holder in enumerate((core, 1 - core)):
                there = pl.ds(pl.multiple_of(first + holder * half, 16), size)
                copies.append(self.start(pieces[1 + 2 * n + m], target.at[there]))
        return copies


def window_heads(scalars, count, rows, text_dev, gathered, width, extra, text, text_t=None):
    half = rows // 2
    for k in range(count):
        there = pl.ds(pl.multiple_of(k * rows + scalars[0] * half, 16), half)
        extra[k] = gathered[there, width:].astype(jnp.float32)
    for i in range(text.shape[0]):
        head = scalars[5] + i
        first = pl.ds(pl.multiple_of(head // 2 * text_dev, 8), text_dev)
        found = jnp.concatenate([extra[k, first, :] for k in range(count)], axis=0)
        found = jnp.where(head % 2 == 0, found[:, :HD], found[:, HD:])
        text[i] = found.astype(jnp.bfloat16)
        if text_t is not None:
            text_t[i] = found.T.astype(jnp.bfloat16)


def project_kernel(slots, count, rows, shard, width, text_dev, scalars, gain, *refs):
    refs = list(refs)
    take = lambda n: [refs.pop(0) for _ in range(n)]
    mod_in = take(9)
    w_in = take(8)
    qkv, k_t, raw_all, inv_all, text, text_t, w_keep, w_give = take(8)
    w_all, mod_all, sems, extra, qkv_s, k_t_s, raw_s, inv_s = take(8)
    inner = slots * HD
    core = scalars[0]
    copies = Copies(sems)
    w_copies = copies.weights(scalars, w_in, w_all, shard)
    row_copies = copies.rows(core, mod_in, mod_all, rows)

    lane = lax.broadcasted_iota(jnp.int32, (1, 2 * inner), 1)
    gains = head_gains(gain, slots) * jnp.where(lane < inner, HD ** (-0.5), 1.0)
    identity = equal_blocks(inner, 1)
    for copy in w_copies:
        copy.wait()
    half = width // 2
    columns = pl.ds(0, w_keep.shape[1])
    out_copies = []
    for holder, target in ((core, w_keep), (1 - core, w_give)):
        source = w_all.at[pl.ds(pl.multiple_of(holder * half, 16), half), columns]
        out_copies.append(copies.start(source, target))
    for copy in row_copies:
        copy.wait()
    projected = jnp.dot(mod_all[:, :width], w_all[:, : 3 * inner], preferred_element_type=jnp.float32)
    raw = projected[:, : 2 * inner]
    raw_s[...] = raw
    out_copies.append(copies.start(raw_s, raw_all))
    inverse = lax.rsqrt(head_means(raw * raw) + 1e-06)
    inv_s[...] = inverse
    out_copies.append(copies.start(inv_s, inv_all))
    qkv_s[:, : 2 * inner] = (raw * inverse * gains).astype(jnp.bfloat16)
    qkv_s[:, 2 * inner :] = projected[:, 2 * inner :].astype(jnp.bfloat16)
    out_copies.append(copies.start(qkv_s, qkv))
    k_t_s[...] = dot(identity, qkv_s[:, inner : 2 * inner], NT).astype(jnp.bfloat16)
    out_copies.append(copies.start(k_t_s, k_t))
    window_heads(scalars, count, rows, text_dev, mod_all, width, extra, text, text_t)
    for copy in out_copies:
        copy.wait()


def attend_kernel(slots, count, rows, shard, width, text_dev, first_column, scalars, gain, *refs):
    refs = list(refs)
    take = lambda n: [refs.pop(0) for _ in range(n)]
    projected = take(8)
    cot_in = take(7)
    w_in = take(4)
    mine_out, theirs_out, rest_out = take(3)
    w_out, cot_all, sems, extra, values_text = take(5)
    d_all, grads, stacked = take(3)
    qkv, k_t, raw_all, inv_all, text, text_t, w_keep, w_give = refs
    inner = slots * HD
    tokens = rows * count
    core = scalars[0]
    copies = Copies(sems)
    w_copies = copies.weights(scalars, w_in, w_out, shard, first_column)
    row_copies = copies.rows(core, cot_in, cot_all, rows)
    pairs = list(zip(projected, refs))
    local_copies = [copies.start(*pairs[n]) for n in (0, 1, 4, 5)]
    score_scale = HD ** (-0.5)
    span = 2 * rows

    text_rows = count * text_dev
    row = lax.broadcasted_iota(jnp.int32, (text_rows, span), 0)
    text_id = row
    for k in range(count):
        inside = (row >= k * text_dev) & (row < (k + 1) * text_dev)
        text_id = jnp.where(inside, row + (scalars[7 + k] - k) * text_dev, text_id)
    bias = jnp.where(text_id < scalars[6], 0.0, -1e30)

    for copy in w_copies:
        copy.wait()
    for copy in row_copies:
        copy.wait()
    out_grad = jnp.dot(cot_all[:, :width], w_out[...], preferred_element_type=jnp.float32)
    d_all[...] = out_grad.astype(jnp.bfloat16)
    window_heads(scalars, count, rows, text_dev, cot_all, width, extra, values_text)
    late_copies = [copies.start(*pairs[n]) for n in (2, 3, 6, 7)]
    for copy in local_copies:
        copy.wait()

    d_first = d_all.shape[1] - inner
    for i in range(slots):
        columns = [slice(n * inner + i * HD, n * inner + (i + 1) * HD) for n in range(3)]
        keys, values = qkv[:, columns[1]], qkv[:, columns[2]]
        keys_t = k_t[i * HD : (i + 1) * HD, :]
        grad_k, grad_v = 0.0, 0.0
        for b in range(count // 2):
            here = slice(b * span, (b + 1) * span)
            query = qkv[here, columns[0]]
            grad = d_all[here, d_first + i * HD : d_first + (i + 1) * HD]
            scores = dot(keys, query, NT)
            text_scores = dot(text[i], query, NT) + bias
            col_max = jnp.maximum(
                jnp.max(scores, axis=0, keepdims=True), jnp.max(text_scores, axis=0, keepdims=True)
            )
            exps = jnp.exp(scores - col_max)
            text_exps = jnp.exp(text_scores - col_max)
            total = jnp.sum(exps, axis=0, keepdims=True) + jnp.sum(text_exps, axis=0, keepdims=True)
            inverse = 1.0 / total
            grad_w = dot(values, grad, NT)
            text_grad_w = dot(values_text[i], grad, NT)
            delta = inverse * (
                jnp.sum(exps * grad_w, axis=0, keepdims=True)
                + jnp.sum(text_exps * text_grad_w, axis=0, keepdims=True)
            )
            weights = exps * inverse
            grad_s = (weights * (grad_w - delta)).astype(jnp.bfloat16)
            text_grad_s = (text_exps * inverse * (text_grad_w - delta)).astype(jnp.bfloat16)
            grad_k += dot(grad_s, query, NN)
            grad_v += dot(weights.astype(jnp.bfloat16), grad, NN)
            grad_q = dot(keys_t, grad_s, NN) + dot(text_t[i], text_grad_s, NN)
            grads[here, columns[0]] = grad_q.T * score_scale
        grads[:, columns[1]] = grad_k
        grads[:, columns[2]] = grad_v

    lane = lax.broadcasted_iota(jnp.int32, (1, inner), 1)
    mine = jnp.zeros((1, inner), jnp.float32)
    for i in range(slots):
        inside = (lane >= i * HD) & (lane < (i + 1) * HD) & (scalars[7 + count + i] > 0)
        mine = jnp.where(inside, 1.0, mine)
    gains = head_gains(gain, slots)
    for copy in late_copies[:2]:
        copy.wait()
    for b in range(count // 2):
        here = slice(b * span, (b + 1) * span)
        scaled = grads[here, : 2 * inner].astype(jnp.bfloat16).astype(jnp.float32) * gains
        raw, inverse = raw_all[here, :], inv_all[here, :]
        back = scaled * inverse - raw * head_means(scaled * raw) * (inverse * inverse * inverse)
        valid = jnp.concatenate([mine, mine], axis=1) > 0.0
        stacked[here, : 2 * inner] = jnp.where(valid, back, 0.0).astype(jnp.bfloat16)
        back = jnp.where(mine > 0.0, grads[here, 2 * inner :], 0.0).astype(jnp.bfloat16)
        stacked[here, 2 * inner : 3 * inner] = back
    stacked[:, 3 * inner :] = jnp.zeros((tokens, stacked.shape[1] - 3 * inner), jnp.bfloat16)
    first = stacked[rows : 2 * rows, :]
    rest_out[: (count - 2) * rows, :] = stacked[2 * rows :, :]
    rest_out[(count - 2) * rows :, :] = stacked[:rows, :]
    for copy in late_copies[2:]:
        copy.wait()
    theirs_out[...] = dot(first, w_give[...], NT).astype(jnp.bfloat16)
    mine_out[...] = dot(first, w_keep[...], NT)


def project_call(scalars, gain, mod, weights, slots, rows, text_dev, count):
    shard = weights[0].shape[0]
    columns = 4 * slots * HD
    width = mod[0].shape[1] - EXTRA
    tokens = rows * count
    text_rows = text_dev * count
    f32, bf16 = jnp.float32, jnp.bfloat16
    vmem, hbm = spec(pltpu.VMEM), spec(pl.ANY)
    inner = slots * HD
    shapes = [((tokens, 3 * inner), bf16), ((inner, tokens), bf16)] + [((tokens, 2 * inner), f32)] * 2
    shapes += [((slots, text_rows, HD), bf16), ((slots, HD, text_rows), bf16)]
    shapes += [((width // 2, whole_tiles(3 * slots * HD)), bf16)] * 2
    return pl.pallas_call(
        functools.partial(project_kernel, slots, count, rows, shard, width, text_dev),
        out_shape=tuple(jax.ShapeDtypeStruct(*one) for one in shapes),
        in_specs=[spec(pltpu.SMEM), vmem] + [hbm] * (len(mod) + len(weights)),
        out_specs=(hbm,) * 4 + (vmem,) * 2 + (hbm,) * 2,
        scratch_shapes=[
            pltpu.VMEM((width, columns), bf16),
            pltpu.VMEM((tokens, width + EXTRA), bf16),
            pltpu.SemaphoreType.DMA((len(mod) + len(weights) + 10,)),
            pltpu.VMEM((count, rows // 2, EXTRA), f32),
        ]
        + [pltpu.VMEM(*one) for one in shapes[:4]],
        compiler_params=pltpu.CompilerParams(vmem_limit_bytes=GRANT),
        cost_estimate=pl.CostEstimate(
            flops=2 * tokens * width * 3 * slots * HD,
            bytes_accessed=2 * (tokens * width + columns * width) + 4 * tokens * columns,
            transcendentals=0,
        ),
    )(scalars, gain, *mod, *weights)


def attend_call(scalars, gain, operands, cot, weights, slots, rows, text_dev):
    count = operands[0].shape[0] // rows
    shard, columns = weights[0].shape
    width = cot[0].shape[1] - EXTRA
    tokens = rows * count
    inner = slots * HD
    stacked = whole_tiles(3 * inner)
    first = (columns - inner) // 128 * 128
    f32, bf16 = jnp.float32, jnp.bfloat16
    vmem, hbm = spec(pltpu.VMEM), spec(pl.ANY)
    shapes = [((rows, width // 2), f32), ((rows, width // 2), bf16), ((tokens - rows, stacked), bf16)]
    return pl.pallas_call(
        functools.partial(attend_kernel, slots, count, rows, shard, width, text_dev, first),
        out_shape=tuple(jax.ShapeDtypeStruct(*one) for one in shapes),
        in_specs=[spec(pltpu.SMEM), vmem] + [hbm] * (len(operands) + len(cot) + len(weights)),
        out_specs=(vmem,) * len(shapes),
        scratch_shapes=[
            pltpu.VMEM((width, columns - first), bf16),
            pltpu.VMEM((tokens, width + EXTRA), bf16),
            pltpu.SemaphoreType.DMA((len(operands) + len(cot) + len(weights),)),
            pltpu.VMEM((count, rows // 2, EXTRA), f32),
            pltpu.VMEM((slots, text_dev * count, HD), bf16),
            pltpu.VMEM((tokens, columns - first), bf16),
            pltpu.VMEM((tokens, 3 * inner), f32),
            pltpu.VMEM((tokens, stacked), bf16),
        ]
        + [pltpu.VMEM(one.shape, one.dtype) for one in operands],
        compiler_params=pltpu.CompilerParams(vmem_limit_bytes=GRANT),
        cost_estimate=pl.CostEstimate(
            flops=2 * tokens * width * inner + 10 * tokens * tokens * inner,
            bytes_accessed=2 * (tokens * width + columns * width),
            transcendentals=slots * tokens * tokens,
        ),
    )(scalars, gain, *operands, *cot, *weights)


def backward_kernel(own, other, w_own, w_other, *outs):
    total = dot(own[...], w_own[...], NT) + dot(other[...], w_other[...], NT)
    part = outs[0].shape[0]
    for n, out in enumerate(outs):
        out[...] = total[n * part : (n + 1) * part].astype(out.dtype)


def backward_call(own, other, w_own, w_other, part, dtype):
    rows, inner = own.shape
    half = w_own.shape[0]
    vmem = spec(pltpu.VMEM)
    return pl.pallas_call(
        backward_kernel,
        out_shape=(jax.ShapeDtypeStruct((part, half), dtype),) * (rows // part),
        in_specs=[vmem] * 4,
        out_specs=(vmem,) * (rows // part),
        compiler_params=pltpu.CompilerParams(vmem_limit_bytes=SMALL_GRANT),
        cost_estimate=pl.CostEstimate(
            flops=4 * rows * half * inner,
            bytes_accessed=4 * (rows + half) * inner + 4 * rows * half,
            transcendentals=0,
        ),
    )(own, other, w_own, w_other)


def sums_kernel(own_near, own_far, near, far, scale, normed, grad_out, sums_out):
    half = near.shape[0]
    for part, (own, moving) in enumerate(((own_near, near), (own_far, far))):
        here = slice(part * half, (part + 1) * half)
        grad = (own[...] + moving[...].astype(jnp.float32)) * scale[...]
        grad_out[here, :] = grad
        first = jnp.sum(grad, axis=-1, keepdims=True)
        second = jnp.sum(grad * normed[here, :], axis=-1, keepdims=True)
        lane = lax.broadcasted_iota(jnp.int32, (half, 128), 1)
        sums_out[here, :] = jnp.where(lane == 0, first, second)


def last_kernel(width, grad, sums, other, normed, base, inv_std, out):
    total = (sums[...] + other[...]) * (1.0 / width)
    rows = base[...] + inv_std[:, 0:1] * (
        grad[...] - total[:, 0:1] - normed[...] * total[:, 1:2]
    )
    out[...] = rows.T


def local_call(kernel, shapes, scalar_count, *operands, grant=SMALL_GRANT):
    vmem = spec(pltpu.VMEM)
    return pl.pallas_call(
        kernel,
        out_shape=tuple(jax.ShapeDtypeStruct(*one) for one in shapes),
        in_specs=[spec(pltpu.SMEM)] * scalar_count + [vmem] * (len(operands) - scalar_count),
        out_specs=(vmem,) * len(shapes),
        compiler_params=pltpu.CompilerParams(vmem_limit_bytes=grant),
        cost_estimate=pl.CostEstimate(
            flops=sum(one.size for one in operands),
            bytes_accessed=sum(one.size * one.dtype.itemsize for one in operands),
            transcendentals=0,
        ),
    )(*operands)


def shards_by_head(states, adjoint, text_kv, text_len, step_index, modulation, w_qkv, qk_gain, w_out):
    hidden_state = states[0]
    adjoint_rows = adjoint[0]
    tok_count, model_width = hidden_state.shape
    seq_count = lax.axis_size("seq")
    inner_dev = w_qkv.shape[2]
    heads_dev = inner_dev // HD
    shard = w_qkv.shape[0]
    slots = -(-heads_dev // seq_count)
    inner = slots * HD
    half_rows = tok_count // 2
    half_width = model_width // 2
    f32, bf16 = jnp.float32, jnp.bfloat16
    core = lax.axis_index("head").astype(jnp.int32)
    seq_index = lax.axis_index("seq")
    dp_index = lax.axis_index("dp")
    pin = lax.optimization_barrier

    seq_order = line_ring(seq_count)
    seq_place = ring_place(seq_order, seq_index)
    seq_next = ring_pairs(seq_order)
    swap = [(0, 1), (1, 0)]
    first_way = [(2 * p + c, 2 * (p ^ (1 + c)) + c) for p in range(4) for c in range(2)]
    second_way = [(2 * p + c, 2 * (p ^ (2 - c)) + c) for p in range(4) for c in range(2)]

    first = seq_index * heads_dev // seq_count
    stop = (seq_index + 1) * heads_dev // seq_count
    window = jnp.minimum(first, heads_dev - slots)
    valid = [(window + i >= first) & (window + i < stop) for i in range(slots)]
    owners = [ring_member(seq_order, (seq_place - k + seq_count) % seq_count) for k in range(seq_count)]
    w_index = [dp_index, dp_index ^ (1 + core), dp_index ^ (2 - core), dp_index ^ 3]
    scalars = [core] + w_index + [window, text_len[0]] + owners + valid
    scalars = jnp.stack([one.astype(jnp.int32) for one in scalars])

    def step(moving):
        return lax.ppermute(moving, "seq", seq_next)

    def other_core(moving):
        return lax.ppermute(moving, "head", swap)

    def step_back(moving):
        return lax.ppermute(moving, "seq", [(b, a) for a, b in seq_next])

    quarter = half_rows // 2

    def spread(moving):
        return [step(moving), step_back(moving)]

    def pass_on(received):
        return [step(received[0][:quarter]), step_back(received[1][quarter:])]

    mod_half, table_rows, extra = first_call(
        step_index, core[None], hidden_state, modulation.transpose(1, 0, 2), adjoint_rows, text_kv[0]
    )
    mod_near = spread(mod_half)

    w_qkv, w_out, mod_half = pin((w_qkv, w_out, mod_half))
    take = lambda c: lax.dynamic_slice(w_qkv, (0, c, window * HD), (shard, 1, inner))[:, 0]
    own_w = [
        jnp.concatenate([take(0), take(1)], axis=1),
        jnp.concatenate([take(2), lax.dynamic_slice_in_dim(w_out, window * HD, inner, 0).T], axis=1),
    ]
    w_first = [lax.ppermute(part, ("dp", "head"), first_way) for part in own_w]
    w_second = [lax.ppermute(part, ("dp", "head"), second_way) for part in own_w]

    text_dev = text_kv.shape[1]
    mod_far = pass_on(mod_near)
    clip_limit = 0.5 * (tok_count * seq_count * model_width) ** 0.5
    extra, *w_first = pin((extra, *w_first))
    cot_half, clip = cotangent_call(
        clip_limit, scalars, adjoint_rows, table_rows, text_kv[0], extra, *mod_near, mod_far[1]
    )
    cot_half, mod_far[0] = pin((cot_half, mod_far[0]))
    cot_near = spread(cot_half)
    modulated, cotangent, normed_share, scale_share, inv_std, base = local_call(
        own_kernel,
        [((tok_count, model_width + EXTRA), bf16)] * 2
        + [
            ((tok_count, half_width), f32),
            ((1, half_width), f32),
            ((tok_count, 128), f32),
            ((tok_count, half_width), f32),
        ],
        1,
        core[None],
        hidden_state,
        adjoint_rows,
        table_rows,
        text_kv[0],
        extra,
        clip,
        grant=GRANT,
    )
    def pieces(own, received):
        return [own] + [one for moved in received for one in (moved, other_core(moved))]

    mod_far = list(pin((*mod_far, modulated))[:2])
    mod_pieces = pieces(modulated, mod_near + mod_far)
    w_diagonal = [lax.ppermute(part, ("dp", "head"), second_way) for part in w_first]
    weights = [part[n] for n in range(2) for part in (own_w, w_first, w_second, w_diagonal)]
    cot_near[0] = pin((cot_near[0], w_second, w_diagonal))[0]
    cot_far = [step(cot_near[0])]

    cot_pieces = pieces(cotangent, cot_near)
    *cot_pieces, mod_pieces[-1] = pin((*cot_pieces, mod_pieces[-1]))
    *operands, w_keep, w_give = project_call(
        scalars, qk_gain, mod_pieces, weights, slots, tok_count, text_dev, seq_count
    )
    w_give, cot_far[0] = pin((w_give, *cot_far))
    cot_pieces += pieces(None, cot_far)[1:]
    given, *cot_pieces = pin((w_give, *cot_pieces))
    w_other = other_core(given)
    mine, theirs, rest = attend_call(
        scalars, qk_gain, operands + [w_keep, w_give], cot_pieces, weights[4:], slots, tok_count, text_dev
    )
    first = (mine + other_core(theirs).astype(f32)).astype(bf16)
    moving = [first[:half_rows], first[half_rows:]]
    other_rest = other_core(rest)
    rest, other_rest, *_ = pin((rest, other_rest, *moving))
    own = backward_call(rest, other_rest, w_keep, w_other, half_rows, f32)
    for j in range(2, seq_count):
        moving = [step(part) for part in moving]
        moving = [
            (a + b.astype(f32)).astype(bf16) for a, b in zip(own[2 * (j - 2) : 2 * (j - 1)], moving)
        ]
    moving = [step(part) for part in moving]

    grad_scaled, sums = local_call(
        sums_kernel,
        [((tok_count, half_width), f32), ((tok_count, 128), f32)],
        0,
        *own[-2:],
        *moving,
        scale_share,
        normed_share,
    )
    (pulled,) = local_call(
        functools.partial(last_kernel, model_width),
        [((half_width, tok_count), f32)],
        0,
        grad_scaled,
        sums,
        other_core(sums),
        normed_share,
        base,
        inv_std,
    )
    return pulled.T[None]


def qk_normalize(values, gains):
    inverse = lax.rsqrt(jnp.mean(values * values, axis=-1, keepdims=True) + 1e-06)
    return ((values * inverse * gains).astype(jnp.bfloat16), inverse)


def qk_backward(values, inverse, cotangent, gains):
    scaled = cotangent.astype(jnp.float32) * gains
    return (
        scaled * inverse - values * jnp.mean(scaled * values, axis=-1, keepdims=True) * inverse**3
    )


def shards_by_row(states, adjoint, text_kv, text_len, step_index, modulation, w_qkv, qk_gain, w_out):
    hidden_state = states[0]
    adjoint_rows = adjoint[0]
    tok_count, model_width = hidden_state.shape
    seq_count = lax.axis_size("seq")
    inner_dev = w_qkv.shape[2]
    heads_dev = inner_dev // HD
    score_scale = HD ** (-0.5)
    squares = lax.psum(jnp.sum(adjoint_rows * adjoint_rows), "seq")
    clip_limit = 0.5 * (tok_count * seq_count * model_width) ** 0.5
    clip_scale = jnp.minimum(1.0, clip_limit / jnp.sqrt(squares + 1e-06))
    table_row = lax.dynamic_index_in_dim(modulation, step_index[0], 0, keepdims=False)
    offset_row = table_row[0]
    stretch = table_row[1]
    gating = table_row[2]
    widened = hidden_state.astype(jnp.float32)
    centered = widened - jnp.mean(widened, axis=-1, keepdims=True)
    inv_std = lax.rsqrt(jnp.mean(centered * centered, axis=-1, keepdims=True) + 1e-06)
    normed = centered * inv_std
    modulated = (normed * (1.0 + stretch) + offset_row).astype(jnp.bfloat16)
    cotangent = (gating * (clip_scale * adjoint_rows)).astype(jnp.bfloat16)
    contract_last = (((1,), (1,)), ((), ()))
    full_weight = lax.all_gather(w_qkv, "dp", axis=0, tiled=True).reshape(
        model_width, 3 * inner_dev
    )
    projected = jnp.dot(modulated, full_weight, preferred_element_type=jnp.float32)
    out_raw = lax.dot_general(
        cotangent,
        lax.all_gather(w_out, "dp", axis=1, tiled=True),
        contract_last,
        preferred_element_type=jnp.float32,
    )
    projected = projected.reshape(tok_count, 3, heads_dev, HD)
    queries, query_inv = qk_normalize(projected[:, 0], qk_gain[0])
    own_keys, key_inv = qk_normalize(projected[:, 1], qk_gain[1])
    own_values = projected[:, 2].astype(jnp.bfloat16)
    out_grad = out_raw.astype(jnp.bfloat16).reshape(tok_count, heads_dev, HD)
    text_keys = text_kv[0, :, 0, :]
    text_values = text_kv[0, :, 1, :]
    text_dev = text_keys.shape[0]
    rows_dev = tok_count + text_dev
    key_local = jnp.concatenate([own_keys.reshape(tok_count, inner_dev), text_keys], axis=0)
    value_local = jnp.concatenate([own_values.reshape(tok_count, inner_dev), text_values], axis=0)
    key_all, value_all = (
        lax.all_gather(key_local, "seq", axis=0, tiled=True),
        lax.all_gather(value_local, "seq", axis=0, tiled=True),
    )
    all_rows = rows_dev * seq_count
    row_ids = jnp.arange(all_rows, dtype=jnp.int32)
    owner = row_ids // rows_dev
    within = row_ids % rows_dev
    allowed = (within < tok_count) | (owner * text_dev + within - tok_count < text_len[0])
    group = 1
    while group * 2 * rows_dev <= 512 and seq_count % (group * 2) == 0:
        group = group * 2
    block_rows = group * rows_dev
    block_count = all_rows // block_rows
    key_blocks = key_all.reshape(block_count, block_rows, heads_dev, HD)
    value_blocks = value_all.reshape(block_count, block_rows, heads_dev, HD)
    mask_blocks = allowed.reshape(block_count, block_rows)

    def block_scores(key_block, mask_block):
        scores = (
            jnp.einsum("qhd,khd->qhk", queries, key_block, preferred_element_type=jnp.float32)
            * score_scale
        )
        return jnp.where(mask_block[None, None, :], scores, -1e30)

    def first_pass(carry, block):
        row_max, row_sum, row_dot = carry
        key_block, value_block, mask_block = block
        scores = block_scores(key_block, mask_block)
        new_max = jnp.maximum(row_max, jnp.max(scores, axis=-1))
        rescale = jnp.exp(row_max - new_max)
        exps = jnp.exp(scores - new_max[:, :, None])
        grad_weights = jnp.einsum(
            "qhd,khd->qhk", out_grad, value_block, preferred_element_type=jnp.float32
        )
        return (
            (
                new_max,
                row_sum * rescale + jnp.sum(exps, axis=-1),
                row_dot * rescale + jnp.sum(exps * grad_weights, axis=-1),
            ),
            None,
        )

    start_state = (
        jnp.full((tok_count, heads_dev), -1e30, jnp.float32),
        jnp.zeros((tok_count, heads_dev), jnp.float32),
        jnp.zeros((tok_count, heads_dev), jnp.float32),
    )
    (row_max, row_sum, row_dot), unused = lax.scan(
        first_pass, start_state, (key_blocks, value_blocks, mask_blocks)
    )
    log_total = row_max + jnp.log(row_sum)
    delta_row = row_dot / row_sum

    def second_pass(running, block):
        key_block, value_block, mask_block = block
        weights = jnp.exp(block_scores(key_block, mask_block) - log_total[:, :, None])
        grad_weights = jnp.einsum(
            "qhd,khd->qhk", out_grad, value_block, preferred_element_type=jnp.float32
        )
        grad_scores = (weights * (grad_weights - delta_row[:, :, None])).astype(jnp.bfloat16)
        return (
            running
            + jnp.einsum(
                "qhk,khd->qhd", grad_scores, key_block, preferred_element_type=jnp.float32
            ),
            None,
        )

    query_sum, unused = lax.scan(
        second_pass,
        jnp.zeros((tok_count, heads_dev, HD), jnp.float32),
        (key_blocks, value_blocks, mask_blocks),
    )
    grad_query = (query_sum * score_scale).astype(jnp.bfloat16)
    log_all, delta_all = (
        lax.all_gather(log_total, "seq", axis=0, tiled=True),
        lax.all_gather(delta_row, "seq", axis=0, tiled=True),
    )
    local_ids = jnp.arange(rows_dev, dtype=jnp.int32)
    local_allowed = (local_ids < tok_count) | (
        lax.axis_index("seq") * text_dev + local_ids - tok_count < text_len[0]
    )
    key_three = key_local.reshape(rows_dev, heads_dev, HD)
    value_three = value_local.reshape(rows_dev, heads_dev, HD)
    query_piece = lax.all_gather(queries.reshape(tok_count, inner_dev), "seq", axis=0, tiled=True)
    grad_piece = lax.all_gather(out_grad.reshape(tok_count, inner_dev), "seq", axis=0, tiled=True)
    piece_rows = query_piece.shape[0]
    query_rows = query_piece.reshape(piece_rows, heads_dev, HD)
    grad_rows = grad_piece.reshape(piece_rows, heads_dev, HD)
    scores = (
        jnp.einsum("qhd,khd->qhk", query_rows, key_three, preferred_element_type=jnp.float32)
        * score_scale
    )
    scores = jnp.where(local_allowed[None, None, :], scores, -1e30)
    weights = jnp.exp(scores - log_all[:, :, None])
    grad_weights = jnp.einsum(
        "qhd,khd->qhk", grad_rows, value_three, preferred_element_type=jnp.float32
    )
    grad_scores = (weights * (grad_weights - delta_all[:, :, None])).astype(jnp.bfloat16)
    rounded = weights.astype(jnp.bfloat16)
    key_sum = jnp.einsum(
        "qhk,qhd->khd", grad_scores, query_rows, preferred_element_type=jnp.float32
    )
    value_sum = jnp.einsum("qhk,qhd->khd", rounded, grad_rows, preferred_element_type=jnp.float32)
    key_sum, value_sum = (key_sum, value_sum)
    grad_key = (key_sum[:tok_count] * score_scale).astype(jnp.bfloat16)
    grad_value = value_sum[:tok_count].astype(jnp.bfloat16)
    raw_query = qk_backward(projected[:, 0], query_inv, grad_query, qk_gain[0])
    raw_key = qk_backward(projected[:, 1], key_inv, grad_key, qk_gain[1])
    stacked = jnp.stack([raw_query, raw_key, grad_value.astype(jnp.float32)], axis=1).astype(
        jnp.bfloat16
    )
    stacked = stacked.reshape(tok_count, 3 * inner_dev)
    partial_grad = lax.dot_general(
        stacked, full_weight, contract_last, preferred_element_type=jnp.float32
    )
    half_width = model_width // lax.axis_size("head")
    first_col = lax.axis_index("head") * half_width
    grad_share = lax.psum_scatter(
        partial_grad.astype(jnp.bfloat16), "head", scatter_dimension=1, tiled=True
    ).astype(jnp.float32)
    normed_share = lax.dynamic_slice_in_dim(normed, first_col, half_width, 1)
    stretch_share = lax.dynamic_slice_in_dim(stretch, first_col, half_width, 0)
    adjoint_share = lax.dynamic_slice_in_dim(adjoint_rows, first_col, half_width, 1)
    grad_scaled = grad_share * (1.0 + stretch_share)
    row_sums = jnp.stack(
        [jnp.sum(grad_scaled, axis=-1), jnp.sum(grad_scaled * normed_share, axis=-1)], axis=-1
    )
    row_sums = lax.psum(row_sums, "head")
    grad_state = inv_std * (
        grad_scaled - row_sums[:, 0:1] / model_width - normed_share * row_sums[:, 1:2] / model_width
    )
    pulled = clip_scale * adjoint_share + grad_state
    return pulled[None]


def solution(mesh):
    in_specs = (
        P("dp", "seq", None),
        P("dp", "seq", None),
        P("dp", "seq", None, "head"),
        P("dp"),
        P("dp"),
        P(),
        P("dp", None, "head"),
        P(),
        P("head", "dp"),
    )
    out_specs = P("dp", "seq", "head")
    by_head = mesh.shape["seq"] == 4 and mesh.shape["dp"] == 4 and mesh.shape["head"] == 2
    shards = shards_by_head if by_head else shards_by_row
    return jax.shard_map(shards, mesh=mesh, in_specs=in_specs, out_specs=out_specs, check_vma=False)
```

profile of v0, /device:TPU:0, one launch (start us, length us, event | category | flops | bytes accessed | tf_op | source)
XLA Modules:
  0.0 109.0 jit_solution(11421806895854281847)
XLA Ops:
  0.7 2.8 %shard_map.91 = (bf16[64,2560]{1,0:T(8,128)(2,1)}, f32[8,2432]{1,0:T(8,128)}, bf16[64,128]{1,0:T(8,128)(2,1)}) custom-call(s32[1]{0:T(128)S(6)} %copy.11.step, s32[1]{0:T(128)} %bitcast.core, bf16[128,2432]{1,0:T(8,128)(2,1)} %bitcast.31, f32[3,28,2432]{2,1,0:T(8,128)} %bitcast.33, f32[128,2432]{1,0:T(8,128)} %bitcast.28, bf16[8,2,640]{2,1,0:T(2,128)(2,1)} %bitcast.34), custom_call_target="tpu_custom_call" | custom-call | flops 1245184 | bytes 2490368 | tf_op jit(solution)/shard_map/pallas_call | solution.py:110
  3.6 4.0 %collective-permute-start.3 = (bf16[64,2560]{1,0:T(8,128)(2,1)}, bf16[64,2560]{1,0:T(8,128)(2,1)S(1)}, u32[]{:S(2)}, u32[]{:S(2)}) collective-permute-start(bf16[64,2560]{1,0:T(8,128)(2,1)} %get-tuple-element.65), channel_id=1, source_target_pairs={{2,0},{6,2},{4,6},{0,4},{3,1},{7,3},{5,7},{1,5},{10,8},{14,10},{12... | collective-permute-start | bytes 983048 | tf_op jit(solution)/shard_map/ppermute | solution.py:569
  7.6 1.7 %dynamic-slice_bitcast_fusion.1 = (bf16[608,192]{1,0:T(8,128)(2,1)S(1)}, bf16[608,192]{1,0:T(8,128)(2,1)S(1)}, bf16[608,192]{1,0:T(8,128)(2,1)S(1)}) fusion(bf16[608,3,640]{2,0,1:T(8,128)(2,1)} %param.15, s32[]{:T(128)S(6)} %select_n.103), kind=kLoop, calls=%fused_computation.8 | loop fusion | bytes 1400836 | tf_op jit(solution)/shard_map/squeeze | solution.py:585
  9.3 0.2 dynamic-slice_bitcast_fusion
  9.5 0.2 pad_maximum_fusion.1.refs_13_.refs_15_
  9.7 1.6 %collective-permute-start.1 = (bf16[608,384]{1,0:T(8,128)(2,1)S(1)}, bf16[608,384]{1,0:T(8,128)(2,1)S(1)}, u32[]{:S(2)}, u32[]{:S(2)}) collective-permute-start(bf16[608,384]{1,0:T(8,128)(2,1)S(1)} %pad_maximum_fusion.1.refs_13_.refs_15_), channel_id=1, source_target_pairs={{0,8},{1,17},{8,0},{9,25},{16,24},{17,1},{24,16},{25,9},{2,10},{3,... | collective-permute-start | bytes 1400840 | tf_op jit(solution)/shard_map/ppermute | solution.py:590
  11.2 0.9 pad_maximum_fusion.refs_9_
  12.2 0.5 collective-permute-start
  12.7 1.5 %collective-permute-start.11 = (bf16[608,384]{1,0:T(8,128)(2,1)S(1)}, bf16[608,384]{1,0:T(8,128)(2,1)S(1)}, u32[]{:S(2)}, u32[]{:S(2)}) collective-permute-start(bf16[608,384]{1,0:T(8,128)(2,1)S(1)} %pad_maximum_fusion.1.refs_13_.refs_15_), channel_id=1, source_target_pairs={{0,16},{1,9},{8,24},{9,1},{16,0},{17,25},{24,8},{25,17},{2,18},{3,... | collective-permute-start | bytes 1400840 | tf_op jit(solution)/shard_map/ppermute | solution.py:591
  14.2 1.9 %collective-permute-done.3.following.refs_3_ = bf16[64,2560]{1,0:T(8,128)(2,1)S(1)} collective-permute-done((bf16[64,2560]{1,0:T(8,128)(2,1)}, bf16[64,2560]{1,0:T(8,128)(2,1)S(1)}, u32[]{:S(2)}, u32[]{:S(2)}) %collective-permute-start.3) | collective-permute-done | bytes 327712 | tf_op jit(solution)/shard_map/ppermute | solution.py:569
  16.1 0.7 slice.16
  16.8 3.3 %collective-permute-start.4 = (bf16[32,2560]{1,0:T(8,128)(2,1)}, bf16[32,2560]{1,0:T(8,128)(2,1)S(1)}, u32[]{:S(2)}, u32[]{:S(2)}) collective-permute-start(bf16[32,2560]{1,0:T(8,128)(2,1)} %slice.16), channel_id=1, source_target_pairs={{2,0},{6,2},{4,6},{0,4},{3,1},{7,3},{5,7},{1,5},{10,8},{14,10},{12... | collective-permute-start | bytes 491528 | tf_op jit(solution)/shard_map/ppermute | solution.py:569
  20.1 4.7 %collective-permute-done.2.previous.refs_1_ = bf16[64,2560]{1,0:T(8,128)(2,1)S(1)} collective-permute-done((bf16[64,2560]{1,0:T(8,128)(2,1)}, bf16[64,2560]{1,0:T(8,128)(2,1)S(1)}, u32[]{:S(2)}, u32[]{:S(2)}) %collective-permute-start.2) | collective-permute-done | bytes 327712 | tf_op jit(solution)/shard_map/ppermute | solution.py:563
  24.8 0.7 slice.17
  25.5 0.7 collective-permute-start.7
  26.2 1.5 %collective-permute-start.10 = (bf16[608,384]{1,0:T(8,128)(2,1)}, bf16[608,384]{1,0:T(8,128)(2,1)}, u32[]{:S(2)}, u32[]{:S(2)}) collective-permute-start(bf16[608,384]{1,0:T(8,128)(2,1)} %pad_maximum_fusion.refs_9_), channel_id=1, source_target_pairs={{0,16},{1,9},{8,24},{9,1},{16,0},{17,25},{24,8},{25,17},{2,18},{3,... | collective-permute-start | bytes 1400840 | tf_op jit(solution)/shard_map/ppermute | solution.py:591
  28.4 0.6 stack.67.core.scalars
  29.1 0.7 copy-done.14
  29.7 2.7 %shard_map.92 = (bf16[64,2560]{1,0:T(8,128)(2,1)}, f32[8,128]{1,0:T(8,128)}) custom-call(s32[14]{0:T(128)} %stack.67.core.scalars, f32[128,2432]{1,0:T(8,128)} %bitcast.29, f32[8,2432]{1,0:T(8,128)} %get-tuple-element.63.table_rows, bf16[8,2,640]{2,1,0:T(2,128)(2,1)} %bitcast.35, bf16[64,128]{1,0:T(8,128)(2,1)} %get-tuple-element.68.extra, ...), custom_call_target="tpu_custom_call" | custom-call | flops 622592 | bytes 933888 | tf_op jit(solution)/shard_map/pallas_call | solution.py:162
  32.5 0.3 collective-permute-done.7.refs_5_
  32.8 2.3 %collective-permute-start.15 = (bf16[64,2560]{1,0:T(8,128)(2,1)}, bf16[64,2560]{1,0:T(8,128)(2,1)}, u32[]{:S(2)}, u32[]{:S(2)}) collective-permute-start(bf16[64,2560]{1,0:T(8,128)(2,1)} %get-tuple-element.76), channel_id=1, source_target_pairs={{2,0},{6,2},{4,6},{0,4},{3,1},{7,3},{5,7},{1,5},{10,8},{14,10},{12... | collective-permute-start | bytes 983048 | tf_op jit(solution)/shard_map/ppermute | solution.py:569
  35.0 1.5 %collective-permute-start.12 = (bf16[608,384]{1,0:T(8,128)(2,1)S(1)}, bf16[608,384]{1,0:T(8,128)(2,1)S(1)}, u32[]{:S(2)}, u32[]{:S(2)}) collective-permute-start(bf16[608,384]{1,0:T(8,128)(2,1)S(1)} %collective-permute-done.refs_10_), channel_id=1, source_target_pairs={{0,16},{1,9},{8,24},{9,1},{16,0},{17,25},{24,8},{25,17},{2,18},{3,... | collective-permute-start | bytes 1400840 | tf_op jit(solution)/shard_map/ppermute | solution.py:626
  36.5 0.5 collective-permute-start.13
  37.1 6.5 %collective-permute-done.15.refs_11_ = bf16[64,2560]{1,0:T(8,128)(2,1)} collective-permute-done((bf16[64,2560]{1,0:T(8,128)(2,1)}, bf16[64,2560]{1,0:T(8,128)(2,1)}, u32[]{:S(2)}, u32[]{:S(2)}) %collective-permute-start.15) | collective-permute-done | bytes 327712 | tf_op jit(solution)/shard_map/ppermute | solution.py:569
  43.6 3.7 %shard_map.93 = (bf16[128,2560]{1,0:T(8,128)(2,1)}, bf16[128,2560]{1,0:T(8,128)(2,1)}, f32[128,1216]{1,0:T(8,128)}, f32[1,1216]{1,0:T(1,128)}, f32[128,128]{1,0:T(8,128)}, /*index=5*/f32[128,1216]{1,0:T(8,128)}) custom-call(s32[1]{0:T(128)} %bitcast.core, bf16[128,2432]{1,0:T(8,128)(2,1)} %bitcast.32, f32[128,2432]{1,0:T(8,128)} %bitcast.30, ...), custom_call_target="tpu_custom_call" | custom-call | flops 661505 | bytes 1986564 | tf_op jit(solution)/shard_map/pallas_call | solution.py:514
  47.3 0.6 collective-permute-start.17
  47.9 3.6 %collective-permute-done.9.refs_9_ = bf16[64,2560]{1,0:T(8,128)(2,1)S(1)} collective-permute-done((bf16[64,2560]{1,0:T(8,128)(2,1)}, bf16[64,2560]{1,0:T(8,128)(2,1)S(1)}, u32[]{:S(2)}, u32[]{:S(2)}) %collective-permute-start.9) | collective-permute-done | bytes 327712 | tf_op jit(solution)/shard_map/ppermute | solution.py:563
  51.4 0.1 collective-permute-start.14
  51.5 0.5 collective-permute-start.5
  52.0 0.1 collective-permute-start.6
  52.1 0.2 collective-permute-start.18
  52.3 0.3 collective-permute-start.8
  52.6 0.5 collective-permute-done.14.refs_10_
  53.1 1.1 %collective-permute-done.8.refs_6_ = bf16[32,2560]{1,0:T(8,128)(2,1)S(1)} collective-permute-done((bf16[32,2560]{1,0:T(8,128)(2,1)}, bf16[32,2560]{1,0:T(8,128)(2,1)S(1)}, u32[]{:S(2)}, u32[]{:S(2)}) %collective-permute-start.8) | collective-permute-done | bytes 163872 | tf_op jit(solution)/shard_map/ppermute | solution.py:566
  54.3 0.7 copy-done.24
  55.0 0.7 copy-done.21
  55.7 7.9 %shard_map.94 = (bf16[512,576]{1,0:T(8,128)(2,1)}, bf16[192,512]{1,0:T(8,128)(2,1)}, f32[512,384]{1,0:T(8,128)}, f32[512,384]{1,0:T(8,128)}, bf16[3,32,64]{2,1,0...) custom-call(s32[14]{0:T(128)} %stack.67.core.scalars, ...), custom_call_target="tpu_custom_call" | custom-call | flops 1434451968 | bytes 7798784 | tf_op jit(solution)/shard_map/pallas_call | solution.py:410
  63.6 0.3 collective-permute-start.19
  64.0 1.3 %collective-permute-done.19.refs_14_ = bf16[64,2560]{1,0:T(8,128)(2,1)S(1)} collective-permute-done((bf16[64,2560]{1,0:T(8,128)(2,1)S(1)}, bf16[64,2560]{1,0:T(8,128)(2,1)S(1)}, u32[]{:S(2)}, u32[]{:S(2)}) %collective-permute-start.19) | collective-permute-done | bytes 327712 | tf_op jit(solution)/shard_map/ppermute | solution.py:566
  65.3 0.3 collective-permute-start.22
  65.6 0.4 copy-done.22
  66.0 11.4 %shard_map.95 = (f32[128,1216]{1,0:T(8,128)}, bf16[128,1216]{1,0:T(8,128)(2,1)}, bf16[384,640]{1,0:T(8,128)(2,1)}) custom-call(s32[14]{0:T(128)} %stack.67.core.scalars, f32[2,64]{1,0:T(2,128)} %gain.3, bf16[512,576]{1,0:T(8,128)(2,1)} %get-tuple-element.81.refs_0_, bf16[192,512]{1,0:T(8,128)(2,1)} %get-tuple-element.82.refs_1_, ...), custom_call_target="tpu_custom_call" | custom-call | flops 981467136 | bytes 4358144 | tf_op jit(solution)/shard_map/pallas_call | solution.py:442
  77.5 0.3 collective-permute-start.21
  77.8 0.2 collective-permute-start.20
  78.1 1.3 %collective-permute-done.21 = bf16[128,1216]{1,0:T(8,128)(2,1)S(1)} collective-permute-done((bf16[128,1216]{1,0:T(8,128)(2,1)}, bf16[128,1216]{1,0:T(8,128)(2,1)S(1)}, u32[]{:S(2)}, u32[]{:S(2)}) %collective-permute-start.21) | collective-permute-done | bytes 311328 | tf_op jit(solution)/shard_map/ppermute | solution.py:566
  79.4 1.2 %add_convert_fusion = bf16[128,1216]{1,0:T(8,128)(2,1)S(1)} fusion(f32[128,1216]{1,0:T(8,128)} %get-tuple-element.104, bf16[128,1216]{1,0:T(8,128)(2,1)S(1)} %collective-permute-done.21), kind=kLoop, calls=%fused_computation | loop fusion | flops 466944 | bytes 1245184 | tf_op jit(solution)/shard_map/convert_element_type | solution.py:643
  80.6 1.6 %collective-permute-start.26 = (bf16[64,1216]{1,0:T(8,128)(2,1)S(1)}, bf16[64,1216]{1,0:T(8,128)(2,1)S(1)}, u32[]{:S(2)}, u32[]{:S(2)}) collective-permute-start(bf16[64,1216]{1,0:T(8,128)(2,1)S(1)} %get-tuple-element.124), channel_id=1, source_target_pairs={{0,2},{2,6},{6,4},{4,0},{1,3},{3,7},{7,5},{5,1},{8,10},{10,14},{14... | collective-permute-start | bytes 466952 | tf_op jit(solution)/shard_map/ppermute | solution.py:563
  82.2 0.7 collective-permute-start.23
  82.9 1.0 copy-done.6
  83.9 1.7 %shard_map.96 = (f32[64,1216]{1,0:T(8,128)S(1)}, f32[64,1216]{1,0:T(8,128)S(1)}, f32[64,1216]{1,0:T(8,128)S(1)}, f32[64,1216]{1,0:T(8,128)S(1)}, f32[64,1216]{1,0:T(8,128)S(1)}, /*index=5*/f32[64,1216]{1,0:T(8,128)S(1)}) custom-call(bf16[384,640]{1,0:T(8,128)(2,1)S(1)} %copy-done.6, bf16[384,640]{1,0:T(8,128)(2,1)S(1)} %collective-permute-done.20.other, ...), custom_call_target="tpu_custom_call" | custom-call | flops 1195376640 | bytes 5963776 | tf_op jit(solution)/shard_map/pallas_call | solution.py:478
  85.7 2.9 %collective-permute-done.26 = bf16[64,1216]{1,0:T(8,128)(2,1)S(1)} collective-permute-done((bf16[64,1216]{1,0:T(8,128)(2,1)S(1)}, bf16[64,1216]{1,0:T(8,128)(2,1)S(1)}, u32[]{:S(2)}, u32[]{:S(2)}) %collective-permute-start.26) | collective-permute-done | bytes 155680 | tf_op jit(solution)/shard_map/ppermute | solution.py:563
  88.6 0.7 collective-permute-start.27
  89.3 2.5 %collective-permute-done.23 = bf16[64,1216]{1,0:T(8,128)(2,1)S(1)} collective-permute-done((bf16[64,1216]{1,0:T(8,128)(2,1)S(1)}, bf16[64,1216]{1,0:T(8,128)(2,1)S(1)}, u32[]{:S(2)}, u32[]{:S(2)}) %collective-permute-start.23) | collective-permute-done | bytes 155680 | tf_op jit(solution)/shard_map/ppermute | solution.py:563
  91.9 0.9 collective-permute-start.24
  92.8 2.5 %collective-permute-done.27 = bf16[64,1216]{1,0:T(8,128)(2,1)S(1)} collective-permute-done((bf16[64,1216]{1,0:T(8,128)(2,1)S(1)}, bf16[64,1216]{1,0:T(8,128)(2,1)S(1)}, u32[]{:S(2)}, u32[]{:S(2)}) %collective-permute-start.27) | collective-permute-done | bytes 155680 | tf_op jit(solution)/shard_map/ppermute | solution.py:563
  95.4 1.1 %collective-permute-start.28 = (bf16[64,1216]{1,0:T(8,128)(2,1)S(1)}, bf16[64,1216]{1,0:T(8,128)(2,1)S(1)}, u32[]{:S(2)}, u32[]{:S(2)}) collective-permute-start(bf16[64,1216]{1,0:T(8,128)(2,1)S(1)} %add_convert_fusion.1), channel_id=1, source_target_pairs={{0,2},{2,6},{6,4},{4,0},{1,3},{3,7},{7,5},{5,1},{8,10},{10,14},{14... | collective-permute-start | bytes 466952 | tf_op jit(solution)/shard_map/ppermute | solution.py:563
  96.5 3.5 %collective-permute-done.24 = bf16[64,1216]{1,0:T(8,128)(2,1)S(1)} collective-permute-done((bf16[64,1216]{1,0:T(8,128)(2,1)S(1)}, bf16[64,1216]{1,0:T(8,128)(2,1)S(1)}, u32[]{:S(2)}, u32[]{:S(2)}) %collective-permute-start.24) | collective-permute-done | bytes 155680 | tf_op jit(solution)/shard_map/ppermute | solution.py:563
  100.0 0.1 collective-permute-start.25
  100.1 3.2 %collective-permute-done.28.far = bf16[64,1216]{1,0:T(8,128)(2,1)S(1)} collective-permute-done((bf16[64,1216]{1,0:T(8,128)(2,1)S(1)}, bf16[64,1216]{1,0:T(8,128)(2,1)S(1)}, u32[]{:S(2)}, u32[]{:S(2)}) %collective-permute-start.28) | collective-permute-done | bytes 155680 | tf_op jit(solution)/shard_map/ppermute | solution.py:563
  103.2 3.0 %collective-permute-done.25.near = bf16[64,1216]{1,0:T(8,128)(2,1)S(1)} collective-permute-done((bf16[64,1216]{1,0:T(8,128)(2,1)S(1)}, bf16[64,1216]{1,0:T(8,128)(2,1)S(1)}, u32[]{:S(2)}, u32[]{:S(2)}) %collective-permute-start.25) | collective-permute-done | bytes 155680 | tf_op jit(solution)/shard_map/ppermute | solution.py:563
  106.3 0.2 shard_map.97
  106.5 0.1 collective-permute-start.29
  106.6 1.2 %collective-permute-done.29.other = f32[128,128]{1,0:T(8,128)S(1)} collective-permute-done((f32[128,128]{1,0:T(8,128)S(1)}, f32[128,128]{1,0:T(8,128)S(1)}, u32[]{:S(2)}, u32[]{:S(2)}) %collective-permute-start.29) | collective-permute-done | bytes 65568 | tf_op jit(solution)/shard_map/ppermute | solution.py:566
  107.8 1.2 %shard_map.98 = f32[1216,128]{1,0:T(8,128)} custom-call(f32[128,1216]{1,0:T(8,128)S(1)} %get-tuple-element.117.grad, f32[128,128]{1,0:T(8,128)S(1)} %get-tuple-element.118.sums, f32[128,128]{1,0:T(8,128)S(1)} %collective-permute-done.29.other, f32[128,1216]{1,0:T(8,128)S(1)} %copy-done.1, f32[128,1216]{1,0:T(8,128)S(1)} %copy-done.3, f32[128,128]{1,0:T(8,128)S(1)} %copy-done.4), custom_call_target="tpu_custom_call" | custom-call | flops 516096 | bytes 2064384 | tf_op jit(solution)/shard_map/pallas_call | solution.py:514
  (67 shorter events, 0.3 us)
Async XLA Ops:
  0.0 9.3 %copy-start = (bf16[640,608]{0,1:T(8,128)(2,1)S(1)}, bf16[640,608]{0,1:T(8,128)(2,1)}, u32[]{:S(2)}) copy-start(bf16[640,608]{0,1:T(8,128)(2,1)} %param.17) | copy-start | bytes 2334724
  3.6 12.5 %collective-permute-start.3 = (bf16[64,2560]{1,0:T(8,128)(2,1)}, bf16[64,2560]{1,0:T(8,128)(2,1)S(1)}, u32[]{:S(2)}, u32[]{:S(2)}) collective-permute-start(bf16[64,2560]{1,0:T(8,128)(2,1)} %get-tuple-element.65), channel_id=1, source_target_pairs={{2,0},{6,2},{4,6},{0,4},{3,1},{7,3},{5,7},{1,5},{10,8},{14,10},{12... | collective-permute-start | bytes 983048 | tf_op jit(solution)/shard_map/ppermute | solution.py:569
  7.6 17.2 %collective-permute-start.2 = (bf16[64,2560]{1,0:T(8,128)(2,1)}, bf16[64,2560]{1,0:T(8,128)(2,1)S(1)}, u32[]{:S(2)}, u32[]{:S(2)}) collective-permute-start(bf16[64,2560]{1,0:T(8,128)(2,1)} %get-tuple-element.65), channel_id=1, source_target_pairs={{0,2},{2,6},{6,4},{4,0},{1,3},{3,7},{7,5},{5,1},{8,10},{10,14},{14... | collective-permute-start | bytes 983048 | tf_op jit(solution)/shard_map/ppermute | solution.py:563
  9.7 22.8 %copy-start.7 = (bf16[608,384]{1,0:T(8,128)(2,1)}, bf16[608,384]{1,0:T(8,128)(2,1)S(1)}, u32[]{:S(2)}) copy-start(bf16[608,384]{1,0:T(8,128)(2,1)S(1)} %pad_maximum_fusion.1.refs_13_.refs_15_) | copy-start | bytes 1400836
  9.7 16.5 %collective-permute-start.1 = (bf16[608,384]{1,0:T(8,128)(2,1)S(1)}, bf16[608,384]{1,0:T(8,128)(2,1)S(1)}, u32[]{:S(2)}, u32[]{:S(2)}) collective-permute-start(bf16[608,384]{1,0:T(8,128)(2,1)S(1)} %pad_maximum_fusion.1.refs_13_.refs_15_), channel_id=1, source_target_pairs={{0,8},{1,17},{8,0},{9,25},{16,24},{17,1},{24,16},{25,9},{2,10},{3,... | collective-permute-start | bytes 1400840 | tf_op jit(solution)/shard_map/ppermute | solution.py:590
  12.2 16.9 %collective-permute-start = (bf16[608,384]{1,0:T(8,128)(2,1)}, bf16[608,384]{1,0:T(8,128)(2,1)S(1)}, u32[]{:S(2)}, u32[]{:S(2)}) collective-permute-start(bf16[608,384]{1,0:T(8,128)(2,1)} %pad_maximum_fusion.refs_9_), channel_id=1, source_target_pairs={{0,8},{1,17},{8,0},{9,25},{16,24},{17,1},{24,16},{25,9},{2,10},{3,... | collective-permute-start | bytes 1400840 | tf_op jit(solution)/shard_map/ppermute | solution.py:590
  12.7 24.4 %collective-permute-start.11 = (bf16[608,384]{1,0:T(8,128)(2,1)S(1)}, bf16[608,384]{1,0:T(8,128)(2,1)S(1)}, u32[]{:S(2)}, u32[]{:S(2)}) collective-permute-start(bf16[608,384]{1,0:T(8,128)(2,1)S(1)} %pad_maximum_fusion.1.refs_13_.refs_15_), channel_id=1, source_target_pairs={{0,16},{1,9},{8,24},{9,1},{16,0},{17,25},{24,8},{25,17},{2,18},{3,... | collective-permute-start | bytes 1400840 | tf_op jit(solution)/shard_map/ppermute | solution.py:591
  16.1 12.9 %copy-start.8 = (bf16[64,2560]{1,0:T(8,128)(2,1)}, bf16[64,2560]{1,0:T(8,128)(2,1)S(1)}, u32[]{:S(2)}) copy-start(bf16[64,2560]{1,0:T(8,128)(2,1)S(1)} %collective-permute-done.3.following.refs_3_) | copy-start | bytes 983044
  16.8 12.2 %collective-permute-start.4 = (bf16[32,2560]{1,0:T(8,128)(2,1)}, bf16[32,2560]{1,0:T(8,128)(2,1)S(1)}, u32[]{:S(2)}, u32[]{:S(2)}) collective-permute-start(bf16[32,2560]{1,0:T(8,128)(2,1)} %slice.16), channel_id=1, source_target_pairs={{2,0},{6,2},{4,6},{0,4},{3,1},{7,3},{5,7},{1,5},{10,8},{14,10},{12... | collective-permute-start | bytes 491528 | tf_op jit(solution)/shard_map/ppermute | solution.py:569
  24.8 4.2 %copy-start.10 = (bf16[64,2560]{1,0:T(8,128)(2,1)}, bf16[64,2560]{1,0:T(8,128)(2,1)S(1)}, u32[]{:S(2)}) copy-start(bf16[64,2560]{1,0:T(8,128)(2,1)S(1)} %collective-permute-done.2.previous.refs_1_) | copy-start | bytes 983044
  25.5 7.2 %collective-permute-start.7 = (bf16[32,2560]{1,0:T(8,128)(2,1)}, bf16[32,2560]{1,0:T(8,128)(2,1)}, u32[]{:S(2)}, u32[]{:S(2)}) collective-permute-start(bf16[32,2560]{1,0:T(8,128)(2,1)} %slice.17), channel_id=1, source_target_pairs={{0,2},{2,6},{6,4},{4,0},{1,3},{3,7},{7,5},{5,1},{8,10},{10,14},{14... | collective-permute-start | bytes 491528 | tf_op jit(solution)/shard_map/ppermute | solution.py:563
  26.2 21.1 %copy-start.12 = (bf16[608,384]{1,0:T(8,128)(2,1)}, bf16[608,384]{1,0:T(8,128)(2,1)S(1)}, u32[]{:S(2)}) copy-start(bf16[608,384]{1,0:T(8,128)(2,1)S(1)} %collective-permute-done.1.refs_14_.refs_16_) | copy-start | bytes 1400836
  26.2 21.1 %collective-permute-start.10 = (bf16[608,384]{1,0:T(8,128)(2,1)}, bf16[608,384]{1,0:T(8,128)(2,1)}, u32[]{:S(2)}, u32[]{:S(2)}) collective-permute-start(bf16[608,384]{1,0:T(8,128)(2,1)} %pad_maximum_fusion.refs_9_), channel_id=1, source_target_pairs={{0,16},{1,9},{8,24},{9,1},{16,0},{17,25},{24,8},{25,17},{2,18},{3,... | collective-permute-start | bytes 1400840 | tf_op jit(solution)/shard_map/ppermute | solution.py:591
  29.0 26.7 %copy-start.16 = (bf16[608,384]{1,0:T(8,128)(2,1)}, bf16[608,384]{1,0:T(8,128)(2,1)S(1)}, u32[]{:S(2)}) copy-start(bf16[608,384]{1,0:T(8,128)(2,1)S(1)} %collective-permute-done.refs_10_) | copy-start | bytes 1400836
  29.0 0.7 copy-start.14
  32.5 14.8 %copy-start.15 = (bf16[32,2560]{1,0:T(8,128)(2,1)S(1)}, bf16[32,2560]{1,0:T(8,128)(2,1)}, u32[]{:S(2)}) copy-start(bf16[32,2560]{1,0:T(8,128)(2,1)} %copy-done.14) | copy-start | bytes 491524
  32.5 19.1 %copy-start.11 = (bf16[64,2560]{1,0:T(8,128)(2,1)S(1)}, bf16[64,2560]{1,0:T(8,128)(2,1)}, u32[]{:S(2)}) copy-start(bf16[64,2560]{1,0:T(8,128)(2,1)} %copy-done.10) | copy-start | bytes 983044
  32.5 19.5 %copy-start.9 = (bf16[64,2560]{1,0:T(8,128)(2,1)S(1)}, bf16[64,2560]{1,0:T(8,128)(2,1)}, u32[]{:S(2)}) copy-start(bf16[64,2560]{1,0:T(8,128)(2,1)} %copy-done.8) | copy-start | bytes 983044
  32.8 10.8 %collective-permute-start.15 = (bf16[64,2560]{1,0:T(8,128)(2,1)}, bf16[64,2560]{1,0:T(8,128)(2,1)}, u32[]{:S(2)}, u32[]{:S(2)}) collective-permute-start(bf16[64,2560]{1,0:T(8,128)(2,1)} %get-tuple-element.76), channel_id=1, source_target_pairs={{2,0},{6,2},{4,6},{0,4},{3,1},{7,3},{5,7},{1,5},{10,8},{14,10},{12... | collective-permute-start | bytes 983048 | tf_op jit(solution)/shard_map/ppermute | solution.py:569
  35.0 16.4 %collective-permute-start.12 = (bf16[608,384]{1,0:T(8,128)(2,1)S(1)}, bf16[608,384]{1,0:T(8,128)(2,1)S(1)}, u32[]{:S(2)}, u32[]{:S(2)}) collective-permute-start(bf16[608,384]{1,0:T(8,128)(2,1)S(1)} %collective-permute-done.refs_10_), channel_id=1, source_target_pairs={{0,16},{1,9},{8,24},{9,1},{16,0},{17,25},{24,8},{25,17},{2,18},{3,... | collective-permute-start | bytes 1400840 | tf_op jit(solution)/shard_map/ppermute | solution.py:626
  36.5 14.9 %collective-permute-start.13 = (bf16[608,384]{1,0:T(8,128)(2,1)S(1)}, bf16[608,384]{1,0:T(8,128)(2,1)}, u32[]{:S(2)}, u32[]{:S(2)}) collective-permute-start(bf16[608,384]{1,0:T(8,128)(2,1)S(1)} %collective-permute-done.1.refs_14_.refs_16_), channel_id=1, source_target_pairs={{0,16},{1,9},{8,24},{9,1},{16,0},{17,25},{24,8},{25,17},{2,18},{3,... | collective-permute-start | bytes 1400840 | tf_op jit(solution)/shard_map/ppermute | solution.py:626
  37.1 18.6 %copy-start.13 = (bf16[608,384]{1,0:T(8,128)(2,1)}, bf16[608,384]{1,0:T(8,128)(2,1)S(1)}, u32[]{:S(2)}) copy-start(bf16[608,384]{1,0:T(8,128)(2,1)S(1)} %collective-permute-done.11.refs_15_.refs_17_) | copy-start | bytes 1400836
  37.1 14.4 %collective-permute-start.9 = (bf16[64,2560]{1,0:T(8,128)(2,1)}, bf16[64,2560]{1,0:T(8,128)(2,1)S(1)}, u32[]{:S(2)}, u32[]{:S(2)}) collective-permute-start(bf16[64,2560]{1,0:T(8,128)(2,1)} %get-tuple-element.76), channel_id=1, source_target_pairs={{0,2},{2,6},{6,4},{4,0},{1,3},{3,7},{7,5},{5,1},{8,10},{10,14},{14... | collective-permute-start | bytes 983048 | tf_op jit(solution)/shard_map/ppermute | solution.py:563
  43.6 8.7 %collective-permute-start.16 = (bf16[64,2560]{1,0:T(8,128)(2,1)}, bf16[64,2560]{1,0:T(8,128)(2,1)}, u32[]{:S(2)}, u32[]{:S(2)}) collective-permute-start(bf16[64,2560]{1,0:T(8,128)(2,1)} %collective-permute-done.15.refs_11_), channel_id=1, source_target_pairs={{0,1},{1,0},{2,3},{3,2},{4,5},{5,4},{6,7},{7,6},{8,9},{9,8},{10,11... | collective-permute-start | bytes 983048 | tf_op jit(solution)/shard_map/ppermute | solution.py:566
  47.3 4.8 %collective-permute-start.17 = (bf16[32,2560]{1,0:T(8,128)(2,1)S(1)}, bf16[32,2560]{1,0:T(8,128)(2,1)S(1)}, u32[]{:S(2)}, u32[]{:S(2)}) collective-permute-start(bf16[32,2560]{1,0:T(8,128)(2,1)S(1)} %copy-done.15), channel_id=1, source_target_pairs={{0,1},{1,0},{2,3},{3,2},{4,5},{5,4},{6,7},{7,6},{8,9},{9,8},{10,11... | collective-permute-start | bytes 491528 | tf_op jit(solution)/shard_map/ppermute | solution.py:566
  51.4 14.2 %copy-start.18 = (bf16[64,2560]{1,0:T(8,128)(2,1)}, bf16[64,2560]{1,0:T(8,128)(2,1)S(1)}, u32[]{:S(2)}) copy-start(bf16[64,2560]{1,0:T(8,128)(2,1)S(1)} %collective-permute-done.9.refs_9_) | copy-start | bytes 983044
  51.4 4.3 %copy-start.17 = (bf16[608,384]{1,0:T(8,128)(2,1)}, bf16[608,384]{1,0:T(8,128)(2,1)S(1)}, u32[]{:S(2)}) copy-start(bf16[608,384]{1,0:T(8,128)(2,1)S(1)} %collective-permute-done.12.refs_12_) | copy-start | bytes 1400836
  51.4 1.7 %collective-permute-start.14 = (bf16[64,2560]{1,0:T(8,128)(2,1)S(1)}, bf16[64,2560]{1,0:T(8,128)(2,1)S(1)}, u32[]{:S(2)}, u32[]{:S(2)}) collective-permute-start(bf16[64,2560]{1,0:T(8,128)(2,1)S(1)} %collective-permute-done.9.refs_9_), channel_id=1, source_target_pairs={{0,1},{1,0},{2,3},{3,2},{4,5},{5,4},{6,7},{7,6},{8,9},{9,8},{10,11... | collective-permute-start | bytes 983048 | tf_op jit(solution)/shard_map/ppermute | solution.py:566
  51.5 2.8 %collective-permute-start.5 = (bf16[64,2560]{1,0:T(8,128)(2,1)S(1)}, bf16[64,2560]{1,0:T(8,128)(2,1)S(1)}, u32[]{:S(2)}, u32[]{:S(2)}) collective-permute-start(bf16[64,2560]{1,0:T(8,128)(2,1)S(1)} %copy-done.11), channel_id=1, source_target_pairs={{0,1},{1,0},{2,3},{3,2},{4,5},{5,4},{6,7},{7,6},{8,9},{9,8},{10,11... | collective-permute-start | bytes 983048 | tf_op jit(solution)/shard_map/ppermute | solution.py:566
  52.0 3.7 %collective-permute-start.6 = (bf16[64,2560]{1,0:T(8,128)(2,1)S(1)}, bf16[64,2560]{1,0:T(8,128)(2,1)}, u32[]{:S(2)}, u32[]{:S(2)}) collective-permute-start(bf16[64,2560]{1,0:T(8,128)(2,1)S(1)} %copy-done.9), channel_id=1, source_target_pairs={{0,1},{1,0},{2,3},{3,2},{4,5},{5,4},{6,7},{7,6},{8,9},{9,8},{10,11... | collective-permute-start | bytes 983048 | tf_op jit(solution)/shard_map/ppermute | solution.py:566
  52.1 2.2 %copy-start.23 = (bf16[32,2560]{1,0:T(8,128)(2,1)}, bf16[32,2560]{1,0:T(8,128)(2,1)S(1)}, u32[]{:S(2)}) copy-start(bf16[32,2560]{1,0:T(8,128)(2,1)S(1)} %collective-permute-done.17.refs_8_) | copy-start | bytes 491524
  52.1 11.5 %collective-permute-start.18 = (bf16[64,2560]{1,0:T(8,128)(2,1)S(1)}, bf16[64,2560]{1,0:T(8,128)(2,1)S(1)}, u32[]{:S(2)}, u32[]{:S(2)}) collective-permute-start(bf16[64,2560]{1,0:T(8,128)(2,1)S(1)} %collective-permute-done.9.refs_9_), channel_id=1, source_target_pairs={{0,2},{2,6},{6,4},{4,0},{1,3},{3,7},{7,5},{5,1},{8,10},{10,14},{14... | collective-permute-start | bytes 983048 | tf_op jit(solution)/shard_map/ppermute | solution.py:563
  52.3 2.0 %collective-permute-start.8 = (bf16[32,2560]{1,0:T(8,128)(2,1)}, bf16[32,2560]{1,0:T(8,128)(2,1)S(1)}, u32[]{:S(2)}, u32[]{:S(2)}) collective-permute-start(bf16[32,2560]{1,0:T(8,128)(2,1)} %collective-permute-done.7.refs_5_), channel_id=1, source_target_pairs={{0,1},{1,0},{2,3},{3,2},{4,5},{5,4},{6,7},{7,6},{8,9},{9,8},{10,11... | collective-permute-start | bytes 491528 | tf_op jit(solution)/shard_map/ppermute | solution.py:566
  53.1 10.5 %copy-start.19 = (bf16[64,2560]{1,0:T(8,128)(2,1)}, bf16[64,2560]{1,0:T(8,128)(2,1)S(1)}, u32[]{:S(2)}) copy-start(bf16[64,2560]{1,0:T(8,128)(2,1)S(1)} %collective-permute-done.14.refs_10_) | copy-start | bytes 983044
  54.3 0.7 copy-start.24
  55.0 0.7 copy-start.21
  63.6 2.0 %copy-start.20 = (bf16[64,2560]{1,0:T(8,128)(2,1)}, bf16[64,2560]{1,0:T(8,128)(2,1)S(1)}, u32[]{:S(2)}) copy-start(bf16[64,2560]{1,0:T(8,128)(2,1)S(1)} %collective-permute-done.18.refs_13_) | copy-start | bytes 983044
  63.6 1.7 %collective-permute-start.19 = (bf16[64,2560]{1,0:T(8,128)(2,1)S(1)}, bf16[64,2560]{1,0:T(8,128)(2,1)S(1)}, u32[]{:S(2)}, u32[]{:S(2)}) collective-permute-start(bf16[64,2560]{1,0:T(8,128)(2,1)S(1)} %collective-permute-done.18.refs_13_), channel_id=1, source_target_pairs={{0,1},{1,0},{2,3},{3,2},{4,5},{5,4},{6,7},{7,6},{8,9},{9,8},{10,11... | collective-permute-start | bytes 983048 | tf_op jit(solution)/shard_map/ppermute | solution.py:566
  65.3 0.7 copy-start.22
  65.3 17.6 %collective-permute-start.22 = (bf16[1216,640]{1,0:T(8,128)(2,1)}, bf16[1216,640]{1,0:T(8,128)(2,1)S(1)}, u32[]{:S(2)}, u32[]{:S(2)}) collective-permute-start(bf16[1216,640]{1,0:T(8,128)(2,1)} %get-tuple-element.108.refs_7_), channel_id=1, source_target_pairs={{0,1},{1,0},{2,3},{3,2},{4,5},{5,4},{6,7},{7,6},{8,9},{9,8},{10,11... | collective-permute-start | bytes 4669448 | tf_op jit(solution)/shard_map/ppermute | solution.py:566
  77.5 5.4 %copy-start.2 = (bf16[1216,640]{1,0:T(8,128)(2,1)S(1)}, bf16[1216,640]{1,0:T(8,128)(2,1)}, u32[]{:S(2)}) copy-start(bf16[1216,640]{1,0:T(8,128)(2,1)} %get-tuple-element.87.refs_6_.w_own) | copy-start | bytes 4669444
  77.5 1.9 %collective-permute-start.21 = (bf16[128,1216]{1,0:T(8,128)(2,1)}, bf16[128,1216]{1,0:T(8,128)(2,1)S(1)}, u32[]{:S(2)}, u32[]{:S(2)}) collective-permute-start(bf16[128,1216]{1,0:T(8,128)(2,1)} %get-tuple-element.105), channel_id=1, source_target_pairs={{0,1},{1,0},{2,3},{3,2},{4,5},{5,4},{6,7},{7,6},{8,9},{9,8},{10,11... | collective-permute-start | bytes 933896 | tf_op jit(solution)/shard_map/ppermute | solution.py:566
  77.8 5.1 %collective-permute-start.20 = (bf16[384,640]{1,0:T(8,128)(2,1)}, bf16[384,640]{1,0:T(8,128)(2,1)S(1)}, u32[]{:S(2)}, u32[]{:S(2)}) collective-permute-start(bf16[384,640]{1,0:T(8,128)(2,1)} %get-tuple-element.106.own), channel_id=1, source_target_pairs={{0,1},{1,0},{2,3},{3,2},{4,5},{5,4},{6,7},{7,6},{8,9},{9,8},{10,11... | collective-permute-start | bytes 1474568 | tf_op jit(solution)/shard_map/ppermute | solution.py:566
  80.6 8.0 %collective-permute-start.26 = (bf16[64,1216]{1,0:T(8,128)(2,1)S(1)}, bf16[64,1216]{1,0:T(8,128)(2,1)S(1)}, u32[]{:S(2)}, u32[]{:S(2)}) collective-permute-start(bf16[64,1216]{1,0:T(8,128)(2,1)S(1)} %get-tuple-element.124), channel_id=1, source_target_pairs={{0,2},{2,6},{6,4},{4,0},{1,3},{3,7},{7,5},{5,1},{8,10},{10,14},{14... | collective-permute-start | bytes 466952 | tf_op jit(solution)/shard_map/ppermute | solution.py:563
  82.2 9.7 %collective-permute-start.23 = (bf16[64,1216]{1,0:T(8,128)(2,1)S(1)}, bf16[64,1216]{1,0:T(8,128)(2,1)S(1)}, u32[]{:S(2)}, u32[]{:S(2)}) collective-permute-start(bf16[64,1216]{1,0:T(8,128)(2,1)S(1)} %get-tuple-element.125), channel_id=1, source_target_pairs={{0,2},{2,6},{6,4},{4,0},{1,3},{3,7},{7,5},{5,1},{8,10},{10,14},{14... | collective-permute-start | bytes 466952 | tf_op jit(solution)/shard_map/ppermute | solution.py:563
  82.9 1.0 copy-start.6
  85.6 20.6 %copy-start.1 = (f32[128,1216]{1,0:T(8,128)S(1)}, f32[128,1216]{1,0:T(8,128)}, u32[]{:S(2)}) copy-start(f32[128,1216]{1,0:T(8,128)} %get-tuple-element.116.normed) | copy-start | bytes 1867780
  85.7 20.6 %copy-start.5 = (f32[1,1216]{1,0:T(1,128)S(1)}, f32[1,1216]{1,0:T(1,128)}, u32[]{:S(2)}) copy-start(f32[1,1216]{1,0:T(1,128)} %get-tuple-element.115.scale) | copy-start | bytes 14596
  88.6 6.7 %collective-permute-start.27 = (bf16[64,1216]{1,0:T(8,128)(2,1)S(1)}, bf16[64,1216]{1,0:T(8,128)(2,1)S(1)}, u32[]{:S(2)}, u32[]{:S(2)}) collective-permute-start(bf16[64,1216]{1,0:T(8,128)(2,1)S(1)} %add_convert_fusion.2), channel_id=1, source_target_pairs={{0,2},{2,6},{6,4},{4,0},{1,3},{3,7},{7,5},{5,1},{8,10},{10,14},{14... | collective-permute-start | bytes 466952 | tf_op jit(solution)/shard_map/ppermute | solution.py:563
  91.9 16.0 %copy-start.3 = (f32[128,1216]{1,0:T(8,128)S(1)}, f32[128,1216]{1,0:T(8,128)}, u32[]{:S(2)}) copy-start(f32[128,1216]{1,0:T(8,128)} %get-tuple-element.119.base) | copy-start | bytes 1867780
  91.9 16.0 %copy-start.4 = (f32[128,128]{1,0:T(8,128)S(1)}, f32[128,128]{1,0:T(8,128)}, u32[]{:S(2)}) copy-start(f32[128,128]{1,0:T(8,128)} %get-tuple-element.120.inv_std) | copy-start | bytes 196612
  91.9 8.1 %collective-permute-start.24 = (bf16[64,1216]{1,0:T(8,128)(2,1)S(1)}, bf16[64,1216]{1,0:T(8,128)(2,1)S(1)}, u32[]{:S(2)}, u32[]{:S(2)}) collective-permute-start(bf16[64,1216]{1,0:T(8,128)(2,1)S(1)} %add_convert_fusion.4), channel_id=1, source_target_pairs={{0,2},{2,6},{6,4},{4,0},{1,3},{3,7},{7,5},{5,1},{8,10},{10,14},{14... | collective-permute-start | bytes 466952 | tf_op jit(solution)/shard_map/ppermute | solution.py:563
  95.4 7.9 %collective-permute-start.28 = (bf16[64,1216]{1,0:T(8,128)(2,1)S(1)}, bf16[64,1216]{1,0:T(8,128)(2,1)S(1)}, u32[]{:S(2)}, u32[]{:S(2)}) collective-permute-start(bf16[64,1216]{1,0:T(8,128)(2,1)S(1)} %add_convert_fusion.1), channel_id=1, source_target_pairs={{0,2},{2,6},{6,4},{4,0},{1,3},{3,7},{7,5},{5,1},{8,10},{10,14},{14... | collective-permute-start | bytes 466952 | tf_op jit(solution)/shard_map/ppermute | solution.py:563
  100.0 6.3 %collective-permute-start.25 = (bf16[64,1216]{1,0:T(8,128)(2,1)S(1)}, bf16[64,1216]{1,0:T(8,128)(2,1)S(1)}, u32[]{:S(2)}, u32[]{:S(2)}) collective-permute-start(bf16[64,1216]{1,0:T(8,128)(2,1)S(1)} %add_convert_fusion.3), channel_id=1, source_target_pairs={{0,2},{2,6},{6,4},{4,0},{1,3},{3,7},{7,5},{5,1},{8,10},{10,14},{14... | collective-permute-start | bytes 466952 | tf_op jit(solution)/shard_map/ppermute | solution.py:563
  106.5 1.3 %collective-permute-start.29 = (f32[128,128]{1,0:T(8,128)S(1)}, f32[128,128]{1,0:T(8,128)S(1)}, u32[]{:S(2)}, u32[]{:S(2)}) collective-permute-start(f32[128,128]{1,0:T(8,128)S(1)} %get-tuple-element.118.sums), channel_id=1, source_target_pairs={{0,1},{1,0},{2,3},{3,2},{4,5},{5,4},{6,7},{7,6},{8,9},{9,8},{10,11... | collective-permute-start | bytes 196616 | tf_op jit(solution)/shard_map/ppermute | solution.py:566
where the time goes:
time: 109 us
  waiting for transfers between devices  40.2 us (37%)
  Pallas kernels  31.7 us (29%)
  starting transfers between devices  25.5 us (23%)
  local copies, waits for them, and re-layouts  7.5 us (7%)
  other arithmetic  2.39 us (2%)
  between operations  1.71 us (2%)
    ppermute x10, waiting for transfers between devices, step(): return lax.ppermute(moving, 'seq', seq_next)  26.2 us
    pallas_call x1, Pallas kernels, attend_call(): pl.pallas_call(functools.partial(attend_kernel, slots, count, rows, shard...  11.4 us
    ppermute x3, starting transfers between devices, step_back(): return lax.ppermute(moving, 'seq', [(b, a) for a, b in seq_next])  9.59 us
    ppermute x3, waiting for transfers between devices, step_back(): return lax.ppermute(moving, 'seq', [(b, a) for a, b in seq_next])  8.36 us
    pallas_call x1, Pallas kernels, project_call(): pl.pallas_call(functools.partial(project_kernel, slots, count, rows, shar...  7.89 us
    ppermute x10, starting transfers between devices, step(): return lax.ppermute(moving, 'seq', seq_next)  5.95 us
    ppermute x11, waiting for transfers between devices, other_core(): return lax.ppermute(moving, 'head', swap)  5.59 us
    pallas_call x3, Pallas kernels, local_call(): pl.pallas_call(kernel, out_shape=tuple((jax.ShapeDtypeStruct(*one) for on...  5.12 us
  transfers between devices with their start and end apart: 30, of which 16 were waited for; matrix products, arithmetic and copies ran while one was open for 6% of the time, Pallas kernels for 25%

commit v1 on v0

--- a/solution.py
+++ b/solution.py
@@ -9,6 +9,7 @@
 
 HD = 64
 GRANT = 60 * 1024 * 1024
+MAIN_GRANT = 54 * 1024 * 1024
 SMALL_GRANT = 24 * 1024 * 1024
 EXTRA = 128
 NT = (((1,), (1,)), ((), ()))
@@ -419,7 +420,7 @@
             pltpu.VMEM((count, rows // 2, EXTRA), f32),
         ]
         + [pltpu.VMEM(*one) for one in shapes[:4]],
-        compiler_params=pltpu.CompilerParams(vmem_limit_bytes=GRANT),
+        compiler_params=pltpu.CompilerParams(vmem_limit_bytes=MAIN_GRANT),
         cost_estimate=pl.CostEstimate(
             flops=2 * tokens * width * 3 * slots * HD,
             bytes_accessed=2 * (tokens * width + columns * width) + 4 * tokens * columns,
@@ -455,7 +456,7 @@
             pltpu.VMEM((tokens, stacked), bf16),
         ]
         + [pltpu.VMEM(one.shape, one.dtype) for one in operands],
-        compiler_params=pltpu.CompilerParams(vmem_limit_bytes=GRANT),
+        compiler_params=pltpu.CompilerParams(vmem_limit_bytes=MAIN_GRANT),
         cost_estimate=pl.CostEstimate(
             flops=2 * tokens * width * inner + 10 * tokens * tokens * inner,
             bytes_accessed=2 * (tokens * width + columns * width),

time: 109 us -> 110 us (level)
    unnamed x50 -> x54, local copies, waits for them, and re-layouts: 3.59 us -> 3.68 us
  transfers between devices with their start and end apart: 30 -> 30, of which waited for: 16 -> 16; matrix products, arithmetic and copies ran while one was open for 6% -> 5% of each run, Pallas kernels for 25% -> 25%
where the time goes in v1:
time: 110 us; the launch traced here: 109 us
  waiting for transfers between devices  40.6 us (37%)
  Pallas kernels  31.8 us (29%)
  starting transfers between devices  25.7 us (23%)
  local copies, waits for them, and re-layouts  7.59 us (7%)
  between operations  1.74 us (2%)
  other arithmetic  1.62 us (1%)
    ppermute x10, waiting for transfers between devices, step(): return lax.ppermute(moving, 'seq', seq_next)  26 us
    pallas_call x1, Pallas kernels, attend_call(): pl.pallas_call(functools.partial(attend_kernel, slots, count, rows, shard...  11.5 us
    ppermute x3, starting transfers between devices, step_back(): return lax.ppermute(moving, 'seq', [(b, a) for a, b in seq_next])  9.87 us
    ppermute x3, waiting for transfers between devices, step_back(): return lax.ppermute(moving, 'seq', [(b, a) for a, b in seq_next])  9.05 us
    pallas_call x1, Pallas kernels, project_call(): pl.pallas_call(functools.partial(project_kernel, slots, count, rows, shar...  7.9 us
    ppermute x10, starting transfers between devices, step(): return lax.ppermute(moving, 'seq', seq_next)  5.92 us
    ppermute x11, waiting for transfers between devices, other_core(): return lax.ppermute(moving, 'head', swap)  5.6 us
    pallas_call x3, Pallas kernels, local_call(): pl.pallas_call(kernel, out_shape=tuple((jax.ShapeDtypeStruct(*one) for on...  5.21 us
  transfers between devices with their start and end apart: 30, of which 16 were waited for; matrix products, arithmetic and copies ran while one was open for 5% of the time, Pallas kernels for 25%

profile of v1, /device:TPU:0, one launch (start us, length us, event | category | flops | bytes accessed | tf_op | source)
XLA Modules:
  0.0 109.1 jit_solution(4488640619557122075)
XLA Ops:
  0.7 2.8 %shard_map.91 = (bf16[64,2560]{1,0:T(8,128)(2,1)}, f32[8,2432]{1,0:T(8,128)}, bf16[64,128]{1,0:T(8,128)(2,1)}) custom-call(s32[1]{0:T(128)S(6)} %copy.11.step, s32[1]{0:T(128)} %bitcast.core, bf16[128,2432]{1,0:T(8,128)(2,1)} %bitcast.31, f32[3,28,2432]{2,1,0:T(8,128)} %bitcast.33, f32[128,2432]{1,0:T(8,128)} %bitcast.28, bf16[8,2,640]{2,1,0:T(2,128)(2,1)} %bitcast.34), custom_call_target="tpu_custom_call" | custom-call | flops 1245184 | bytes 2490368 | tf_op jit(solution)/shard_map/pallas_call | solution.py:111
  3.6 4.0 %collective-permute-start.3 = (bf16[64,2560]{1,0:T(8,128)(2,1)}, bf16[64,2560]{1,0:T(8,128)(2,1)S(1)}, u32[]{:S(2)}, u32[]{:S(2)}) collective-permute-start(bf16[64,2560]{1,0:T(8,128)(2,1)} %get-tuple-element.65), channel_id=1, source_target_pairs={{2,0},{6,2},{4,6},{0,4},{3,1},{7,3},{5,7},{1,5},{10,8},{14,10},{12... | collective-permute-start | bytes 983048 | tf_op jit(solution)/shard_map/ppermute | solution.py:570
  7.6 1.7 %dynamic-slice_bitcast_fusion.1 = (bf16[608,192]{1,0:T(8,128)(2,1)S(1)}, bf16[608,192]{1,0:T(8,128)(2,1)S(1)}, bf16[608,192]{1,0:T(8,128)(2,1)S(1)}) fusion(bf16[608,3,640]{2,0,1:T(8,128)(2,1)} %param.15, s32[]{:T(128)S(6)} %select_n.103), kind=kLoop, calls=%fused_computation.8 | loop fusion | bytes 1400836 | tf_op jit(solution)/shard_map/squeeze | solution.py:586
  9.3 0.2 dynamic-slice_bitcast_fusion
  9.5 0.2 pad_maximum_fusion.1.refs_13_.refs_15_
  9.7 1.6 %collective-permute-start.1 = (bf16[608,384]{1,0:T(8,128)(2,1)S(1)}, bf16[608,384]{1,0:T(8,128)(2,1)S(1)}, u32[]{:S(2)}, u32[]{:S(2)}) collective-permute-start(bf16[608,384]{1,0:T(8,128)(2,1)S(1)} %pad_maximum_fusion.1.refs_13_.refs_15_), channel_id=1, source_target_pairs={{0,8},{1,17},{8,0},{9,25},{16,24},{17,1},{24,16},{25,9},{2,10},{3,... | collective-permute-start | bytes 1400840 | tf_op jit(solution)/shard_map/ppermute | solution.py:591
  11.2 0.2 pad_maximum_fusion.refs_9_
  11.4 0.6 collective-permute-start
  12.0 1.5 %collective-permute-start.11 = (bf16[608,384]{1,0:T(8,128)(2,1)S(1)}, bf16[608,384]{1,0:T(8,128)(2,1)S(1)}, u32[]{:S(2)}, u32[]{:S(2)}) collective-permute-start(bf16[608,384]{1,0:T(8,128)(2,1)S(1)} %pad_maximum_fusion.1.refs_13_.refs_15_), channel_id=1, source_target_pairs={{0,16},{1,9},{8,24},{9,1},{16,0},{17,25},{24,8},{25,17},{2,18},{3,... | collective-permute-start | bytes 1400840 | tf_op jit(solution)/shard_map/ppermute | solution.py:592
  13.5 2.6 %collective-permute-done.3.following.refs_3_ = bf16[64,2560]{1,0:T(8,128)(2,1)S(1)} collective-permute-done((bf16[64,2560]{1,0:T(8,128)(2,1)}, bf16[64,2560]{1,0:T(8,128)(2,1)S(1)}, u32[]{:S(2)}, u32[]{:S(2)}) %collective-permute-start.3) | collective-permute-done | bytes 327712 | tf_op jit(solution)/shard_map/ppermute | solution.py:570
  16.1 0.7 slice.16
  16.8 3.3 %collective-permute-start.4 = (bf16[32,2560]{1,0:T(8,128)(2,1)}, bf16[32,2560]{1,0:T(8,128)(2,1)S(1)}, u32[]{:S(2)}, u32[]{:S(2)}) collective-permute-start(bf16[32,2560]{1,0:T(8,128)(2,1)} %slice.16), channel_id=1, source_target_pairs={{2,0},{6,2},{4,6},{0,4},{3,1},{7,3},{5,7},{1,5},{10,8},{14,10},{12... | collective-permute-start | bytes 491528 | tf_op jit(solution)/shard_map/ppermute | solution.py:570
  20.1 4.7 %collective-permute-done.2.previous.refs_1_ = bf16[64,2560]{1,0:T(8,128)(2,1)S(1)} collective-permute-done((bf16[64,2560]{1,0:T(8,128)(2,1)}, bf16[64,2560]{1,0:T(8,128)(2,1)S(1)}, u32[]{:S(2)}, u32[]{:S(2)}) %collective-permute-start.2) | collective-permute-done | bytes 327712 | tf_op jit(solution)/shard_map/ppermute | solution.py:564
  24.8 0.7 slice.17
  25.5 0.7 collective-permute-start.7
  26.2 1.5 %collective-permute-start.10 = (bf16[608,384]{1,0:T(8,128)(2,1)S(1)}, bf16[608,384]{1,0:T(8,128)(2,1)}, u32[]{:S(2)}, u32[]{:S(2)}) collective-permute-start(bf16[608,384]{1,0:T(8,128)(2,1)S(1)} %pad_maximum_fusion.refs_9_), channel_id=1, source_target_pairs={{0,16},{1,9},{8,24},{9,1},{16,0},{17,25},{24,8},{25,17},{2,18},{3,... | collective-permute-start | bytes 1400840 | tf_op jit(solution)/shard_map/ppermute | solution.py:592
  28.4 0.6 stack.67.core.scalars
  29.0 0.6 copy-done.15
  29.6 2.7 %shard_map.92 = (bf16[64,2560]{1,0:T(8,128)(2,1)}, f32[8,128]{1,0:T(8,128)}) custom-call(s32[14]{0:T(128)} %stack.67.core.scalars, f32[128,2432]{1,0:T(8,128)} %bitcast.29, f32[8,2432]{1,0:T(8,128)} %get-tuple-element.63.table_rows, bf16[8,2,640]{2,1,0:T(2,128)(2,1)} %bitcast.35, bf16[64,128]{1,0:T(8,128)(2,1)} %get-tuple-element.68.extra, ...), custom_call_target="tpu_custom_call" | custom-call | flops 622592 | bytes 933888 | tf_op jit(solution)/shard_map/pallas_call | solution.py:163
  32.4 0.3 collective-permute-done.7.refs_5_
  32.8 2.6 %collective-permute-start.15 = (bf16[64,2560]{1,0:T(8,128)(2,1)}, bf16[64,2560]{1,0:T(8,128)(2,1)S(1)}, u32[]{:S(2)}, u32[]{:S(2)}) collective-permute-start(bf16[64,2560]{1,0:T(8,128)(2,1)} %get-tuple-element.76), channel_id=1, source_target_pairs={{2,0},{6,2},{4,6},{0,4},{3,1},{7,3},{5,7},{1,5},{10,8},{14,10},{12... | collective-permute-start | bytes 983048 | tf_op jit(solution)/shard_map/ppermute | solution.py:570
  35.3 1.5 %collective-permute-start.12 = (bf16[608,384]{1,0:T(8,128)(2,1)}, bf16[608,384]{1,0:T(8,128)(2,1)}, u32[]{:S(2)}, u32[]{:S(2)}) collective-permute-start(bf16[608,384]{1,0:T(8,128)(2,1)} %collective-permute-done.refs_10_), channel_id=1, source_target_pairs={{0,16},{1,9},{8,24},{9,1},{16,0},{17,25},{24,8},{25,17},{2,18},{3,... | collective-permute-start | bytes 1400840 | tf_op jit(solution)/shard_map/ppermute | solution.py:627
  36.8 0.5 collective-permute-start.13
  37.3 6.5 %collective-permute-done.15.refs_11_ = bf16[64,2560]{1,0:T(8,128)(2,1)S(1)} collective-permute-done((bf16[64,2560]{1,0:T(8,128)(2,1)}, bf16[64,2560]{1,0:T(8,128)(2,1)S(1)}, u32[]{:S(2)}, u32[]{:S(2)}) %collective-permute-start.15) | collective-permute-done | bytes 327712 | tf_op jit(solution)/shard_map/ppermute | solution.py:570
  43.8 3.8 %shard_map.93 = (bf16[128,2560]{1,0:T(8,128)(2,1)}, bf16[128,2560]{1,0:T(8,128)(2,1)}, f32[128,1216]{1,0:T(8,128)}, f32[1,1216]{1,0:T(1,128)}, f32[128,128]{1,0:T(8,128)}, /*index=5*/f32[128,1216]{1,0:T(8,128)}) custom-call(s32[1]{0:T(128)} %bitcast.core, bf16[128,2432]{1,0:T(8,128)(2,1)} %bitcast.32, f32[128,2432]{1,0:T(8,128)} %bitcast.30, ...), custom_call_target="tpu_custom_call" | custom-call | flops 661505 | bytes 1986564 | tf_op jit(solution)/shard_map/pallas_call | solution.py:515
  47.7 0.5 collective-permute-start.17
  48.1 3.2 %collective-permute-done.9.refs_9_ = bf16[64,2560]{1,0:T(8,128)(2,1)S(1)} collective-permute-done((bf16[64,2560]{1,0:T(8,128)(2,1)}, bf16[64,2560]{1,0:T(8,128)(2,1)S(1)}, u32[]{:S(2)}, u32[]{:S(2)}) %collective-permute-start.9) | collective-permute-done | bytes 327712 | tf_op jit(solution)/shard_map/ppermute | solution.py:564
  51.4 0.1 collective-permute-start.14
  51.5 0.5 collective-permute-start.5
  51.9 0.1 collective-permute-start.6
  52.0 0.2 collective-permute-start.18
  52.2 0.3 collective-permute-start.8
  52.6 0.5 collective-permute-done.14.refs_10_
  53.1 1.1 %collective-permute-done.8.refs_6_ = bf16[32,2560]{1,0:T(8,128)(2,1)S(1)} collective-permute-done((bf16[32,2560]{1,0:T(8,128)(2,1)}, bf16[32,2560]{1,0:T(8,128)(2,1)S(1)}, u32[]{:S(2)}, u32[]{:S(2)}) %collective-permute-start.8) | collective-permute-done | bytes 163872 | tf_op jit(solution)/shard_map/ppermute | solution.py:567
  54.3 0.6 copy-done.26
  54.9 0.1 copy-done.22
  55.0 0.7 copy-done.23
  55.7 7.9 %shard_map.94 = (bf16[512,576]{1,0:T(8,128)(2,1)}, bf16[192,512]{1,0:T(8,128)(2,1)}, f32[512,384]{1,0:T(8,128)}, f32[512,384]{1,0:T(8,128)}, bf16[3,32,64]{2,1,0...) custom-call(s32[14]{0:T(128)} %stack.67.core.scalars, ...), custom_call_target="tpu_custom_call" | custom-call | flops 1434451968 | bytes 7798784 | tf_op jit(solution)/shard_map/pallas_call | solution.py:411
  63.7 0.3 collective-permute-start.19
  64.0 1.3 %collective-permute-done.19.refs_14_ = bf16[64,2560]{1,0:T(8,128)(2,1)S(1)} collective-permute-done((bf16[64,2560]{1,0:T(8,128)(2,1)S(1)}, bf16[64,2560]{1,0:T(8,128)(2,1)S(1)}, u32[]{:S(2)}, u32[]{:S(2)}) %collective-permute-start.19) | collective-permute-done | bytes 327712 | tf_op jit(solution)/shard_map/ppermute | solution.py:567
  65.4 0.3 collective-permute-start.22
  65.7 0.4 copy-done.24
  66.1 11.5 %shard_map.95 = (f32[128,1216]{1,0:T(8,128)}, bf16[128,1216]{1,0:T(8,128)(2,1)}, bf16[384,640]{1,0:T(8,128)(2,1)}) custom-call(s32[14]{0:T(128)} %stack.67.core.scalars, f32[2,64]{1,0:T(2,128)} %gain.3, bf16[512,576]{1,0:T(8,128)(2,1)} %get-tuple-element.81.refs_0_, bf16[192,512]{1,0:T(8,128)(2,1)} %get-tuple-element.82.refs_1_, ...), custom_call_target="tpu_custom_call" | custom-call | flops 981467136 | bytes 4358144 | tf_op jit(solution)/shard_map/pallas_call | solution.py:443
  77.6 0.3 collective-permute-start.21
  77.9 0.2 collective-permute-start.20
  78.2 1.3 %collective-permute-done.21 = bf16[128,1216]{1,0:T(8,128)(2,1)S(1)} collective-permute-done((bf16[128,1216]{1,0:T(8,128)(2,1)}, bf16[128,1216]{1,0:T(8,128)(2,1)S(1)}, u32[]{:S(2)}, u32[]{:S(2)}) %collective-permute-start.21) | collective-permute-done | bytes 311328 | tf_op jit(solution)/shard_map/ppermute | solution.py:567
  79.5 1.2 %add_convert_fusion = bf16[128,1216]{1,0:T(8,128)(2,1)S(1)} fusion(f32[128,1216]{1,0:T(8,128)} %get-tuple-element.104, bf16[128,1216]{1,0:T(8,128)(2,1)S(1)} %collective-permute-done.21), kind=kLoop, calls=%fused_computation | loop fusion | flops 466944 | bytes 1245184 | tf_op jit(solution)/shard_map/convert_element_type | solution.py:644
  80.7 1.6 %collective-permute-start.26 = (bf16[64,1216]{1,0:T(8,128)(2,1)S(1)}, bf16[64,1216]{1,0:T(8,128)(2,1)S(1)}, u32[]{:S(2)}, u32[]{:S(2)}) collective-permute-start(bf16[64,1216]{1,0:T(8,128)(2,1)S(1)} %get-tuple-element.124), channel_id=1, source_target_pairs={{0,2},{2,6},{6,4},{4,0},{1,3},{3,7},{7,5},{5,1},{8,10},{10,14},{14... | collective-permute-start | bytes 466952 | tf_op jit(solution)/shard_map/ppermute | solution.py:564
  82.3 0.7 collective-permute-start.23
  83.0 1.0 copy-done.6
  84.0 1.7 %shard_map.96 = (f32[64,1216]{1,0:T(8,128)S(1)}, f32[64,1216]{1,0:T(8,128)S(1)}, f32[64,1216]{1,0:T(8,128)S(1)}, f32[64,1216]{1,0:T(8,128)S(1)}, f32[64,1216]{1,0:T(8,128)S(1)}, /*index=5*/f32[64,1216]{1,0:T(8,128)S(1)}) custom-call(bf16[384,640]{1,0:T(8,128)(2,1)S(1)} %copy-done.6, bf16[384,640]{1,0:T(8,128)(2,1)S(1)} %collective-permute-done.20.other, ...), custom_call_target="tpu_custom_call" | custom-call | flops 1195376640 | bytes 5963776 | tf_op jit(solution)/shard_map/pallas_call | solution.py:479
  85.7 2.9 %collective-permute-done.26 = bf16[64,1216]{1,0:T(8,128)(2,1)S(1)} collective-permute-done((bf16[64,1216]{1,0:T(8,128)(2,1)S(1)}, bf16[64,1216]{1,0:T(8,128)(2,1)S(1)}, u32[]{:S(2)}, u32[]{:S(2)}) %collective-permute-start.26) | collective-permute-done | bytes 155680 | tf_op jit(solution)/shard_map/ppermute | solution.py:564
  88.7 0.7 collective-permute-start.27
  89.4 2.6 %collective-permute-done.23 = bf16[64,1216]{1,0:T(8,128)(2,1)S(1)} collective-permute-done((bf16[64,1216]{1,0:T(8,128)(2,1)S(1)}, bf16[64,1216]{1,0:T(8,128)(2,1)S(1)}, u32[]{:S(2)}, u32[]{:S(2)}) %collective-permute-start.23) | collective-permute-done | bytes 155680 | tf_op jit(solution)/shard_map/ppermute | solution.py:564
  92.0 0.9 collective-permute-start.24
  92.9 2.5 %collective-permute-done.27 = bf16[64,1216]{1,0:T(8,128)(2,1)S(1)} collective-permute-done((bf16[64,1216]{1,0:T(8,128)(2,1)S(1)}, bf16[64,1216]{1,0:T(8,128)(2,1)S(1)}, u32[]{:S(2)}, u32[]{:S(2)}) %collective-permute-start.27) | collective-permute-done | bytes 155680 | tf_op jit(solution)/shard_map/ppermute | solution.py:564
  95.5 1.1 %collective-permute-start.28 = (bf16[64,1216]{1,0:T(8,128)(2,1)S(1)}, bf16[64,1216]{1,0:T(8,128)(2,1)S(1)}, u32[]{:S(2)}, u32[]{:S(2)}) collective-permute-start(bf16[64,1216]{1,0:T(8,128)(2,1)S(1)} %add_convert_fusion.1), channel_id=1, source_target_pairs={{0,2},{2,6},{6,4},{4,0},{1,3},{3,7},{7,5},{5,1},{8,10},{10,14},{14... | collective-permute-start | bytes 466952 | tf_op jit(solution)/shard_map/ppermute | solution.py:564
  96.6 3.5 %collective-permute-done.24 = bf16[64,1216]{1,0:T(8,128)(2,1)S(1)} collective-permute-done((bf16[64,1216]{1,0:T(8,128)(2,1)S(1)}, bf16[64,1216]{1,0:T(8,128)(2,1)S(1)}, u32[]{:S(2)}, u32[]{:S(2)}) %collective-permute-start.24) | collective-permute-done | bytes 155680 | tf_op jit(solution)/shard_map/ppermute | solution.py:564
  100.2 3.2 %collective-permute-done.28.far = bf16[64,1216]{1,0:T(8,128)(2,1)S(1)} collective-permute-done((bf16[64,1216]{1,0:T(8,128)(2,1)S(1)}, bf16[64,1216]{1,0:T(8,128)(2,1)S(1)}, u32[]{:S(2)}, u32[]{:S(2)}) %collective-permute-start.28) | collective-permute-done | bytes 155680 | tf_op jit(solution)/shard_map/ppermute | solution.py:564
  103.3 3.0 %collective-permute-done.25.near = bf16[64,1216]{1,0:T(8,128)(2,1)S(1)} collective-permute-done((bf16[64,1216]{1,0:T(8,128)(2,1)S(1)}, bf16[64,1216]{1,0:T(8,128)(2,1)S(1)}, u32[]{:S(2)}, u32[]{:S(2)}) %collective-permute-start.25) | collective-permute-done | bytes 155680 | tf_op jit(solution)/shard_map/ppermute | solution.py:564
  106.4 0.2 shard_map.97
  106.6 0.1 collective-permute-start.29
  106.7 1.2 %collective-permute-done.29.other = f32[128,128]{1,0:T(8,128)S(1)} collective-permute-done((f32[128,128]{1,0:T(8,128)S(1)}, f32[128,128]{1,0:T(8,128)S(1)}, u32[]{:S(2)}, u32[]{:S(2)}) %collective-permute-start.29) | collective-permute-done | bytes 65568 | tf_op jit(solution)/shard_map/ppermute | solution.py:567
  107.9 1.2 %shard_map.98 = f32[1216,128]{1,0:T(8,128)} custom-call(f32[128,1216]{1,0:T(8,128)S(1)} %get-tuple-element.117.grad, f32[128,128]{1,0:T(8,128)S(1)} %get-tuple-element.118.sums, f32[128,128]{1,0:T(8,128)S(1)} %collective-permute-done.29.other, f32[128,1216]{1,0:T(8,128)S(1)} %copy-done.1, f32[128,1216]{1,0:T(8,128)S(1)} %copy-done.3, f32[128,128]{1,0:T(8,128)S(1)} %copy-done.4), custom_call_target="tpu_custom_call" | custom-call | flops 516096 | bytes 2064384 | tf_op jit(solution)/shard_map/pallas_call | solution.py:515
  (71 shorter events, 0.4 us)
Async XLA Ops:
  0.0 9.3 %copy-start = (bf16[640,608]{0,1:T(8,128)(2,1)S(1)}, bf16[640,608]{0,1:T(8,128)(2,1)}, u32[]{:S(2)}) copy-start(bf16[640,608]{0,1:T(8,128)(2,1)} %param.17) | copy-start | bytes 2334724
  3.6 12.5 %collective-permute-start.3 = (bf16[64,2560]{1,0:T(8,128)(2,1)}, bf16[64,2560]{1,0:T(8,128)(2,1)S(1)}, u32[]{:S(2)}, u32[]{:S(2)}) collective-permute-start(bf16[64,2560]{1,0:T(8,128)(2,1)} %get-tuple-element.65), channel_id=1, source_target_pairs={{2,0},{6,2},{4,6},{0,4},{3,1},{7,3},{5,7},{1,5},{10,8},{14,10},{12... | collective-permute-start | bytes 983048 | tf_op jit(solution)/shard_map/ppermute | solution.py:570
  7.6 17.2 %collective-permute-start.2 = (bf16[64,2560]{1,0:T(8,128)(2,1)}, bf16[64,2560]{1,0:T(8,128)(2,1)S(1)}, u32[]{:S(2)}, u32[]{:S(2)}) collective-permute-start(bf16[64,2560]{1,0:T(8,128)(2,1)} %get-tuple-element.65), channel_id=1, source_target_pairs={{0,2},{2,6},{6,4},{4,0},{1,3},{3,7},{7,5},{5,1},{8,10},{10,14},{14... | collective-permute-start | bytes 983048 | tf_op jit(solution)/shard_map/ppermute | solution.py:564
  9.6 22.7 %copy-start.7 = (bf16[608,384]{1,0:T(8,128)(2,1)}, bf16[608,384]{1,0:T(8,128)(2,1)S(1)}, u32[]{:S(2)}) copy-start(bf16[608,384]{1,0:T(8,128)(2,1)S(1)} %pad_maximum_fusion.1.refs_13_.refs_15_) | copy-start | bytes 1400836
  9.7 16.5 %collective-permute-start.1 = (bf16[608,384]{1,0:T(8,128)(2,1)S(1)}, bf16[608,384]{1,0:T(8,128)(2,1)S(1)}, u32[]{:S(2)}, u32[]{:S(2)}) collective-permute-start(bf16[608,384]{1,0:T(8,128)(2,1)S(1)} %pad_maximum_fusion.1.refs_13_.refs_15_), channel_id=1, source_target_pairs={{0,8},{1,17},{8,0},{9,25},{16,24},{17,1},{24,16},{25,9},{2,10},{3,... | collective-permute-start | bytes 1400840 | tf_op jit(solution)/shard_map/ppermute | solution.py:591
  11.4 42.8 %copy-start.14 = (bf16[608,384]{1,0:T(8,128)(2,1)}, bf16[608,384]{1,0:T(8,128)(2,1)S(1)}, u32[]{:S(2)}) copy-start(bf16[608,384]{1,0:T(8,128)(2,1)S(1)} %pad_maximum_fusion.refs_9_) | copy-start | bytes 1400836
  11.4 17.6 %collective-permute-start = (bf16[608,384]{1,0:T(8,128)(2,1)S(1)}, bf16[608,384]{1,0:T(8,128)(2,1)}, u32[]{:S(2)}, u32[]{:S(2)}) collective-permute-start(bf16[608,384]{1,0:T(8,128)(2,1)S(1)} %pad_maximum_fusion.refs_9_), channel_id=1, source_target_pairs={{0,8},{1,17},{8,0},{9,25},{16,24},{17,1},{24,16},{25,9},{2,10},{3,... | collective-permute-start | bytes 1400840 | tf_op jit(solution)/shard_map/ppermute | solution.py:591
  12.0 25.3 %collective-permute-start.11 = (bf16[608,384]{1,0:T(8,128)(2,1)S(1)}, bf16[608,384]{1,0:T(8,128)(2,1)S(1)}, u32[]{:S(2)}, u32[]{:S(2)}) collective-permute-start(bf16[608,384]{1,0:T(8,128)(2,1)S(1)} %pad_maximum_fusion.1.refs_13_.refs_15_), channel_id=1, source_target_pairs={{0,16},{1,9},{8,24},{9,1},{16,0},{17,25},{24,8},{25,17},{2,18},{3,... | collective-permute-start | bytes 1400840 | tf_op jit(solution)/shard_map/ppermute | solution.py:592
  16.1 12.9 %copy-start.8 = (bf16[64,2560]{1,0:T(8,128)(2,1)}, bf16[64,2560]{1,0:T(8,128)(2,1)S(1)}, u32[]{:S(2)}) copy-start(bf16[64,2560]{1,0:T(8,128)(2,1)S(1)} %collective-permute-done.3.following.refs_3_) | copy-start | bytes 983044
  16.8 12.2 %collective-permute-start.4 = (bf16[32,2560]{1,0:T(8,128)(2,1)}, bf16[32,2560]{1,0:T(8,128)(2,1)S(1)}, u32[]{:S(2)}, u32[]{:S(2)}) collective-permute-start(bf16[32,2560]{1,0:T(8,128)(2,1)} %slice.16), channel_id=1, source_target_pairs={{2,0},{6,2},{4,6},{0,4},{3,1},{7,3},{5,7},{1,5},{10,8},{14,10},{12... | collective-permute-start | bytes 491528 | tf_op jit(solution)/shard_map/ppermute | solution.py:570
  24.8 4.2 %copy-start.10 = (bf16[64,2560]{1,0:T(8,128)(2,1)}, bf16[64,2560]{1,0:T(8,128)(2,1)S(1)}, u32[]{:S(2)}) copy-start(bf16[64,2560]{1,0:T(8,128)(2,1)S(1)} %collective-permute-done.2.previous.refs_1_) | copy-start | bytes 983044
  25.5 7.2 %collective-permute-start.7 = (bf16[32,2560]{1,0:T(8,128)(2,1)}, bf16[32,2560]{1,0:T(8,128)(2,1)}, u32[]{:S(2)}, u32[]{:S(2)}) collective-permute-start(bf16[32,2560]{1,0:T(8,128)(2,1)} %slice.17), channel_id=1, source_target_pairs={{0,2},{2,6},{6,4},{4,0},{1,3},{3,7},{7,5},{5,1},{8,10},{10,14},{14... | collective-permute-start | bytes 491528 | tf_op jit(solution)/shard_map/ppermute | solution.py:564
  26.2 21.5 %copy-start.12 = (bf16[608,384]{1,0:T(8,128)(2,1)}, bf16[608,384]{1,0:T(8,128)(2,1)S(1)}, u32[]{:S(2)}) copy-start(bf16[608,384]{1,0:T(8,128)(2,1)S(1)} %collective-permute-done.1.refs_14_.refs_16_) | copy-start | bytes 1400836
  26.2 21.5 %collective-permute-start.10 = (bf16[608,384]{1,0:T(8,128)(2,1)S(1)}, bf16[608,384]{1,0:T(8,128)(2,1)}, u32[]{:S(2)}, u32[]{:S(2)}) collective-permute-start(bf16[608,384]{1,0:T(8,128)(2,1)S(1)} %pad_maximum_fusion.refs_9_), channel_id=1, source_target_pairs={{0,16},{1,9},{8,24},{9,1},{16,0},{17,25},{24,8},{25,17},{2,18},{3,... | collective-permute-start | bytes 1400840 | tf_op jit(solution)/shard_map/ppermute | solution.py:592
  29.0 0.7 copy-start.15
  32.4 15.3 %copy-start.16 = (bf16[32,2560]{1,0:T(8,128)(2,1)S(1)}, bf16[32,2560]{1,0:T(8,128)(2,1)}, u32[]{:S(2)}) copy-start(bf16[32,2560]{1,0:T(8,128)(2,1)} %copy-done.15) | copy-start | bytes 491524
  32.4 19.1 %copy-start.11 = (bf16[64,2560]{1,0:T(8,128)(2,1)S(1)}, bf16[64,2560]{1,0:T(8,128)(2,1)}, u32[]{:S(2)}) copy-start(bf16[64,2560]{1,0:T(8,128)(2,1)} %copy-done.10) | copy-start | bytes 983044
  32.4 19.5 %copy-start.9 = (bf16[64,2560]{1,0:T(8,128)(2,1)S(1)}, bf16[64,2560]{1,0:T(8,128)(2,1)}, u32[]{:S(2)}) copy-start(bf16[64,2560]{1,0:T(8,128)(2,1)} %copy-done.8) | copy-start | bytes 983044
  32.8 11.1 %collective-permute-start.15 = (bf16[64,2560]{1,0:T(8,128)(2,1)}, bf16[64,2560]{1,0:T(8,128)(2,1)S(1)}, u32[]{:S(2)}, u32[]{:S(2)}) collective-permute-start(bf16[64,2560]{1,0:T(8,128)(2,1)} %get-tuple-element.76), channel_id=1, source_target_pairs={{2,0},{6,2},{4,6},{0,4},{3,1},{7,3},{5,7},{1,5},{10,8},{14,10},{12... | collective-permute-start | bytes 983048 | tf_op jit(solution)/shard_map/ppermute | solution.py:570
  35.3 16.1 %collective-permute-start.12 = (bf16[608,384]{1,0:T(8,128)(2,1)}, bf16[608,384]{1,0:T(8,128)(2,1)}, u32[]{:S(2)}, u32[]{:S(2)}) collective-permute-start(bf16[608,384]{1,0:T(8,128)(2,1)} %collective-permute-done.refs_10_), channel_id=1, source_target_pairs={{0,16},{1,9},{8,24},{9,1},{16,0},{17,25},{24,8},{25,17},{2,18},{3,... | collective-permute-start | bytes 1400840 | tf_op jit(solution)/shard_map/ppermute | solution.py:627
  36.8 14.5 %collective-permute-start.13 = (bf16[608,384]{1,0:T(8,128)(2,1)S(1)}, bf16[608,384]{1,0:T(8,128)(2,1)}, u32[]{:S(2)}, u32[]{:S(2)}) collective-permute-start(bf16[608,384]{1,0:T(8,128)(2,1)S(1)} %collective-permute-done.1.refs_14_.refs_16_), channel_id=1, source_target_pairs={{0,16},{1,9},{8,24},{9,1},{16,0},{17,25},{24,8},{25,17},{2,18},{3,... | collective-permute-start | bytes 1400840 | tf_op jit(solution)/shard_map/ppermute | solution.py:627
  37.3 16.9 %copy-start.13 = (bf16[608,384]{1,0:T(8,128)(2,1)}, bf16[608,384]{1,0:T(8,128)(2,1)S(1)}, u32[]{:S(2)}) copy-start(bf16[608,384]{1,0:T(8,128)(2,1)S(1)} %collective-permute-done.11.refs_15_.refs_17_) | copy-start | bytes 1400836
  37.3 14.0 %collective-permute-start.9 = (bf16[64,2560]{1,0:T(8,128)(2,1)}, bf16[64,2560]{1,0:T(8,128)(2,1)S(1)}, u32[]{:S(2)}, u32[]{:S(2)}) collective-permute-start(bf16[64,2560]{1,0:T(8,128)(2,1)} %get-tuple-element.76), channel_id=1, source_target_pairs={{0,2},{2,6},{6,4},{4,0},{1,3},{3,7},{7,5},{5,1},{8,10},{10,14},{14... | collective-permute-start | bytes 983048 | tf_op jit(solution)/shard_map/ppermute | solution.py:564
  43.8 19.8 %copy-start.17 = (bf16[64,2560]{1,0:T(8,128)(2,1)}, bf16[64,2560]{1,0:T(8,128)(2,1)S(1)}, u32[]{:S(2)}) copy-start(bf16[64,2560]{1,0:T(8,128)(2,1)S(1)} %collective-permute-done.15.refs_11_) | copy-start | bytes 983044
  43.8 8.4 %collective-permute-start.16 = (bf16[64,2560]{1,0:T(8,128)(2,1)S(1)}, bf16[64,2560]{1,0:T(8,128)(2,1)S(1)}, u32[]{:S(2)}, u32[]{:S(2)}) collective-permute-start(bf16[64,2560]{1,0:T(8,128)(2,1)S(1)} %collective-permute-done.15.refs_11_), channel_id=1, source_target_pairs={{0,1},{1,0},{2,3},{3,2},{4,5},{5,4},{6,7},{7,6},{8,9},{9,8},{10,11... | collective-permute-start | bytes 983048 | tf_op jit(solution)/shard_map/ppermute | solution.py:567
  47.7 4.4 %collective-permute-start.17 = (bf16[32,2560]{1,0:T(8,128)(2,1)S(1)}, bf16[32,2560]{1,0:T(8,128)(2,1)S(1)}, u32[]{:S(2)}, u32[]{:S(2)}) collective-permute-start(bf16[32,2560]{1,0:T(8,128)(2,1)S(1)} %copy-done.16), channel_id=1, source_target_pairs={{0,1},{1,0},{2,3},{3,2},{4,5},{5,4},{6,7},{7,6},{8,9},{9,8},{10,11... | collective-permute-start | bytes 491528 | tf_op jit(solution)/shard_map/ppermute | solution.py:567
  51.4 12.3 %copy-start.18 = (bf16[64,2560]{1,0:T(8,128)(2,1)}, bf16[64,2560]{1,0:T(8,128)(2,1)S(1)}, u32[]{:S(2)}) copy-start(bf16[64,2560]{1,0:T(8,128)(2,1)S(1)} %collective-permute-done.9.refs_9_) | copy-start | bytes 983044
  51.4 1.7 %collective-permute-start.14 = (bf16[64,2560]{1,0:T(8,128)(2,1)S(1)}, bf16[64,2560]{1,0:T(8,128)(2,1)S(1)}, u32[]{:S(2)}, u32[]{:S(2)}) collective-permute-start(bf16[64,2560]{1,0:T(8,128)(2,1)S(1)} %collective-permute-done.9.refs_9_), channel_id=1, source_target_pairs={{0,1},{1,0},{2,3},{3,2},{4,5},{5,4},{6,7},{7,6},{8,9},{9,8},{10,11... | collective-permute-start | bytes 983048 | tf_op jit(solution)/shard_map/ppermute | solution.py:567
  51.5 2.8 %collective-permute-start.5 = (bf16[64,2560]{1,0:T(8,128)(2,1)S(1)}, bf16[64,2560]{1,0:T(8,128)(2,1)S(1)}, u32[]{:S(2)}, u32[]{:S(2)}) collective-permute-start(bf16[64,2560]{1,0:T(8,128)(2,1)S(1)} %copy-done.11), channel_id=1, source_target_pairs={{0,1},{1,0},{2,3},{3,2},{4,5},{5,4},{6,7},{7,6},{8,9},{9,8},{10,11... | collective-permute-start | bytes 983048 | tf_op jit(solution)/shard_map/ppermute | solution.py:567
  51.9 2.3 %collective-permute-start.6 = (bf16[64,2560]{1,0:T(8,128)(2,1)S(1)}, bf16[64,2560]{1,0:T(8,128)(2,1)S(1)}, u32[]{:S(2)}, u32[]{:S(2)}) collective-permute-start(bf16[64,2560]{1,0:T(8,128)(2,1)S(1)} %copy-done.9), channel_id=1, source_target_pairs={{0,1},{1,0},{2,3},{3,2},{4,5},{5,4},{6,7},{7,6},{8,9},{9,8},{10,11... | collective-permute-start | bytes 983048 | tf_op jit(solution)/shard_map/ppermute | solution.py:567
  52.0 2.2 %copy-start.25 = (bf16[32,2560]{1,0:T(8,128)(2,1)}, bf16[32,2560]{1,0:T(8,128)(2,1)S(1)}, u32[]{:S(2)}) copy-start(bf16[32,2560]{1,0:T(8,128)(2,1)S(1)} %collective-permute-done.17.refs_8_) | copy-start | bytes 491524
  52.0 11.6 %collective-permute-start.18 = (bf16[64,2560]{1,0:T(8,128)(2,1)S(1)}, bf16[64,2560]{1,0:T(8,128)(2,1)S(1)}, u32[]{:S(2)}, u32[]{:S(2)}) collective-permute-start(bf16[64,2560]{1,0:T(8,128)(2,1)S(1)} %collective-permute-done.9.refs_9_), channel_id=1, source_target_pairs={{0,2},{2,6},{6,4},{4,0},{1,3},{3,7},{7,5},{5,1},{8,10},{10,14},{14... | collective-permute-start | bytes 983048 | tf_op jit(solution)/shard_map/ppermute | solution.py:564
  52.2 11.4 %copy-start.19 = (bf16[64,2560]{1,0:T(8,128)(2,1)}, bf16[64,2560]{1,0:T(8,128)(2,1)S(1)}, u32[]{:S(2)}) copy-start(bf16[64,2560]{1,0:T(8,128)(2,1)S(1)} %collective-permute-done.16.refs_12_) | copy-start | bytes 983044
  52.2 2.0 %collective-permute-start.8 = (bf16[32,2560]{1,0:T(8,128)(2,1)}, bf16[32,2560]{1,0:T(8,128)(2,1)S(1)}, u32[]{:S(2)}, u32[]{:S(2)}) collective-permute-start(bf16[32,2560]{1,0:T(8,128)(2,1)} %collective-permute-done.7.refs_5_), channel_id=1, source_target_pairs={{0,1},{1,0},{2,3},{3,2},{4,5},{5,4},{6,7},{7,6},{8,9},{9,8},{10,11... | collective-permute-start | bytes 491528 | tf_op jit(solution)/shard_map/ppermute | solution.py:567
  53.1 10.6 %copy-start.20 = (bf16[64,2560]{1,0:T(8,128)(2,1)}, bf16[64,2560]{1,0:T(8,128)(2,1)S(1)}, u32[]{:S(2)}) copy-start(bf16[64,2560]{1,0:T(8,128)(2,1)S(1)} %collective-permute-done.14.refs_10_) | copy-start | bytes 983044
  54.2 0.7 copy-start.26
  54.2 0.8 copy-start.22
  55.0 0.7 copy-start.23
  63.7 2.0 %copy-start.21 = (bf16[64,2560]{1,0:T(8,128)(2,1)}, bf16[64,2560]{1,0:T(8,128)(2,1)S(1)}, u32[]{:S(2)}) copy-start(bf16[64,2560]{1,0:T(8,128)(2,1)S(1)} %collective-permute-done.18.refs_13_) | copy-start | bytes 983044
  63.7 1.7 %collective-permute-start.19 = (bf16[64,2560]{1,0:T(8,128)(2,1)S(1)}, bf16[64,2560]{1,0:T(8,128)(2,1)S(1)}, u32[]{:S(2)}, u32[]{:S(2)}) collective-permute-start(bf16[64,2560]{1,0:T(8,128)(2,1)S(1)} %collective-permute-done.18.refs_13_), channel_id=1, source_target_pairs={{0,1},{1,0},{2,3},{3,2},{4,5},{5,4},{6,7},{7,6},{8,9},{9,8},{10,11... | collective-permute-start | bytes 983048 | tf_op jit(solution)/shard_map/ppermute | solution.py:567
  65.4 0.7 copy-start.24
  65.4 17.6 %collective-permute-start.22 = (bf16[1216,640]{1,0:T(8,128)(2,1)}, bf16[1216,640]{1,0:T(8,128)(2,1)S(1)}, u32[]{:S(2)}, u32[]{:S(2)}) collective-permute-start(bf16[1216,640]{1,0:T(8,128)(2,1)} %get-tuple-element.108.refs_7_), channel_id=1, source_target_pairs={{0,1},{1,0},{2,3},{3,2},{4,5},{5,4},{6,7},{7,6},{8,9},{9,8},{10,11... | collective-permute-start | bytes 4669448 | tf_op jit(solution)/shard_map/ppermute | solution.py:567
  77.6 5.4 %copy-start.2 = (bf16[1216,640]{1,0:T(8,128)(2,1)S(1)}, bf16[1216,640]{1,0:T(8,128)(2,1)}, u32[]{:S(2)}) copy-start(bf16[1216,640]{1,0:T(8,128)(2,1)} %get-tuple-element.87.refs_6_.w_own) | copy-start | bytes 4669444
  77.6 1.9 %collective-permute-start.21 = (bf16[128,1216]{1,0:T(8,128)(2,1)}, bf16[128,1216]{1,0:T(8,128)(2,1)S(1)}, u32[]{:S(2)}, u32[]{:S(2)}) collective-permute-start(bf16[128,1216]{1,0:T(8,128)(2,1)} %get-tuple-element.105), channel_id=1, source_target_pairs={{0,1},{1,0},{2,3},{3,2},{4,5},{5,4},{6,7},{7,6},{8,9},{9,8},{10,11... | collective-permute-start | bytes 933896 | tf_op jit(solution)/shard_map/ppermute | solution.py:567
  77.9 5.0 %collective-permute-start.20 = (bf16[384,640]{1,0:T(8,128)(2,1)}, bf16[384,640]{1,0:T(8,128)(2,1)S(1)}, u32[]{:S(2)}, u32[]{:S(2)}) collective-permute-start(bf16[384,640]{1,0:T(8,128)(2,1)} %get-tuple-element.106.own), channel_id=1, source_target_pairs={{0,1},{1,0},{2,3},{3,2},{4,5},{5,4},{6,7},{7,6},{8,9},{9,8},{10,11... | collective-permute-start | bytes 1474568 | tf_op jit(solution)/shard_map/ppermute | solution.py:567
  80.7 8.0 %collective-permute-start.26 = (bf16[64,1216]{1,0:T(8,128)(2,1)S(1)}, bf16[64,1216]{1,0:T(8,128)(2,1)S(1)}, u32[]{:S(2)}, u32[]{:S(2)}) collective-permute-start(bf16[64,1216]{1,0:T(8,128)(2,1)S(1)} %get-tuple-element.124), channel_id=1, source_target_pairs={{0,2},{2,6},{6,4},{4,0},{1,3},{3,7},{7,5},{5,1},{8,10},{10,14},{14... | collective-permute-start | bytes 466952 | tf_op jit(solution)/shard_map/ppermute | solution.py:564
  82.3 9.7 %collective-permute-start.23 = (bf16[64,1216]{1,0:T(8,128)(2,1)S(1)}, bf16[64,1216]{1,0:T(8,128)(2,1)S(1)}, u32[]{:S(2)}, u32[]{:S(2)}) collective-permute-start(bf16[64,1216]{1,0:T(8,128)(2,1)S(1)} %get-tuple-element.125), channel_id=1, source_target_pairs={{0,2},{2,6},{6,4},{4,0},{1,3},{3,7},{7,5},{5,1},{8,10},{10,14},{14... | collective-permute-start | bytes 466952 | tf_op jit(solution)/shard_map/ppermute | solution.py:564
  83.0 1.0 copy-start.6
  85.7 20.7 %copy-start.1 = (f32[128,1216]{1,0:T(8,128)S(1)}, f32[128,1216]{1,0:T(8,128)}, u32[]{:S(2)}) copy-start(f32[128,1216]{1,0:T(8,128)} %get-tuple-element.116.normed) | copy-start | bytes 1867780
  85.7 20.7 %copy-start.5 = (f32[1,1216]{1,0:T(1,128)S(1)}, f32[1,1216]{1,0:T(1,128)}, u32[]{:S(2)}) copy-start(f32[1,1216]{1,0:T(1,128)} %get-tuple-element.115.scale) | copy-start | bytes 14596
  88.7 6.7 %collective-permute-start.27 = (bf16[64,1216]{1,0:T(8,128)(2,1)S(1)}, bf16[64,1216]{1,0:T(8,128)(2,1)S(1)}, u32[]{:S(2)}, u32[]{:S(2)}) collective-permute-start(bf16[64,1216]{1,0:T(8,128)(2,1)S(1)} %add_convert_fusion.2), channel_id=1, source_target_pairs={{0,2},{2,6},{6,4},{4,0},{1,3},{3,7},{7,5},{5,1},{8,10},{10,14},{14... | collective-permute-start | bytes 466952 | tf_op jit(solution)/shard_map/ppermute | solution.py:564
  92.0 16.0 %copy-start.3 = (f32[128,1216]{1,0:T(8,128)S(1)}, f32[128,1216]{1,0:T(8,128)}, u32[]{:S(2)}) copy-start(f32[128,1216]{1,0:T(8,128)} %get-tuple-element.119.base) | copy-start | bytes 1867780
  92.0 16.0 %copy-start.4 = (f32[128,128]{1,0:T(8,128)S(1)}, f32[128,128]{1,0:T(8,128)}, u32[]{:S(2)}) copy-start(f32[128,128]{1,0:T(8,128)} %get-tuple-element.120.inv_std) | copy-start | bytes 196612
  92.0 8.1 %collective-permute-start.24 = (bf16[64,1216]{1,0:T(8,128)(2,1)S(1)}, bf16[64,1216]{1,0:T(8,128)(2,1)S(1)}, u32[]{:S(2)}, u32[]{:S(2)}) collective-permute-start(bf16[64,1216]{1,0:T(8,128)(2,1)S(1)} %add_convert_fusion.4), channel_id=1, source_target_pairs={{0,2},{2,6},{6,4},{4,0},{1,3},{3,7},{7,5},{5,1},{8,10},{10,14},{14... | collective-permute-start | bytes 466952 | tf_op jit(solution)/shard_map/ppermute | solution.py:564
  95.5 7.9 %collective-permute-start.28 = (bf16[64,1216]{1,0:T(8,128)(2,1)S(1)}, bf16[64,1216]{1,0:T(8,128)(2,1)S(1)}, u32[]{:S(2)}, u32[]{:S(2)}) collective-permute-start(bf16[64,1216]{1,0:T(8,128)(2,1)S(1)} %add_convert_fusion.1), channel_id=1, source_target_pairs={{0,2},{2,6},{6,4},{4,0},{1,3},{3,7},{7,5},{5,1},{8,10},{10,14},{14... | collective-permute-start | bytes 466952 | tf_op jit(solution)/shard_map/ppermute | solution.py:564
  100.1 6.3 %collective-permute-start.25 = (bf16[64,1216]{1,0:T(8,128)(2,1)S(1)}, bf16[64,1216]{1,0:T(8,128)(2,1)S(1)}, u32[]{:S(2)}, u32[]{:S(2)}) collective-permute-start(bf16[64,1216]{1,0:T(8,128)(2,1)S(1)} %add_convert_fusion.3), channel_id=1, source_target_pairs={{0,2},{2,6},{6,4},{4,0},{1,3},{3,7},{7,5},{5,1},{8,10},{10,14},{14... | collective-permute-start | bytes 466952 | tf_op jit(solution)/shard_map/ppermute | solution.py:564
  106.6 1.3 %collective-permute-start.29 = (f32[128,128]{1,0:T(8,128)S(1)}, f32[128,128]{1,0:T(8,128)S(1)}, u32[]{:S(2)}, u32[]{:S(2)}) collective-permute-start(f32[128,128]{1,0:T(8,128)S(1)} %get-tuple-element.118.sums), channel_id=1, source_target_pairs={{0,1},{1,0},{2,3},{3,2},{4,5},{5,4},{6,7},{7,6},{8,9},{9,8},{10,11... | collective-permute-start | bytes 196616 | tf_op jit(solution)/shard_map/ppermute | solution.py:567

commit v2 on v0

--- a/solution.py
+++ b/solution.py
@@ -210,17 +210,21 @@
         return copy
 
     def weights(self, scalars, w_in, w_all, shard, first=0):
-        columns = w_in[0].shape[1] - first
-        return [
-            self.start(
-                piece.at[:, pl.ds(first, columns)],
-                w_all.at[
-                    pl.ds(pl.multiple_of(scalars[1 + n % 4] * shard, 16), shard),
-                    pl.ds(n // 4 * columns, columns),
-                ],
+        part = w_in[0].shape[1]
+        copies = []
+        for n, piece in enumerate(w_in):
+            there = n // 4 * (part - first)
+            columns = min(part - first, w_all.shape[1] - there)
+            copies.append(
+                self.start(
+                    piece.at[:, pl.ds(first, columns)],
+                    w_all.at[
+                        pl.ds(pl.multiple_of(scalars[1 + n % 4] * shard, 16), shard),
+                        pl.ds(there, columns),
+                    ],
+                )
             )
-            for n, piece in enumerate(w_in)
-        ]
+        return copies
 
     def rows(self, core, pieces, target, rows):
         half = rows // 2
@@ -269,10 +273,9 @@
     for copy in w_copies:
         copy.wait()
     half = width // 2
-    columns = pl.ds(0, w_keep.shape[1])
     out_copies = []
     for holder, target in ((core, w_keep), (1 - core, w_give)):
-        source = w_all.at[pl.ds(pl.multiple_of(holder * half, 16), half), columns]
+        source = w_all.at[pl.ds(pl.multiple_of(holder * half, 16), half)]
         out_copies.append(copies.start(source, target))
     for copy in row_copies:
         copy.wait()
@@ -309,8 +312,7 @@
     copies = Copies(sems)
     w_copies = copies.weights(scalars, w_in, w_out, shard, first_column)
     row_copies = copies.rows(core, cot_in, cot_all, rows)
-    pairs = list(zip(projected, refs))
-    local_copies = [copies.start(*pairs[n]) for n in (0, 1, 4, 5)]
+    local_copies = [copies.start(*one) for one in zip(projected, refs)]
     score_scale = HD ** (-0.5)
     span = 2 * rows
 
@@ -324,13 +326,15 @@
 
     for copy in w_copies:
         copy.wait()
-    for copy in row_copies:
-        copy.wait()
-    out_grad = jnp.dot(cot_all[:, :width], w_out[...], preferred_element_type=jnp.float32)
-    d_all[...] = out_grad.astype(jnp.bfloat16)
+    arrivals = [row_copies[:3], row_copies[3:]]
+    for b in range(count // 2):
+        for copy in arrivals[b]:
+            copy.wait()
+        here = slice(b * span, (b + 1) * span)
+        out_grad = jnp.dot(cot_all[here, :width], w_out[...], preferred_element_type=jnp.float32)
+        d_all[here, :] = out_grad.astype(jnp.bfloat16)
     window_heads(scalars, count, rows, text_dev, cot_all, width, extra, values_text)
-    late_copies = [copies.start(*pairs[n]) for n in (2, 3, 6, 7)]
-    for copy in local_copies:
+    for copy in local_copies[:6]:
         copy.wait()
 
     d_first = d_all.shape[1] - inner
@@ -374,8 +378,6 @@
         inside = (lane >= i * HD) & (lane < (i + 1) * HD) & (scalars[7 + count + i] > 0)
         mine = jnp.where(inside, 1.0, mine)
     gains = head_gains(gain, slots)
-    for copy in late_copies[:2]:
-        copy.wait()
     for b in range(count // 2):
         here = slice(b * span, (b + 1) * span)
         scaled = grads[here, : 2 * inner].astype(jnp.bfloat16).astype(jnp.float32) * gains
@@ -389,7 +391,7 @@
     first = stacked[rows : 2 * rows, :]
     rest_out[: (count - 2) * rows, :] = stacked[2 * rows :, :]
     rest_out[(count - 2) * rows :, :] = stacked[:rows, :]
-    for copy in late_copies[2:]:
+    for copy in local_copies[6:]:
         copy.wait()
     theirs_out[...] = dot(first, w_give[...], NT).astype(jnp.bfloat16)
     mine_out[...] = dot(first, w_keep[...], NT)
@@ -397,7 +399,7 @@
 
 def project_call(scalars, gain, mod, weights, slots, rows, text_dev, count):
     shard = weights[0].shape[0]
-    columns = 4 * slots * HD
+    columns = whole_tiles(3 * slots * HD)
     width = mod[0].shape[1] - EXTRA
     tokens = rows * count
     text_rows = text_dev * count

time: 109 us -> 109 us (level)
  no operation moved by 1% of the time
where the time goes in v2:
time: 109 us; the launch traced here: 108 us
  waiting for transfers between devices  40.2 us (37%)
  Pallas kernels  30.8 us (28%)
  starting transfers between devices  25.5 us (23%)
  local copies, waits for them, and re-layouts  7.5 us (7%)
  other arithmetic  2.39 us (2%)
  between operations  1.71 us (2%)
    ppermute x10, waiting for transfers between devices, step(): return lax.ppermute(moving, 'seq', seq_next)  26.2 us
    pallas_call x1, Pallas kernels, attend_call(): pl.pallas_call(functools.partial(attend_kernel, slots, count, rows, shard...  10.7 us
    ppermute x3, starting transfers between devices, step_back(): return lax.ppermute(moving, 'seq', [(b, a) for a, b in seq_next])  9.59 us
    ppermute x3, waiting for transfers between devices, step_back(): return lax.ppermute(moving, 'seq', [(b, a) for a, b in seq_next])  8.36 us
    pallas_call x1, Pallas kernels, project_call(): pl.pallas_call(functools.partial(project_kernel, slots, count, rows, shar...  7.78 us
    ppermute x10, starting transfers between devices, step(): return lax.ppermute(moving, 'seq', seq_next)  5.97 us
    ppermute x11, waiting for transfers between devices, other_core(): return lax.ppermute(moving, 'head', swap)  5.59 us
    pallas_call x3, Pallas kernels, local_call(): pl.pallas_call(kernel, out_shape=tuple((jax.ShapeDtypeStruct(*one) for on...  5.12 us
  transfers between devices with their start and end apart: 30, of which 16 were waited for; matrix products, arithmetic and copies ran while one was open for 6% of the time, Pallas kernels for 25%

profile of v2, /device:TPU:0, one launch (start us, length us, event | category | flops | bytes accessed | tf_op | source)
XLA Modules:
  0.0 108.1 jit_solution(11125202806953118573)
XLA Ops:
  0.7 2.8 %shard_map.91 = (bf16[64,2560]{1,0:T(8,128)(2,1)}, f32[8,2432]{1,0:T(8,128)}, bf16[64,128]{1,0:T(8,128)(2,1)}) custom-call(s32[1]{0:T(128)S(6)} %copy.11.step, s32[1]{0:T(128)} %bitcast.core, bf16[128,2432]{1,0:T(8,128)(2,1)} %bitcast.31, f32[3,28,2432]{2,1,0:T(8,128)} %bitcast.33, f32[128,2432]{1,0:T(8,128)} %bitcast.28, bf16[8,2,640]{2,1,0:T(2,128)(2,1)} %bitcast.34), custom_call_target="tpu_custom_call" | custom-call | flops 1245184 | bytes 2490368 | tf_op jit(solution)/shard_map/pallas_call | solution.py:110
  3.6 4.0 %collective-permute-start.3 = (bf16[64,2560]{1,0:T(8,128)(2,1)}, bf16[64,2560]{1,0:T(8,128)(2,1)S(1)}, u32[]{:S(2)}, u32[]{:S(2)}) collective-permute-start(bf16[64,2560]{1,0:T(8,128)(2,1)} %get-tuple-element.65), channel_id=1, source_target_pairs={{2,0},{6,2},{4,6},{0,4},{3,1},{7,3},{5,7},{1,5},{10,8},{14,10},{12... | collective-permute-start | bytes 983048 | tf_op jit(solution)/shard_map/ppermute | solution.py:571
  7.6 1.7 %dynamic-slice_bitcast_fusion.1 = (bf16[608,192]{1,0:T(8,128)(2,1)S(1)}, bf16[608,192]{1,0:T(8,128)(2,1)S(1)}, bf16[608,192]{1,0:T(8,128)(2,1)S(1)}) fusion(bf16[608,3,640]{2,0,1:T(8,128)(2,1)} %param.15, s32[]{:T(128)S(6)} %select_n.103), kind=kLoop, calls=%fused_computation.8 | loop fusion | bytes 1400836 | tf_op jit(solution)/shard_map/squeeze | solution.py:587
  9.3 0.2 dynamic-slice_bitcast_fusion
  9.5 0.2 pad_maximum_fusion.1.refs_13_.refs_15_
  9.7 1.6 %collective-permute-start.1 = (bf16[608,384]{1,0:T(8,128)(2,1)S(1)}, bf16[608,384]{1,0:T(8,128)(2,1)S(1)}, u32[]{:S(2)}, u32[]{:S(2)}) collective-permute-start(bf16[608,384]{1,0:T(8,128)(2,1)S(1)} %pad_maximum_fusion.1.refs_13_.refs_15_), channel_id=1, source_target_pairs={{0,8},{1,17},{8,0},{9,25},{16,24},{17,1},{24,16},{25,9},{2,10},{3,... | collective-permute-start | bytes 1400840 | tf_op jit(solution)/shard_map/ppermute | solution.py:592
  11.2 0.9 pad_maximum_fusion.refs_9_
  12.2 0.5 collective-permute-start
  12.7 1.5 %collective-permute-start.11 = (bf16[608,384]{1,0:T(8,128)(2,1)S(1)}, bf16[608,384]{1,0:T(8,128)(2,1)S(1)}, u32[]{:S(2)}, u32[]{:S(2)}) collective-permute-start(bf16[608,384]{1,0:T(8,128)(2,1)S(1)} %pad_maximum_fusion.1.refs_13_.refs_15_), channel_id=1, source_target_pairs={{0,16},{1,9},{8,24},{9,1},{16,0},{17,25},{24,8},{25,17},{2,18},{3,... | collective-permute-start | bytes 1400840 | tf_op jit(solution)/shard_map/ppermute | solution.py:593
  14.2 1.9 %collective-permute-done.3.following.refs_3_ = bf16[64,2560]{1,0:T(8,128)(2,1)S(1)} collective-permute-done((bf16[64,2560]{1,0:T(8,128)(2,1)}, bf16[64,2560]{1,0:T(8,128)(2,1)S(1)}, u32[]{:S(2)}, u32[]{:S(2)}) %collective-permute-start.3) | collective-permute-done | bytes 327712 | tf_op jit(solution)/shard_map/ppermute | solution.py:571
  16.1 0.7 slice.16
  16.8 3.3 %collective-permute-start.4 = (bf16[32,2560]{1,0:T(8,128)(2,1)}, bf16[32,2560]{1,0:T(8,128)(2,1)S(1)}, u32[]{:S(2)}, u32[]{:S(2)}) collective-permute-start(bf16[32,2560]{1,0:T(8,128)(2,1)} %slice.16), channel_id=1, source_target_pairs={{2,0},{6,2},{4,6},{0,4},{3,1},{7,3},{5,7},{1,5},{10,8},{14,10},{12... | collective-permute-start | bytes 491528 | tf_op jit(solution)/shard_map/ppermute | solution.py:571
  20.1 4.7 %collective-permute-done.2.previous.refs_1_ = bf16[64,2560]{1,0:T(8,128)(2,1)S(1)} collective-permute-done((bf16[64,2560]{1,0:T(8,128)(2,1)}, bf16[64,2560]{1,0:T(8,128)(2,1)S(1)}, u32[]{:S(2)}, u32[]{:S(2)}) %collective-permute-start.2) | collective-permute-done | bytes 327712 | tf_op jit(solution)/shard_map/ppermute | solution.py:565
  24.8 0.7 slice.17
  25.5 0.7 collective-permute-start.7
  26.2 1.5 %collective-permute-start.10 = (bf16[608,384]{1,0:T(8,128)(2,1)}, bf16[608,384]{1,0:T(8,128)(2,1)}, u32[]{:S(2)}, u32[]{:S(2)}) collective-permute-start(bf16[608,384]{1,0:T(8,128)(2,1)} %pad_maximum_fusion.refs_9_), channel_id=1, source_target_pairs={{0,16},{1,9},{8,24},{9,1},{16,0},{17,25},{24,8},{25,17},{2,18},{3,... | collective-permute-start | bytes 1400840 | tf_op jit(solution)/shard_map/ppermute | solution.py:593
  28.4 0.6 stack.67.core.scalars
  29.1 0.7 copy-done.14
  29.7 2.7 %shard_map.92 = (bf16[64,2560]{1,0:T(8,128)(2,1)}, f32[8,128]{1,0:T(8,128)}) custom-call(s32[14]{0:T(128)} %stack.67.core.scalars, f32[128,2432]{1,0:T(8,128)} %bitcast.29, f32[8,2432]{1,0:T(8,128)} %get-tuple-element.63.table_rows, bf16[8,2,640]{2,1,0:T(2,128)(2,1)} %bitcast.35, bf16[64,128]{1,0:T(8,128)(2,1)} %get-tuple-element.68.extra, ...), custom_call_target="tpu_custom_call" | custom-call | flops 622592 | bytes 933888 | tf_op jit(solution)/shard_map/pallas_call | solution.py:162
  32.5 0.3 collective-permute-done.7.refs_5_
  32.8 2.3 %collective-permute-start.15 = (bf16[64,2560]{1,0:T(8,128)(2,1)}, bf16[64,2560]{1,0:T(8,128)(2,1)}, u32[]{:S(2)}, u32[]{:S(2)}) collective-permute-start(bf16[64,2560]{1,0:T(8,128)(2,1)} %get-tuple-element.76), channel_id=1, source_target_pairs={{2,0},{6,2},{4,6},{0,4},{3,1},{7,3},{5,7},{1,5},{10,8},{14,10},{12... | collective-permute-start | bytes 983048 | tf_op jit(solution)/shard_map/ppermute | solution.py:571
  35.0 1.5 %collective-permute-start.12 = (bf16[608,384]{1,0:T(8,128)(2,1)S(1)}, bf16[608,384]{1,0:T(8,128)(2,1)S(1)}, u32[]{:S(2)}, u32[]{:S(2)}) collective-permute-start(bf16[608,384]{1,0:T(8,128)(2,1)S(1)} %collective-permute-done.refs_10_), channel_id=1, source_target_pairs={{0,16},{1,9},{8,24},{9,1},{16,0},{17,25},{24,8},{25,17},{2,18},{3,... | collective-permute-start | bytes 1400840 | tf_op jit(solution)/shard_map/ppermute | solution.py:628
  36.5 0.5 collective-permute-start.13
  37.1 6.5 %collective-permute-done.15.refs_11_ = bf16[64,2560]{1,0:T(8,128)(2,1)} collective-permute-done((bf16[64,2560]{1,0:T(8,128)(2,1)}, bf16[64,2560]{1,0:T(8,128)(2,1)}, u32[]{:S(2)}, u32[]{:S(2)}) %collective-permute-start.15) | collective-permute-done | bytes 327712 | tf_op jit(solution)/shard_map/ppermute | solution.py:571
  43.6 3.7 %shard_map.93 = (bf16[128,2560]{1,0:T(8,128)(2,1)}, bf16[128,2560]{1,0:T(8,128)(2,1)}, f32[128,1216]{1,0:T(8,128)}, f32[1,1216]{1,0:T(1,128)}, f32[128,128]{1,0:T(8,128)}, /*index=5*/f32[128,1216]{1,0:T(8,128)}) custom-call(s32[1]{0:T(128)} %bitcast.core, bf16[128,2432]{1,0:T(8,128)(2,1)} %bitcast.32, f32[128,2432]{1,0:T(8,128)} %bitcast.30, ...), custom_call_target="tpu_custom_call" | custom-call | flops 661505 | bytes 1986564 | tf_op jit(solution)/shard_map/pallas_call | solution.py:516
  47.3 0.6 collective-permute-start.17
  47.9 3.6 %collective-permute-done.9.refs_9_ = bf16[64,2560]{1,0:T(8,128)(2,1)S(1)} collective-permute-done((bf16[64,2560]{1,0:T(8,128)(2,1)}, bf16[64,2560]{1,0:T(8,128)(2,1)S(1)}, u32[]{:S(2)}, u32[]{:S(2)}) %collective-permute-start.9) | collective-permute-done | bytes 327712 | tf_op jit(solution)/shard_map/ppermute | solution.py:565
  51.4 0.1 collective-permute-start.14
  51.5 0.5 collective-permute-start.5
  52.0 0.1 collective-permute-start.6
  52.1 0.2 collective-permute-start.18
  52.3 0.3 collective-permute-start.8
  52.6 0.5 collective-permute-done.14.refs_10_
  53.1 1.1 %collective-permute-done.8.refs_6_ = bf16[32,2560]{1,0:T(8,128)(2,1)S(1)} collective-permute-done((bf16[32,2560]{1,0:T(8,128)(2,1)}, bf16[32,2560]{1,0:T(8,128)(2,1)S(1)}, u32[]{:S(2)}, u32[]{:S(2)}) %collective-permute-start.8) | collective-permute-done | bytes 163872 | tf_op jit(solution)/shard_map/ppermute | solution.py:568
  54.3 0.7 copy-done.24
  55.0 0.7 copy-done.21
  55.7 7.8 %shard_map.94 = (bf16[512,576]{1,0:T(8,128)(2,1)}, bf16[192,512]{1,0:T(8,128)(2,1)}, f32[512,384]{1,0:T(8,128)}, f32[512,384]{1,0:T(8,128)}, bf16[3,32,64]{2,1,0...) custom-call(s32[14]{0:T(128)} %stack.67.core.scalars, ...), custom_call_target="tpu_custom_call" | custom-call | flops 1434451968 | bytes 6914048 | tf_op jit(solution)/shard_map/pallas_call | solution.py:412
  63.5 0.3 collective-permute-start.19
  63.9 1.3 %collective-permute-done.19.refs_14_ = bf16[64,2560]{1,0:T(8,128)(2,1)S(1)} collective-permute-done((bf16[64,2560]{1,0:T(8,128)(2,1)S(1)}, bf16[64,2560]{1,0:T(8,128)(2,1)S(1)}, u32[]{:S(2)}, u32[]{:S(2)}) %collective-permute-start.19) | collective-permute-done | bytes 327712 | tf_op jit(solution)/shard_map/ppermute | solution.py:568
  65.2 0.3 collective-permute-start.22
  65.5 0.4 copy-done.22
  65.9 10.7 %shard_map.95 = (f32[128,1216]{1,0:T(8,128)}, bf16[128,1216]{1,0:T(8,128)(2,1)}, bf16[384,640]{1,0:T(8,128)(2,1)}) custom-call(s32[14]{0:T(128)} %stack.67.core.scalars, f32[2,64]{1,0:T(2,128)} %gain.3, bf16[512,576]{1,0:T(8,128)(2,1)} %get-tuple-element.81.refs_0_, bf16[192,512]{1,0:T(8,128)(2,1)} %get-tuple-element.82.refs_1_, ...), custom_call_target="tpu_custom_call" | custom-call | flops 981467136 | bytes 4358144 | tf_op jit(solution)/shard_map/pallas_call | solution.py:444
  76.6 0.3 collective-permute-start.21
  77.0 0.2 collective-permute-start.20
  77.2 1.3 %collective-permute-done.21 = bf16[128,1216]{1,0:T(8,128)(2,1)S(1)} collective-permute-done((bf16[128,1216]{1,0:T(8,128)(2,1)}, bf16[128,1216]{1,0:T(8,128)(2,1)S(1)}, u32[]{:S(2)}, u32[]{:S(2)}) %collective-permute-start.21) | collective-permute-done | bytes 311328 | tf_op jit(solution)/shard_map/ppermute | solution.py:568
  78.5 1.2 %add_convert_fusion = bf16[128,1216]{1,0:T(8,128)(2,1)S(1)} fusion(f32[128,1216]{1,0:T(8,128)} %get-tuple-element.104, bf16[128,1216]{1,0:T(8,128)(2,1)S(1)} %collective-permute-done.21), kind=kLoop, calls=%fused_computation | loop fusion | flops 466944 | bytes 1245184 | tf_op jit(solution)/shard_map/convert_element_type | solution.py:645
  79.7 1.6 %collective-permute-start.26 = (bf16[64,1216]{1,0:T(8,128)(2,1)S(1)}, bf16[64,1216]{1,0:T(8,128)(2,1)S(1)}, u32[]{:S(2)}, u32[]{:S(2)}) collective-permute-start(bf16[64,1216]{1,0:T(8,128)(2,1)S(1)} %get-tuple-element.124), channel_id=1, source_target_pairs={{0,2},{2,6},{6,4},{4,0},{1,3},{3,7},{7,5},{5,1},{8,10},{10,14},{14... | collective-permute-start | bytes 466952 | tf_op jit(solution)/shard_map/ppermute | solution.py:565
  81.3 0.7 collective-permute-start.23
  82.0 1.0 copy-done.6
  83.0 1.7 %shard_map.96 = (f32[64,1216]{1,0:T(8,128)S(1)}, f32[64,1216]{1,0:T(8,128)S(1)}, f32[64,1216]{1,0:T(8,128)S(1)}, f32[64,1216]{1,0:T(8,128)S(1)}, f32[64,1216]{1,0:T(8,128)S(1)}, /*index=5*/f32[64,1216]{1,0:T(8,128)S(1)}) custom-call(bf16[384,640]{1,0:T(8,128)(2,1)S(1)} %copy-done.6, bf16[384,640]{1,0:T(8,128)(2,1)S(1)} %collective-permute-done.20.other, ...), custom_call_target="tpu_custom_call" | custom-call | flops 1195376640 | bytes 5963776 | tf_op jit(solution)/shard_map/pallas_call | solution.py:480
  84.8 2.9 %collective-permute-done.26 = bf16[64,1216]{1,0:T(8,128)(2,1)S(1)} collective-permute-done((bf16[64,1216]{1,0:T(8,128)(2,1)S(1)}, bf16[64,1216]{1,0:T(8,128)(2,1)S(1)}, u32[]{:S(2)}, u32[]{:S(2)}) %collective-permute-start.26) | collective-permute-done | bytes 155680 | tf_op jit(solution)/shard_map/ppermute | solution.py:565
  87.7 0.7 collective-permute-start.27
  88.4 2.5 %collective-permute-done.23 = bf16[64,1216]{1,0:T(8,128)(2,1)S(1)} collective-permute-done((bf16[64,1216]{1,0:T(8,128)(2,1)S(1)}, bf16[64,1216]{1,0:T(8,128)(2,1)S(1)}, u32[]{:S(2)}, u32[]{:S(2)}) %collective-permute-start.23) | collective-permute-done | bytes 155680 | tf_op jit(solution)/shard_map/ppermute | solution.py:565
  91.0 0.9 collective-permute-start.24
  91.9 2.5 %collective-permute-done.27 = bf16[64,1216]{1,0:T(8,128)(2,1)S(1)} collective-permute-done((bf16[64,1216]{1,0:T(8,128)(2,1)S(1)}, bf16[64,1216]{1,0:T(8,128)(2,1)S(1)}, u32[]{:S(2)}, u32[]{:S(2)}) %collective-permute-start.27) | collective-permute-done | bytes 155680 | tf_op jit(solution)/shard_map/ppermute | solution.py:565
  94.5 1.1 %collective-permute-start.28 = (bf16[64,1216]{1,0:T(8,128)(2,1)S(1)}, bf16[64,1216]{1,0:T(8,128)(2,1)S(1)}, u32[]{:S(2)}, u32[]{:S(2)}) collective-permute-start(bf16[64,1216]{1,0:T(8,128)(2,1)S(1)} %add_convert_fusion.1), channel_id=1, source_target_pairs={{0,2},{2,6},{6,4},{4,0},{1,3},{3,7},{7,5},{5,1},{8,10},{10,14},{14... | collective-permute-start | bytes 466952 | tf_op jit(solution)/shard_map/ppermute | solution.py:565
  95.6 3.5 %collective-permute-done.24 = bf16[64,1216]{1,0:T(8,128)(2,1)S(1)} collective-permute-done((bf16[64,1216]{1,0:T(8,128)(2,1)S(1)}, bf16[64,1216]{1,0:T(8,128)(2,1)S(1)}, u32[]{:S(2)}, u32[]{:S(2)}) %collective-permute-start.24) | collective-permute-done | bytes 155680 | tf_op jit(solution)/shard_map/ppermute | solution.py:565
  99.1 0.1 collective-permute-start.25
  99.2 3.2 %collective-permute-done.28.far = bf16[64,1216]{1,0:T(8,128)(2,1)S(1)} collective-permute-done((bf16[64,1216]{1,0:T(8,128)(2,1)S(1)}, bf16[64,1216]{1,0:T(8,128)(2,1)S(1)}, u32[]{:S(2)}, u32[]{:S(2)}) %collective-permute-start.28) | collective-permute-done | bytes 155680 | tf_op jit(solution)/shard_map/ppermute | solution.py:565
  102.4 3.0 %collective-permute-done.25.near = bf16[64,1216]{1,0:T(8,128)(2,1)S(1)} collective-permute-done((bf16[64,1216]{1,0:T(8,128)(2,1)S(1)}, bf16[64,1216]{1,0:T(8,128)(2,1)S(1)}, u32[]{:S(2)}, u32[]{:S(2)}) %collective-permute-start.25) | collective-permute-done | bytes 155680 | tf_op jit(solution)/shard_map/ppermute | solution.py:565
  105.4 0.2 shard_map.97
  105.6 0.1 collective-permute-start.29
  105.7 1.2 %collective-permute-done.29.other = f32[128,128]{1,0:T(8,128)S(1)} collective-permute-done((f32[128,128]{1,0:T(8,128)S(1)}, f32[128,128]{1,0:T(8,128)S(1)}, u32[]{:S(2)}, u32[]{:S(2)}) %collective-permute-start.29) | collective-permute-done | bytes 65568 | tf_op jit(solution)/shard_map/ppermute | solution.py:568
  107.0 1.2 %shard_map.98 = f32[1216,128]{1,0:T(8,128)} custom-call(f32[128,1216]{1,0:T(8,128)S(1)} %get-tuple-element.117.grad, f32[128,128]{1,0:T(8,128)S(1)} %get-tuple-element.118.sums, f32[128,128]{1,0:T(8,128)S(1)} %collective-permute-done.29.other, f32[128,1216]{1,0:T(8,128)S(1)} %copy-done.1, f32[128,1216]{1,0:T(8,128)S(1)} %copy-done.3, f32[128,128]{1,0:T(8,128)S(1)} %copy-done.4), custom_call_target="tpu_custom_call" | custom-call | flops 516096 | bytes 2064384 | tf_op jit(solution)/shard_map/pallas_call | solution.py:516
  (67 shorter events, 0.3 us)
Async XLA Ops:
  0.0 9.3 %copy-start = (bf16[640,608]{0,1:T(8,128)(2,1)S(1)}, bf16[640,608]{0,1:T(8,128)(2,1)}, u32[]{:S(2)}) copy-start(bf16[640,608]{0,1:T(8,128)(2,1)} %param.17) | copy-start | bytes 2334724
  3.6 12.5 %collective-permute-start.3 = (bf16[64,2560]{1,0:T(8,128)(2,1)}, bf16[64,2560]{1,0:T(8,128)(2,1)S(1)}, u32[]{:S(2)}, u32[]{:S(2)}) collective-permute-start(bf16[64,2560]{1,0:T(8,128)(2,1)} %get-tuple-element.65), channel_id=1, source_target_pairs={{2,0},{6,2},{4,6},{0,4},{3,1},{7,3},{5,7},{1,5},{10,8},{14,10},{12... | collective-permute-start | bytes 983048 | tf_op jit(solution)/shard_map/ppermute | solution.py:571
  7.6 17.2 %collective-permute-start.2 = (bf16[64,2560]{1,0:T(8,128)(2,1)}, bf16[64,2560]{1,0:T(8,128)(2,1)S(1)}, u32[]{:S(2)}, u32[]{:S(2)}) collective-permute-start(bf16[64,2560]{1,0:T(8,128)(2,1)} %get-tuple-element.65), channel_id=1, source_target_pairs={{0,2},{2,6},{6,4},{4,0},{1,3},{3,7},{7,5},{5,1},{8,10},{10,14},{14... | collective-permute-start | bytes 983048 | tf_op jit(solution)/shard_map/ppermute | solution.py:565
  9.7 22.8 %copy-start.7 = (bf16[608,384]{1,0:T(8,128)(2,1)}, bf16[608,384]{1,0:T(8,128)(2,1)S(1)}, u32[]{:S(2)}) copy-start(bf16[608,384]{1,0:T(8,128)(2,1)S(1)} %pad_maximum_fusion.1.refs_13_.refs_15_) | copy-start | bytes 1400836
  9.7 16.5 %collective-permute-start.1 = (bf16[608,384]{1,0:T(8,128)(2,1)S(1)}, bf16[608,384]{1,0:T(8,128)(2,1)S(1)}, u32[]{:S(2)}, u32[]{:S(2)}) collective-permute-start(bf16[608,384]{1,0:T(8,128)(2,1)S(1)} %pad_maximum_fusion.1.refs_13_.refs_15_), channel_id=1, source_target_pairs={{0,8},{1,17},{8,0},{9,25},{16,24},{17,1},{24,16},{25,9},{2,10},{3,... | collective-permute-start | bytes 1400840 | tf_op jit(solution)/shard_map/ppermute | solution.py:592
  12.2 16.9 %collective-permute-start = (bf16[608,384]{1,0:T(8,128)(2,1)}, bf16[608,384]{1,0:T(8,128)(2,1)S(1)}, u32[]{:S(2)}, u32[]{:S(2)}) collective-permute-start(bf16[608,384]{1,0:T(8,128)(2,1)} %pad_maximum_fusion.refs_9_), channel_id=1, source_target_pairs={{0,8},{1,17},{8,0},{9,25},{16,24},{17,1},{24,16},{25,9},{2,10},{3,... | collective-permute-start | bytes 1400840 | tf_op jit(solution)/shard_map/ppermute | solution.py:592
  12.7 24.4 %collective-permute-start.11 = (bf16[608,384]{1,0:T(8,128)(2,1)S(1)}, bf16[608,384]{1,0:T(8,128)(2,1)S(1)}, u32[]{:S(2)}, u32[]{:S(2)}) collective-permute-start(bf16[608,384]{1,0:T(8,128)(2,1)S(1)} %pad_maximum_fusion.1.refs_13_.refs_15_), channel_id=1, source_target_pairs={{0,16},{1,9},{8,24},{9,1},{16,0},{17,25},{24,8},{25,17},{2,18},{3,... | collective-permute-start | bytes 1400840 | tf_op jit(solution)/shard_map/ppermute | solution.py:593
  16.1 12.9 %copy-start.8 = (bf16[64,2560]{1,0:T(8,128)(2,1)}, bf16[64,2560]{1,0:T(8,128)(2,1)S(1)}, u32[]{:S(2)}) copy-start(bf16[64,2560]{1,0:T(8,128)(2,1)S(1)} %collective-permute-done.3.following.refs_3_) | copy-start | bytes 983044
  16.8 12.2 %collective-permute-start.4 = (bf16[32,2560]{1,0:T(8,128)(2,1)}, bf16[32,2560]{1,0:T(8,128)(2,1)S(1)}, u32[]{:S(2)}, u32[]{:S(2)}) collective-permute-start(bf16[32,2560]{1,0:T(8,128)(2,1)} %slice.16), channel_id=1, source_target_pairs={{2,0},{6,2},{4,6},{0,4},{3,1},{7,3},{5,7},{1,5},{10,8},{14,10},{12... | collective-permute-start | bytes 491528 | tf_op jit(solution)/shard_map/ppermute | solution.py:571
  24.8 4.2 %copy-start.10 = (bf16[64,2560]{1,0:T(8,128)(2,1)}, bf16[64,2560]{1,0:T(8,128)(2,1)S(1)}, u32[]{:S(2)}) copy-start(bf16[64,2560]{1,0:T(8,128)(2,1)S(1)} %collective-permute-done.2.previous.refs_1_) | copy-start | bytes 983044
  25.5 7.2 %collective-permute-start.7 = (bf16[32,2560]{1,0:T(8,128)(2,1)}, bf16[32,2560]{1,0:T(8,128)(2,1)}, u32[]{:S(2)}, u32[]{:S(2)}) collective-permute-start(bf16[32,2560]{1,0:T(8,128)(2,1)} %slice.17), channel_id=1, source_target_pairs={{0,2},{2,6},{6,4},{4,0},{1,3},{3,7},{7,5},{5,1},{8,10},{10,14},{14... | collective-permute-start | bytes 491528 | tf_op jit(solution)/shard_map/ppermute | solution.py:565
  26.2 21.1 %copy-start.12 = (bf16[608,384]{1,0:T(8,128)(2,1)}, bf16[608,384]{1,0:T(8,128)(2,1)S(1)}, u32[]{:S(2)}) copy-start(bf16[608,384]{1,0:T(8,128)(2,1)S(1)} %collective-permute-done.1.refs_14_.refs_16_) | copy-start | bytes 1400836
  26.2 21.1 %collective-permute-start.10 = (bf16[608,384]{1,0:T(8,128)(2,1)}, bf16[608,384]{1,0:T(8,128)(2,1)}, u32[]{:S(2)}, u32[]{:S(2)}) collective-permute-start(bf16[608,384]{1,0:T(8,128)(2,1)} %pad_maximum_fusion.refs_9_), channel_id=1, source_target_pairs={{0,16},{1,9},{8,24},{9,1},{16,0},{17,25},{24,8},{25,17},{2,18},{3,... | collective-permute-start | bytes 1400840 | tf_op jit(solution)/shard_map/ppermute | solution.py:593
  29.0 26.7 %copy-start.16 = (bf16[608,384]{1,0:T(8,128)(2,1)}, bf16[608,384]{1,0:T(8,128)(2,1)S(1)}, u32[]{:S(2)}) copy-start(bf16[608,384]{1,0:T(8,128)(2,1)S(1)} %collective-permute-done.refs_10_) | copy-start | bytes 1400836
  29.0 0.7 copy-start.14
  32.5 14.8 %copy-start.15 = (bf16[32,2560]{1,0:T(8,128)(2,1)S(1)}, bf16[32,2560]{1,0:T(8,128)(2,1)}, u32[]{:S(2)}) copy-start(bf16[32,2560]{1,0:T(8,128)(2,1)} %copy-done.14) | copy-start | bytes 491524
  32.5 19.1 %copy-start.11 = (bf16[64,2560]{1,0:T(8,128)(2,1)S(1)}, bf16[64,2560]{1,0:T(8,128)(2,1)}, u32[]{:S(2)}) copy-start(bf16[64,2560]{1,0:T(8,128)(2,1)} %copy-done.10) | copy-start | bytes 983044
  32.5 19.5 %copy-start.9 = (bf16[64,2560]{1,0:T(8,128)(2,1)S(1)}, bf16[64,2560]{1,0:T(8,128)(2,1)}, u32[]{:S(2)}) copy-start(bf16[64,2560]{1,0:T(8,128)(2,1)} %copy-done.8) | copy-start | bytes 983044
  32.8 10.8 %collective-permute-start.15 = (bf16[64,2560]{1,0:T(8,128)(2,1)}, bf16[64,2560]{1,0:T(8,128)(2,1)}, u32[]{:S(2)}, u32[]{:S(2)}) collective-permute-start(bf16[64,2560]{1,0:T(8,128)(2,1)} %get-tuple-element.76), channel_id=1, source_target_pairs={{2,0},{6,2},{4,6},{0,4},{3,1},{7,3},{5,7},{1,5},{10,8},{14,10},{12... | collective-permute-start | bytes 983048 | tf_op jit(solution)/shard_map/ppermute | solution.py:571
  35.0 16.4 %collective-permute-start.12 = (bf16[608,384]{1,0:T(8,128)(2,1)S(1)}, bf16[608,384]{1,0:T(8,128)(2,1)S(1)}, u32[]{:S(2)}, u32[]{:S(2)}) collective-permute-start(bf16[608,384]{1,0:T(8,128)(2,1)S(1)} %collective-permute-done.refs_10_), channel_id=1, source_target_pairs={{0,16},{1,9},{8,24},{9,1},{16,0},{17,25},{24,8},{25,17},{2,18},{3,... | collective-permute-start | bytes 1400840 | tf_op jit(solution)/shard_map/ppermute | solution.py:628
  36.5 14.9 %collective-permute-start.13 = (bf16[608,384]{1,0:T(8,128)(2,1)S(1)}, bf16[608,384]{1,0:T(8,128)(2,1)}, u32[]{:S(2)}, u32[]{:S(2)}) collective-permute-start(bf16[608,384]{1,0:T(8,128)(2,1)S(1)} %collective-permute-done.1.refs_14_.refs_16_), channel_id=1, source_target_pairs={{0,16},{1,9},{8,24},{9,1},{16,0},{17,25},{24,8},{25,17},{2,18},{3,... | collective-permute-start | bytes 1400840 | tf_op jit(solution)/shard_map/ppermute | solution.py:628
  37.1 18.6 %copy-start.13 = (bf16[608,384]{1,0:T(8,128)(2,1)}, bf16[608,384]{1,0:T(8,128)(2,1)S(1)}, u32[]{:S(2)}) copy-start(bf16[608,384]{1,0:T(8,128)(2,1)S(1)} %collective-permute-done.11.refs_15_.refs_17_) | copy-start | bytes 1400836
  37.1 14.4 %collective-permute-start.9 = (bf16[64,2560]{1,0:T(8,128)(2,1)}, bf16[64,2560]{1,0:T(8,128)(2,1)S(1)}, u32[]{:S(2)}, u32[]{:S(2)}) collective-permute-start(bf16[64,2560]{1,0:T(8,128)(2,1)} %get-tuple-element.76), channel_id=1, source_target_pairs={{0,2},{2,6},{6,4},{4,0},{1,3},{3,7},{7,5},{5,1},{8,10},{10,14},{14... | collective-permute-start | bytes 983048 | tf_op jit(solution)/shard_map/ppermute | solution.py:565
  43.6 8.7 %collective-permute-start.16 = (bf16[64,2560]{1,0:T(8,128)(2,1)}, bf16[64,2560]{1,0:T(8,128)(2,1)}, u32[]{:S(2)}, u32[]{:S(2)}) collective-permute-start(bf16[64,2560]{1,0:T(8,128)(2,1)} %collective-permute-done.15.refs_11_), channel_id=1, source_target_pairs={{0,1},{1,0},{2,3},{3,2},{4,5},{5,4},{6,7},{7,6},{8,9},{9,8},{10,11... | collective-permute-start | bytes 983048 | tf_op jit(solution)/shard_map/ppermute | solution.py:568
  47.3 4.8 %collective-permute-start.17 = (bf16[32,2560]{1,0:T(8,128)(2,1)S(1)}, bf16[32,2560]{1,0:T(8,128)(2,1)S(1)}, u32[]{:S(2)}, u32[]{:S(2)}) collective-permute-start(bf16[32,2560]{1,0:T(8,128)(2,1)S(1)} %copy-done.15), channel_id=1, source_target_pairs={{0,1},{1,0},{2,3},{3,2},{4,5},{5,4},{6,7},{7,6},{8,9},{9,8},{10,11... | collective-permute-start | bytes 491528 | tf_op jit(solution)/shard_map/ppermute | solution.py:568
  51.4 14.1 %copy-start.18 = (bf16[64,2560]{1,0:T(8,128)(2,1)}, bf16[64,2560]{1,0:T(8,128)(2,1)S(1)}, u32[]{:S(2)}) copy-start(bf16[64,2560]{1,0:T(8,128)(2,1)S(1)} %collective-permute-done.9.refs_9_) | copy-start | bytes 983044
  51.4 4.3 %copy-start.17 = (bf16[608,384]{1,0:T(8,128)(2,1)}, bf16[608,384]{1,0:T(8,128)(2,1)S(1)}, u32[]{:S(2)}) copy-start(bf16[608,384]{1,0:T(8,128)(2,1)S(1)} %collective-permute-done.12.refs_12_) | copy-start | bytes 1400836
  51.4 1.7 %collective-permute-start.14 = (bf16[64,2560]{1,0:T(8,128)(2,1)S(1)}, bf16[64,2560]{1,0:T(8,128)(2,1)S(1)}, u32[]{:S(2)}, u32[]{:S(2)}) collective-permute-start(bf16[64,2560]{1,0:T(8,128)(2,1)S(1)} %collective-permute-done.9.refs_9_), channel_id=1, source_target_pairs={{0,1},{1,0},{2,3},{3,2},{4,5},{5,4},{6,7},{7,6},{8,9},{9,8},{10,11... | collective-permute-start | bytes 983048 | tf_op jit(solution)/shard_map/ppermute | solution.py:568
  51.5 2.8 %collective-permute-start.5 = (bf16[64,2560]{1,0:T(8,128)(2,1)S(1)}, bf16[64,2560]{1,0:T(8,128)(2,1)S(1)}, u32[]{:S(2)}, u32[]{:S(2)}) collective-permute-start(bf16[64,2560]{1,0:T(8,128)(2,1)S(1)} %copy-done.11), channel_id=1, source_target_pairs={{0,1},{1,0},{2,3},{3,2},{4,5},{5,4},{6,7},{7,6},{8,9},{9,8},{10,11... | collective-permute-start | bytes 983048 | tf_op jit(solution)/shard_map/ppermute | solution.py:568
  52.0 3.7 %collective-permute-start.6 = (bf16[64,2560]{1,0:T(8,128)(2,1)S(1)}, bf16[64,2560]{1,0:T(8,128)(2,1)}, u32[]{:S(2)}, u32[]{:S(2)}) collective-permute-start(bf16[64,2560]{1,0:T(8,128)(2,1)S(1)} %copy-done.9), channel_id=1, source_target_pairs={{0,1},{1,0},{2,3},{3,2},{4,5},{5,4},{6,7},{7,6},{8,9},{9,8},{10,11... | collective-permute-start | bytes 983048 | tf_op jit(solution)/shard_map/ppermute | solution.py:568
  52.1 2.2 %copy-start.23 = (bf16[32,2560]{1,0:T(8,128)(2,1)}, bf16[32,2560]{1,0:T(8,128)(2,1)S(1)}, u32[]{:S(2)}) copy-start(bf16[32,2560]{1,0:T(8,128)(2,1)S(1)} %collective-permute-done.17.refs_8_) | copy-start | bytes 491524
  52.1 11.4 %collective-permute-start.18 = (bf16[64,2560]{1,0:T(8,128)(2,1)S(1)}, bf16[64,2560]{1,0:T(8,128)(2,1)S(1)}, u32[]{:S(2)}, u32[]{:S(2)}) collective-permute-start(bf16[64,2560]{1,0:T(8,128)(2,1)S(1)} %collective-permute-done.9.refs_9_), channel_id=1, source_target_pairs={{0,2},{2,6},{6,4},{4,0},{1,3},{3,7},{7,5},{5,1},{8,10},{10,14},{14... | collective-permute-start | bytes 983048 | tf_op jit(solution)/shard_map/ppermute | solution.py:565
  52.3 2.0 %collective-permute-start.8 = (bf16[32,2560]{1,0:T(8,128)(2,1)}, bf16[32,2560]{1,0:T(8,128)(2,1)S(1)}, u32[]{:S(2)}, u32[]{:S(2)}) collective-permute-start(bf16[32,2560]{1,0:T(8,128)(2,1)} %collective-permute-done.7.refs_5_), channel_id=1, source_target_pairs={{0,1},{1,0},{2,3},{3,2},{4,5},{5,4},{6,7},{7,6},{8,9},{9,8},{10,11... | collective-permute-start | bytes 491528 | tf_op jit(solution)/shard_map/ppermute | solution.py:568
  53.1 10.3 %copy-start.19 = (bf16[64,2560]{1,0:T(8,128)(2,1)}, bf16[64,2560]{1,0:T(8,128)(2,1)S(1)}, u32[]{:S(2)}) copy-start(bf16[64,2560]{1,0:T(8,128)(2,1)S(1)} %collective-permute-done.14.refs_10_) | copy-start | bytes 983044
  54.3 0.7 copy-start.24
  55.0 0.7 copy-start.21
  63.5 2.0 %copy-start.20 = (bf16[64,2560]{1,0:T(8,128)(2,1)}, bf16[64,2560]{1,0:T(8,128)(2,1)S(1)}, u32[]{:S(2)}) copy-start(bf16[64,2560]{1,0:T(8,128)(2,1)S(1)} %collective-permute-done.18.refs_13_) | copy-start | bytes 983044
  63.5 1.7 %collective-permute-start.19 = (bf16[64,2560]{1,0:T(8,128)(2,1)S(1)}, bf16[64,2560]{1,0:T(8,128)(2,1)S(1)}, u32[]{:S(2)}, u32[]{:S(2)}) collective-permute-start(bf16[64,2560]{1,0:T(8,128)(2,1)S(1)} %collective-permute-done.18.refs_13_), channel_id=1, source_target_pairs={{0,1},{1,0},{2,3},{3,2},{4,5},{5,4},{6,7},{7,6},{8,9},{9,8},{10,11... | collective-permute-start | bytes 983048 | tf_op jit(solution)/shard_map/ppermute | solution.py:568
  65.2 0.7 copy-start.22
  65.2 16.8 %collective-permute-start.22 = (bf16[1216,640]{1,0:T(8,128)(2,1)}, bf16[1216,640]{1,0:T(8,128)(2,1)S(1)}, u32[]{:S(2)}, u32[]{:S(2)}) collective-permute-start(bf16[1216,640]{1,0:T(8,128)(2,1)} %get-tuple-element.108.refs_7_), channel_id=1, source_target_pairs={{0,1},{1,0},{2,3},{3,2},{4,5},{5,4},{6,7},{7,6},{8,9},{9,8},{10,11... | collective-permute-start | bytes 4669448 | tf_op jit(solution)/shard_map/ppermute | solution.py:568
  76.6 5.4 %copy-start.2 = (bf16[1216,640]{1,0:T(8,128)(2,1)S(1)}, bf16[1216,640]{1,0:T(8,128)(2,1)}, u32[]{:S(2)}) copy-start(bf16[1216,640]{1,0:T(8,128)(2,1)} %get-tuple-element.87.refs_6_.w_own) | copy-start | bytes 4669444
  76.6 1.9 %collective-permute-start.21 = (bf16[128,1216]{1,0:T(8,128)(2,1)}, bf16[128,1216]{1,0:T(8,128)(2,1)S(1)}, u32[]{:S(2)}, u32[]{:S(2)}) collective-permute-start(bf16[128,1216]{1,0:T(8,128)(2,1)} %get-tuple-element.105), channel_id=1, source_target_pairs={{0,1},{1,0},{2,3},{3,2},{4,5},{5,4},{6,7},{7,6},{8,9},{9,8},{10,11... | collective-permute-start | bytes 933896 | tf_op jit(solution)/shard_map/ppermute | solution.py:568
  77.0 5.0 %collective-permute-start.20 = (bf16[384,640]{1,0:T(8,128)(2,1)}, bf16[384,640]{1,0:T(8,128)(2,1)S(1)}, u32[]{:S(2)}, u32[]{:S(2)}) collective-permute-start(bf16[384,640]{1,0:T(8,128)(2,1)} %get-tuple-element.106.own), channel_id=1, source_target_pairs={{0,1},{1,0},{2,3},{3,2},{4,5},{5,4},{6,7},{7,6},{8,9},{9,8},{10,11... | collective-permute-start | bytes 1474568 | tf_op jit(solution)/shard_map/ppermute | solution.py:568
  79.7 8.0 %collective-permute-start.26 = (bf16[64,1216]{1,0:T(8,128)(2,1)S(1)}, bf16[64,1216]{1,0:T(8,128)(2,1)S(1)}, u32[]{:S(2)}, u32[]{:S(2)}) collective-permute-start(bf16[64,1216]{1,0:T(8,128)(2,1)S(1)} %get-tuple-element.124), channel_id=1, source_target_pairs={{0,2},{2,6},{6,4},{4,0},{1,3},{3,7},{7,5},{5,1},{8,10},{10,14},{14... | collective-permute-start | bytes 466952 | tf_op jit(solution)/shard_map/ppermute | solution.py:565
  81.3 9.7 %collective-permute-start.23 = (bf16[64,1216]{1,0:T(8,128)(2,1)S(1)}, bf16[64,1216]{1,0:T(8,128)(2,1)S(1)}, u32[]{:S(2)}, u32[]{:S(2)}) collective-permute-start(bf16[64,1216]{1,0:T(8,128)(2,1)S(1)} %get-tuple-element.125), channel_id=1, source_target_pairs={{0,2},{2,6},{6,4},{4,0},{1,3},{3,7},{7,5},{5,1},{8,10},{10,14},{14... | collective-permute-start | bytes 466952 | tf_op jit(solution)/shard_map/ppermute | solution.py:565
  82.0 1.0 copy-start.6
  84.7 20.7 %copy-start.1 = (f32[128,1216]{1,0:T(8,128)S(1)}, f32[128,1216]{1,0:T(8,128)}, u32[]{:S(2)}) copy-start(f32[128,1216]{1,0:T(8,128)} %get-tuple-element.116.normed) | copy-start | bytes 1867780
  84.8 20.6 %copy-start.5 = (f32[1,1216]{1,0:T(1,128)S(1)}, f32[1,1216]{1,0:T(1,128)}, u32[]{:S(2)}) copy-start(f32[1,1216]{1,0:T(1,128)} %get-tuple-element.115.scale) | copy-start | bytes 14596
  87.7 6.7 %collective-permute-start.27 = (bf16[64,1216]{1,0:T(8,128)(2,1)S(1)}, bf16[64,1216]{1,0:T(8,128)(2,1)S(1)}, u32[]{:S(2)}, u32[]{:S(2)}) collective-permute-start(bf16[64,1216]{1,0:T(8,128)(2,1)S(1)} %add_convert_fusion.2), channel_id=1, source_target_pairs={{0,2},{2,6},{6,4},{4,0},{1,3},{3,7},{7,5},{5,1},{8,10},{10,14},{14... | collective-permute-start | bytes 466952 | tf_op jit(solution)/shard_map/ppermute | solution.py:565
  91.0 16.0 %copy-start.3 = (f32[128,1216]{1,0:T(8,128)S(1)}, f32[128,1216]{1,0:T(8,128)}, u32[]{:S(2)}) copy-start(f32[128,1216]{1,0:T(8,128)} %get-tuple-element.119.base) | copy-start | bytes 1867780
  91.0 16.0 %copy-start.4 = (f32[128,128]{1,0:T(8,128)S(1)}, f32[128,128]{1,0:T(8,128)}, u32[]{:S(2)}) copy-start(f32[128,128]{1,0:T(8,128)} %get-tuple-element.120.inv_std) | copy-start | bytes 196612
  91.0 8.1 %collective-permute-start.24 = (bf16[64,1216]{1,0:T(8,128)(2,1)S(1)}, bf16[64,1216]{1,0:T(8,128)(2,1)S(1)}, u32[]{:S(2)}, u32[]{:S(2)}) collective-permute-start(bf16[64,1216]{1,0:T(8,128)(2,1)S(1)} %add_convert_fusion.4), channel_id=1, source_target_pairs={{0,2},{2,6},{6,4},{4,0},{1,3},{3,7},{7,5},{5,1},{8,10},{10,14},{14... | collective-permute-start | bytes 466952 | tf_op jit(solution)/shard_map/ppermute | solution.py:565
  94.5 7.9 %collective-permute-start.28 = (bf16[64,1216]{1,0:T(8,128)(2,1)S(1)}, bf16[64,1216]{1,0:T(8,128)(2,1)S(1)}, u32[]{:S(2)}, u32[]{:S(2)}) collective-permute-start(bf16[64,1216]{1,0:T(8,128)(2,1)S(1)} %add_convert_fusion.1), channel_id=1, source_target_pairs={{0,2},{2,6},{6,4},{4,0},{1,3},{3,7},{7,5},{5,1},{8,10},{10,14},{14... | collective-permute-start | bytes 466952 | tf_op jit(solution)/shard_map/ppermute | solution.py:565
  99.1 6.3 %collective-permute-start.25 = (bf16[64,1216]{1,0:T(8,128)(2,1)S(1)}, bf16[64,1216]{1,0:T(8,128)(2,1)S(1)}, u32[]{:S(2)}, u32[]{:S(2)}) collective-permute-start(bf16[64,1216]{1,0:T(8,128)(2,1)S(1)} %add_convert_fusion.3), channel_id=1, source_target_pairs={{0,2},{2,6},{6,4},{4,0},{1,3},{3,7},{7,5},{5,1},{8,10},{10,14},{14... | collective-permute-start | bytes 466952 | tf_op jit(solution)/shard_map/ppermute | solution.py:565
  105.6 1.3 %collective-permute-start.29 = (f32[128,128]{1,0:T(8,128)S(1)}, f32[128,128]{1,0:T(8,128)S(1)}, u32[]{:S(2)}, u32[]{:S(2)}) collective-permute-start(f32[128,128]{1,0:T(8,128)S(1)} %get-tuple-element.118.sums), channel_id=1, source_target_pairs={{0,1},{1,0},{2,3},{3,2},{4,5},{5,4},{6,7},{7,6},{8,9},{9,8},{10,11... | collective-permute-start | bytes 196616 | tf_op jit(solution)/shard_map/ppermute | solution.py:568

commit v3 on v2

--- a/solution.py
+++ b/solution.py
@@ -264,30 +264,31 @@
     inner = slots * HD
     core = scalars[0]
     copies = Copies(sems)
+    row_copies = copies.rows(core, mod_in, mod_all, rows)
     w_copies = copies.weights(scalars, w_in, w_all, shard)
-    row_copies = copies.rows(core, mod_in, mod_all, rows)
 
     lane = lax.broadcasted_iota(jnp.int32, (1, 2 * inner), 1)
     gains = head_gains(gain, slots) * jnp.where(lane < inner, HD ** (-0.5), 1.0)
     identity = equal_blocks(inner, 1)
-    for copy in w_copies:
+    out_copies = []
+    for copy in row_copies + w_copies[:4]:
         copy.wait()
-    half = width // 2
-    out_copies = []
-    for holder, target in ((core, w_keep), (1 - core, w_give)):
-        source = w_all.at[pl.ds(pl.multiple_of(holder * half, 16), half)]
-        out_copies.append(copies.start(source, target))
-    for copy in row_copies:
-        copy.wait()
-    projected = jnp.dot(mod_all[:, :width], w_all[:, : 3 * inner], preferred_element_type=jnp.float32)
-    raw = projected[:, : 2 * inner]
+    raw = dot(mod_all[:, :width], w_all[:, : 2 * inner], NN)
     raw_s[...] = raw
     out_copies.append(copies.start(raw_s, raw_all))
     inverse = lax.rsqrt(head_means(raw * raw) + 1e-06)
     inv_s[...] = inverse
     out_copies.append(copies.start(inv_s, inv_all))
     qkv_s[:, : 2 * inner] = (raw * inverse * gains).astype(jnp.bfloat16)
-    qkv_s[:, 2 * inner :] = projected[:, 2 * inner :].astype(jnp.bfloat16)
+    for copy in w_copies[4:]:
+        copy.wait()
+    half = width // 2
+    for holder, target in ((core, w_keep), (1 - core, w_give)):
+        source = w_all.at[pl.ds(pl.multiple_of(holder * half, 16), half)]
+        out_copies.append(copies.start(source, target))
+    qkv_s[:, 2 * inner :] = dot(
+        mod_all[:, :width], w_all[:, 2 * inner : 3 * inner], NN
+    ).astype(jnp.bfloat16)
     out_copies.append(copies.start(qkv_s, qkv))
     k_t_s[...] = dot(identity, qkv_s[:, inner : 2 * inner], NT).astype(jnp.bfloat16)
     out_copies.append(copies.start(k_t_s, k_t))
@@ -302,7 +303,7 @@
     projected = take(8)
     cot_in = take(7)
     w_in = take(4)
-    mine_out, theirs_out, rest_out = take(3)
+    mine_near, mine_far, theirs_near, theirs_far, rest_out = take(5)
     w_out, cot_all, sems, extra, values_text = take(5)
     d_all, grads, stacked = take(3)
     qkv, k_t, raw_all, inv_all, text, text_t, w_keep, w_give = refs
@@ -393,8 +394,12 @@
     rest_out[(count - 2) * rows :, :] = stacked[:rows, :]
     for copy in local_copies[6:]:
         copy.wait()
-    theirs_out[...] = dot(first, w_give[...], NT).astype(jnp.bfloat16)
-    mine_out[...] = dot(first, w_keep[...], NT)
+    theirs = dot(first, w_give[...], NT).astype(jnp.bfloat16)
+    theirs_near[...] = theirs[: rows // 2]
+    theirs_far[...] = theirs[rows // 2 :]
+    mine = dot(first, w_keep[...], NT)
+    mine_near[...] = mine[: rows // 2]
+    mine_far[...] = mine[rows // 2 :]
 
 
 def project_call(scalars, gain, mod, weights, slots, rows, text_dev, count):
@@ -440,7 +445,8 @@
     first = (columns - inner) // 128 * 128
     f32, bf16 = jnp.float32, jnp.bfloat16
     vmem, hbm = spec(pltpu.VMEM), spec(pl.ANY)
-    shapes = [((rows, width // 2), f32), ((rows, width // 2), bf16), ((tokens - rows, stacked), bf16)]
+    part = (rows // 2, width // 2)
+    shapes = [(part, f32)] * 2 + [(part, bf16)] * 2 + [((tokens - rows, stacked), bf16)]
     return pl.pallas_call(
         functools.partial(attend_kernel, slots, count, rows, shard, width, text_dev, first),
         out_shape=tuple(jax.ShapeDtypeStruct(*one) for one in shapes),
@@ -639,11 +645,10 @@
     cot_pieces += pieces(None, cot_far)[1:]
     given, *cot_pieces = pin((w_give, *cot_pieces))
     w_other = other_core(given)
-    mine, theirs, rest = attend_call(
+    *first, rest = attend_call(
         scalars, qk_gain, operands + [w_keep, w_give], cot_pieces, weights[4:], slots, tok_count, text_dev
     )
-    first = (mine + other_core(theirs).astype(f32)).astype(bf16)
-    moving = [first[:half_rows], first[half_rows:]]
+    moving = [(a + other_core(b).astype(f32)).astype(bf16) for a, b in zip(first[:2], first[2:])]
     other_rest = other_core(rest)
     rest, other_rest, *_ = pin((rest, other_rest, *moving))
     own = backward_call(rest, other_rest, w_keep, w_other, half_rows, f32)

time: 109 us -> 109 us (level)
  waiting for transfers between devices: 40.2 us -> 33.7 us
  starting transfers between devices: 25.5 us -> 29.5 us
  Pallas kernels: 30.8 us -> 33.9 us
  local copies, waits for them, and re-layouts: 7.5 us -> 6.21 us
    ppermute x10, waiting for transfers between devices: 26.2 us -> 20.4 us  [step(): return lax.ppermute(moving, 'seq', seq_next)]
    ppermute x10, starting transfers between devices: 5.97 us -> 9.51 us  [step(): return lax.ppermute(moving, 'seq', seq_next)]
    pallas_call x1, Pallas kernels: 7.78 us -> 9.3 us  [project_call(): pl.pallas_call(functools.partial(project_kernel, slots, count, rows, shar...]
    pallas_call x1, Pallas kernels: 1.69 us -> 3.11 us  [backward_call(): pl.pallas_call(backward_kernel, out_shape=(jax.ShapeDtypeStruct((part, ha...]
    ppermute x11 -> x12, waiting for transfers between devices: 5.59 us -> 4.86 us  [other_core(): return lax.ppermute(moving, 'head', swap)]
    unnamed x50 -> x52, local copies, waits for them, and re-layouts: 3.59 us -> 2.95 us
    ppermute x11 -> x12, starting transfers between devices: 2.82 us -> 2.99 us  [other_core(): return lax.ppermute(moving, 'head', swap)]
  transfers between devices with their start and end apart: 30 -> 31, of which waited for: 16 -> 16; matrix products, arithmetic and copies ran while one was open for 6% -> 6% of each run, Pallas kernels for 25% -> 27%
where the time goes in v3:
time: 109 us; the launch traced here: 108 us
  Pallas kernels  33.9 us (31%)
  waiting for transfers between devices  33.7 us (31%)
  starting transfers between devices  29.5 us (27%)
  local copies, waits for them, and re-layouts  6.21 us (6%)
  other arithmetic  3.24 us (3%)
  between operations  1.72 us (2%)
    ppermute x10, waiting for transfers between devices, step(): return lax.ppermute(moving, 'seq', seq_next)  20.4 us
    pallas_call x1, Pallas kernels, attend_call(): pl.pallas_call(functools.partial(attend_kernel, slots, count, rows, shard...  10.7 us
    ppermute x3, starting transfers between devices, step_back(): return lax.ppermute(moving, 'seq', [(b, a) for a, b in seq_next])  9.8 us
    ppermute x10, starting transfers between devices, step(): return lax.ppermute(moving, 'seq', seq_next)  9.51 us
    pallas_call x1, Pallas kernels, project_call(): pl.pallas_call(functools.partial(project_kernel, slots, count, rows, shar...  9.3 us
    ppermute x3, waiting for transfers between devices, step_back(): return lax.ppermute(moving, 'seq', [(b, a) for a, b in seq_next])  8.36 us
    pallas_call x3, Pallas kernels, local_call(): pl.pallas_call(kernel, out_shape=tuple((jax.ShapeDtypeStruct(*one) for on...  5.21 us
    ppermute x4, starting transfers between devices, shards_by_head(): lax.ppermute(part, ('dp', 'head'), second_way)  5.06 us
  transfers between devices with their start and end apart: 31, of which 16 were waited for; matrix products, arithmetic and copies ran while one was open for 6% of the time, Pallas kernels for 27%

profile of v3, /device:TPU:0, one launch (start us, length us, event | category | flops | bytes accessed | tf_op | source)
XLA Modules:
  0.0 108.2 jit_solution(13548728573705203885)
XLA Ops:
  0.7 2.8 %shard_map.91 = (bf16[64,2560]{1,0:T(8,128)(2,1)}, f32[8,2432]{1,0:T(8,128)}, bf16[64,128]{1,0:T(8,128)(2,1)}) custom-call(s32[1]{0:T(128)S(6)} %copy.11.step, s32[1]{0:T(128)} %bitcast.core, bf16[128,2432]{1,0:T(8,128)(2,1)} %bitcast.31, f32[3,28,2432]{2,1,0:T(8,128)} %bitcast.33, f32[128,2432]{1,0:T(8,128)} %bitcast.28, bf16[8,2,640]{2,1,0:T(2,128)(2,1)} %bitcast.34), custom_call_target="tpu_custom_call" | custom-call | flops 1245184 | bytes 2490368 | tf_op jit(solution)/shard_map/pallas_call | solution.py:110
  3.6 4.0 %collective-permute-start.3 = (bf16[64,2560]{1,0:T(8,128)(2,1)}, bf16[64,2560]{1,0:T(8,128)(2,1)S(1)}, u32[]{:S(2)}, u32[]{:S(2)}) collective-permute-start(bf16[64,2560]{1,0:T(8,128)(2,1)} %get-tuple-element.67), channel_id=1, source_target_pairs={{2,0},{6,2},{4,6},{0,4},{3,1},{7,3},{5,7},{1,5},{10,8},{14,10},{12... | collective-permute-start | bytes 983048 | tf_op jit(solution)/shard_map/ppermute | solution.py:577
  7.6 1.7 %dynamic-slice_bitcast_fusion.1 = (bf16[608,192]{1,0:T(8,128)(2,1)S(1)}, bf16[608,192]{1,0:T(8,128)(2,1)S(1)}, bf16[608,192]{1,0:T(8,128)(2,1)S(1)}) fusion(bf16[608,3,640]{2,0,1:T(8,128)(2,1)} %param.15, s32[]{:T(128)S(6)} %select_n.103), kind=kLoop, calls=%fused_computation.9 | loop fusion | bytes 1400836 | tf_op jit(solution)/shard_map/squeeze | solution.py:593
  9.3 0.2 dynamic-slice_bitcast_fusion
  9.5 0.2 pad_maximum_fusion.1.refs_13_.refs_15_
  9.7 1.6 %collective-permute-start.1 = (bf16[608,384]{1,0:T(8,128)(2,1)S(1)}, bf16[608,384]{1,0:T(8,128)(2,1)S(1)}, u32[]{:S(2)}, u32[]{:S(2)}) collective-permute-start(bf16[608,384]{1,0:T(8,128)(2,1)S(1)} %pad_maximum_fusion.1.refs_13_.refs_15_), channel_id=1, source_target_pairs={{0,8},{1,17},{8,0},{9,25},{16,24},{17,1},{24,16},{25,9},{2,10},{3,... | collective-permute-start | bytes 1400840 | tf_op jit(solution)/shard_map/ppermute | solution.py:598
  11.2 0.9 pad_maximum_fusion.refs_9_
  12.1 0.5 collective-permute-start
  12.7 1.5 %collective-permute-start.11 = (bf16[608,384]{1,0:T(8,128)(2,1)S(1)}, bf16[608,384]{1,0:T(8,128)(2,1)S(1)}, u32[]{:S(2)}, u32[]{:S(2)}) collective-permute-start(bf16[608,384]{1,0:T(8,128)(2,1)S(1)} %pad_maximum_fusion.1.refs_13_.refs_15_), channel_id=1, source_target_pairs={{0,16},{1,9},{8,24},{9,1},{16,0},{17,25},{24,8},{25,17},{2,18},{3,... | collective-permute-start | bytes 1400840 | tf_op jit(solution)/shard_map/ppermute | solution.py:599
  14.2 1.9 %collective-permute-done.3.following.refs_3_ = bf16[64,2560]{1,0:T(8,128)(2,1)S(1)} collective-permute-done((bf16[64,2560]{1,0:T(8,128)(2,1)}, bf16[64,2560]{1,0:T(8,128)(2,1)S(1)}, u32[]{:S(2)}, u32[]{:S(2)}) %collective-permute-start.3) | collective-permute-done | bytes 327712 | tf_op jit(solution)/shard_map/ppermute | solution.py:577
  16.1 3.3 %collective-permute-start.4 = (bf16[32,2560]{1,0:T(8,128)(2,1)S(1)}, bf16[32,2560]{1,0:T(8,128)(2,1)S(1)}, u32[]{:S(2)}, u32[]{:S(2)}) collective-permute-start(bf16[32,2560]{1,0:T(8,128)(2,1)S(1)} %slice.8), channel_id=1, source_target_pairs={{2,0},{6,2},{4,6},{0,4},{3,1},{7,3},{5,7},{1,5},{10,8},{14,10},{12... | collective-permute-start | bytes 491528 | tf_op jit(solution)/shard_map/ppermute | solution.py:577
  19.4 5.4 %collective-permute-done.2.previous.refs_1_ = bf16[64,2560]{1,0:T(8,128)(2,1)S(1)} collective-permute-done((bf16[64,2560]{1,0:T(8,128)(2,1)}, bf16[64,2560]{1,0:T(8,128)(2,1)S(1)}, u32[]{:S(2)}, u32[]{:S(2)}) %collective-permute-start.2) | collective-permute-done | bytes 327712 | tf_op jit(solution)/shard_map/ppermute | solution.py:571
  24.8 0.7 slice.9
  25.5 0.7 collective-permute-start.7
  26.2 1.5 %collective-permute-start.10 = (bf16[608,384]{1,0:T(8,128)(2,1)}, bf16[608,384]{1,0:T(8,128)(2,1)}, u32[]{:S(2)}, u32[]{:S(2)}) collective-permute-start(bf16[608,384]{1,0:T(8,128)(2,1)} %pad_maximum_fusion.refs_9_), channel_id=1, source_target_pairs={{0,16},{1,9},{8,24},{9,1},{16,0},{17,25},{24,8},{25,17},{2,18},{3,... | collective-permute-start | bytes 1400840 | tf_op jit(solution)/shard_map/ppermute | solution.py:599
  28.4 0.7 stack.67.core.scalars
  29.1 0.6 copy-done.14
  29.7 2.7 %shard_map.92 = (bf16[64,2560]{1,0:T(8,128)(2,1)}, f32[8,128]{1,0:T(8,128)}) custom-call(s32[14]{0:T(128)} %stack.67.core.scalars, f32[128,2432]{1,0:T(8,128)} %bitcast.29, f32[8,2432]{1,0:T(8,128)} %get-tuple-element.65.table_rows, bf16[8,2,640]{2,1,0:T(2,128)(2,1)} %bitcast.35, bf16[64,128]{1,0:T(8,128)(2,1)} %get-tuple-element.70.extra, ...), custom_call_target="tpu_custom_call" | custom-call | flops 622592 | bytes 933888 | tf_op jit(solution)/shard_map/pallas_call | solution.py:162
  32.5 0.1 collective-permute-done.7.refs_5_
  32.7 2.4 %collective-permute-start.15 = (bf16[64,2560]{1,0:T(8,128)(2,1)}, bf16[64,2560]{1,0:T(8,128)(2,1)S(1)}, u32[]{:S(2)}, u32[]{:S(2)}) collective-permute-start(bf16[64,2560]{1,0:T(8,128)(2,1)} %get-tuple-element.78), channel_id=1, source_target_pairs={{2,0},{6,2},{4,6},{0,4},{3,1},{7,3},{5,7},{1,5},{10,8},{14,10},{12... | collective-permute-start | bytes 983048 | tf_op jit(solution)/shard_map/ppermute | solution.py:577
  35.1 1.5 %collective-permute-start.12 = (bf16[608,384]{1,0:T(8,128)(2,1)}, bf16[608,384]{1,0:T(8,128)(2,1)}, u32[]{:S(2)}, u32[]{:S(2)}) collective-permute-start(bf16[608,384]{1,0:T(8,128)(2,1)} %collective-permute-done.refs_10_), channel_id=1, source_target_pairs={{0,16},{1,9},{8,24},{9,1},{16,0},{17,25},{24,8},{25,17},{2,18},{3,... | collective-permute-start | bytes 1400840 | tf_op jit(solution)/shard_map/ppermute | solution.py:634
  36.6 0.5 collective-permute-start.13
  37.1 6.5 %collective-permute-done.15.refs_11_ = bf16[64,2560]{1,0:T(8,128)(2,1)S(1)} collective-permute-done((bf16[64,2560]{1,0:T(8,128)(2,1)}, bf16[64,2560]{1,0:T(8,128)(2,1)S(1)}, u32[]{:S(2)}, u32[]{:S(2)}) %collective-permute-start.15) | collective-permute-done | bytes 327712 | tf_op jit(solution)/shard_map/ppermute | solution.py:577
  43.6 3.8 %shard_map.93 = (bf16[128,2560]{1,0:T(8,128)(2,1)}, bf16[128,2560]{1,0:T(8,128)(2,1)}, f32[128,1216]{1,0:T(8,128)}, f32[1,1216]{1,0:T(1,128)}, f32[128,128]{1,0:T(8,128)}, /*index=5*/f32[128,1216]{1,0:T(8,128)}) custom-call(s32[1]{0:T(128)} %bitcast.core, bf16[128,2432]{1,0:T(8,128)(2,1)} %bitcast.32, f32[128,2432]{1,0:T(8,128)} %bitcast.30, ...), custom_call_target="tpu_custom_call" | custom-call | flops 661505 | bytes 1986564 | tf_op jit(solution)/shard_map/pallas_call | solution.py:522
  47.4 0.5 collective-permute-start.17
  47.9 3.6 %collective-permute-done.9.refs_9_ = bf16[64,2560]{1,0:T(8,128)(2,1)S(1)} collective-permute-done((bf16[64,2560]{1,0:T(8,128)(2,1)}, bf16[64,2560]{1,0:T(8,128)(2,1)S(1)}, u32[]{:S(2)}, u32[]{:S(2)}) %collective-permute-start.9) | collective-permute-done | bytes 327712 | tf_op jit(solution)/shard_map/ppermute | solution.py:571
  51.5 0.1 collective-permute-start.14
  51.6 0.5 collective-permute-start.5
  52.1 0.1 collective-permute-start.6
  52.1 0.2 collective-permute-start.18
  52.3 0.3 collective-permute-start.8
  52.7 0.5 collective-permute-done.14.refs_10_
  53.2 0.9 collective-permute-done.8.refs_6_
  54.1 0.8 copy-done.21
  54.9 9.3 %shard_map.94 = (bf16[512,576]{1,0:T(8,128)(2,1)}, bf16[192,512]{1,0:T(8,128)(2,1)}, f32[512,384]{1,0:T(8,128)}, f32[512,384]{1,0:T(8,128)}, bf16[3,32,64]{2,1,0...) custom-call(s32[14]{0:T(128)} %stack.67.core.scalars, ...), custom_call_target="tpu_custom_call" | custom-call | flops 1434451968 | bytes 6914048 | tf_op jit(solution)/shard_map/pallas_call | solution.py:417
  64.3 0.3 collective-permute-start.19
  64.6 1.4 %collective-permute-done.19.refs_14_ = bf16[64,2560]{1,0:T(8,128)(2,1)S(1)} collective-permute-done((bf16[64,2560]{1,0:T(8,128)(2,1)S(1)}, bf16[64,2560]{1,0:T(8,128)(2,1)S(1)}, u32[]{:S(2)}, u32[]{:S(2)}) %collective-permute-start.19) | collective-permute-done | bytes 327712 | tf_op jit(solution)/shard_map/ppermute | solution.py:574
  66.0 0.3 collective-permute-start.23
  66.2 0.4 copy-done.22
  66.7 10.7 %shard_map.95 = (f32[64,1216]{1,0:T(8,128)}, f32[64,1216]{1,0:T(8,128)}, bf16[64,1216]{1,0:T(8,128)(2,1)}, bf16[64,1216]{1,0:T(8,128)(2,1)}, bf16[384,640]{1,0:T(8,128)(2,1)}) custom-call(s32[14]{0:T(128)} %stack.67.core.scalars, f32[2,64]{1,0:T(2,128)} %gain.3, bf16[512,576]{1,0:T(8,128)(2,1)} %get-tuple-element.83.refs_0_, ...), custom_call_target="tpu_custom_call" | custom-call | flops 981467136 | bytes 4358144 | tf_op jit(solution)/shard_map/pallas_call | solution.py:450
  77.4 0.3 collective-permute-start.22
  77.8 0.2 collective-permute-start.21
  78.0 0.3 collective-permute-start.20
  78.3 0.8 collective-permute-done.22
  79.1 1.0 add_convert_fusion.4
  80.1 1.6 %collective-permute-start.27 = (bf16[64,1216]{1,0:T(8,128)(2,1)S(1)}, bf16[64,1216]{1,0:T(8,128)(2,1)S(1)}, u32[]{:S(2)}, u32[]{:S(2)}) collective-permute-start(bf16[64,1216]{1,0:T(8,128)(2,1)S(1)} %add_convert_fusion.4), channel_id=1, source_target_pairs={{0,2},{2,6},{6,4},{4,0},{1,3},{3,7},{7,5},{5,1},{8,10},{10,14},{14... | collective-permute-start | bytes 466952 | tf_op jit(solution)/shard_map/ppermute | solution.py:571
  81.7 1.0 add_convert_fusion.5
  82.7 0.8 collective-permute-start.24
  83.5 1.0 copy-done.6
  84.5 3.1 %shard_map.96 = (f32[64,1216]{1,0:T(8,128)S(1)}, f32[64,1216]{1,0:T(8,128)S(1)}, f32[64,1216]{1,0:T(8,128)S(1)}, f32[64,1216]{1,0:T(8,128)S(1)}, f32[64,1216]{1,0:T(8,128)S(1)}, /*index=5*/f32[64,1216]{1,0:T(8,128)S(1)}) custom-call(bf16[384,640]{1,0:T(8,128)(2,1)S(1)} %copy-done.6, bf16[384,640]{1,0:T(8,128)(2,1)S(1)} %collective-permute-done.20.other, ...), custom_call_target="tpu_custom_call" | custom-call | flops 1195376640 | bytes 5963776 | tf_op jit(solution)/shard_map/pallas_call | solution.py:486
  87.6 0.5 collective-permute-done.27
  88.1 1.9 %collective-permute-start.28 = (bf16[64,1216]{1,0:T(8,128)(2,1)S(1)}, bf16[64,1216]{1,0:T(8,128)(2,1)S(1)}, u32[]{:S(2)}, u32[]{:S(2)}) collective-permute-start(bf16[64,1216]{1,0:T(8,128)(2,1)S(1)} %add_convert_fusion.1), channel_id=1, source_target_pairs={{0,2},{2,6},{6,4},{4,0},{1,3},{3,7},{7,5},{5,1},{8,10},{10,14},{14... | collective-permute-start | bytes 466952 | tf_op jit(solution)/shard_map/ppermute | solution.py:571
  90.1 1.0 collective-permute-done.24
  91.1 0.5 collective-permute-start.25
  91.6 3.3 %collective-permute-done.28 = bf16[64,1216]{1,0:T(8,128)(2,1)S(1)} collective-permute-done((bf16[64,1216]{1,0:T(8,128)(2,1)S(1)}, bf16[64,1216]{1,0:T(8,128)(2,1)S(1)}, u32[]{:S(2)}, u32[]{:S(2)}) %collective-permute-start.28) | collective-permute-done | bytes 155680 | tf_op jit(solution)/shard_map/ppermute | solution.py:571
  94.9 2.4 %collective-permute-start.29 = (bf16[64,1216]{1,0:T(8,128)(2,1)S(1)}, bf16[64,1216]{1,0:T(8,128)(2,1)S(1)}, u32[]{:S(2)}, u32[]{:S(2)}) collective-permute-start(bf16[64,1216]{1,0:T(8,128)(2,1)S(1)} %add_convert_fusion), channel_id=1, source_target_pairs={{0,2},{2,6},{6,4},{4,0},{1,3},{3,7},{7,5},{5,1},{8,10},{10,14},{14... | collective-permute-start | bytes 466952 | tf_op jit(solution)/shard_map/ppermute | solution.py:571
  97.3 1.9 %collective-permute-done.25 = bf16[64,1216]{1,0:T(8,128)(2,1)S(1)} collective-permute-done((bf16[64,1216]{1,0:T(8,128)(2,1)S(1)}, bf16[64,1216]{1,0:T(8,128)(2,1)S(1)}, u32[]{:S(2)}, u32[]{:S(2)}) %collective-permute-start.25) | collective-permute-done | bytes 155680 | tf_op jit(solution)/shard_map/ppermute | solution.py:571
  99.2 1.6 %collective-permute-start.26 = (bf16[64,1216]{1,0:T(8,128)(2,1)S(1)}, bf16[64,1216]{1,0:T(8,128)(2,1)S(1)}, u32[]{:S(2)}, u32[]{:S(2)}) collective-permute-start(bf16[64,1216]{1,0:T(8,128)(2,1)S(1)} %add_convert_fusion.2), channel_id=1, source_target_pairs={{0,2},{2,6},{6,4},{4,0},{1,3},{3,7},{7,5},{5,1},{8,10},{10,14},{14... | collective-permute-start | bytes 466952 | tf_op jit(solution)/shard_map/ppermute | solution.py:571
  100.8 1.7 %collective-permute-done.29.far = bf16[64,1216]{1,0:T(8,128)(2,1)S(1)} collective-permute-done((bf16[64,1216]{1,0:T(8,128)(2,1)S(1)}, bf16[64,1216]{1,0:T(8,128)(2,1)S(1)}, u32[]{:S(2)}, u32[]{:S(2)}) %collective-permute-start.29) | collective-permute-done | bytes 155680 | tf_op jit(solution)/shard_map/ppermute | solution.py:571
  102.5 3.0 %collective-permute-done.26.near = bf16[64,1216]{1,0:T(8,128)(2,1)S(1)} collective-permute-done((bf16[64,1216]{1,0:T(8,128)(2,1)S(1)}, bf16[64,1216]{1,0:T(8,128)(2,1)S(1)}, u32[]{:S(2)}, u32[]{:S(2)}) %collective-permute-start.26) | collective-permute-done | bytes 155680 | tf_op jit(solution)/shard_map/ppermute | solution.py:571
  105.5 0.2 shard_map.97
  105.7 0.1 collective-permute-start.30
  105.8 1.2 %collective-permute-done.30.other = f32[128,128]{1,0:T(8,128)S(1)} collective-permute-done((f32[128,128]{1,0:T(8,128)S(1)}, f32[128,128]{1,0:T(8,128)S(1)}, u32[]{:S(2)}, u32[]{:S(2)}) %collective-permute-start.30) | collective-permute-done | bytes 65568 | tf_op jit(solution)/shard_map/ppermute | solution.py:574
  107.1 1.2 %shard_map.98 = f32[1216,128]{1,0:T(8,128)} custom-call(f32[128,1216]{1,0:T(8,128)S(1)} %get-tuple-element.121.grad, f32[128,128]{1,0:T(8,128)S(1)} %get-tuple-element.122.sums, f32[128,128]{1,0:T(8,128)S(1)} %collective-permute-done.30.other, f32[128,1216]{1,0:T(8,128)S(1)} %copy-done.1, f32[128,1216]{1,0:T(8,128)S(1)} %copy-done.3, f32[128,128]{1,0:T(8,128)S(1)} %copy-done.4), custom_call_target="tpu_custom_call" | custom-call | flops 516096 | bytes 2064384 | tf_op jit(solution)/shard_map/pallas_call | solution.py:522
  (71 shorter events, 0.3 us)
Async XLA Ops:
  0.0 9.3 %copy-start = (bf16[640,608]{0,1:T(8,128)(2,1)S(1)}, bf16[640,608]{0,1:T(8,128)(2,1)}, u32[]{:S(2)}) copy-start(bf16[640,608]{0,1:T(8,128)(2,1)} %param.17) | copy-start | bytes 2334724
  3.6 12.5 %collective-permute-start.3 = (bf16[64,2560]{1,0:T(8,128)(2,1)}, bf16[64,2560]{1,0:T(8,128)(2,1)S(1)}, u32[]{:S(2)}, u32[]{:S(2)}) collective-permute-start(bf16[64,2560]{1,0:T(8,128)(2,1)} %get-tuple-element.67), channel_id=1, source_target_pairs={{2,0},{6,2},{4,6},{0,4},{3,1},{7,3},{5,7},{1,5},{10,8},{14,10},{12... | collective-permute-start | bytes 983048 | tf_op jit(solution)/shard_map/ppermute | solution.py:577
  7.6 17.2 %collective-permute-start.2 = (bf16[64,2560]{1,0:T(8,128)(2,1)}, bf16[64,2560]{1,0:T(8,128)(2,1)S(1)}, u32[]{:S(2)}, u32[]{:S(2)}) collective-permute-start(bf16[64,2560]{1,0:T(8,128)(2,1)} %get-tuple-element.67), channel_id=1, source_target_pairs={{0,2},{2,6},{6,4},{4,0},{1,3},{3,7},{7,5},{5,1},{8,10},{10,14},{14... | collective-permute-start | bytes 983048 | tf_op jit(solution)/shard_map/ppermute | solution.py:571
  9.6 22.8 %copy-start.7 = (bf16[608,384]{1,0:T(8,128)(2,1)}, bf16[608,384]{1,0:T(8,128)(2,1)S(1)}, u32[]{:S(2)}) copy-start(bf16[608,384]{1,0:T(8,128)(2,1)S(1)} %pad_maximum_fusion.1.refs_13_.refs_15_) | copy-start | bytes 1400836
  9.7 16.5 %collective-permute-start.1 = (bf16[608,384]{1,0:T(8,128)(2,1)S(1)}, bf16[608,384]{1,0:T(8,128)(2,1)S(1)}, u32[]{:S(2)}, u32[]{:S(2)}) collective-permute-start(bf16[608,384]{1,0:T(8,128)(2,1)S(1)} %pad_maximum_fusion.1.refs_13_.refs_15_), channel_id=1, source_target_pairs={{0,8},{1,17},{8,0},{9,25},{16,24},{17,1},{24,16},{25,9},{2,10},{3,... | collective-permute-start | bytes 1400840 | tf_op jit(solution)/shard_map/ppermute | solution.py:598
  12.1 16.9 %collective-permute-start = (bf16[608,384]{1,0:T(8,128)(2,1)}, bf16[608,384]{1,0:T(8,128)(2,1)}, u32[]{:S(2)}, u32[]{:S(2)}) collective-permute-start(bf16[608,384]{1,0:T(8,128)(2,1)} %pad_maximum_fusion.refs_9_), channel_id=1, source_target_pairs={{0,8},{1,17},{8,0},{9,25},{16,24},{17,1},{24,16},{25,9},{2,10},{3,... | collective-permute-start | bytes 1400840 | tf_op jit(solution)/shard_map/ppermute | solution.py:598
  12.7 24.4 %collective-permute-start.11 = (bf16[608,384]{1,0:T(8,128)(2,1)S(1)}, bf16[608,384]{1,0:T(8,128)(2,1)S(1)}, u32[]{:S(2)}, u32[]{:S(2)}) collective-permute-start(bf16[608,384]{1,0:T(8,128)(2,1)S(1)} %pad_maximum_fusion.1.refs_13_.refs_15_), channel_id=1, source_target_pairs={{0,16},{1,9},{8,24},{9,1},{16,0},{17,25},{24,8},{25,17},{2,18},{3,... | collective-permute-start | bytes 1400840 | tf_op jit(solution)/shard_map/ppermute | solution.py:599
  16.1 13.0 %copy-start.8 = (bf16[64,2560]{1,0:T(8,128)(2,1)}, bf16[64,2560]{1,0:T(8,128)(2,1)S(1)}, u32[]{:S(2)}) copy-start(bf16[64,2560]{1,0:T(8,128)(2,1)S(1)} %collective-permute-done.3.following.refs_3_) | copy-start | bytes 983044
  16.1 13.0 %collective-permute-start.4 = (bf16[32,2560]{1,0:T(8,128)(2,1)S(1)}, bf16[32,2560]{1,0:T(8,128)(2,1)S(1)}, u32[]{:S(2)}, u32[]{:S(2)}) collective-permute-start(bf16[32,2560]{1,0:T(8,128)(2,1)S(1)} %slice.8), channel_id=1, source_target_pairs={{2,0},{6,2},{4,6},{0,4},{3,1},{7,3},{5,7},{1,5},{10,8},{14,10},{12... | collective-permute-start | bytes 491528 | tf_op jit(solution)/shard_map/ppermute | solution.py:577
  24.8 4.3 %copy-start.10 = (bf16[64,2560]{1,0:T(8,128)(2,1)}, bf16[64,2560]{1,0:T(8,128)(2,1)S(1)}, u32[]{:S(2)}) copy-start(bf16[64,2560]{1,0:T(8,128)(2,1)S(1)} %collective-permute-done.2.previous.refs_1_) | copy-start | bytes 983044
  25.5 7.1 %collective-permute-start.7 = (bf16[32,2560]{1,0:T(8,128)(2,1)}, bf16[32,2560]{1,0:T(8,128)(2,1)S(1)}, u32[]{:S(2)}, u32[]{:S(2)}) collective-permute-start(bf16[32,2560]{1,0:T(8,128)(2,1)} %slice.9), channel_id=1, source_target_pairs={{0,2},{2,6},{6,4},{4,0},{1,3},{3,7},{7,5},{5,1},{8,10},{10,14},{14... | collective-permute-start | bytes 491528 | tf_op jit(solution)/shard_map/ppermute | solution.py:571
  26.2 21.2 %copy-start.12 = (bf16[608,384]{1,0:T(8,128)(2,1)}, bf16[608,384]{1,0:T(8,128)(2,1)S(1)}, u32[]{:S(2)}) copy-start(bf16[608,384]{1,0:T(8,128)(2,1)S(1)} %collective-permute-done.1.refs_14_.refs_16_) | copy-start | bytes 1400836
  26.2 21.2 %collective-permute-start.10 = (bf16[608,384]{1,0:T(8,128)(2,1)}, bf16[608,384]{1,0:T(8,128)(2,1)}, u32[]{:S(2)}, u32[]{:S(2)}) collective-permute-start(bf16[608,384]{1,0:T(8,128)(2,1)} %pad_maximum_fusion.refs_9_), channel_id=1, source_target_pairs={{0,16},{1,9},{8,24},{9,1},{16,0},{17,25},{24,8},{25,17},{2,18},{3,... | collective-permute-start | bytes 1400840 | tf_op jit(solution)/shard_map/ppermute | solution.py:599
  29.1 0.7 copy-start.14
  32.5 14.9 %copy-start.15 = (bf16[32,2560]{1,0:T(8,128)(2,1)S(1)}, bf16[32,2560]{1,0:T(8,128)(2,1)}, u32[]{:S(2)}) copy-start(bf16[32,2560]{1,0:T(8,128)(2,1)} %copy-done.14) | copy-start | bytes 491524
  32.5 19.1 %copy-start.11 = (bf16[64,2560]{1,0:T(8,128)(2,1)S(1)}, bf16[64,2560]{1,0:T(8,128)(2,1)}, u32[]{:S(2)}) copy-start(bf16[64,2560]{1,0:T(8,128)(2,1)} %copy-done.10) | copy-start | bytes 983044
  32.5 19.6 %copy-start.9 = (bf16[64,2560]{1,0:T(8,128)(2,1)S(1)}, bf16[64,2560]{1,0:T(8,128)(2,1)}, u32[]{:S(2)}) copy-start(bf16[64,2560]{1,0:T(8,128)(2,1)} %copy-done.8) | copy-start | bytes 983044
  32.7 22.2 %copy-start.23 = (bf16[32,2560]{1,0:T(8,128)(2,1)}, bf16[32,2560]{1,0:T(8,128)(2,1)S(1)}, u32[]{:S(2)}) copy-start(bf16[32,2560]{1,0:T(8,128)(2,1)S(1)} %collective-permute-done.7.refs_5_) | copy-start | bytes 491524
  32.7 11.0 %collective-permute-start.15 = (bf16[64,2560]{1,0:T(8,128)(2,1)}, bf16[64,2560]{1,0:T(8,128)(2,1)S(1)}, u32[]{:S(2)}, u32[]{:S(2)}) collective-permute-start(bf16[64,2560]{1,0:T(8,128)(2,1)} %get-tuple-element.78), channel_id=1, source_target_pairs={{2,0},{6,2},{4,6},{0,4},{3,1},{7,3},{5,7},{1,5},{10,8},{14,10},{12... | collective-permute-start | bytes 983048 | tf_op jit(solution)/shard_map/ppermute | solution.py:577
  35.1 16.4 %collective-permute-start.12 = (bf16[608,384]{1,0:T(8,128)(2,1)}, bf16[608,384]{1,0:T(8,128)(2,1)}, u32[]{:S(2)}, u32[]{:S(2)}) collective-permute-start(bf16[608,384]{1,0:T(8,128)(2,1)} %collective-permute-done.refs_10_), channel_id=1, source_target_pairs={{0,16},{1,9},{8,24},{9,1},{16,0},{17,25},{24,8},{25,17},{2,18},{3,... | collective-permute-start | bytes 1400840 | tf_op jit(solution)/shard_map/ppermute | solution.py:634
  36.6 14.9 %collective-permute-start.13 = (bf16[608,384]{1,0:T(8,128)(2,1)S(1)}, bf16[608,384]{1,0:T(8,128)(2,1)}, u32[]{:S(2)}, u32[]{:S(2)}) collective-permute-start(bf16[608,384]{1,0:T(8,128)(2,1)S(1)} %collective-permute-done.1.refs_14_.refs_16_), channel_id=1, source_target_pairs={{0,16},{1,9},{8,24},{9,1},{16,0},{17,25},{24,8},{25,17},{2,18},{3,... | collective-permute-start | bytes 1400840 | tf_op jit(solution)/shard_map/ppermute | solution.py:634
  37.1 17.8 %copy-start.13 = (bf16[608,384]{1,0:T(8,128)(2,1)}, bf16[608,384]{1,0:T(8,128)(2,1)S(1)}, u32[]{:S(2)}) copy-start(bf16[608,384]{1,0:T(8,128)(2,1)S(1)} %collective-permute-done.11.refs_15_.refs_17_) | copy-start | bytes 1400836
  37.1 14.3 %collective-permute-start.9 = (bf16[64,2560]{1,0:T(8,128)(2,1)}, bf16[64,2560]{1,0:T(8,128)(2,1)S(1)}, u32[]{:S(2)}, u32[]{:S(2)}) collective-permute-start(bf16[64,2560]{1,0:T(8,128)(2,1)} %get-tuple-element.78), channel_id=1, source_target_pairs={{0,2},{2,6},{6,4},{4,0},{1,3},{3,7},{7,5},{5,1},{8,10},{10,14},{14... | collective-permute-start | bytes 983048 | tf_op jit(solution)/shard_map/ppermute | solution.py:571
  43.6 20.6 %copy-start.16 = (bf16[64,2560]{1,0:T(8,128)(2,1)}, bf16[64,2560]{1,0:T(8,128)(2,1)S(1)}, u32[]{:S(2)}) copy-start(bf16[64,2560]{1,0:T(8,128)(2,1)S(1)} %collective-permute-done.15.refs_11_) | copy-start | bytes 983044
  43.6 8.7 %collective-permute-start.16 = (bf16[64,2560]{1,0:T(8,128)(2,1)S(1)}, bf16[64,2560]{1,0:T(8,128)(2,1)S(1)}, u32[]{:S(2)}, u32[]{:S(2)}) collective-permute-start(bf16[64,2560]{1,0:T(8,128)(2,1)S(1)} %collective-permute-done.15.refs_11_), channel_id=1, source_target_pairs={{0,1},{1,0},{2,3},{3,2},{4,5},{5,4},{6,7},{7,6},{8,9},{9,8},{10,11... | collective-permute-start | bytes 983048 | tf_op jit(solution)/shard_map/ppermute | solution.py:574
  47.4 4.7 %collective-permute-start.17 = (bf16[32,2560]{1,0:T(8,128)(2,1)S(1)}, bf16[32,2560]{1,0:T(8,128)(2,1)S(1)}, u32[]{:S(2)}, u32[]{:S(2)}) collective-permute-start(bf16[32,2560]{1,0:T(8,128)(2,1)S(1)} %copy-done.15), channel_id=1, source_target_pairs={{0,1},{1,0},{2,3},{3,2},{4,5},{5,4},{6,7},{7,6},{8,9},{9,8},{10,11... | collective-permute-start | bytes 491528 | tf_op jit(solution)/shard_map/ppermute | solution.py:574
  51.5 12.8 %copy-start.17 = (bf16[64,2560]{1,0:T(8,128)(2,1)}, bf16[64,2560]{1,0:T(8,128)(2,1)S(1)}, u32[]{:S(2)}) copy-start(bf16[64,2560]{1,0:T(8,128)(2,1)S(1)} %collective-permute-done.9.refs_9_) | copy-start | bytes 983044
  51.5 1.7 %collective-permute-start.14 = (bf16[64,2560]{1,0:T(8,128)(2,1)S(1)}, bf16[64,2560]{1,0:T(8,128)(2,1)S(1)}, u32[]{:S(2)}, u32[]{:S(2)}) collective-permute-start(bf16[64,2560]{1,0:T(8,128)(2,1)S(1)} %collective-permute-done.9.refs_9_), channel_id=1, source_target_pairs={{0,1},{1,0},{2,3},{3,2},{4,5},{5,4},{6,7},{7,6},{8,9},{9,8},{10,11... | collective-permute-start | bytes 983048 | tf_op jit(solution)/shard_map/ppermute | solution.py:574
  51.6 2.5 %collective-permute-start.5 = (bf16[64,2560]{1,0:T(8,128)(2,1)S(1)}, bf16[64,2560]{1,0:T(8,128)(2,1)S(1)}, u32[]{:S(2)}, u32[]{:S(2)}) collective-permute-start(bf16[64,2560]{1,0:T(8,128)(2,1)S(1)} %copy-done.11), channel_id=1, source_target_pairs={{0,1},{1,0},{2,3},{3,2},{4,5},{5,4},{6,7},{7,6},{8,9},{9,8},{10,11... | collective-permute-start | bytes 983048 | tf_op jit(solution)/shard_map/ppermute | solution.py:574
  52.1 2.8 %collective-permute-start.6 = (bf16[64,2560]{1,0:T(8,128)(2,1)S(1)}, bf16[64,2560]{1,0:T(8,128)(2,1)}, u32[]{:S(2)}, u32[]{:S(2)}) collective-permute-start(bf16[64,2560]{1,0:T(8,128)(2,1)S(1)} %copy-done.9), channel_id=1, source_target_pairs={{0,1},{1,0},{2,3},{3,2},{4,5},{5,4},{6,7},{7,6},{8,9},{9,8},{10,11... | collective-permute-start | bytes 983048 | tf_op jit(solution)/shard_map/ppermute | solution.py:574
  52.1 2.0 %copy-start.24 = (bf16[32,2560]{1,0:T(8,128)(2,1)}, bf16[32,2560]{1,0:T(8,128)(2,1)S(1)}, u32[]{:S(2)}) copy-start(bf16[32,2560]{1,0:T(8,128)(2,1)S(1)} %collective-permute-done.17.refs_8_) | copy-start | bytes 491524
  52.1 12.1 %collective-permute-start.18 = (bf16[64,2560]{1,0:T(8,128)(2,1)S(1)}, bf16[64,2560]{1,0:T(8,128)(2,1)S(1)}, u32[]{:S(2)}, u32[]{:S(2)}) collective-permute-start(bf16[64,2560]{1,0:T(8,128)(2,1)S(1)} %collective-permute-done.9.refs_9_), channel_id=1, source_target_pairs={{0,2},{2,6},{6,4},{4,0},{1,3},{3,7},{7,5},{5,1},{8,10},{10,14},{14... | collective-permute-start | bytes 983048 | tf_op jit(solution)/shard_map/ppermute | solution.py:571
  52.3 11.9 %copy-start.18 = (bf16[64,2560]{1,0:T(8,128)(2,1)}, bf16[64,2560]{1,0:T(8,128)(2,1)S(1)}, u32[]{:S(2)}) copy-start(bf16[64,2560]{1,0:T(8,128)(2,1)S(1)} %collective-permute-done.16.refs_12_) | copy-start | bytes 983044
  52.3 1.8 %collective-permute-start.8 = (bf16[32,2560]{1,0:T(8,128)(2,1)S(1)}, bf16[32,2560]{1,0:T(8,128)(2,1)S(1)}, u32[]{:S(2)}, u32[]{:S(2)}) collective-permute-start(bf16[32,2560]{1,0:T(8,128)(2,1)S(1)} %collective-permute-done.7.refs_5_), channel_id=1, source_target_pairs={{0,1},{1,0},{2,3},{3,2},{4,5},{5,4},{6,7},{7,6},{8,9},{9,8},{10,11... | collective-permute-start | bytes 491528 | tf_op jit(solution)/shard_map/ppermute | solution.py:574
  53.2 11.1 %copy-start.19 = (bf16[64,2560]{1,0:T(8,128)(2,1)}, bf16[64,2560]{1,0:T(8,128)(2,1)S(1)}, u32[]{:S(2)}) copy-start(bf16[64,2560]{1,0:T(8,128)(2,1)S(1)} %collective-permute-done.14.refs_10_) | copy-start | bytes 983044
  54.1 0.8 copy-start.25
  54.1 0.8 copy-start.21
  64.3 2.0 %copy-start.20 = (bf16[64,2560]{1,0:T(8,128)(2,1)}, bf16[64,2560]{1,0:T(8,128)(2,1)S(1)}, u32[]{:S(2)}) copy-start(bf16[64,2560]{1,0:T(8,128)(2,1)S(1)} %collective-permute-done.18.refs_13_) | copy-start | bytes 983044
  64.3 1.7 %collective-permute-start.19 = (bf16[64,2560]{1,0:T(8,128)(2,1)S(1)}, bf16[64,2560]{1,0:T(8,128)(2,1)S(1)}, u32[]{:S(2)}, u32[]{:S(2)}) collective-permute-start(bf16[64,2560]{1,0:T(8,128)(2,1)S(1)} %collective-permute-done.18.refs_13_), channel_id=1, source_target_pairs={{0,1},{1,0},{2,3},{3,2},{4,5},{5,4},{6,7},{7,6},{8,9},{9,8},{10,11... | collective-permute-start | bytes 983048 | tf_op jit(solution)/shard_map/ppermute | solution.py:574
  66.0 0.7 copy-start.22
  66.0 17.5 %collective-permute-start.23 = (bf16[1216,640]{1,0:T(8,128)(2,1)}, bf16[1216,640]{1,0:T(8,128)(2,1)}, u32[]{:S(2)}, u32[]{:S(2)}) collective-permute-start(bf16[1216,640]{1,0:T(8,128)(2,1)} %get-tuple-element.112.refs_7_), channel_id=1, source_target_pairs={{0,1},{1,0},{2,3},{3,2},{4,5},{5,4},{6,7},{7,6},{8,9},{9,8},{10,11... | collective-permute-start | bytes 4669448 | tf_op jit(solution)/shard_map/ppermute | solution.py:574
  66.7 16.8 %copy-start.2 = (bf16[1216,640]{1,0:T(8,128)(2,1)S(1)}, bf16[1216,640]{1,0:T(8,128)(2,1)}, u32[]{:S(2)}) copy-start(bf16[1216,640]{1,0:T(8,128)(2,1)} %get-tuple-element.89.refs_6_.w_own) | copy-start | bytes 4669444
  77.4 1.7 %collective-permute-start.22 = (bf16[64,1216]{1,0:T(8,128)(2,1)}, bf16[64,1216]{1,0:T(8,128)(2,1)S(1)}, u32[]{:S(2)}, u32[]{:S(2)}) collective-permute-start(bf16[64,1216]{1,0:T(8,128)(2,1)} %get-tuple-element.109), channel_id=1, source_target_pairs={{0,1},{1,0},{2,3},{3,2},{4,5},{5,4},{6,7},{7,6},{8,9},{9,8},{10,11... | collective-permute-start | bytes 466952 | tf_op jit(solution)/shard_map/ppermute | solution.py:574
  77.8 3.9 %collective-permute-start.21 = (bf16[64,1216]{1,0:T(8,128)(2,1)}, bf16[64,1216]{1,0:T(8,128)(2,1)S(1)}, u32[]{:S(2)}, u32[]{:S(2)}) collective-permute-start(bf16[64,1216]{1,0:T(8,128)(2,1)} %get-tuple-element.107), channel_id=1, source_target_pairs={{0,1},{1,0},{2,3},{3,2},{4,5},{5,4},{6,7},{7,6},{8,9},{9,8},{10,11... | collective-permute-start | bytes 466952 | tf_op jit(solution)/shard_map/ppermute | solution.py:574
  78.0 5.4 %collective-permute-start.20 = (bf16[384,640]{1,0:T(8,128)(2,1)}, bf16[384,640]{1,0:T(8,128)(2,1)S(1)}, u32[]{:S(2)}, u32[]{:S(2)}) collective-permute-start(bf16[384,640]{1,0:T(8,128)(2,1)} %get-tuple-element.110.own), channel_id=1, source_target_pairs={{0,1},{1,0},{2,3},{3,2},{4,5},{5,4},{6,7},{7,6},{8,9},{9,8},{10,11... | collective-permute-start | bytes 1474568 | tf_op jit(solution)/shard_map/ppermute | solution.py:574
  80.1 8.0 %collective-permute-start.27 = (bf16[64,1216]{1,0:T(8,128)(2,1)S(1)}, bf16[64,1216]{1,0:T(8,128)(2,1)S(1)}, u32[]{:S(2)}, u32[]{:S(2)}) collective-permute-start(bf16[64,1216]{1,0:T(8,128)(2,1)S(1)} %add_convert_fusion.4), channel_id=1, source_target_pairs={{0,2},{2,6},{6,4},{4,0},{1,3},{3,7},{7,5},{5,1},{8,10},{10,14},{14... | collective-permute-start | bytes 466952 | tf_op jit(solution)/shard_map/ppermute | solution.py:571
  82.7 8.3 %collective-permute-start.24 = (bf16[64,1216]{1,0:T(8,128)(2,1)S(1)}, bf16[64,1216]{1,0:T(8,128)(2,1)S(1)}, u32[]{:S(2)}, u32[]{:S(2)}) collective-permute-start(bf16[64,1216]{1,0:T(8,128)(2,1)S(1)} %add_convert_fusion.5), channel_id=1, source_target_pairs={{0,2},{2,6},{6,4},{4,0},{1,3},{3,7},{7,5},{5,1},{8,10},{10,14},{14... | collective-permute-start | bytes 466952 | tf_op jit(solution)/shard_map/ppermute | solution.py:571
  83.5 1.0 copy-start.6
  87.6 17.9 %copy-start.1 = (f32[128,1216]{1,0:T(8,128)S(1)}, f32[128,1216]{1,0:T(8,128)}, u32[]{:S(2)}) copy-start(f32[128,1216]{1,0:T(8,128)} %get-tuple-element.120.normed) | copy-start | bytes 1867780
  87.6 17.9 %copy-start.5 = (f32[1,1216]{1,0:T(1,128)S(1)}, f32[1,1216]{1,0:T(1,128)}, u32[]{:S(2)}) copy-start(f32[1,1216]{1,0:T(1,128)} %get-tuple-element.119.scale) | copy-start | bytes 14596
  88.1 6.7 %collective-permute-start.28 = (bf16[64,1216]{1,0:T(8,128)(2,1)S(1)}, bf16[64,1216]{1,0:T(8,128)(2,1)S(1)}, u32[]{:S(2)}, u32[]{:S(2)}) collective-permute-start(bf16[64,1216]{1,0:T(8,128)(2,1)S(1)} %add_convert_fusion.1), channel_id=1, source_target_pairs={{0,2},{2,6},{6,4},{4,0},{1,3},{3,7},{7,5},{5,1},{8,10},{10,14},{14... | collective-permute-start | bytes 466952 | tf_op jit(solution)/shard_map/ppermute | solution.py:571
  91.1 16.0 %copy-start.3 = (f32[128,1216]{1,0:T(8,128)S(1)}, f32[128,1216]{1,0:T(8,128)}, u32[]{:S(2)}) copy-start(f32[128,1216]{1,0:T(8,128)} %get-tuple-element.123.base) | copy-start | bytes 1867780
  91.1 16.0 %copy-start.4 = (f32[128,128]{1,0:T(8,128)S(1)}, f32[128,128]{1,0:T(8,128)}, u32[]{:S(2)}) copy-start(f32[128,128]{1,0:T(8,128)} %get-tuple-element.124.inv_std) | copy-start | bytes 196612
  91.1 8.1 %collective-permute-start.25 = (bf16[64,1216]{1,0:T(8,128)(2,1)S(1)}, bf16[64,1216]{1,0:T(8,128)(2,1)S(1)}, u32[]{:S(2)}, u32[]{:S(2)}) collective-permute-start(bf16[64,1216]{1,0:T(8,128)(2,1)S(1)} %add_convert_fusion.3), channel_id=1, source_target_pairs={{0,2},{2,6},{6,4},{4,0},{1,3},{3,7},{7,5},{5,1},{8,10},{10,14},{14... | collective-permute-start | bytes 466952 | tf_op jit(solution)/shard_map/ppermute | solution.py:571
  94.9 7.6 %collective-permute-start.29 = (bf16[64,1216]{1,0:T(8,128)(2,1)S(1)}, bf16[64,1216]{1,0:T(8,128)(2,1)S(1)}, u32[]{:S(2)}, u32[]{:S(2)}) collective-permute-start(bf16[64,1216]{1,0:T(8,128)(2,1)S(1)} %add_convert_fusion), channel_id=1, source_target_pairs={{0,2},{2,6},{6,4},{4,0},{1,3},{3,7},{7,5},{5,1},{8,10},{10,14},{14... | collective-permute-start | bytes 466952 | tf_op jit(solution)/shard_map/ppermute | solution.py:571
  99.2 6.3 %collective-permute-start.26 = (bf16[64,1216]{1,0:T(8,128)(2,1)S(1)}, bf16[64,1216]{1,0:T(8,128)(2,1)S(1)}, u32[]{:S(2)}, u32[]{:S(2)}) collective-permute-start(bf16[64,1216]{1,0:T(8,128)(2,1)S(1)} %add_convert_fusion.2), channel_id=1, source_target_pairs={{0,2},{2,6},{6,4},{4,0},{1,3},{3,7},{7,5},{5,1},{8,10},{10,14},{14... | collective-permute-start | bytes 466952 | tf_op jit(solution)/shard_map/ppermute | solution.py:571
  105.7 1.3 %collective-permute-start.30 = (f32[128,128]{1,0:T(8,128)S(1)}, f32[128,128]{1,0:T(8,128)S(1)}, u32[]{:S(2)}, u32[]{:S(2)}) collective-permute-start(f32[128,128]{1,0:T(8,128)S(1)} %get-tuple-element.122.sums), channel_id=1, source_target_pairs={{0,1},{1,0},{2,3},{3,2},{4,5},{5,4},{6,7},{7,6},{8,9},{9,8},{10,11... | collective-permute-start | bytes 196616 | tf_op jit(solution)/shard_map/ppermute | solution.py:574

commit v4 on v2

--- a/solution.py
+++ b/solution.py
@@ -302,7 +302,7 @@
     projected = take(8)
     cot_in = take(7)
     w_in = take(4)
-    mine_out, theirs_out, rest_out = take(3)
+    mine_near, mine_far, theirs_near, theirs_far, rest_out = take(5)
     w_out, cot_all, sems, extra, values_text = take(5)
     d_all, grads, stacked = take(3)
     qkv, k_t, raw_all, inv_all, text, text_t, w_keep, w_give = refs
@@ -393,8 +393,12 @@
     rest_out[(count - 2) * rows :, :] = stacked[:rows, :]
     for copy in local_copies[6:]:
         copy.wait()
-    theirs_out[...] = dot(first, w_give[...], NT).astype(jnp.bfloat16)
-    mine_out[...] = dot(first, w_keep[...], NT)
+    theirs = dot(first, w_give[...], NT).astype(jnp.bfloat16)
+    theirs_near[...] = theirs[: rows // 2]
+    theirs_far[...] = theirs[rows // 2 :]
+    mine = dot(first, w_keep[...], NT)
+    mine_near[...] = mine[: rows // 2]
+    mine_far[...] = mine[rows // 2 :]
 
 
 def project_call(scalars, gain, mod, weights, slots, rows, text_dev, count):
@@ -440,7 +444,8 @@
     first = (columns - inner) // 128 * 128
     f32, bf16 = jnp.float32, jnp.bfloat16
     vmem, hbm = spec(pltpu.VMEM), spec(pl.ANY)
-    shapes = [((rows, width // 2), f32), ((rows, width // 2), bf16), ((tokens - rows, stacked), bf16)]
+    part = (rows // 2, width // 2)
+    shapes = [(part, f32)] * 2 + [(part, bf16)] * 2 + [((tokens - rows, stacked), bf16)]
     return pl.pallas_call(
         functools.partial(attend_kernel, slots, count, rows, shard, width, text_dev, first),
         out_shape=tuple(jax.ShapeDtypeStruct(*one) for one in shapes),
@@ -639,11 +644,10 @@
     cot_pieces += pieces(None, cot_far)[1:]
     given, *cot_pieces = pin((w_give, *cot_pieces))
     w_other = other_core(given)
-    mine, theirs, rest = attend_call(
+    *first, rest = attend_call(
         scalars, qk_gain, operands + [w_keep, w_give], cot_pieces, weights[4:], slots, tok_count, text_dev
     )
-    first = (mine + other_core(theirs).astype(f32)).astype(bf16)
-    moving = [first[:half_rows], first[half_rows:]]
+    moving = [(a + other_core(b).astype(f32)).astype(bf16) for a, b in zip(first[:2], first[2:])]
     other_rest = other_core(rest)
     rest, other_rest, *_ = pin((rest, other_rest, *moving))
     own = backward_call(rest, other_rest, w_keep, w_other, half_rows, f32)

time: 109 us -> 107 us (0.982)
  waiting for transfers between devices: 40.2 us -> 35.7 us
  starting transfers between devices: 25.5 us -> 27.5 us
  Pallas kernels: 30.8 us -> 32.5 us
  local copies, waits for them, and re-layouts: 7.5 us -> 6.35 us
    ppermute x10, waiting for transfers between devices: 26.2 us -> 22.1 us  [step(): return lax.ppermute(moving, 'seq', seq_next)]
    ppermute x10, starting transfers between devices: 5.97 us -> 8.16 us  [step(): return lax.ppermute(moving, 'seq', seq_next)]
    pallas_call x1, Pallas kernels: 1.69 us -> 3.11 us  [backward_call(): pl.pallas_call(backward_kernel, out_shape=(jax.ShapeDtypeStruct((part, ha...]
    unnamed x50 -> x52, local copies, waits for them, and re-layouts: 3.59 us -> 3.09 us
    ppermute x11 -> x12, starting transfers between devices: 2.82 us -> 2.39 us  [other_core(): return lax.ppermute(moving, 'head', swap)]
    ppermute x11 -> x12, waiting for transfers between devices: 5.59 us -> 5.25 us  [other_core(): return lax.ppermute(moving, 'head', swap)]
  transfers between devices with their start and end apart: 30 -> 31, of which waited for: 16 -> 17; matrix products, arithmetic and copies ran while one was open for 6% -> 6% of each run, Pallas kernels for 25% -> 26%
where the time goes in v4:
time: 107 us
  waiting for transfers between devices  35.7 us (33%)
  Pallas kernels  32.5 us (30%)
  starting transfers between devices  27.5 us (26%)
  local copies, waits for them, and re-layouts  6.35 us (6%)
  other arithmetic  3.24 us (3%)
  between operations  1.71 us (2%)
    ppermute x10, waiting for transfers between devices, step(): return lax.ppermute(moving, 'seq', seq_next)  22.1 us
    pallas_call x1, Pallas kernels, attend_call(): pl.pallas_call(functools.partial(attend_kernel, slots, count, rows, shard...  10.7 us
    ppermute x3, starting transfers between devices, step_back(): return lax.ppermute(moving, 'seq', [(b, a) for a, b in seq_next])  9.8 us
    ppermute x3, waiting for transfers between devices, step_back(): return lax.ppermute(moving, 'seq', [(b, a) for a, b in seq_next])  8.36 us
    ppermute x10, starting transfers between devices, step(): return lax.ppermute(moving, 'seq', seq_next)  8.16 us
    pallas_call x1, Pallas kernels, project_call(): pl.pallas_call(functools.partial(project_kernel, slots, count, rows, shar...  7.82 us
    ppermute x12, waiting for transfers between devices, other_core(): return lax.ppermute(moving, 'head', swap)  5.25 us
    pallas_call x3, Pallas kernels, local_call(): pl.pallas_call(kernel, out_shape=tuple((jax.ShapeDtypeStruct(*one) for on...  5.21 us
  transfers between devices with their start and end apart: 31, of which 17 were waited for; matrix products, arithmetic and copies ran while one was open for 6% of the time, Pallas kernels for 26%

profile of v4, /device:TPU:0, one launch (start us, length us, event | category | flops | bytes accessed | tf_op | source)
XLA Modules:
  0.0 107.0 jit_solution(3818820164852768256)
XLA Ops:
  0.7 2.8 %shard_map.91 = (bf16[64,2560]{1,0:T(8,128)(2,1)}, f32[8,2432]{1,0:T(8,128)}, bf16[64,128]{1,0:T(8,128)(2,1)}) custom-call(s32[1]{0:T(128)S(6)} %copy.11.step, s32[1]{0:T(128)} %bitcast.core, bf16[128,2432]{1,0:T(8,128)(2,1)} %bitcast.31, f32[3,28,2432]{2,1,0:T(8,128)} %bitcast.33, f32[128,2432]{1,0:T(8,128)} %bitcast.28, bf16[8,2,640]{2,1,0:T(2,128)(2,1)} %bitcast.34), custom_call_target="tpu_custom_call" | custom-call | flops 1245184 | bytes 2490368 | tf_op jit(solution)/shard_map/pallas_call | solution.py:110
  3.6 4.0 %collective-permute-start.3 = (bf16[64,2560]{1,0:T(8,128)(2,1)}, bf16[64,2560]{1,0:T(8,128)(2,1)S(1)}, u32[]{:S(2)}, u32[]{:S(2)}) collective-permute-start(bf16[64,2560]{1,0:T(8,128)(2,1)} %get-tuple-element.67), channel_id=1, source_target_pairs={{2,0},{6,2},{4,6},{0,4},{3,1},{7,3},{5,7},{1,5},{10,8},{14,10},{12... | collective-permute-start | bytes 983048 | tf_op jit(solution)/shard_map/ppermute | solution.py:576
  7.6 1.7 %dynamic-slice_bitcast_fusion.1 = (bf16[608,192]{1,0:T(8,128)(2,1)S(1)}, bf16[608,192]{1,0:T(8,128)(2,1)S(1)}, bf16[608,192]{1,0:T(8,128)(2,1)S(1)}) fusion(bf16[608,3,640]{2,0,1:T(8,128)(2,1)} %param.15, s32[]{:T(128)S(6)} %select_n.103), kind=kLoop, calls=%fused_computation.9 | loop fusion | bytes 1400836 | tf_op jit(solution)/shard_map/squeeze | solution.py:592
  9.3 0.2 dynamic-slice_bitcast_fusion
  9.5 0.2 pad_maximum_fusion.1.refs_13_.refs_15_
  9.7 1.6 %collective-permute-start.1 = (bf16[608,384]{1,0:T(8,128)(2,1)S(1)}, bf16[608,384]{1,0:T(8,128)(2,1)S(1)}, u32[]{:S(2)}, u32[]{:S(2)}) collective-permute-start(bf16[608,384]{1,0:T(8,128)(2,1)S(1)} %pad_maximum_fusion.1.refs_13_.refs_15_), channel_id=1, source_target_pairs={{0,8},{1,17},{8,0},{9,25},{16,24},{17,1},{24,16},{25,9},{2,10},{3,... | collective-permute-start | bytes 1400840 | tf_op jit(solution)/shard_map/ppermute | solution.py:597
  11.2 0.9 pad_maximum_fusion.refs_9_
  12.1 0.5 collective-permute-start
  12.7 1.5 %collective-permute-start.11 = (bf16[608,384]{1,0:T(8,128)(2,1)S(1)}, bf16[608,384]{1,0:T(8,128)(2,1)S(1)}, u32[]{:S(2)}, u32[]{:S(2)}) collective-permute-start(bf16[608,384]{1,0:T(8,128)(2,1)S(1)} %pad_maximum_fusion.1.refs_13_.refs_15_), channel_id=1, source_target_pairs={{0,16},{1,9},{8,24},{9,1},{16,0},{17,25},{24,8},{25,17},{2,18},{3,... | collective-permute-start | bytes 1400840 | tf_op jit(solution)/shard_map/ppermute | solution.py:598
  14.2 1.9 %collective-permute-done.3.following.refs_3_ = bf16[64,2560]{1,0:T(8,128)(2,1)S(1)} collective-permute-done((bf16[64,2560]{1,0:T(8,128)(2,1)}, bf16[64,2560]{1,0:T(8,128)(2,1)S(1)}, u32[]{:S(2)}, u32[]{:S(2)}) %collective-permute-start.3) | collective-permute-done | bytes 327712 | tf_op jit(solution)/shard_map/ppermute | solution.py:576
  16.1 3.3 %collective-permute-start.4 = (bf16[32,2560]{1,0:T(8,128)(2,1)S(1)}, bf16[32,2560]{1,0:T(8,128)(2,1)S(1)}, u32[]{:S(2)}, u32[]{:S(2)}) collective-permute-start(bf16[32,2560]{1,0:T(8,128)(2,1)S(1)} %slice.8), channel_id=1, source_target_pairs={{2,0},{6,2},{4,6},{0,4},{3,1},{7,3},{5,7},{1,5},{10,8},{14,10},{12... | collective-permute-start | bytes 491528 | tf_op jit(solution)/shard_map/ppermute | solution.py:576
  19.4 5.4 %collective-permute-done.2.previous.refs_1_ = bf16[64,2560]{1,0:T(8,128)(2,1)S(1)} collective-permute-done((bf16[64,2560]{1,0:T(8,128)(2,1)}, bf16[64,2560]{1,0:T(8,128)(2,1)S(1)}, u32[]{:S(2)}, u32[]{:S(2)}) %collective-permute-start.2) | collective-permute-done | bytes 327712 | tf_op jit(solution)/shard_map/ppermute | solution.py:570
  24.8 0.7 slice.9
  25.5 0.7 collective-permute-start.7
  26.2 1.5 %collective-permute-start.10 = (bf16[608,384]{1,0:T(8,128)(2,1)}, bf16[608,384]{1,0:T(8,128)(2,1)}, u32[]{:S(2)}, u32[]{:S(2)}) collective-permute-start(bf16[608,384]{1,0:T(8,128)(2,1)} %pad_maximum_fusion.refs_9_), channel_id=1, source_target_pairs={{0,16},{1,9},{8,24},{9,1},{16,0},{17,25},{24,8},{25,17},{2,18},{3,... | collective-permute-start | bytes 1400840 | tf_op jit(solution)/shard_map/ppermute | solution.py:598
  28.4 0.7 stack.67.core.scalars
  29.1 0.6 copy-done.14
  29.7 2.7 %shard_map.92 = (bf16[64,2560]{1,0:T(8,128)(2,1)}, f32[8,128]{1,0:T(8,128)}) custom-call(s32[14]{0:T(128)} %stack.67.core.scalars, f32[128,2432]{1,0:T(8,128)} %bitcast.29, f32[8,2432]{1,0:T(8,128)} %get-tuple-element.65.table_rows, bf16[8,2,640]{2,1,0:T(2,128)(2,1)} %bitcast.35, bf16[64,128]{1,0:T(8,128)(2,1)} %get-tuple-element.70.extra, ...), custom_call_target="tpu_custom_call" | custom-call | flops 622592 | bytes 933888 | tf_op jit(solution)/shard_map/pallas_call | solution.py:162
  32.5 0.1 collective-permute-done.7.refs_5_
  32.7 2.4 %collective-permute-start.15 = (bf16[64,2560]{1,0:T(8,128)(2,1)}, bf16[64,2560]{1,0:T(8,128)(2,1)S(1)}, u32[]{:S(2)}, u32[]{:S(2)}) collective-permute-start(bf16[64,2560]{1,0:T(8,128)(2,1)} %get-tuple-element.78), channel_id=1, source_target_pairs={{2,0},{6,2},{4,6},{0,4},{3,1},{7,3},{5,7},{1,5},{10,8},{14,10},{12... | collective-permute-start | bytes 983048 | tf_op jit(solution)/shard_map/ppermute | solution.py:576
  35.1 1.5 %collective-permute-start.12 = (bf16[608,384]{1,0:T(8,128)(2,1)}, bf16[608,384]{1,0:T(8,128)(2,1)}, u32[]{:S(2)}, u32[]{:S(2)}) collective-permute-start(bf16[608,384]{1,0:T(8,128)(2,1)} %collective-permute-done.refs_10_), channel_id=1, source_target_pairs={{0,16},{1,9},{8,24},{9,1},{16,0},{17,25},{24,8},{25,17},{2,18},{3,... | collective-permute-start | bytes 1400840 | tf_op jit(solution)/shard_map/ppermute | solution.py:633
  36.6 0.5 collective-permute-start.13
  37.1 6.5 %collective-permute-done.15.refs_11_ = bf16[64,2560]{1,0:T(8,128)(2,1)S(1)} collective-permute-done((bf16[64,2560]{1,0:T(8,128)(2,1)}, bf16[64,2560]{1,0:T(8,128)(2,1)S(1)}, u32[]{:S(2)}, u32[]{:S(2)}) %collective-permute-start.15) | collective-permute-done | bytes 327712 | tf_op jit(solution)/shard_map/ppermute | solution.py:576
  43.6 3.8 %shard_map.93 = (bf16[128,2560]{1,0:T(8,128)(2,1)}, bf16[128,2560]{1,0:T(8,128)(2,1)}, f32[128,1216]{1,0:T(8,128)}, f32[1,1216]{1,0:T(1,128)}, f32[128,128]{1,0:T(8,128)}, /*index=5*/f32[128,1216]{1,0:T(8,128)}) custom-call(s32[1]{0:T(128)} %bitcast.core, bf16[128,2432]{1,0:T(8,128)(2,1)} %bitcast.32, f32[128,2432]{1,0:T(8,128)} %bitcast.30, ...), custom_call_target="tpu_custom_call" | custom-call | flops 661505 | bytes 1986564 | tf_op jit(solution)/shard_map/pallas_call | solution.py:521
  47.4 0.5 collective-permute-start.17
  47.9 3.6 %collective-permute-done.9.refs_9_ = bf16[64,2560]{1,0:T(8,128)(2,1)S(1)} collective-permute-done((bf16[64,2560]{1,0:T(8,128)(2,1)}, bf16[64,2560]{1,0:T(8,128)(2,1)S(1)}, u32[]{:S(2)}, u32[]{:S(2)}) %collective-permute-start.9) | collective-permute-done | bytes 327712 | tf_op jit(solution)/shard_map/ppermute | solution.py:570
  51.5 0.1 collective-permute-start.14
  51.6 0.5 collective-permute-start.5
  52.1 0.1 collective-permute-start.6
  52.1 0.2 collective-permute-start.18
  52.3 0.3 collective-permute-start.8
  52.7 0.5 collective-permute-done.14.refs_10_
  53.2 0.9 collective-permute-done.8.refs_6_
  54.1 0.8 copy-done.21
  54.9 7.8 %shard_map.94 = (bf16[512,576]{1,0:T(8,128)(2,1)}, bf16[192,512]{1,0:T(8,128)(2,1)}, f32[512,384]{1,0:T(8,128)}, f32[512,384]{1,0:T(8,128)}, bf16[3,32,64]{2,1,0...) custom-call(s32[14]{0:T(128)} %stack.67.core.scalars, ...), custom_call_target="tpu_custom_call" | custom-call | flops 1434451968 | bytes 6914048 | tf_op jit(solution)/shard_map/pallas_call | solution.py:416
  62.8 0.3 collective-permute-done.18.refs_13_
  63.1 1.6 %collective-permute-done.19.refs_14_ = bf16[64,2560]{1,0:T(8,128)(2,1)S(1)} collective-permute-done((bf16[64,2560]{1,0:T(8,128)(2,1)S(1)}, bf16[64,2560]{1,0:T(8,128)(2,1)S(1)}, u32[]{:S(2)}, u32[]{:S(2)}) %collective-permute-start.19) | collective-permute-done | bytes 327712 | tf_op jit(solution)/shard_map/ppermute | solution.py:573
  64.7 0.1 collective-permute-start.23
  64.9 0.6 copy-done.22
  65.4 10.7 %shard_map.95 = (f32[64,1216]{1,0:T(8,128)}, f32[64,1216]{1,0:T(8,128)}, bf16[64,1216]{1,0:T(8,128)(2,1)}, bf16[64,1216]{1,0:T(8,128)(2,1)}, bf16[384,640]{1,0:T(8,128)(2,1)}) custom-call(s32[14]{0:T(128)} %stack.67.core.scalars, f32[2,64]{1,0:T(2,128)} %gain.3, bf16[512,576]{1,0:T(8,128)(2,1)} %get-tuple-element.83.refs_0_, ...), custom_call_target="tpu_custom_call" | custom-call | flops 981467136 | bytes 4358144 | tf_op jit(solution)/shard_map/pallas_call | solution.py:449
  76.2 0.2 collective-permute-start.22
  76.4 0.4 collective-permute-start.21
  76.8 0.1 collective-permute-start.20
  76.9 1.0 collective-permute-done.22
  77.9 1.0 add_convert_fusion.4
  78.9 1.3 %collective-permute-start.27 = (bf16[64,1216]{1,0:T(8,128)(2,1)S(1)}, bf16[64,1216]{1,0:T(8,128)(2,1)S(1)}, u32[]{:S(2)}, u32[]{:S(2)}) collective-permute-start(bf16[64,1216]{1,0:T(8,128)(2,1)S(1)} %add_convert_fusion.4), channel_id=1, source_target_pairs={{0,2},{2,6},{6,4},{4,0},{1,3},{3,7},{7,5},{5,1},{8,10},{10,14},{14... | collective-permute-start | bytes 466952 | tf_op jit(solution)/shard_map/ppermute | solution.py:570
  80.2 1.0 add_convert_fusion.5
  81.2 0.8 collective-permute-start.24
  82.0 1.0 copy-done.6
  83.0 3.1 %shard_map.96 = (f32[64,1216]{1,0:T(8,128)S(1)}, f32[64,1216]{1,0:T(8,128)S(1)}, f32[64,1216]{1,0:T(8,128)S(1)}, f32[64,1216]{1,0:T(8,128)S(1)}, f32[64,1216]{1,0:T(8,128)S(1)}, /*index=5*/f32[64,1216]{1,0:T(8,128)S(1)}) custom-call(bf16[384,640]{1,0:T(8,128)(2,1)S(1)} %copy-done.6, bf16[384,640]{1,0:T(8,128)(2,1)S(1)} %collective-permute-done.20.other, ...), custom_call_target="tpu_custom_call" | custom-call | flops 1195376640 | bytes 5963776 | tf_op jit(solution)/shard_map/pallas_call | solution.py:485
  86.2 0.7 collective-permute-done.27
  86.9 1.7 %collective-permute-start.28 = (bf16[64,1216]{1,0:T(8,128)(2,1)S(1)}, bf16[64,1216]{1,0:T(8,128)(2,1)S(1)}, u32[]{:S(2)}, u32[]{:S(2)}) collective-permute-start(bf16[64,1216]{1,0:T(8,128)(2,1)S(1)} %add_convert_fusion.1), channel_id=1, source_target_pairs={{0,2},{2,6},{6,4},{4,0},{1,3},{3,7},{7,5},{5,1},{8,10},{10,14},{14... | collective-permute-start | bytes 466952 | tf_op jit(solution)/shard_map/ppermute | solution.py:570
  88.6 1.2 %collective-permute-done.24 = bf16[64,1216]{1,0:T(8,128)(2,1)S(1)} collective-permute-done((bf16[64,1216]{1,0:T(8,128)(2,1)S(1)}, bf16[64,1216]{1,0:T(8,128)(2,1)S(1)}, u32[]{:S(2)}, u32[]{:S(2)}) %collective-permute-start.24) | collective-permute-done | bytes 155680 | tf_op jit(solution)/shard_map/ppermute | solution.py:570
  89.8 0.3 collective-permute-start.25
  90.1 3.8 %collective-permute-done.28 = bf16[64,1216]{1,0:T(8,128)(2,1)S(1)} collective-permute-done((bf16[64,1216]{1,0:T(8,128)(2,1)S(1)}, bf16[64,1216]{1,0:T(8,128)(2,1)S(1)}, u32[]{:S(2)}, u32[]{:S(2)}) %collective-permute-start.28) | collective-permute-done | bytes 155680 | tf_op jit(solution)/shard_map/ppermute | solution.py:570
  93.9 1.9 %collective-permute-start.29 = (bf16[64,1216]{1,0:T(8,128)(2,1)S(1)}, bf16[64,1216]{1,0:T(8,128)(2,1)S(1)}, u32[]{:S(2)}, u32[]{:S(2)}) collective-permute-start(bf16[64,1216]{1,0:T(8,128)(2,1)S(1)} %add_convert_fusion), channel_id=1, source_target_pairs={{0,2},{2,6},{6,4},{4,0},{1,3},{3,7},{7,5},{5,1},{8,10},{10,14},{14... | collective-permute-start | bytes 466952 | tf_op jit(solution)/shard_map/ppermute | solution.py:570
  95.8 2.1 %collective-permute-done.25 = bf16[64,1216]{1,0:T(8,128)(2,1)S(1)} collective-permute-done((bf16[64,1216]{1,0:T(8,128)(2,1)S(1)}, bf16[64,1216]{1,0:T(8,128)(2,1)S(1)}, u32[]{:S(2)}, u32[]{:S(2)}) %collective-permute-start.25) | collective-permute-done | bytes 155680 | tf_op jit(solution)/shard_map/ppermute | solution.py:570
  97.9 1.4 %collective-permute-start.26 = (bf16[64,1216]{1,0:T(8,128)(2,1)S(1)}, bf16[64,1216]{1,0:T(8,128)(2,1)S(1)}, u32[]{:S(2)}, u32[]{:S(2)}) collective-permute-start(bf16[64,1216]{1,0:T(8,128)(2,1)S(1)} %add_convert_fusion.2), channel_id=1, source_target_pairs={{0,2},{2,6},{6,4},{4,0},{1,3},{3,7},{7,5},{5,1},{8,10},{10,14},{14... | collective-permute-start | bytes 466952 | tf_op jit(solution)/shard_map/ppermute | solution.py:570
  99.3 2.0 %collective-permute-done.29.far = bf16[64,1216]{1,0:T(8,128)(2,1)S(1)} collective-permute-done((bf16[64,1216]{1,0:T(8,128)(2,1)S(1)}, bf16[64,1216]{1,0:T(8,128)(2,1)S(1)}, u32[]{:S(2)}, u32[]{:S(2)}) %collective-permute-start.29) | collective-permute-done | bytes 155680 | tf_op jit(solution)/shard_map/ppermute | solution.py:570
  101.3 2.9 %collective-permute-done.26.near = bf16[64,1216]{1,0:T(8,128)(2,1)S(1)} collective-permute-done((bf16[64,1216]{1,0:T(8,128)(2,1)S(1)}, bf16[64,1216]{1,0:T(8,128)(2,1)S(1)}, u32[]{:S(2)}, u32[]{:S(2)}) %collective-permute-start.26) | collective-permute-done | bytes 155680 | tf_op jit(solution)/shard_map/ppermute | solution.py:570
  104.2 0.2 shard_map.97
  104.5 0.1 collective-permute-start.30
  104.5 1.2 %collective-permute-done.30.other = f32[128,128]{1,0:T(8,128)S(1)} collective-permute-done((f32[128,128]{1,0:T(8,128)S(1)}, f32[128,128]{1,0:T(8,128)S(1)}, u32[]{:S(2)}, u32[]{:S(2)}) %collective-permute-start.30) | collective-permute-done | bytes 65568 | tf_op jit(solution)/shard_map/ppermute | solution.py:573
  105.8 1.2 %shard_map.98 = f32[1216,128]{1,0:T(8,128)} custom-call(f32[128,1216]{1,0:T(8,128)S(1)} %get-tuple-element.121.grad, f32[128,128]{1,0:T(8,128)S(1)} %get-tuple-element.122.sums, f32[128,128]{1,0:T(8,128)S(1)} %collective-permute-done.30.other, f32[128,1216]{1,0:T(8,128)S(1)} %copy-done.1, f32[128,1216]{1,0:T(8,128)S(1)} %copy-done.3, f32[128,128]{1,0:T(8,128)S(1)} %copy-done.4), custom_call_target="tpu_custom_call" | custom-call | flops 516096 | bytes 2064384 | tf_op jit(solution)/shard_map/pallas_call | solution.py:521
  (71 shorter events, 0.3 us)
Async XLA Ops:
  0.0 9.3 %copy-start = (bf16[640,608]{0,1:T(8,128)(2,1)S(1)}, bf16[640,608]{0,1:T(8,128)(2,1)}, u32[]{:S(2)}) copy-start(bf16[640,608]{0,1:T(8,128)(2,1)} %param.17) | copy-start | bytes 2334724
  3.6 12.5 %collective-permute-start.3 = (bf16[64,2560]{1,0:T(8,128)(2,1)}, bf16[64,2560]{1,0:T(8,128)(2,1)S(1)}, u32[]{:S(2)}, u32[]{:S(2)}) collective-permute-start(bf16[64,2560]{1,0:T(8,128)(2,1)} %get-tuple-element.67), channel_id=1, source_target_pairs={{2,0},{6,2},{4,6},{0,4},{3,1},{7,3},{5,7},{1,5},{10,8},{14,10},{12... | collective-permute-start | bytes 983048 | tf_op jit(solution)/shard_map/ppermute | solution.py:576
  7.6 17.2 %collective-permute-start.2 = (bf16[64,2560]{1,0:T(8,128)(2,1)}, bf16[64,2560]{1,0:T(8,128)(2,1)S(1)}, u32[]{:S(2)}, u32[]{:S(2)}) collective-permute-start(bf16[64,2560]{1,0:T(8,128)(2,1)} %get-tuple-element.67), channel_id=1, source_target_pairs={{0,2},{2,6},{6,4},{4,0},{1,3},{3,7},{7,5},{5,1},{8,10},{10,14},{14... | collective-permute-start | bytes 983048 | tf_op jit(solution)/shard_map/ppermute | solution.py:570
  9.6 22.8 %copy-start.7 = (bf16[608,384]{1,0:T(8,128)(2,1)}, bf16[608,384]{1,0:T(8,128)(2,1)S(1)}, u32[]{:S(2)}) copy-start(bf16[608,384]{1,0:T(8,128)(2,1)S(1)} %pad_maximum_fusion.1.refs_13_.refs_15_) | copy-start | bytes 1400836
  9.7 16.5 %collective-permute-start.1 = (bf16[608,384]{1,0:T(8,128)(2,1)S(1)}, bf16[608,384]{1,0:T(8,128)(2,1)S(1)}, u32[]{:S(2)}, u32[]{:S(2)}) collective-permute-start(bf16[608,384]{1,0:T(8,128)(2,1)S(1)} %pad_maximum_fusion.1.refs_13_.refs_15_), channel_id=1, source_target_pairs={{0,8},{1,17},{8,0},{9,25},{16,24},{17,1},{24,16},{25,9},{2,10},{3,... | collective-permute-start | bytes 1400840 | tf_op jit(solution)/shard_map/ppermute | solution.py:597
  12.1 16.9 %collective-permute-start = (bf16[608,384]{1,0:T(8,128)(2,1)}, bf16[608,384]{1,0:T(8,128)(2,1)}, u32[]{:S(2)}, u32[]{:S(2)}) collective-permute-start(bf16[608,384]{1,0:T(8,128)(2,1)} %pad_maximum_fusion.refs_9_), channel_id=1, source_target_pairs={{0,8},{1,17},{8,0},{9,25},{16,24},{17,1},{24,16},{25,9},{2,10},{3,... | collective-permute-start | bytes 1400840 | tf_op jit(solution)/shard_map/ppermute | solution.py:597
  12.7 24.4 %collective-permute-start.11 = (bf16[608,384]{1,0:T(8,128)(2,1)S(1)}, bf16[608,384]{1,0:T(8,128)(2,1)S(1)}, u32[]{:S(2)}, u32[]{:S(2)}) collective-permute-start(bf16[608,384]{1,0:T(8,128)(2,1)S(1)} %pad_maximum_fusion.1.refs_13_.refs_15_), channel_id=1, source_target_pairs={{0,16},{1,9},{8,24},{9,1},{16,0},{17,25},{24,8},{25,17},{2,18},{3,... | collective-permute-start | bytes 1400840 | tf_op jit(solution)/shard_map/ppermute | solution.py:598
  16.1 13.0 %copy-start.8 = (bf16[64,2560]{1,0:T(8,128)(2,1)}, bf16[64,2560]{1,0:T(8,128)(2,1)S(1)}, u32[]{:S(2)}) copy-start(bf16[64,2560]{1,0:T(8,128)(2,1)S(1)} %collective-permute-done.3.following.refs_3_) | copy-start | bytes 983044
  16.1 13.0 %collective-permute-start.4 = (bf16[32,2560]{1,0:T(8,128)(2,1)S(1)}, bf16[32,2560]{1,0:T(8,128)(2,1)S(1)}, u32[]{:S(2)}, u32[]{:S(2)}) collective-permute-start(bf16[32,2560]{1,0:T(8,128)(2,1)S(1)} %slice.8), channel_id=1, source_target_pairs={{2,0},{6,2},{4,6},{0,4},{3,1},{7,3},{5,7},{1,5},{10,8},{14,10},{12... | collective-permute-start | bytes 491528 | tf_op jit(solution)/shard_map/ppermute | solution.py:576
  24.8 4.3 %copy-start.10 = (bf16[64,2560]{1,0:T(8,128)(2,1)}, bf16[64,2560]{1,0:T(8,128)(2,1)S(1)}, u32[]{:S(2)}) copy-start(bf16[64,2560]{1,0:T(8,128)(2,1)S(1)} %collective-permute-done.2.previous.refs_1_) | copy-start | bytes 983044
  25.5 7.1 %collective-permute-start.7 = (bf16[32,2560]{1,0:T(8,128)(2,1)}, bf16[32,2560]{1,0:T(8,128)(2,1)S(1)}, u32[]{:S(2)}, u32[]{:S(2)}) collective-permute-start(bf16[32,2560]{1,0:T(8,128)(2,1)} %slice.9), channel_id=1, source_target_pairs={{0,2},{2,6},{6,4},{4,0},{1,3},{3,7},{7,5},{5,1},{8,10},{10,14},{14... | collective-permute-start | bytes 491528 | tf_op jit(solution)/shard_map/ppermute | solution.py:570
  26.2 21.2 %copy-start.12 = (bf16[608,384]{1,0:T(8,128)(2,1)}, bf16[608,384]{1,0:T(8,128)(2,1)S(1)}, u32[]{:S(2)}) copy-start(bf16[608,384]{1,0:T(8,128)(2,1)S(1)} %collective-permute-done.1.refs_14_.refs_16_) | copy-start | bytes 1400836
  26.2 21.2 %collective-permute-start.10 = (bf16[608,384]{1,0:T(8,128)(2,1)}, bf16[608,384]{1,0:T(8,128)(2,1)}, u32[]{:S(2)}, u32[]{:S(2)}) collective-permute-start(bf16[608,384]{1,0:T(8,128)(2,1)} %pad_maximum_fusion.refs_9_), channel_id=1, source_target_pairs={{0,16},{1,9},{8,24},{9,1},{16,0},{17,25},{24,8},{25,17},{2,18},{3,... | collective-permute-start | bytes 1400840 | tf_op jit(solution)/shard_map/ppermute | solution.py:598
  29.1 0.7 copy-start.14
  32.5 14.9 %copy-start.15 = (bf16[32,2560]{1,0:T(8,128)(2,1)S(1)}, bf16[32,2560]{1,0:T(8,128)(2,1)}, u32[]{:S(2)}) copy-start(bf16[32,2560]{1,0:T(8,128)(2,1)} %copy-done.14) | copy-start | bytes 491524
  32.5 19.1 %copy-start.11 = (bf16[64,2560]{1,0:T(8,128)(2,1)S(1)}, bf16[64,2560]{1,0:T(8,128)(2,1)}, u32[]{:S(2)}) copy-start(bf16[64,2560]{1,0:T(8,128)(2,1)} %copy-done.10) | copy-start | bytes 983044
  32.5 19.6 %copy-start.9 = (bf16[64,2560]{1,0:T(8,128)(2,1)S(1)}, bf16[64,2560]{1,0:T(8,128)(2,1)}, u32[]{:S(2)}) copy-start(bf16[64,2560]{1,0:T(8,128)(2,1)} %copy-done.8) | copy-start | bytes 983044
  32.7 22.2 %copy-start.23 = (bf16[32,2560]{1,0:T(8,128)(2,1)}, bf16[32,2560]{1,0:T(8,128)(2,1)S(1)}, u32[]{:S(2)}) copy-start(bf16[32,2560]{1,0:T(8,128)(2,1)S(1)} %collective-permute-done.7.refs_5_) | copy-start | bytes 491524
  32.7 11.0 %collective-permute-start.15 = (bf16[64,2560]{1,0:T(8,128)(2,1)}, bf16[64,2560]{1,0:T(8,128)(2,1)S(1)}, u32[]{:S(2)}, u32[]{:S(2)}) collective-permute-start(bf16[64,2560]{1,0:T(8,128)(2,1)} %get-tuple-element.78), channel_id=1, source_target_pairs={{2,0},{6,2},{4,6},{0,4},{3,1},{7,3},{5,7},{1,5},{10,8},{14,10},{12... | collective-permute-start | bytes 983048 | tf_op jit(solution)/shard_map/ppermute | solution.py:576
  35.1 16.4 %collective-permute-start.12 = (bf16[608,384]{1,0:T(8,128)(2,1)}, bf16[608,384]{1,0:T(8,128)(2,1)}, u32[]{:S(2)}, u32[]{:S(2)}) collective-permute-start(bf16[608,384]{1,0:T(8,128)(2,1)} %collective-permute-done.refs_10_), channel_id=1, source_target_pairs={{0,16},{1,9},{8,24},{9,1},{16,0},{17,25},{24,8},{25,17},{2,18},{3,... | collective-permute-start | bytes 1400840 | tf_op jit(solution)/shard_map/ppermute | solution.py:633
  36.6 14.9 %collective-permute-start.13 = (bf16[608,384]{1,0:T(8,128)(2,1)S(1)}, bf16[608,384]{1,0:T(8,128)(2,1)}, u32[]{:S(2)}, u32[]{:S(2)}) collective-permute-start(bf16[608,384]{1,0:T(8,128)(2,1)S(1)} %collective-permute-done.1.refs_14_.refs_16_), channel_id=1, source_target_pairs={{0,16},{1,9},{8,24},{9,1},{16,0},{17,25},{24,8},{25,17},{2,18},{3,... | collective-permute-start | bytes 1400840 | tf_op jit(solution)/shard_map/ppermute | solution.py:633
  37.1 17.8 %copy-start.13 = (bf16[608,384]{1,0:T(8,128)(2,1)}, bf16[608,384]{1,0:T(8,128)(2,1)S(1)}, u32[]{:S(2)}) copy-start(bf16[608,384]{1,0:T(8,128)(2,1)S(1)} %collective-permute-done.11.refs_15_.refs_17_) | copy-start | bytes 1400836
  37.1 14.3 %collective-permute-start.9 = (bf16[64,2560]{1,0:T(8,128)(2,1)}, bf16[64,2560]{1,0:T(8,128)(2,1)S(1)}, u32[]{:S(2)}, u32[]{:S(2)}) collective-permute-start(bf16[64,2560]{1,0:T(8,128)(2,1)} %get-tuple-element.78), channel_id=1, source_target_pairs={{0,2},{2,6},{6,4},{4,0},{1,3},{3,7},{7,5},{5,1},{8,10},{10,14},{14... | collective-permute-start | bytes 983048 | tf_op jit(solution)/shard_map/ppermute | solution.py:570
  43.6 19.1 %copy-start.16 = (bf16[64,2560]{1,0:T(8,128)(2,1)}, bf16[64,2560]{1,0:T(8,128)(2,1)S(1)}, u32[]{:S(2)}) copy-start(bf16[64,2560]{1,0:T(8,128)(2,1)S(1)} %collective-permute-done.15.refs_11_) | copy-start | bytes 983044
  43.6 8.7 %collective-permute-start.16 = (bf16[64,2560]{1,0:T(8,128)(2,1)S(1)}, bf16[64,2560]{1,0:T(8,128)(2,1)S(1)}, u32[]{:S(2)}, u32[]{:S(2)}) collective-permute-start(bf16[64,2560]{1,0:T(8,128)(2,1)S(1)} %collective-permute-done.15.refs_11_), channel_id=1, source_target_pairs={{0,1},{1,0},{2,3},{3,2},{4,5},{5,4},{6,7},{7,6},{8,9},{9,8},{10,11... | collective-permute-start | bytes 983048 | tf_op jit(solution)/shard_map/ppermute | solution.py:573
  47.4 4.7 %collective-permute-start.17 = (bf16[32,2560]{1,0:T(8,128)(2,1)S(1)}, bf16[32,2560]{1,0:T(8,128)(2,1)S(1)}, u32[]{:S(2)}, u32[]{:S(2)}) collective-permute-start(bf16[32,2560]{1,0:T(8,128)(2,1)S(1)} %copy-done.15), channel_id=1, source_target_pairs={{0,1},{1,0},{2,3},{3,2},{4,5},{5,4},{6,7},{7,6},{8,9},{9,8},{10,11... | collective-permute-start | bytes 491528 | tf_op jit(solution)/shard_map/ppermute | solution.py:573
  51.5 11.3 %copy-start.17 = (bf16[64,2560]{1,0:T(8,128)(2,1)}, bf16[64,2560]{1,0:T(8,128)(2,1)S(1)}, u32[]{:S(2)}) copy-start(bf16[64,2560]{1,0:T(8,128)(2,1)S(1)} %collective-permute-done.9.refs_9_) | copy-start | bytes 983044
  51.5 1.7 %collective-permute-start.14 = (bf16[64,2560]{1,0:T(8,128)(2,1)S(1)}, bf16[64,2560]{1,0:T(8,128)(2,1)S(1)}, u32[]{:S(2)}, u32[]{:S(2)}) collective-permute-start(bf16[64,2560]{1,0:T(8,128)(2,1)S(1)} %collective-permute-done.9.refs_9_), channel_id=1, source_target_pairs={{0,1},{1,0},{2,3},{3,2},{4,5},{5,4},{6,7},{7,6},{8,9},{9,8},{10,11... | collective-permute-start | bytes 983048 | tf_op jit(solution)/shard_map/ppermute | solution.py:573
  51.6 2.5 %collective-permute-start.5 = (bf16[64,2560]{1,0:T(8,128)(2,1)S(1)}, bf16[64,2560]{1,0:T(8,128)(2,1)S(1)}, u32[]{:S(2)}, u32[]{:S(2)}) collective-permute-start(bf16[64,2560]{1,0:T(8,128)(2,1)S(1)} %copy-done.11), channel_id=1, source_target_pairs={{0,1},{1,0},{2,3},{3,2},{4,5},{5,4},{6,7},{7,6},{8,9},{9,8},{10,11... | collective-permute-start | bytes 983048 | tf_op jit(solution)/shard_map/ppermute | solution.py:573
  52.1 2.8 %collective-permute-start.6 = (bf16[64,2560]{1,0:T(8,128)(2,1)S(1)}, bf16[64,2560]{1,0:T(8,128)(2,1)}, u32[]{:S(2)}, u32[]{:S(2)}) collective-permute-start(bf16[64,2560]{1,0:T(8,128)(2,1)S(1)} %copy-done.9), channel_id=1, source_target_pairs={{0,1},{1,0},{2,3},{3,2},{4,5},{5,4},{6,7},{7,6},{8,9},{9,8},{10,11... | collective-permute-start | bytes 983048 | tf_op jit(solution)/shard_map/ppermute | solution.py:573
  52.1 2.0 %copy-start.24 = (bf16[32,2560]{1,0:T(8,128)(2,1)}, bf16[32,2560]{1,0:T(8,128)(2,1)S(1)}, u32[]{:S(2)}) copy-start(bf16[32,2560]{1,0:T(8,128)(2,1)S(1)} %collective-permute-done.17.refs_8_) | copy-start | bytes 491524
  52.1 10.9 %collective-permute-start.18 = (bf16[64,2560]{1,0:T(8,128)(2,1)S(1)}, bf16[64,2560]{1,0:T(8,128)(2,1)S(1)}, u32[]{:S(2)}, u32[]{:S(2)}) collective-permute-start(bf16[64,2560]{1,0:T(8,128)(2,1)S(1)} %collective-permute-done.9.refs_9_), channel_id=1, source_target_pairs={{0,2},{2,6},{6,4},{4,0},{1,3},{3,7},{7,5},{5,1},{8,10},{10,14},{14... | collective-permute-start | bytes 983048 | tf_op jit(solution)/shard_map/ppermute | solution.py:570
  52.3 10.4 %copy-start.18 = (bf16[64,2560]{1,0:T(8,128)(2,1)}, bf16[64,2560]{1,0:T(8,128)(2,1)S(1)}, u32[]{:S(2)}) copy-start(bf16[64,2560]{1,0:T(8,128)(2,1)S(1)} %collective-permute-done.16.refs_12_) | copy-start | bytes 983044
  52.3 1.8 %collective-permute-start.8 = (bf16[32,2560]{1,0:T(8,128)(2,1)S(1)}, bf16[32,2560]{1,0:T(8,128)(2,1)S(1)}, u32[]{:S(2)}, u32[]{:S(2)}) collective-permute-start(bf16[32,2560]{1,0:T(8,128)(2,1)S(1)} %collective-permute-done.7.refs_5_), channel_id=1, source_target_pairs={{0,1},{1,0},{2,3},{3,2},{4,5},{5,4},{6,7},{7,6},{8,9},{9,8},{10,11... | collective-permute-start | bytes 491528 | tf_op jit(solution)/shard_map/ppermute | solution.py:573
  53.2 9.6 %copy-start.19 = (bf16[64,2560]{1,0:T(8,128)(2,1)}, bf16[64,2560]{1,0:T(8,128)(2,1)S(1)}, u32[]{:S(2)}) copy-start(bf16[64,2560]{1,0:T(8,128)(2,1)S(1)} %collective-permute-done.14.refs_10_) | copy-start | bytes 983044
  54.1 0.8 copy-start.25
  54.1 0.8 copy-start.21
  63.1 1.8 %copy-start.20 = (bf16[64,2560]{1,0:T(8,128)(2,1)}, bf16[64,2560]{1,0:T(8,128)(2,1)S(1)}, u32[]{:S(2)}) copy-start(bf16[64,2560]{1,0:T(8,128)(2,1)S(1)} %collective-permute-done.18.refs_13_) | copy-start | bytes 983044
  63.1 1.6 %collective-permute-start.19 = (bf16[64,2560]{1,0:T(8,128)(2,1)S(1)}, bf16[64,2560]{1,0:T(8,128)(2,1)S(1)}, u32[]{:S(2)}, u32[]{:S(2)}) collective-permute-start(bf16[64,2560]{1,0:T(8,128)(2,1)S(1)} %collective-permute-done.18.refs_13_), channel_id=1, source_target_pairs={{0,1},{1,0},{2,3},{3,2},{4,5},{5,4},{6,7},{7,6},{8,9},{9,8},{10,11... | collective-permute-start | bytes 983048 | tf_op jit(solution)/shard_map/ppermute | solution.py:573
  64.7 0.7 copy-start.22
  64.7 17.3 %collective-permute-start.23 = (bf16[1216,640]{1,0:T(8,128)(2,1)}, bf16[1216,640]{1,0:T(8,128)(2,1)}, u32[]{:S(2)}, u32[]{:S(2)}) collective-permute-start(bf16[1216,640]{1,0:T(8,128)(2,1)} %get-tuple-element.112.refs_7_), channel_id=1, source_target_pairs={{0,1},{1,0},{2,3},{3,2},{4,5},{5,4},{6,7},{7,6},{8,9},{9,8},{10,11... | collective-permute-start | bytes 4669448 | tf_op jit(solution)/shard_map/ppermute | solution.py:573
  65.4 16.6 %copy-start.2 = (bf16[1216,640]{1,0:T(8,128)(2,1)S(1)}, bf16[1216,640]{1,0:T(8,128)(2,1)}, u32[]{:S(2)}) copy-start(bf16[1216,640]{1,0:T(8,128)(2,1)} %get-tuple-element.89.refs_6_.w_own) | copy-start | bytes 4669444
  76.2 1.7 %collective-permute-start.22 = (bf16[64,1216]{1,0:T(8,128)(2,1)}, bf16[64,1216]{1,0:T(8,128)(2,1)S(1)}, u32[]{:S(2)}, u32[]{:S(2)}) collective-permute-start(bf16[64,1216]{1,0:T(8,128)(2,1)} %get-tuple-element.109), channel_id=1, source_target_pairs={{0,1},{1,0},{2,3},{3,2},{4,5},{5,4},{6,7},{7,6},{8,9},{9,8},{10,11... | collective-permute-start | bytes 466952 | tf_op jit(solution)/shard_map/ppermute | solution.py:573
  76.4 3.8 %collective-permute-start.21 = (bf16[64,1216]{1,0:T(8,128)(2,1)}, bf16[64,1216]{1,0:T(8,128)(2,1)S(1)}, u32[]{:S(2)}, u32[]{:S(2)}) collective-permute-start(bf16[64,1216]{1,0:T(8,128)(2,1)} %get-tuple-element.107), channel_id=1, source_target_pairs={{0,1},{1,0},{2,3},{3,2},{4,5},{5,4},{6,7},{7,6},{8,9},{9,8},{10,11... | collective-permute-start | bytes 466952 | tf_op jit(solution)/shard_map/ppermute | solution.py:573
  76.8 5.2 %collective-permute-start.20 = (bf16[384,640]{1,0:T(8,128)(2,1)}, bf16[384,640]{1,0:T(8,128)(2,1)S(1)}, u32[]{:S(2)}, u32[]{:S(2)}) collective-permute-start(bf16[384,640]{1,0:T(8,128)(2,1)} %get-tuple-element.110.own), channel_id=1, source_target_pairs={{0,1},{1,0},{2,3},{3,2},{4,5},{5,4},{6,7},{7,6},{8,9},{9,8},{10,11... | collective-permute-start | bytes 1474568 | tf_op jit(solution)/shard_map/ppermute | solution.py:573
  78.9 8.0 %collective-permute-start.27 = (bf16[64,1216]{1,0:T(8,128)(2,1)S(1)}, bf16[64,1216]{1,0:T(8,128)(2,1)S(1)}, u32[]{:S(2)}, u32[]{:S(2)}) collective-permute-start(bf16[64,1216]{1,0:T(8,128)(2,1)S(1)} %add_convert_fusion.4), channel_id=1, source_target_pairs={{0,2},{2,6},{6,4},{4,0},{1,3},{3,7},{7,5},{5,1},{8,10},{10,14},{14... | collective-permute-start | bytes 466952 | tf_op jit(solution)/shard_map/ppermute | solution.py:570
  81.2 8.5 %collective-permute-start.24 = (bf16[64,1216]{1,0:T(8,128)(2,1)S(1)}, bf16[64,1216]{1,0:T(8,128)(2,1)S(1)}, u32[]{:S(2)}, u32[]{:S(2)}) collective-permute-start(bf16[64,1216]{1,0:T(8,128)(2,1)S(1)} %add_convert_fusion.5), channel_id=1, source_target_pairs={{0,2},{2,6},{6,4},{4,0},{1,3},{3,7},{7,5},{5,1},{8,10},{10,14},{14... | collective-permute-start | bytes 466952 | tf_op jit(solution)/shard_map/ppermute | solution.py:570
  82.0 1.0 copy-start.6
  86.1 18.1 %copy-start.1 = (f32[128,1216]{1,0:T(8,128)S(1)}, f32[128,1216]{1,0:T(8,128)}, u32[]{:S(2)}) copy-start(f32[128,1216]{1,0:T(8,128)} %get-tuple-element.120.normed) | copy-start | bytes 1867780
  86.2 18.1 %copy-start.5 = (f32[1,1216]{1,0:T(1,128)S(1)}, f32[1,1216]{1,0:T(1,128)}, u32[]{:S(2)}) copy-start(f32[1,1216]{1,0:T(1,128)} %get-tuple-element.119.scale) | copy-start | bytes 14596
  86.9 6.9 %collective-permute-start.28 = (bf16[64,1216]{1,0:T(8,128)(2,1)S(1)}, bf16[64,1216]{1,0:T(8,128)(2,1)S(1)}, u32[]{:S(2)}, u32[]{:S(2)}) collective-permute-start(bf16[64,1216]{1,0:T(8,128)(2,1)S(1)} %add_convert_fusion.1), channel_id=1, source_target_pairs={{0,2},{2,6},{6,4},{4,0},{1,3},{3,7},{7,5},{5,1},{8,10},{10,14},{14... | collective-permute-start | bytes 466952 | tf_op jit(solution)/shard_map/ppermute | solution.py:570
  89.8 16.0 %copy-start.3 = (f32[128,1216]{1,0:T(8,128)S(1)}, f32[128,1216]{1,0:T(8,128)}, u32[]{:S(2)}) copy-start(f32[128,1216]{1,0:T(8,128)} %get-tuple-element.123.base) | copy-start | bytes 1867780
  89.8 16.0 %copy-start.4 = (f32[128,128]{1,0:T(8,128)S(1)}, f32[128,128]{1,0:T(8,128)}, u32[]{:S(2)}) copy-start(f32[128,128]{1,0:T(8,128)} %get-tuple-element.124.inv_std) | copy-start | bytes 196612
  89.8 8.1 %collective-permute-start.25 = (bf16[64,1216]{1,0:T(8,128)(2,1)S(1)}, bf16[64,1216]{1,0:T(8,128)(2,1)S(1)}, u32[]{:S(2)}, u32[]{:S(2)}) collective-permute-start(bf16[64,1216]{1,0:T(8,128)(2,1)S(1)} %add_convert_fusion.3), channel_id=1, source_target_pairs={{0,2},{2,6},{6,4},{4,0},{1,3},{3,7},{7,5},{5,1},{8,10},{10,14},{14... | collective-permute-start | bytes 466952 | tf_op jit(solution)/shard_map/ppermute | solution.py:570
  93.9 7.4 %collective-permute-start.29 = (bf16[64,1216]{1,0:T(8,128)(2,1)S(1)}, bf16[64,1216]{1,0:T(8,128)(2,1)S(1)}, u32[]{:S(2)}, u32[]{:S(2)}) collective-permute-start(bf16[64,1216]{1,0:T(8,128)(2,1)S(1)} %add_convert_fusion), channel_id=1, source_target_pairs={{0,2},{2,6},{6,4},{4,0},{1,3},{3,7},{7,5},{5,1},{8,10},{10,14},{14... | collective-permute-start | bytes 466952 | tf_op jit(solution)/shard_map/ppermute | solution.py:570
  97.9 6.3 %collective-permute-start.26 = (bf16[64,1216]{1,0:T(8,128)(2,1)S(1)}, bf16[64,1216]{1,0:T(8,128)(2,1)S(1)}, u32[]{:S(2)}, u32[]{:S(2)}) collective-permute-start(bf16[64,1216]{1,0:T(8,128)(2,1)S(1)} %add_convert_fusion.2), channel_id=1, source_target_pairs={{0,2},{2,6},{6,4},{4,0},{1,3},{3,7},{7,5},{5,1},{8,10},{10,14},{14... | collective-permute-start | bytes 466952 | tf_op jit(solution)/shard_map/ppermute | solution.py:570
  104.5 1.3 %collective-permute-start.30 = (f32[128,128]{1,0:T(8,128)S(1)}, f32[128,128]{1,0:T(8,128)S(1)}, u32[]{:S(2)}, u32[]{:S(2)}) collective-permute-start(f32[128,128]{1,0:T(8,128)S(1)} %get-tuple-element.122.sums), channel_id=1, source_target_pairs={{0,1},{1,0},{2,3},{3,2},{4,5},{5,4},{6,7},{7,6},{8,9},{9,8},{10,11... | collective-permute-start | bytes 196616 | tf_op jit(solution)/shard_map/ppermute | solution.py:573

commit v5 on v4

--- a/solution.py
+++ b/solution.py
@@ -82,7 +82,7 @@
 
 
 def first_kernel(step, core, states, table, adjoint, text, out, rows_out, extra_out):
-    rows = [table[c, pl.ds(step[0], 1), :] for c in range(3)]
+    rows = [table[c, pl.ds(step[0] % 8, 1), :] for c in range(3)]
     widened = states[...].astype(jnp.float32)
     centered = widened - jnp.mean(widened, axis=-1, keepdims=True)
     inv_std = lax.rsqrt(jnp.mean(centered * centered, axis=-1, keepdims=True) + 1e-06)
@@ -119,7 +119,7 @@
             grid=(1,),
             in_specs=[
                 pl.BlockSpec((half, width), lambda i, step, core: (core[0], 0)),
-                whole(*table.shape),
+                pl.BlockSpec((3, 8, width), lambda i, step, core: (0, step[0] // 8, 0)),
                 whole(*adjoint.shape),
                 whole(*text.shape),
             ],
@@ -340,7 +340,8 @@
     d_first = d_all.shape[1] - inner
     for i in range(slots):
         columns = [slice(n * inner + i * HD, n * inner + (i + 1) * HD) for n in range(3)]
-        keys, values = qkv[:, columns[1]], qkv[:, columns[2]]
+        keys = jnp.concatenate([qkv[:, columns[1]], text[i]], axis=0)
+        values = jnp.concatenate([qkv[:, columns[2]], values_text[i]], axis=0)
         keys_t = k_t[i * HD : (i + 1) * HD, :]
         grad_k, grad_v = 0.0, 0.0
         for b in range(count // 2):
@@ -348,7 +349,8 @@
             query = qkv[here, columns[0]]
             grad = d_all[here, d_first + i * HD : d_first + (i + 1) * HD]
             scores = dot(keys, query, NT)
-            text_scores = dot(text[i], query, NT) + bias
+            text_scores = scores[tokens:] + bias
+            scores = scores[:tokens]
             col_max = jnp.maximum(
                 jnp.max(scores, axis=0, keepdims=True), jnp.max(text_scores, axis=0, keepdims=True)
             )
@@ -357,7 +359,8 @@
             total = jnp.sum(exps, axis=0, keepdims=True) + jnp.sum(text_exps, axis=0, keepdims=True)
             inverse = 1.0 / total
             grad_w = dot(values, grad, NT)
-            text_grad_w = dot(values_text[i], grad, NT)
+            text_grad_w = grad_w[tokens:]
+            grad_w = grad_w[:tokens]
             delta = inverse * (
                 jnp.sum(exps * grad_w, axis=0, keepdims=True)
                 + jnp.sum(text_exps * text_grad_w, axis=0, keepdims=True)

time: 107 us -> 107 us (level)
  no operation moved by 1% of the time
where the time goes in v5:
time: 107 us
  waiting for transfers between devices  35.7 us (33%)
  Pallas kernels  32.1 us (30%)
  starting transfers between devices  27.5 us (26%)
  local copies, waits for them, and re-layouts  6.35 us (6%)
  other arithmetic  3.24 us (3%)
  between operations  1.71 us (2%)
    ppermute x10, waiting for transfers between devices, step(): return lax.ppermute(moving, 'seq', seq_next)  22 us
    pallas_call x1, Pallas kernels, attend_call(): pl.pallas_call(functools.partial(attend_kernel, slots, count, rows, shard...  10.5 us
    ppermute x3, starting transfers between devices, step_back(): return lax.ppermute(moving, 'seq', [(b, a) for a, b in seq_next])  9.8 us
    ppermute x3, waiting for transfers between devices, step_back(): return lax.ppermute(moving, 'seq', [(b, a) for a, b in seq_next])  8.36 us
    ppermute x10, starting transfers between devices, step(): return lax.ppermute(moving, 'seq', seq_next)  8.17 us
    pallas_call x1, Pallas kernels, project_call(): pl.pallas_call(functools.partial(project_kernel, slots, count, rows, shar...  7.82 us
    ppermute x12, waiting for transfers between devices, other_core(): return lax.ppermute(moving, 'head', swap)  5.24 us
    pallas_call x3, Pallas kernels, local_call(): pl.pallas_call(kernel, out_shape=tuple((jax.ShapeDtypeStruct(*one) for on...  5.21 us
  transfers between devices with their start and end apart: 31, of which 17 were waited for; matrix products, arithmetic and copies ran while one was open for 6% of the time, Pallas kernels for 26%

profile of v5, /device:TPU:0, one launch (start us, length us, event | category | flops | bytes accessed | tf_op | source)
XLA Modules:
  0.0 106.6 jit_solution(7999892499059537032)
XLA Ops:
  0.7 2.7 %shard_map.91 = (bf16[64,2560]{1,0:T(8,128)(2,1)}, f32[8,2432]{1,0:T(8,128)}, bf16[64,128]{1,0:T(8,128)(2,1)}) custom-call(s32[1]{0:T(128)S(6)} %copy.11.step, s32[1]{0:T(128)} %bitcast.core, bf16[128,2432]{1,0:T(8,128)(2,1)} %bitcast.31, f32[3,28,2432]{2,1,0:T(8,128)} %bitcast.33, f32[128,2432]{1,0:T(8,128)} %bitcast.28, bf16[8,2,640]{2,1,0:T(2,128)(2,1)} %bitcast.34), custom_call_target="tpu_custom_call" | custom-call | flops 1245184 | bytes 2490368 | tf_op jit(solution)/shard_map/pallas_call | solution.py:110
  3.4 4.0 %collective-permute-start.3 = (bf16[64,2560]{1,0:T(8,128)(2,1)}, bf16[64,2560]{1,0:T(8,128)(2,1)S(1)}, u32[]{:S(2)}, u32[]{:S(2)}) collective-permute-start(bf16[64,2560]{1,0:T(8,128)(2,1)} %get-tuple-element.67), channel_id=1, source_target_pairs={{2,0},{6,2},{4,6},{0,4},{3,1},{7,3},{5,7},{1,5},{10,8},{14,10},{12... | collective-permute-start | bytes 983048 | tf_op jit(solution)/shard_map/ppermute | solution.py:579
  7.5 1.7 %dynamic-slice_bitcast_fusion.1 = (bf16[608,192]{1,0:T(8,128)(2,1)S(1)}, bf16[608,192]{1,0:T(8,128)(2,1)S(1)}, bf16[608,192]{1,0:T(8,128)(2,1)S(1)}) fusion(bf16[608,3,640]{2,0,1:T(8,128)(2,1)} %param.15, s32[]{:T(128)S(6)} %select_n.103), kind=kLoop, calls=%fused_computation.9 | loop fusion | bytes 1400836 | tf_op jit(solution)/shard_map/squeeze | solution.py:595
  9.2 0.2 dynamic-slice_bitcast_fusion
  9.3 0.2 pad_maximum_fusion.1.refs_13_.refs_15_
  9.5 1.6 %collective-permute-start.1 = (bf16[608,384]{1,0:T(8,128)(2,1)S(1)}, bf16[608,384]{1,0:T(8,128)(2,1)S(1)}, u32[]{:S(2)}, u32[]{:S(2)}) collective-permute-start(bf16[608,384]{1,0:T(8,128)(2,1)S(1)} %pad_maximum_fusion.1.refs_13_.refs_15_), channel_id=1, source_target_pairs={{0,8},{1,17},{8,0},{9,25},{16,24},{17,1},{24,16},{25,9},{2,10},{3,... | collective-permute-start | bytes 1400840 | tf_op jit(solution)/shard_map/ppermute | solution.py:600
  11.1 0.9 pad_maximum_fusion.refs_9_
  12.0 0.5 collective-permute-start
  12.5 1.5 %collective-permute-start.11 = (bf16[608,384]{1,0:T(8,128)(2,1)S(1)}, bf16[608,384]{1,0:T(8,128)(2,1)S(1)}, u32[]{:S(2)}, u32[]{:S(2)}) collective-permute-start(bf16[608,384]{1,0:T(8,128)(2,1)S(1)} %pad_maximum_fusion.1.refs_13_.refs_15_), channel_id=1, source_target_pairs={{0,16},{1,9},{8,24},{9,1},{16,0},{17,25},{24,8},{25,17},{2,18},{3,... | collective-permute-start | bytes 1400840 | tf_op jit(solution)/shard_map/ppermute | solution.py:601
  14.1 1.9 %collective-permute-done.3.following.refs_3_ = bf16[64,2560]{1,0:T(8,128)(2,1)S(1)} collective-permute-done((bf16[64,2560]{1,0:T(8,128)(2,1)}, bf16[64,2560]{1,0:T(8,128)(2,1)S(1)}, u32[]{:S(2)}, u32[]{:S(2)}) %collective-permute-start.3) | collective-permute-done | bytes 327712 | tf_op jit(solution)/shard_map/ppermute | solution.py:579
  15.9 3.3 %collective-permute-start.4 = (bf16[32,2560]{1,0:T(8,128)(2,1)S(1)}, bf16[32,2560]{1,0:T(8,128)(2,1)S(1)}, u32[]{:S(2)}, u32[]{:S(2)}) collective-permute-start(bf16[32,2560]{1,0:T(8,128)(2,1)S(1)} %slice.8), channel_id=1, source_target_pairs={{2,0},{6,2},{4,6},{0,4},{3,1},{7,3},{5,7},{1,5},{10,8},{14,10},{12... | collective-permute-start | bytes 491528 | tf_op jit(solution)/shard_map/ppermute | solution.py:579
  19.3 5.4 %collective-permute-done.2.previous.refs_1_ = bf16[64,2560]{1,0:T(8,128)(2,1)S(1)} collective-permute-done((bf16[64,2560]{1,0:T(8,128)(2,1)}, bf16[64,2560]{1,0:T(8,128)(2,1)S(1)}, u32[]{:S(2)}, u32[]{:S(2)}) %collective-permute-start.2) | collective-permute-done | bytes 327712 | tf_op jit(solution)/shard_map/ppermute | solution.py:573
  24.7 0.7 slice.9
  25.4 0.7 collective-permute-start.7
  26.1 1.5 %collective-permute-start.10 = (bf16[608,384]{1,0:T(8,128)(2,1)}, bf16[608,384]{1,0:T(8,128)(2,1)}, u32[]{:S(2)}, u32[]{:S(2)}) collective-permute-start(bf16[608,384]{1,0:T(8,128)(2,1)} %pad_maximum_fusion.refs_9_), channel_id=1, source_target_pairs={{0,16},{1,9},{8,24},{9,1},{16,0},{17,25},{24,8},{25,17},{2,18},{3,... | collective-permute-start | bytes 1400840 | tf_op jit(solution)/shard_map/ppermute | solution.py:601
  28.2 0.7 stack.67.core.scalars
  29.0 0.6 copy-done.14
  29.6 2.7 %shard_map.92 = (bf16[64,2560]{1,0:T(8,128)(2,1)}, f32[8,128]{1,0:T(8,128)}) custom-call(s32[14]{0:T(128)} %stack.67.core.scalars, f32[128,2432]{1,0:T(8,128)} %bitcast.29, f32[8,2432]{1,0:T(8,128)} %get-tuple-element.65.table_rows, bf16[8,2,640]{2,1,0:T(2,128)(2,1)} %bitcast.35, bf16[64,128]{1,0:T(8,128)(2,1)} %get-tuple-element.70.extra, ...), custom_call_target="tpu_custom_call" | custom-call | flops 622592 | bytes 933888 | tf_op jit(solution)/shard_map/pallas_call | solution.py:162
  32.4 0.1 collective-permute-done.7.refs_5_
  32.5 2.4 %collective-permute-start.15 = (bf16[64,2560]{1,0:T(8,128)(2,1)}, bf16[64,2560]{1,0:T(8,128)(2,1)S(1)}, u32[]{:S(2)}, u32[]{:S(2)}) collective-permute-start(bf16[64,2560]{1,0:T(8,128)(2,1)} %get-tuple-element.78), channel_id=1, source_target_pairs={{2,0},{6,2},{4,6},{0,4},{3,1},{7,3},{5,7},{1,5},{10,8},{14,10},{12... | collective-permute-start | bytes 983048 | tf_op jit(solution)/shard_map/ppermute | solution.py:579
  34.9 1.5 %collective-permute-start.12 = (bf16[608,384]{1,0:T(8,128)(2,1)}, bf16[608,384]{1,0:T(8,128)(2,1)}, u32[]{:S(2)}, u32[]{:S(2)}) collective-permute-start(bf16[608,384]{1,0:T(8,128)(2,1)} %collective-permute-done.refs_10_), channel_id=1, source_target_pairs={{0,16},{1,9},{8,24},{9,1},{16,0},{17,25},{24,8},{25,17},{2,18},{3,... | collective-permute-start | bytes 1400840 | tf_op jit(solution)/shard_map/ppermute | solution.py:636
  36.5 0.5 collective-permute-start.13
  37.0 6.5 %collective-permute-done.15.refs_11_ = bf16[64,2560]{1,0:T(8,128)(2,1)S(1)} collective-permute-done((bf16[64,2560]{1,0:T(8,128)(2,1)}, bf16[64,2560]{1,0:T(8,128)(2,1)S(1)}, u32[]{:S(2)}, u32[]{:S(2)}) %collective-permute-start.15) | collective-permute-done | bytes 327712 | tf_op jit(solution)/shard_map/ppermute | solution.py:579
  43.5 3.8 %shard_map.93 = (bf16[128,2560]{1,0:T(8,128)(2,1)}, bf16[128,2560]{1,0:T(8,128)(2,1)}, f32[128,1216]{1,0:T(8,128)}, f32[1,1216]{1,0:T(1,128)}, f32[128,128]{1,0:T(8,128)}, /*index=5*/f32[128,1216]{1,0:T(8,128)}) custom-call(s32[1]{0:T(128)} %bitcast.core, bf16[128,2432]{1,0:T(8,128)(2,1)} %bitcast.32, f32[128,2432]{1,0:T(8,128)} %bitcast.30, ...), custom_call_target="tpu_custom_call" | custom-call | flops 661505 | bytes 1986564 | tf_op jit(solution)/shard_map/pallas_call | solution.py:524
  47.3 0.5 collective-permute-start.17
  47.8 3.6 %collective-permute-done.9.refs_9_ = bf16[64,2560]{1,0:T(8,128)(2,1)S(1)} collective-permute-done((bf16[64,2560]{1,0:T(8,128)(2,1)}, bf16[64,2560]{1,0:T(8,128)(2,1)S(1)}, u32[]{:S(2)}, u32[]{:S(2)}) %collective-permute-start.9) | collective-permute-done | bytes 327712 | tf_op jit(solution)/shard_map/ppermute | solution.py:573
  51.3 0.1 collective-permute-start.14
  51.4 0.5 collective-permute-start.5
  51.9 0.1 collective-permute-start.6
  52.0 0.2 collective-permute-start.18
  52.2 0.3 collective-permute-start.8
  52.5 0.5 collective-permute-done.14.refs_10_
  53.0 0.9 collective-permute-done.8.refs_6_
  54.0 0.8 copy-done.21
  54.8 7.8 %shard_map.94 = (bf16[512,576]{1,0:T(8,128)(2,1)}, bf16[192,512]{1,0:T(8,128)(2,1)}, f32[512,384]{1,0:T(8,128)}, f32[512,384]{1,0:T(8,128)}, bf16[3,32,64]{2,1,0...) custom-call(s32[14]{0:T(128)} %stack.67.core.scalars, ...), custom_call_target="tpu_custom_call" | custom-call | flops 1434451968 | bytes 6914048 | tf_op jit(solution)/shard_map/pallas_call | solution.py:419
  62.6 0.3 collective-permute-done.18.refs_13_
  63.0 1.6 %collective-permute-done.19.refs_14_ = bf16[64,2560]{1,0:T(8,128)(2,1)S(1)} collective-permute-done((bf16[64,2560]{1,0:T(8,128)(2,1)S(1)}, bf16[64,2560]{1,0:T(8,128)(2,1)S(1)}, u32[]{:S(2)}, u32[]{:S(2)}) %collective-permute-start.19) | collective-permute-done | bytes 327712 | tf_op jit(solution)/shard_map/ppermute | solution.py:576
  64.6 0.1 collective-permute-start.23
  64.7 0.6 copy-done.22
  65.3 10.5 %shard_map.95 = (f32[64,1216]{1,0:T(8,128)}, f32[64,1216]{1,0:T(8,128)}, bf16[64,1216]{1,0:T(8,128)(2,1)}, bf16[64,1216]{1,0:T(8,128)(2,1)}, bf16[384,640]{1,0:T(8,128)(2,1)}) custom-call(s32[14]{0:T(128)} %stack.67.core.scalars, f32[2,64]{1,0:T(2,128)} %gain.3, bf16[512,576]{1,0:T(8,128)(2,1)} %get-tuple-element.83.refs_0_, ...), custom_call_target="tpu_custom_call" | custom-call | flops 981467136 | bytes 4358144 | tf_op jit(solution)/shard_map/pallas_call | solution.py:452
  75.8 0.2 collective-permute-start.22
  76.0 0.4 collective-permute-start.21
  76.4 0.1 collective-permute-start.20
  76.5 1.0 collective-permute-done.22
  77.5 1.0 add_convert_fusion.4
  78.5 1.3 %collective-permute-start.27 = (bf16[64,1216]{1,0:T(8,128)(2,1)S(1)}, bf16[64,1216]{1,0:T(8,128)(2,1)S(1)}, u32[]{:S(2)}, u32[]{:S(2)}) collective-permute-start(bf16[64,1216]{1,0:T(8,128)(2,1)S(1)} %add_convert_fusion.4), channel_id=1, source_target_pairs={{0,2},{2,6},{6,4},{4,0},{1,3},{3,7},{7,5},{5,1},{8,10},{10,14},{14... | collective-permute-start | bytes 466952 | tf_op jit(solution)/shard_map/ppermute | solution.py:573
  79.8 1.0 add_convert_fusion.5
  80.8 0.8 collective-permute-start.24
  81.6 1.0 copy-done.6
  82.6 3.1 %shard_map.96 = (f32[64,1216]{1,0:T(8,128)S(1)}, f32[64,1216]{1,0:T(8,128)S(1)}, f32[64,1216]{1,0:T(8,128)S(1)}, f32[64,1216]{1,0:T(8,128)S(1)}, f32[64,1216]{1,0:T(8,128)S(1)}, /*index=5*/f32[64,1216]{1,0:T(8,128)S(1)}) custom-call(bf16[384,640]{1,0:T(8,128)(2,1)S(1)} %copy-done.6, bf16[384,640]{1,0:T(8,128)(2,1)S(1)} %collective-permute-done.20.other, ...), custom_call_target="tpu_custom_call" | custom-call | flops 1195376640 | bytes 5963776 | tf_op jit(solution)/shard_map/pallas_call | solution.py:488
  85.8 0.7 collective-permute-done.27
  86.5 1.7 %collective-permute-start.28 = (bf16[64,1216]{1,0:T(8,128)(2,1)S(1)}, bf16[64,1216]{1,0:T(8,128)(2,1)S(1)}, u32[]{:S(2)}, u32[]{:S(2)}) collective-permute-start(bf16[64,1216]{1,0:T(8,128)(2,1)S(1)} %add_convert_fusion.1), channel_id=1, source_target_pairs={{0,2},{2,6},{6,4},{4,0},{1,3},{3,7},{7,5},{5,1},{8,10},{10,14},{14... | collective-permute-start | bytes 466952 | tf_op jit(solution)/shard_map/ppermute | solution.py:573
  88.2 1.2 %collective-permute-done.24 = bf16[64,1216]{1,0:T(8,128)(2,1)S(1)} collective-permute-done((bf16[64,1216]{1,0:T(8,128)(2,1)S(1)}, bf16[64,1216]{1,0:T(8,128)(2,1)S(1)}, u32[]{:S(2)}, u32[]{:S(2)}) %collective-permute-start.24) | collective-permute-done | bytes 155680 | tf_op jit(solution)/shard_map/ppermute | solution.py:573
  89.4 0.3 collective-permute-start.25
  89.7 3.8 %collective-permute-done.28 = bf16[64,1216]{1,0:T(8,128)(2,1)S(1)} collective-permute-done((bf16[64,1216]{1,0:T(8,128)(2,1)S(1)}, bf16[64,1216]{1,0:T(8,128)(2,1)S(1)}, u32[]{:S(2)}, u32[]{:S(2)}) %collective-permute-start.28) | collective-permute-done | bytes 155680 | tf_op jit(solution)/shard_map/ppermute | solution.py:573
  93.5 1.9 %collective-permute-start.29 = (bf16[64,1216]{1,0:T(8,128)(2,1)S(1)}, bf16[64,1216]{1,0:T(8,128)(2,1)S(1)}, u32[]{:S(2)}, u32[]{:S(2)}) collective-permute-start(bf16[64,1216]{1,0:T(8,128)(2,1)S(1)} %add_convert_fusion), channel_id=1, source_target_pairs={{0,2},{2,6},{6,4},{4,0},{1,3},{3,7},{7,5},{5,1},{8,10},{10,14},{14... | collective-permute-start | bytes 466952 | tf_op jit(solution)/shard_map/ppermute | solution.py:573
  95.4 2.1 %collective-permute-done.25 = bf16[64,1216]{1,0:T(8,128)(2,1)S(1)} collective-permute-done((bf16[64,1216]{1,0:T(8,128)(2,1)S(1)}, bf16[64,1216]{1,0:T(8,128)(2,1)S(1)}, u32[]{:S(2)}, u32[]{:S(2)}) %collective-permute-start.25) | collective-permute-done | bytes 155680 | tf_op jit(solution)/shard_map/ppermute | solution.py:573
  97.5 1.4 %collective-permute-start.26 = (bf16[64,1216]{1,0:T(8,128)(2,1)S(1)}, bf16[64,1216]{1,0:T(8,128)(2,1)S(1)}, u32[]{:S(2)}, u32[]{:S(2)}) collective-permute-start(bf16[64,1216]{1,0:T(8,128)(2,1)S(1)} %add_convert_fusion.2), channel_id=1, source_target_pairs={{0,2},{2,6},{6,4},{4,0},{1,3},{3,7},{7,5},{5,1},{8,10},{10,14},{14... | collective-permute-start | bytes 466952 | tf_op jit(solution)/shard_map/ppermute | solution.py:573
  98.9 2.0 %collective-permute-done.29.far = bf16[64,1216]{1,0:T(8,128)(2,1)S(1)} collective-permute-done((bf16[64,1216]{1,0:T(8,128)(2,1)S(1)}, bf16[64,1216]{1,0:T(8,128)(2,1)S(1)}, u32[]{:S(2)}, u32[]{:S(2)}) %collective-permute-start.29) | collective-permute-done | bytes 155680 | tf_op jit(solution)/shard_map/ppermute | solution.py:573
  100.9 2.9 %collective-permute-done.26.near = bf16[64,1216]{1,0:T(8,128)(2,1)S(1)} collective-permute-done((bf16[64,1216]{1,0:T(8,128)(2,1)S(1)}, bf16[64,1216]{1,0:T(8,128)(2,1)S(1)}, u32[]{:S(2)}, u32[]{:S(2)}) %collective-permute-start.26) | collective-permute-done | bytes 155680 | tf_op jit(solution)/shard_map/ppermute | solution.py:573
  103.8 0.2 shard_map.97
  104.0 0.1 collective-permute-start.30
  104.1 1.2 %collective-permute-done.30.other = f32[128,128]{1,0:T(8,128)S(1)} collective-permute-done((f32[128,128]{1,0:T(8,128)S(1)}, f32[128,128]{1,0:T(8,128)S(1)}, u32[]{:S(2)}, u32[]{:S(2)}) %collective-permute-start.30) | collective-permute-done | bytes 65568 | tf_op jit(solution)/shard_map/ppermute | solution.py:576
  105.4 1.2 %shard_map.98 = f32[1216,128]{1,0:T(8,128)} custom-call(f32[128,1216]{1,0:T(8,128)S(1)} %get-tuple-element.121.grad, f32[128,128]{1,0:T(8,128)S(1)} %get-tuple-element.122.sums, f32[128,128]{1,0:T(8,128)S(1)} %collective-permute-done.30.other, f32[128,1216]{1,0:T(8,128)S(1)} %copy-done.1, f32[128,1216]{1,0:T(8,128)S(1)} %copy-done.3, f32[128,128]{1,0:T(8,128)S(1)} %copy-done.4), custom_call_target="tpu_custom_call" | custom-call | flops 516096 | bytes 2064384 | tf_op jit(solution)/shard_map/pallas_call | solution.py:524
  (71 shorter events, 0.3 us)
Async XLA Ops:
  0.0 9.1 %copy-start = (bf16[640,608]{0,1:T(8,128)(2,1)S(1)}, bf16[640,608]{0,1:T(8,128)(2,1)}, u32[]{:S(2)}) copy-start(bf16[640,608]{0,1:T(8,128)(2,1)} %param.17) | copy-start | bytes 2334724
  3.4 12.5 %collective-permute-start.3 = (bf16[64,2560]{1,0:T(8,128)(2,1)}, bf16[64,2560]{1,0:T(8,128)(2,1)S(1)}, u32[]{:S(2)}, u32[]{:S(2)}) collective-permute-start(bf16[64,2560]{1,0:T(8,128)(2,1)} %get-tuple-element.67), channel_id=1, source_target_pairs={{2,0},{6,2},{4,6},{0,4},{3,1},{7,3},{5,7},{1,5},{10,8},{14,10},{12... | collective-permute-start | bytes 983048 | tf_op jit(solution)/shard_map/ppermute | solution.py:579
  7.5 17.2 %collective-permute-start.2 = (bf16[64,2560]{1,0:T(8,128)(2,1)}, bf16[64,2560]{1,0:T(8,128)(2,1)S(1)}, u32[]{:S(2)}, u32[]{:S(2)}) collective-permute-start(bf16[64,2560]{1,0:T(8,128)(2,1)} %get-tuple-element.67), channel_id=1, source_target_pairs={{0,2},{2,6},{6,4},{4,0},{1,3},{3,7},{7,5},{5,1},{8,10},{10,14},{14... | collective-permute-start | bytes 983048 | tf_op jit(solution)/shard_map/ppermute | solution.py:573
  9.5 22.8 %copy-start.7 = (bf16[608,384]{1,0:T(8,128)(2,1)}, bf16[608,384]{1,0:T(8,128)(2,1)S(1)}, u32[]{:S(2)}) copy-start(bf16[608,384]{1,0:T(8,128)(2,1)S(1)} %pad_maximum_fusion.1.refs_13_.refs_15_) | copy-start | bytes 1400836
  9.5 16.5 %collective-permute-start.1 = (bf16[608,384]{1,0:T(8,128)(2,1)S(1)}, bf16[608,384]{1,0:T(8,128)(2,1)S(1)}, u32[]{:S(2)}, u32[]{:S(2)}) collective-permute-start(bf16[608,384]{1,0:T(8,128)(2,1)S(1)} %pad_maximum_fusion.1.refs_13_.refs_15_), channel_id=1, source_target_pairs={{0,8},{1,17},{8,0},{9,25},{16,24},{17,1},{24,16},{25,9},{2,10},{3,... | collective-permute-start | bytes 1400840 | tf_op jit(solution)/shard_map/ppermute | solution.py:600
  12.0 16.9 %collective-permute-start = (bf16[608,384]{1,0:T(8,128)(2,1)}, bf16[608,384]{1,0:T(8,128)(2,1)}, u32[]{:S(2)}, u32[]{:S(2)}) collective-permute-start(bf16[608,384]{1,0:T(8,128)(2,1)} %pad_maximum_fusion.refs_9_), channel_id=1, source_target_pairs={{0,8},{1,17},{8,0},{9,25},{16,24},{17,1},{24,16},{25,9},{2,10},{3,... | collective-permute-start | bytes 1400840 | tf_op jit(solution)/shard_map/ppermute | solution.py:600
  12.5 24.4 %collective-permute-start.11 = (bf16[608,384]{1,0:T(8,128)(2,1)S(1)}, bf16[608,384]{1,0:T(8,128)(2,1)S(1)}, u32[]{:S(2)}, u32[]{:S(2)}) collective-permute-start(bf16[608,384]{1,0:T(8,128)(2,1)S(1)} %pad_maximum_fusion.1.refs_13_.refs_15_), channel_id=1, source_target_pairs={{0,16},{1,9},{8,24},{9,1},{16,0},{17,25},{24,8},{25,17},{2,18},{3,... | collective-permute-start | bytes 1400840 | tf_op jit(solution)/shard_map/ppermute | solution.py:601
  15.9 13.0 %copy-start.8 = (bf16[64,2560]{1,0:T(8,128)(2,1)}, bf16[64,2560]{1,0:T(8,128)(2,1)S(1)}, u32[]{:S(2)}) copy-start(bf16[64,2560]{1,0:T(8,128)(2,1)S(1)} %collective-permute-done.3.following.refs_3_) | copy-start | bytes 983044
  15.9 13.0 %collective-permute-start.4 = (bf16[32,2560]{1,0:T(8,128)(2,1)S(1)}, bf16[32,2560]{1,0:T(8,128)(2,1)S(1)}, u32[]{:S(2)}, u32[]{:S(2)}) collective-permute-start(bf16[32,2560]{1,0:T(8,128)(2,1)S(1)} %slice.8), channel_id=1, source_target_pairs={{2,0},{6,2},{4,6},{0,4},{3,1},{7,3},{5,7},{1,5},{10,8},{14,10},{12... | collective-permute-start | bytes 491528 | tf_op jit(solution)/shard_map/ppermute | solution.py:579
  24.7 4.3 %copy-start.10 = (bf16[64,2560]{1,0:T(8,128)(2,1)}, bf16[64,2560]{1,0:T(8,128)(2,1)S(1)}, u32[]{:S(2)}) copy-start(bf16[64,2560]{1,0:T(8,128)(2,1)S(1)} %collective-permute-done.2.previous.refs_1_) | copy-start | bytes 983044
  25.4 7.1 %collective-permute-start.7 = (bf16[32,2560]{1,0:T(8,128)(2,1)}, bf16[32,2560]{1,0:T(8,128)(2,1)S(1)}, u32[]{:S(2)}, u32[]{:S(2)}) collective-permute-start(bf16[32,2560]{1,0:T(8,128)(2,1)} %slice.9), channel_id=1, source_target_pairs={{0,2},{2,6},{6,4},{4,0},{1,3},{3,7},{7,5},{5,1},{8,10},{10,14},{14... | collective-permute-start | bytes 491528 | tf_op jit(solution)/shard_map/ppermute | solution.py:573
  26.1 21.2 %copy-start.12 = (bf16[608,384]{1,0:T(8,128)(2,1)}, bf16[608,384]{1,0:T(8,128)(2,1)S(1)}, u32[]{:S(2)}) copy-start(bf16[608,384]{1,0:T(8,128)(2,1)S(1)} %collective-permute-done.1.refs_14_.refs_16_) | copy-start | bytes 1400836
  26.1 21.2 %collective-permute-start.10 = (bf16[608,384]{1,0:T(8,128)(2,1)}, bf16[608,384]{1,0:T(8,128)(2,1)}, u32[]{:S(2)}, u32[]{:S(2)}) collective-permute-start(bf16[608,384]{1,0:T(8,128)(2,1)} %pad_maximum_fusion.refs_9_), channel_id=1, source_target_pairs={{0,16},{1,9},{8,24},{9,1},{16,0},{17,25},{24,8},{25,17},{2,18},{3,... | collective-permute-start | bytes 1400840 | tf_op jit(solution)/shard_map/ppermute | solution.py:601
  28.9 0.7 copy-start.14
  32.3 14.9 %copy-start.15 = (bf16[32,2560]{1,0:T(8,128)(2,1)S(1)}, bf16[32,2560]{1,0:T(8,128)(2,1)}, u32[]{:S(2)}) copy-start(bf16[32,2560]{1,0:T(8,128)(2,1)} %copy-done.14) | copy-start | bytes 491524
  32.3 19.1 %copy-start.11 = (bf16[64,2560]{1,0:T(8,128)(2,1)S(1)}, bf16[64,2560]{1,0:T(8,128)(2,1)}, u32[]{:S(2)}) copy-start(bf16[64,2560]{1,0:T(8,128)(2,1)} %copy-done.10) | copy-start | bytes 983044
  32.4 19.6 %copy-start.9 = (bf16[64,2560]{1,0:T(8,128)(2,1)S(1)}, bf16[64,2560]{1,0:T(8,128)(2,1)}, u32[]{:S(2)}) copy-start(bf16[64,2560]{1,0:T(8,128)(2,1)} %copy-done.8) | copy-start | bytes 983044
  32.5 22.2 %copy-start.23 = (bf16[32,2560]{1,0:T(8,128)(2,1)}, bf16[32,2560]{1,0:T(8,128)(2,1)S(1)}, u32[]{:S(2)}) copy-start(bf16[32,2560]{1,0:T(8,128)(2,1)S(1)} %collective-permute-done.7.refs_5_) | copy-start | bytes 491524
  32.5 11.0 %collective-permute-start.15 = (bf16[64,2560]{1,0:T(8,128)(2,1)}, bf16[64,2560]{1,0:T(8,128)(2,1)S(1)}, u32[]{:S(2)}, u32[]{:S(2)}) collective-permute-start(bf16[64,2560]{1,0:T(8,128)(2,1)} %get-tuple-element.78), channel_id=1, source_target_pairs={{2,0},{6,2},{4,6},{0,4},{3,1},{7,3},{5,7},{1,5},{10,8},{14,10},{12... | collective-permute-start | bytes 983048 | tf_op jit(solution)/shard_map/ppermute | solution.py:579
  34.9 16.4 %collective-permute-start.12 = (bf16[608,384]{1,0:T(8,128)(2,1)}, bf16[608,384]{1,0:T(8,128)(2,1)}, u32[]{:S(2)}, u32[]{:S(2)}) collective-permute-start(bf16[608,384]{1,0:T(8,128)(2,1)} %collective-permute-done.refs_10_), channel_id=1, source_target_pairs={{0,16},{1,9},{8,24},{9,1},{16,0},{17,25},{24,8},{25,17},{2,18},{3,... | collective-permute-start | bytes 1400840 | tf_op jit(solution)/shard_map/ppermute | solution.py:636
  36.5 14.9 %collective-permute-start.13 = (bf16[608,384]{1,0:T(8,128)(2,1)S(1)}, bf16[608,384]{1,0:T(8,128)(2,1)}, u32[]{:S(2)}, u32[]{:S(2)}) collective-permute-start(bf16[608,384]{1,0:T(8,128)(2,1)S(1)} %collective-permute-done.1.refs_14_.refs_16_), channel_id=1, source_target_pairs={{0,16},{1,9},{8,24},{9,1},{16,0},{17,25},{24,8},{25,17},{2,18},{3,... | collective-permute-start | bytes 1400840 | tf_op jit(solution)/shard_map/ppermute | solution.py:636
  37.0 17.8 %copy-start.13 = (bf16[608,384]{1,0:T(8,128)(2,1)}, bf16[608,384]{1,0:T(8,128)(2,1)S(1)}, u32[]{:S(2)}) copy-start(bf16[608,384]{1,0:T(8,128)(2,1)S(1)} %collective-permute-done.11.refs_15_.refs_17_) | copy-start | bytes 1400836
  37.0 14.3 %collective-permute-start.9 = (bf16[64,2560]{1,0:T(8,128)(2,1)}, bf16[64,2560]{1,0:T(8,128)(2,1)S(1)}, u32[]{:S(2)}, u32[]{:S(2)}) collective-permute-start(bf16[64,2560]{1,0:T(8,128)(2,1)} %get-tuple-element.78), channel_id=1, source_target_pairs={{0,2},{2,6},{6,4},{4,0},{1,3},{3,7},{7,5},{5,1},{8,10},{10,14},{14... | collective-permute-start | bytes 983048 | tf_op jit(solution)/shard_map/ppermute | solution.py:573
  43.5 19.1 %copy-start.16 = (bf16[64,2560]{1,0:T(8,128)(2,1)}, bf16[64,2560]{1,0:T(8,128)(2,1)S(1)}, u32[]{:S(2)}) copy-start(bf16[64,2560]{1,0:T(8,128)(2,1)S(1)} %collective-permute-done.15.refs_11_) | copy-start | bytes 983044
  43.5 8.7 %collective-permute-start.16 = (bf16[64,2560]{1,0:T(8,128)(2,1)S(1)}, bf16[64,2560]{1,0:T(8,128)(2,1)S(1)}, u32[]{:S(2)}, u32[]{:S(2)}) collective-permute-start(bf16[64,2560]{1,0:T(8,128)(2,1)S(1)} %collective-permute-done.15.refs_11_), channel_id=1, source_target_pairs={{0,1},{1,0},{2,3},{3,2},{4,5},{5,4},{6,7},{7,6},{8,9},{9,8},{10,11... | collective-permute-start | bytes 983048 | tf_op jit(solution)/shard_map/ppermute | solution.py:576
  47.3 4.7 %collective-permute-start.17 = (bf16[32,2560]{1,0:T(8,128)(2,1)S(1)}, bf16[32,2560]{1,0:T(8,128)(2,1)S(1)}, u32[]{:S(2)}, u32[]{:S(2)}) collective-permute-start(bf16[32,2560]{1,0:T(8,128)(2,1)S(1)} %copy-done.15), channel_id=1, source_target_pairs={{0,1},{1,0},{2,3},{3,2},{4,5},{5,4},{6,7},{7,6},{8,9},{9,8},{10,11... | collective-permute-start | bytes 491528 | tf_op jit(solution)/shard_map/ppermute | solution.py:576
  51.3 11.3 %copy-start.17 = (bf16[64,2560]{1,0:T(8,128)(2,1)}, bf16[64,2560]{1,0:T(8,128)(2,1)S(1)}, u32[]{:S(2)}) copy-start(bf16[64,2560]{1,0:T(8,128)(2,1)S(1)} %collective-permute-done.9.refs_9_) | copy-start | bytes 983044
  51.3 1.7 %collective-permute-start.14 = (bf16[64,2560]{1,0:T(8,128)(2,1)S(1)}, bf16[64,2560]{1,0:T(8,128)(2,1)S(1)}, u32[]{:S(2)}, u32[]{:S(2)}) collective-permute-start(bf16[64,2560]{1,0:T(8,128)(2,1)S(1)} %collective-permute-done.9.refs_9_), channel_id=1, source_target_pairs={{0,1},{1,0},{2,3},{3,2},{4,5},{5,4},{6,7},{7,6},{8,9},{9,8},{10,11... | collective-permute-start | bytes 983048 | tf_op jit(solution)/shard_map/ppermute | solution.py:576
  51.4 2.5 %collective-permute-start.5 = (bf16[64,2560]{1,0:T(8,128)(2,1)S(1)}, bf16[64,2560]{1,0:T(8,128)(2,1)S(1)}, u32[]{:S(2)}, u32[]{:S(2)}) collective-permute-start(bf16[64,2560]{1,0:T(8,128)(2,1)S(1)} %copy-done.11), channel_id=1, source_target_pairs={{0,1},{1,0},{2,3},{3,2},{4,5},{5,4},{6,7},{7,6},{8,9},{9,8},{10,11... | collective-permute-start | bytes 983048 | tf_op jit(solution)/shard_map/ppermute | solution.py:576
  51.9 2.8 %collective-permute-start.6 = (bf16[64,2560]{1,0:T(8,128)(2,1)S(1)}, bf16[64,2560]{1,0:T(8,128)(2,1)}, u32[]{:S(2)}, u32[]{:S(2)}) collective-permute-start(bf16[64,2560]{1,0:T(8,128)(2,1)S(1)} %copy-done.9), channel_id=1, source_target_pairs={{0,1},{1,0},{2,3},{3,2},{4,5},{5,4},{6,7},{7,6},{8,9},{9,8},{10,11... | collective-permute-start | bytes 983048 | tf_op jit(solution)/shard_map/ppermute | solution.py:576
  52.0 2.0 %copy-start.24 = (bf16[32,2560]{1,0:T(8,128)(2,1)}, bf16[32,2560]{1,0:T(8,128)(2,1)S(1)}, u32[]{:S(2)}) copy-start(bf16[32,2560]{1,0:T(8,128)(2,1)S(1)} %collective-permute-done.17.refs_8_) | copy-start | bytes 491524
  52.0 10.9 %collective-permute-start.18 = (bf16[64,2560]{1,0:T(8,128)(2,1)S(1)}, bf16[64,2560]{1,0:T(8,128)(2,1)S(1)}, u32[]{:S(2)}, u32[]{:S(2)}) collective-permute-start(bf16[64,2560]{1,0:T(8,128)(2,1)S(1)} %collective-permute-done.9.refs_9_), channel_id=1, source_target_pairs={{0,2},{2,6},{6,4},{4,0},{1,3},{3,7},{7,5},{5,1},{8,10},{10,14},{14... | collective-permute-start | bytes 983048 | tf_op jit(solution)/shard_map/ppermute | solution.py:573
  52.2 10.4 %copy-start.18 = (bf16[64,2560]{1,0:T(8,128)(2,1)}, bf16[64,2560]{1,0:T(8,128)(2,1)S(1)}, u32[]{:S(2)}) copy-start(bf16[64,2560]{1,0:T(8,128)(2,1)S(1)} %collective-permute-done.16.refs_12_) | copy-start | bytes 983044
  52.2 1.8 %collective-permute-start.8 = (bf16[32,2560]{1,0:T(8,128)(2,1)S(1)}, bf16[32,2560]{1,0:T(8,128)(2,1)S(1)}, u32[]{:S(2)}, u32[]{:S(2)}) collective-permute-start(bf16[32,2560]{1,0:T(8,128)(2,1)S(1)} %collective-permute-done.7.refs_5_), channel_id=1, source_target_pairs={{0,1},{1,0},{2,3},{3,2},{4,5},{5,4},{6,7},{7,6},{8,9},{9,8},{10,11... | collective-permute-start | bytes 491528 | tf_op jit(solution)/shard_map/ppermute | solution.py:576
  53.0 9.6 %copy-start.19 = (bf16[64,2560]{1,0:T(8,128)(2,1)}, bf16[64,2560]{1,0:T(8,128)(2,1)S(1)}, u32[]{:S(2)}) copy-start(bf16[64,2560]{1,0:T(8,128)(2,1)S(1)} %collective-permute-done.14.refs_10_) | copy-start | bytes 983044
  54.0 0.8 copy-start.25
  54.0 0.8 copy-start.21
  62.9 1.8 %copy-start.20 = (bf16[64,2560]{1,0:T(8,128)(2,1)}, bf16[64,2560]{1,0:T(8,128)(2,1)S(1)}, u32[]{:S(2)}) copy-start(bf16[64,2560]{1,0:T(8,128)(2,1)S(1)} %collective-permute-done.18.refs_13_) | copy-start | bytes 983044
  62.9 1.6 %collective-permute-start.19 = (bf16[64,2560]{1,0:T(8,128)(2,1)S(1)}, bf16[64,2560]{1,0:T(8,128)(2,1)S(1)}, u32[]{:S(2)}, u32[]{:S(2)}) collective-permute-start(bf16[64,2560]{1,0:T(8,128)(2,1)S(1)} %collective-permute-done.18.refs_13_), channel_id=1, source_target_pairs={{0,1},{1,0},{2,3},{3,2},{4,5},{5,4},{6,7},{7,6},{8,9},{9,8},{10,11... | collective-permute-start | bytes 983048 | tf_op jit(solution)/shard_map/ppermute | solution.py:576
  64.6 0.7 copy-start.22
  64.6 17.0 %collective-permute-start.23 = (bf16[1216,640]{1,0:T(8,128)(2,1)}, bf16[1216,640]{1,0:T(8,128)(2,1)}, u32[]{:S(2)}, u32[]{:S(2)}) collective-permute-start(bf16[1216,640]{1,0:T(8,128)(2,1)} %get-tuple-element.112.refs_7_), channel_id=1, source_target_pairs={{0,1},{1,0},{2,3},{3,2},{4,5},{5,4},{6,7},{7,6},{8,9},{9,8},{10,11... | collective-permute-start | bytes 4669448 | tf_op jit(solution)/shard_map/ppermute | solution.py:576
  65.3 16.3 %copy-start.2 = (bf16[1216,640]{1,0:T(8,128)(2,1)S(1)}, bf16[1216,640]{1,0:T(8,128)(2,1)}, u32[]{:S(2)}) copy-start(bf16[1216,640]{1,0:T(8,128)(2,1)} %get-tuple-element.89.refs_6_.w_own) | copy-start | bytes 4669444
  75.8 1.7 %collective-permute-start.22 = (bf16[64,1216]{1,0:T(8,128)(2,1)}, bf16[64,1216]{1,0:T(8,128)(2,1)S(1)}, u32[]{:S(2)}, u32[]{:S(2)}) collective-permute-start(bf16[64,1216]{1,0:T(8,128)(2,1)} %get-tuple-element.109), channel_id=1, source_target_pairs={{0,1},{1,0},{2,3},{3,2},{4,5},{5,4},{6,7},{7,6},{8,9},{9,8},{10,11... | collective-permute-start | bytes 466952 | tf_op jit(solution)/shard_map/ppermute | solution.py:576
  76.0 3.8 %collective-permute-start.21 = (bf16[64,1216]{1,0:T(8,128)(2,1)}, bf16[64,1216]{1,0:T(8,128)(2,1)S(1)}, u32[]{:S(2)}, u32[]{:S(2)}) collective-permute-start(bf16[64,1216]{1,0:T(8,128)(2,1)} %get-tuple-element.107), channel_id=1, source_target_pairs={{0,1},{1,0},{2,3},{3,2},{4,5},{5,4},{6,7},{7,6},{8,9},{9,8},{10,11... | collective-permute-start | bytes 466952 | tf_op jit(solution)/shard_map/ppermute | solution.py:576
  76.4 5.2 %collective-permute-start.20 = (bf16[384,640]{1,0:T(8,128)(2,1)}, bf16[384,640]{1,0:T(8,128)(2,1)S(1)}, u32[]{:S(2)}, u32[]{:S(2)}) collective-permute-start(bf16[384,640]{1,0:T(8,128)(2,1)} %get-tuple-element.110.own), channel_id=1, source_target_pairs={{0,1},{1,0},{2,3},{3,2},{4,5},{5,4},{6,7},{7,6},{8,9},{9,8},{10,11... | collective-permute-start | bytes 1474568 | tf_op jit(solution)/shard_map/ppermute | solution.py:576
  78.5 8.0 %collective-permute-start.27 = (bf16[64,1216]{1,0:T(8,128)(2,1)S(1)}, bf16[64,1216]{1,0:T(8,128)(2,1)S(1)}, u32[]{:S(2)}, u32[]{:S(2)}) collective-permute-start(bf16[64,1216]{1,0:T(8,128)(2,1)S(1)} %add_convert_fusion.4), channel_id=1, source_target_pairs={{0,2},{2,6},{6,4},{4,0},{1,3},{3,7},{7,5},{5,1},{8,10},{10,14},{14... | collective-permute-start | bytes 466952 | tf_op jit(solution)/shard_map/ppermute | solution.py:573
  80.8 8.5 %collective-permute-start.24 = (bf16[64,1216]{1,0:T(8,128)(2,1)S(1)}, bf16[64,1216]{1,0:T(8,128)(2,1)S(1)}, u32[]{:S(2)}, u32[]{:S(2)}) collective-permute-start(bf16[64,1216]{1,0:T(8,128)(2,1)S(1)} %add_convert_fusion.5), channel_id=1, source_target_pairs={{0,2},{2,6},{6,4},{4,0},{1,3},{3,7},{7,5},{5,1},{8,10},{10,14},{14... | collective-permute-start | bytes 466952 | tf_op jit(solution)/shard_map/ppermute | solution.py:573
  81.6 1.0 copy-start.6
  85.8 18.1 %copy-start.1 = (f32[128,1216]{1,0:T(8,128)S(1)}, f32[128,1216]{1,0:T(8,128)}, u32[]{:S(2)}) copy-start(f32[128,1216]{1,0:T(8,128)} %get-tuple-element.120.normed) | copy-start | bytes 1867780
  85.8 18.1 %copy-start.5 = (f32[1,1216]{1,0:T(1,128)S(1)}, f32[1,1216]{1,0:T(1,128)}, u32[]{:S(2)}) copy-start(f32[1,1216]{1,0:T(1,128)} %get-tuple-element.119.scale) | copy-start | bytes 14596
  86.5 6.9 %collective-permute-start.28 = (bf16[64,1216]{1,0:T(8,128)(2,1)S(1)}, bf16[64,1216]{1,0:T(8,128)(2,1)S(1)}, u32[]{:S(2)}, u32[]{:S(2)}) collective-permute-start(bf16[64,1216]{1,0:T(8,128)(2,1)S(1)} %add_convert_fusion.1), channel_id=1, source_target_pairs={{0,2},{2,6},{6,4},{4,0},{1,3},{3,7},{7,5},{5,1},{8,10},{10,14},{14... | collective-permute-start | bytes 466952 | tf_op jit(solution)/shard_map/ppermute | solution.py:573
  89.4 16.0 %copy-start.3 = (f32[128,1216]{1,0:T(8,128)S(1)}, f32[128,1216]{1,0:T(8,128)}, u32[]{:S(2)}) copy-start(f32[128,1216]{1,0:T(8,128)} %get-tuple-element.123.base) | copy-start | bytes 1867780
  89.4 16.0 %copy-start.4 = (f32[128,128]{1,0:T(8,128)S(1)}, f32[128,128]{1,0:T(8,128)}, u32[]{:S(2)}) copy-start(f32[128,128]{1,0:T(8,128)} %get-tuple-element.124.inv_std) | copy-start | bytes 196612
  89.4 8.1 %collective-permute-start.25 = (bf16[64,1216]{1,0:T(8,128)(2,1)S(1)}, bf16[64,1216]{1,0:T(8,128)(2,1)S(1)}, u32[]{:S(2)}, u32[]{:S(2)}) collective-permute-start(bf16[64,1216]{1,0:T(8,128)(2,1)S(1)} %add_convert_fusion.3), channel_id=1, source_target_pairs={{0,2},{2,6},{6,4},{4,0},{1,3},{3,7},{7,5},{5,1},{8,10},{10,14},{14... | collective-permute-start | bytes 466952 | tf_op jit(solution)/shard_map/ppermute | solution.py:573
  93.5 7.4 %collective-permute-start.29 = (bf16[64,1216]{1,0:T(8,128)(2,1)S(1)}, bf16[64,1216]{1,0:T(8,128)(2,1)S(1)}, u32[]{:S(2)}, u32[]{:S(2)}) collective-permute-start(bf16[64,1216]{1,0:T(8,128)(2,1)S(1)} %add_convert_fusion), channel_id=1, source_target_pairs={{0,2},{2,6},{6,4},{4,0},{1,3},{3,7},{7,5},{5,1},{8,10},{10,14},{14... | collective-permute-start | bytes 466952 | tf_op jit(solution)/shard_map/ppermute | solution.py:573
  97.5 6.3 %collective-permute-start.26 = (bf16[64,1216]{1,0:T(8,128)(2,1)S(1)}, bf16[64,1216]{1,0:T(8,128)(2,1)S(1)}, u32[]{:S(2)}, u32[]{:S(2)}) collective-permute-start(bf16[64,1216]{1,0:T(8,128)(2,1)S(1)} %add_convert_fusion.2), channel_id=1, source_target_pairs={{0,2},{2,6},{6,4},{4,0},{1,3},{3,7},{7,5},{5,1},{8,10},{10,14},{14... | collective-permute-start | bytes 466952 | tf_op jit(solution)/shard_map/ppermute | solution.py:573
  104.0 1.3 %collective-permute-start.30 = (f32[128,128]{1,0:T(8,128)S(1)}, f32[128,128]{1,0:T(8,128)S(1)}, u32[]{:S(2)}, u32[]{:S(2)}) collective-permute-start(f32[128,128]{1,0:T(8,128)S(1)} %get-tuple-element.122.sums), channel_id=1, source_target_pairs={{0,1},{1,0},{2,3},{3,2},{4,5},{5,4},{6,7},{7,6},{8,9},{9,8},{10,11... | collective-permute-start | bytes 196616 | tf_op jit(solution)/shard_map/ppermute | solution.py:576

commit v6 on v5

--- a/solution.py
+++ b/solution.py
@@ -44,7 +44,7 @@
 def equal_blocks(columns, block):
     row = lax.broadcasted_iota(jnp.int32, (columns, columns), 0)
     column = lax.broadcasted_iota(jnp.int32, (columns, columns), 1)
-    return jnp.where(row // block == column // block, 1.0, 0.0).astype(jnp.bfloat16)
+    return jnp.where((row ^ column) < block, 1.0, 0.0).astype(jnp.bfloat16)
 
 
 def head_means(values):
@@ -82,7 +82,7 @@
 
 
 def first_kernel(step, core, states, table, adjoint, text, out, rows_out, extra_out):
-    rows = [table[c, pl.ds(step[0] % 8, 1), :] for c in range(3)]
+    rows = [table[c, pl.ds(step[0], 1), :] for c in range(3)]
     widened = states[...].astype(jnp.float32)
     centered = widened - jnp.mean(widened, axis=-1, keepdims=True)
     inv_std = lax.rsqrt(jnp.mean(centered * centered, axis=-1, keepdims=True) + 1e-06)
@@ -119,7 +119,7 @@
             grid=(1,),
             in_specs=[
                 pl.BlockSpec((half, width), lambda i, step, core: (core[0], 0)),
-                pl.BlockSpec((3, 8, width), lambda i, step, core: (0, step[0] // 8, 0)),
+                whole(*table.shape),
                 whole(*adjoint.shape),
                 whole(*text.shape),
             ],

time: 107 us -> 107 us (level)
  waiting for transfers between devices: 35.7 us -> 33.7 us
  starting transfers between devices: 27.5 us -> 29.4 us
    ppermute x10, waiting for transfers between devices: 22 us -> 20.5 us  [step(): return lax.ppermute(moving, 'seq', seq_next)]
    ppermute x10, starting transfers between devices: 8.17 us -> 9.52 us  [step(): return lax.ppermute(moving, 'seq', seq_next)]
where the time goes in v6:
time: 107 us
  waiting for transfers between devices  33.7 us (31%)
  Pallas kernels  32.5 us (30%)
  starting transfers between devices  29.4 us (27%)
  local copies, waits for them, and re-layouts  6.21 us (6%)
  other arithmetic  3.24 us (3%)
  between operations  1.71 us (2%)
    ppermute x10, waiting for transfers between devices, step(): return lax.ppermute(moving, 'seq', seq_next)  20.5 us
    pallas_call x1, Pallas kernels, attend_call(): pl.pallas_call(functools.partial(attend_kernel, slots, count, rows, shard...  10.5 us
    ppermute x3, starting transfers between devices, step_back(): return lax.ppermute(moving, 'seq', [(b, a) for a, b in seq_next])  9.8 us
    ppermute x10, starting transfers between devices, step(): return lax.ppermute(moving, 'seq', seq_next)  9.52 us
    ppermute x3, waiting for transfers between devices, step_back(): return lax.ppermute(moving, 'seq', [(b, a) for a, b in seq_next])  8.36 us
    pallas_call x1, Pallas kernels, project_call(): pl.pallas_call(functools.partial(project_kernel, slots, count, rows, shar...  8.09 us
    pallas_call x3, Pallas kernels, local_call(): pl.pallas_call(kernel, out_shape=tuple((jax.ShapeDtypeStruct(*one) for on...  5.21 us
    ppermute x4, starting transfers between devices, shards_by_head(): lax.ppermute(part, ('dp', 'head'), second_way)  5.07 us
  transfers between devices with their start and end apart: 31, of which 17 were waited for; matrix products, arithmetic and copies ran while one was open for 6% of the time, Pallas kernels for 26%

profile of v6, /device:TPU:0, one launch (start us, length us, event | category | flops | bytes accessed | tf_op | source)
XLA Modules:
  0.0 106.8 jit_solution(11694004067681930863)
XLA Ops:
  0.7 2.8 %shard_map.91 = (bf16[64,2560]{1,0:T(8,128)(2,1)}, f32[8,2432]{1,0:T(8,128)}, bf16[64,128]{1,0:T(8,128)(2,1)}) custom-call(s32[1]{0:T(128)S(6)} %copy.11.step, s32[1]{0:T(128)} %bitcast.core, bf16[128,2432]{1,0:T(8,128)(2,1)} %bitcast.31, f32[3,28,2432]{2,1,0:T(8,128)} %bitcast.33, f32[128,2432]{1,0:T(8,128)} %bitcast.28, bf16[8,2,640]{2,1,0:T(2,128)(2,1)} %bitcast.34), custom_call_target="tpu_custom_call" | custom-call | flops 1245184 | bytes 2490368 | tf_op jit(solution)/shard_map/pallas_call | solution.py:110
  3.6 4.0 %collective-permute-start.3 = (bf16[64,2560]{1,0:T(8,128)(2,1)}, bf16[64,2560]{1,0:T(8,128)(2,1)S(1)}, u32[]{:S(2)}, u32[]{:S(2)}) collective-permute-start(bf16[64,2560]{1,0:T(8,128)(2,1)} %get-tuple-element.67), channel_id=1, source_target_pairs={{2,0},{6,2},{4,6},{0,4},{3,1},{7,3},{5,7},{1,5},{10,8},{14,10},{12... | collective-permute-start | bytes 983048 | tf_op jit(solution)/shard_map/ppermute | solution.py:579
  7.6 1.7 %dynamic-slice_bitcast_fusion.1 = (bf16[608,192]{1,0:T(8,128)(2,1)S(1)}, bf16[608,192]{1,0:T(8,128)(2,1)S(1)}, bf16[608,192]{1,0:T(8,128)(2,1)S(1)}) fusion(bf16[608,3,640]{2,0,1:T(8,128)(2,1)} %param.15, s32[]{:T(128)S(6)} %select_n.103), kind=kLoop, calls=%fused_computation.9 | loop fusion | bytes 1400836 | tf_op jit(solution)/shard_map/squeeze | solution.py:595
  9.3 0.2 dynamic-slice_bitcast_fusion
  9.5 0.2 pad_maximum_fusion.1.refs_13_.refs_15_
  9.7 1.6 %collective-permute-start.1 = (bf16[608,384]{1,0:T(8,128)(2,1)S(1)}, bf16[608,384]{1,0:T(8,128)(2,1)S(1)}, u32[]{:S(2)}, u32[]{:S(2)}) collective-permute-start(bf16[608,384]{1,0:T(8,128)(2,1)S(1)} %pad_maximum_fusion.1.refs_13_.refs_15_), channel_id=1, source_target_pairs={{0,8},{1,17},{8,0},{9,25},{16,24},{17,1},{24,16},{25,9},{2,10},{3,... | collective-permute-start | bytes 1400840 | tf_op jit(solution)/shard_map/ppermute | solution.py:600
  11.2 0.9 pad_maximum_fusion.refs_9_
  12.1 0.5 collective-permute-start
  12.7 1.5 %collective-permute-start.11 = (bf16[608,384]{1,0:T(8,128)(2,1)S(1)}, bf16[608,384]{1,0:T(8,128)(2,1)S(1)}, u32[]{:S(2)}, u32[]{:S(2)}) collective-permute-start(bf16[608,384]{1,0:T(8,128)(2,1)S(1)} %pad_maximum_fusion.1.refs_13_.refs_15_), channel_id=1, source_target_pairs={{0,16},{1,9},{8,24},{9,1},{16,0},{17,25},{24,8},{25,17},{2,18},{3,... | collective-permute-start | bytes 1400840 | tf_op jit(solution)/shard_map/ppermute | solution.py:601
  14.2 1.9 %collective-permute-done.3.following.refs_3_ = bf16[64,2560]{1,0:T(8,128)(2,1)S(1)} collective-permute-done((bf16[64,2560]{1,0:T(8,128)(2,1)}, bf16[64,2560]{1,0:T(8,128)(2,1)S(1)}, u32[]{:S(2)}, u32[]{:S(2)}) %collective-permute-start.3) | collective-permute-done | bytes 327712 | tf_op jit(solution)/shard_map/ppermute | solution.py:579
  16.1 3.3 %collective-permute-start.4 = (bf16[32,2560]{1,0:T(8,128)(2,1)S(1)}, bf16[32,2560]{1,0:T(8,128)(2,1)S(1)}, u32[]{:S(2)}, u32[]{:S(2)}) collective-permute-start(bf16[32,2560]{1,0:T(8,128)(2,1)S(1)} %slice.8), channel_id=1, source_target_pairs={{2,0},{6,2},{4,6},{0,4},{3,1},{7,3},{5,7},{1,5},{10,8},{14,10},{12... | collective-permute-start | bytes 491528 | tf_op jit(solution)/shard_map/ppermute | solution.py:579
  19.4 5.4 %collective-permute-done.2.previous.refs_1_ = bf16[64,2560]{1,0:T(8,128)(2,1)S(1)} collective-permute-done((bf16[64,2560]{1,0:T(8,128)(2,1)}, bf16[64,2560]{1,0:T(8,128)(2,1)S(1)}, u32[]{:S(2)}, u32[]{:S(2)}) %collective-permute-start.2) | collective-permute-done | bytes 327712 | tf_op jit(solution)/shard_map/ppermute | solution.py:573
  24.8 0.7 slice.9
  25.5 0.7 collective-permute-start.7
  26.2 1.5 %collective-permute-start.10 = (bf16[608,384]{1,0:T(8,128)(2,1)}, bf16[608,384]{1,0:T(8,128)(2,1)}, u32[]{:S(2)}, u32[]{:S(2)}) collective-permute-start(bf16[608,384]{1,0:T(8,128)(2,1)} %pad_maximum_fusion.refs_9_), channel_id=1, source_target_pairs={{0,16},{1,9},{8,24},{9,1},{16,0},{17,25},{24,8},{25,17},{2,18},{3,... | collective-permute-start | bytes 1400840 | tf_op jit(solution)/shard_map/ppermute | solution.py:601
  28.4 0.7 stack.67.core.scalars
  29.1 0.6 copy-done.14
  29.7 2.7 %shard_map.92 = (bf16[64,2560]{1,0:T(8,128)(2,1)}, f32[8,128]{1,0:T(8,128)}) custom-call(s32[14]{0:T(128)} %stack.67.core.scalars, f32[128,2432]{1,0:T(8,128)} %bitcast.29, f32[8,2432]{1,0:T(8,128)} %get-tuple-element.65.table_rows, bf16[8,2,640]{2,1,0:T(2,128)(2,1)} %bitcast.35, bf16[64,128]{1,0:T(8,128)(2,1)} %get-tuple-element.70.extra, ...), custom_call_target="tpu_custom_call" | custom-call | flops 622592 | bytes 933888 | tf_op jit(solution)/shard_map/pallas_call | solution.py:162
  32.5 0.1 collective-permute-done.7.refs_5_
  32.7 2.4 %collective-permute-start.15 = (bf16[64,2560]{1,0:T(8,128)(2,1)}, bf16[64,2560]{1,0:T(8,128)(2,1)S(1)}, u32[]{:S(2)}, u32[]{:S(2)}) collective-permute-start(bf16[64,2560]{1,0:T(8,128)(2,1)} %get-tuple-element.78), channel_id=1, source_target_pairs={{2,0},{6,2},{4,6},{0,4},{3,1},{7,3},{5,7},{1,5},{10,8},{14,10},{12... | collective-permute-start | bytes 983048 | tf_op jit(solution)/shard_map/ppermute | solution.py:579
  35.1 1.5 %collective-permute-start.12 = (bf16[608,384]{1,0:T(8,128)(2,1)}, bf16[608,384]{1,0:T(8,128)(2,1)}, u32[]{:S(2)}, u32[]{:S(2)}) collective-permute-start(bf16[608,384]{1,0:T(8,128)(2,1)} %collective-permute-done.refs_10_), channel_id=1, source_target_pairs={{0,16},{1,9},{8,24},{9,1},{16,0},{17,25},{24,8},{25,17},{2,18},{3,... | collective-permute-start | bytes 1400840 | tf_op jit(solution)/shard_map/ppermute | solution.py:636
  36.6 0.5 collective-permute-start.13
  37.1 6.5 %collective-permute-done.15.refs_11_ = bf16[64,2560]{1,0:T(8,128)(2,1)S(1)} collective-permute-done((bf16[64,2560]{1,0:T(8,128)(2,1)}, bf16[64,2560]{1,0:T(8,128)(2,1)S(1)}, u32[]{:S(2)}, u32[]{:S(2)}) %collective-permute-start.15) | collective-permute-done | bytes 327712 | tf_op jit(solution)/shard_map/ppermute | solution.py:579
  43.6 3.8 %shard_map.93 = (bf16[128,2560]{1,0:T(8,128)(2,1)}, bf16[128,2560]{1,0:T(8,128)(2,1)}, f32[128,1216]{1,0:T(8,128)}, f32[1,1216]{1,0:T(1,128)}, f32[128,128]{1,0:T(8,128)}, /*index=5*/f32[128,1216]{1,0:T(8,128)}) custom-call(s32[1]{0:T(128)} %bitcast.core, bf16[128,2432]{1,0:T(8,128)(2,1)} %bitcast.32, f32[128,2432]{1,0:T(8,128)} %bitcast.30, ...), custom_call_target="tpu_custom_call" | custom-call | flops 661505 | bytes 1986564 | tf_op jit(solution)/shard_map/pallas_call | solution.py:524
  47.4 0.5 collective-permute-start.17
  47.9 3.6 %collective-permute-done.9.refs_9_ = bf16[64,2560]{1,0:T(8,128)(2,1)S(1)} collective-permute-done((bf16[64,2560]{1,0:T(8,128)(2,1)}, bf16[64,2560]{1,0:T(8,128)(2,1)S(1)}, u32[]{:S(2)}, u32[]{:S(2)}) %collective-permute-start.9) | collective-permute-done | bytes 327712 | tf_op jit(solution)/shard_map/ppermute | solution.py:573
  51.5 0.1 collective-permute-start.14
  51.6 0.5 collective-permute-start.5
  52.1 0.1 collective-permute-start.6
  52.1 0.2 collective-permute-start.18
  52.3 0.3 collective-permute-start.8
  52.7 0.5 collective-permute-done.14.refs_10_
  53.2 0.9 collective-permute-done.8.refs_6_
  54.1 0.8 copy-done.21
  54.9 8.1 %shard_map.94 = (bf16[512,576]{1,0:T(8,128)(2,1)}, bf16[192,512]{1,0:T(8,128)(2,1)}, f32[512,384]{1,0:T(8,128)}, f32[512,384]{1,0:T(8,128)}, bf16[3,32,64]{2,1,0...) custom-call(s32[14]{0:T(128)} %stack.67.core.scalars, ...), custom_call_target="tpu_custom_call" | custom-call | flops 1434451968 | bytes 6914048 | tf_op jit(solution)/shard_map/pallas_call | solution.py:419
  63.1 0.3 collective-permute-start.19
  63.4 1.4 %collective-permute-done.19.refs_14_ = bf16[64,2560]{1,0:T(8,128)(2,1)S(1)} collective-permute-done((bf16[64,2560]{1,0:T(8,128)(2,1)S(1)}, bf16[64,2560]{1,0:T(8,128)(2,1)S(1)}, u32[]{:S(2)}, u32[]{:S(2)}) %collective-permute-start.19) | collective-permute-done | bytes 327712 | tf_op jit(solution)/shard_map/ppermute | solution.py:576
  64.7 0.3 collective-permute-start.23
  65.0 0.4 copy-done.22
  65.5 10.5 %shard_map.95 = (f32[64,1216]{1,0:T(8,128)}, f32[64,1216]{1,0:T(8,128)}, bf16[64,1216]{1,0:T(8,128)(2,1)}, bf16[64,1216]{1,0:T(8,128)(2,1)}, bf16[384,640]{1,0:T(8,128)(2,1)}) custom-call(s32[14]{0:T(128)} %stack.67.core.scalars, f32[2,64]{1,0:T(2,128)} %gain.3, bf16[512,576]{1,0:T(8,128)(2,1)} %get-tuple-element.83.refs_0_, ...), custom_call_target="tpu_custom_call" | custom-call | flops 981467136 | bytes 4358144 | tf_op jit(solution)/shard_map/pallas_call | solution.py:452
  76.0 0.3 collective-permute-start.22
  76.3 0.2 collective-permute-start.21
  76.6 0.3 collective-permute-start.20
  76.8 0.8 collective-permute-done.22
  77.6 1.0 add_convert_fusion.4
  78.7 1.6 %collective-permute-start.27 = (bf16[64,1216]{1,0:T(8,128)(2,1)S(1)}, bf16[64,1216]{1,0:T(8,128)(2,1)S(1)}, u32[]{:S(2)}, u32[]{:S(2)}) collective-permute-start(bf16[64,1216]{1,0:T(8,128)(2,1)S(1)} %add_convert_fusion.4), channel_id=1, source_target_pairs={{0,2},{2,6},{6,4},{4,0},{1,3},{3,7},{7,5},{5,1},{8,10},{10,14},{14... | collective-permute-start | bytes 466952 | tf_op jit(solution)/shard_map/ppermute | solution.py:573
  80.2 1.0 add_convert_fusion.5
  81.2 0.8 collective-permute-start.24
  82.0 1.0 copy-done.6
  83.0 3.1 %shard_map.96 = (f32[64,1216]{1,0:T(8,128)S(1)}, f32[64,1216]{1,0:T(8,128)S(1)}, f32[64,1216]{1,0:T(8,128)S(1)}, f32[64,1216]{1,0:T(8,128)S(1)}, f32[64,1216]{1,0:T(8,128)S(1)}, /*index=5*/f32[64,1216]{1,0:T(8,128)S(1)}) custom-call(bf16[384,640]{1,0:T(8,128)(2,1)S(1)} %copy-done.6, bf16[384,640]{1,0:T(8,128)(2,1)S(1)} %collective-permute-done.20.other, ...), custom_call_target="tpu_custom_call" | custom-call | flops 1195376640 | bytes 5963776 | tf_op jit(solution)/shard_map/pallas_call | solution.py:488
  86.2 0.5 collective-permute-done.27
  86.7 1.9 %collective-permute-start.28 = (bf16[64,1216]{1,0:T(8,128)(2,1)S(1)}, bf16[64,1216]{1,0:T(8,128)(2,1)S(1)}, u32[]{:S(2)}, u32[]{:S(2)}) collective-permute-start(bf16[64,1216]{1,0:T(8,128)(2,1)S(1)} %add_convert_fusion.1), channel_id=1, source_target_pairs={{0,2},{2,6},{6,4},{4,0},{1,3},{3,7},{7,5},{5,1},{8,10},{10,14},{14... | collective-permute-start | bytes 466952 | tf_op jit(solution)/shard_map/ppermute | solution.py:573
  88.6 1.0 collective-permute-done.24
  89.6 0.5 collective-permute-start.25
  90.1 3.3 %collective-permute-done.28 = bf16[64,1216]{1,0:T(8,128)(2,1)S(1)} collective-permute-done((bf16[64,1216]{1,0:T(8,128)(2,1)S(1)}, bf16[64,1216]{1,0:T(8,128)(2,1)S(1)}, u32[]{:S(2)}, u32[]{:S(2)}) %collective-permute-start.28) | collective-permute-done | bytes 155680 | tf_op jit(solution)/shard_map/ppermute | solution.py:573
  93.4 2.4 %collective-permute-start.29 = (bf16[64,1216]{1,0:T(8,128)(2,1)S(1)}, bf16[64,1216]{1,0:T(8,128)(2,1)S(1)}, u32[]{:S(2)}, u32[]{:S(2)}) collective-permute-start(bf16[64,1216]{1,0:T(8,128)(2,1)S(1)} %add_convert_fusion), channel_id=1, source_target_pairs={{0,2},{2,6},{6,4},{4,0},{1,3},{3,7},{7,5},{5,1},{8,10},{10,14},{14... | collective-permute-start | bytes 466952 | tf_op jit(solution)/shard_map/ppermute | solution.py:573
  95.8 1.9 %collective-permute-done.25 = bf16[64,1216]{1,0:T(8,128)(2,1)S(1)} collective-permute-done((bf16[64,1216]{1,0:T(8,128)(2,1)S(1)}, bf16[64,1216]{1,0:T(8,128)(2,1)S(1)}, u32[]{:S(2)}, u32[]{:S(2)}) %collective-permute-start.25) | collective-permute-done | bytes 155680 | tf_op jit(solution)/shard_map/ppermute | solution.py:573
  97.7 1.6 %collective-permute-start.26 = (bf16[64,1216]{1,0:T(8,128)(2,1)S(1)}, bf16[64,1216]{1,0:T(8,128)(2,1)S(1)}, u32[]{:S(2)}, u32[]{:S(2)}) collective-permute-start(bf16[64,1216]{1,0:T(8,128)(2,1)S(1)} %add_convert_fusion.2), channel_id=1, source_target_pairs={{0,2},{2,6},{6,4},{4,0},{1,3},{3,7},{7,5},{5,1},{8,10},{10,14},{14... | collective-permute-start | bytes 466952 | tf_op jit(solution)/shard_map/ppermute | solution.py:573
  99.3 1.7 %collective-permute-done.29.far = bf16[64,1216]{1,0:T(8,128)(2,1)S(1)} collective-permute-done((bf16[64,1216]{1,0:T(8,128)(2,1)S(1)}, bf16[64,1216]{1,0:T(8,128)(2,1)S(1)}, u32[]{:S(2)}, u32[]{:S(2)}) %collective-permute-start.29) | collective-permute-done | bytes 155680 | tf_op jit(solution)/shard_map/ppermute | solution.py:573
  101.0 3.0 %collective-permute-done.26.near = bf16[64,1216]{1,0:T(8,128)(2,1)S(1)} collective-permute-done((bf16[64,1216]{1,0:T(8,128)(2,1)S(1)}, bf16[64,1216]{1,0:T(8,128)(2,1)S(1)}, u32[]{:S(2)}, u32[]{:S(2)}) %collective-permute-start.26) | collective-permute-done | bytes 155680 | tf_op jit(solution)/shard_map/ppermute | solution.py:573
  104.0 0.2 shard_map.97
  104.3 0.1 collective-permute-start.30
  104.3 1.2 %collective-permute-done.30.other = f32[128,128]{1,0:T(8,128)S(1)} collective-permute-done((f32[128,128]{1,0:T(8,128)S(1)}, f32[128,128]{1,0:T(8,128)S(1)}, u32[]{:S(2)}, u32[]{:S(2)}) %collective-permute-start.30) | collective-permute-done | bytes 65568 | tf_op jit(solution)/shard_map/ppermute | solution.py:576
  105.6 1.2 %shard_map.98 = f32[1216,128]{1,0:T(8,128)} custom-call(f32[128,1216]{1,0:T(8,128)S(1)} %get-tuple-element.121.grad, f32[128,128]{1,0:T(8,128)S(1)} %get-tuple-element.122.sums, f32[128,128]{1,0:T(8,128)S(1)} %collective-permute-done.30.other, f32[128,1216]{1,0:T(8,128)S(1)} %copy-done.1, f32[128,1216]{1,0:T(8,128)S(1)} %copy-done.3, f32[128,128]{1,0:T(8,128)S(1)} %copy-done.4), custom_call_target="tpu_custom_call" | custom-call | flops 516096 | bytes 2064384 | tf_op jit(solution)/shard_map/pallas_call | solution.py:524
  (71 shorter events, 0.3 us)
Async XLA Ops:
  0.0 9.3 %copy-start = (bf16[640,608]{0,1:T(8,128)(2,1)S(1)}, bf16[640,608]{0,1:T(8,128)(2,1)}, u32[]{:S(2)}) copy-start(bf16[640,608]{0,1:T(8,128)(2,1)} %param.17) | copy-start | bytes 2334724
  3.6 12.5 %collective-permute-start.3 = (bf16[64,2560]{1,0:T(8,128)(2,1)}, bf16[64,2560]{1,0:T(8,128)(2,1)S(1)}, u32[]{:S(2)}, u32[]{:S(2)}) collective-permute-start(bf16[64,2560]{1,0:T(8,128)(2,1)} %get-tuple-element.67), channel_id=1, source_target_pairs={{2,0},{6,2},{4,6},{0,4},{3,1},{7,3},{5,7},{1,5},{10,8},{14,10},{12... | collective-permute-start | bytes 983048 | tf_op jit(solution)/shard_map/ppermute | solution.py:579
  7.6 17.2 %collective-permute-start.2 = (bf16[64,2560]{1,0:T(8,128)(2,1)}, bf16[64,2560]{1,0:T(8,128)(2,1)S(1)}, u32[]{:S(2)}, u32[]{:S(2)}) collective-permute-start(bf16[64,2560]{1,0:T(8,128)(2,1)} %get-tuple-element.67), channel_id=1, source_target_pairs={{0,2},{2,6},{6,4},{4,0},{1,3},{3,7},{7,5},{5,1},{8,10},{10,14},{14... | collective-permute-start | bytes 983048 | tf_op jit(solution)/shard_map/ppermute | solution.py:573
  9.6 22.8 %copy-start.7 = (bf16[608,384]{1,0:T(8,128)(2,1)}, bf16[608,384]{1,0:T(8,128)(2,1)S(1)}, u32[]{:S(2)}) copy-start(bf16[608,384]{1,0:T(8,128)(2,1)S(1)} %pad_maximum_fusion.1.refs_13_.refs_15_) | copy-start | bytes 1400836
  9.7 16.5 %collective-permute-start.1 = (bf16[608,384]{1,0:T(8,128)(2,1)S(1)}, bf16[608,384]{1,0:T(8,128)(2,1)S(1)}, u32[]{:S(2)}, u32[]{:S(2)}) collective-permute-start(bf16[608,384]{1,0:T(8,128)(2,1)S(1)} %pad_maximum_fusion.1.refs_13_.refs_15_), channel_id=1, source_target_pairs={{0,8},{1,17},{8,0},{9,25},{16,24},{17,1},{24,16},{25,9},{2,10},{3,... | collective-permute-start | bytes 1400840 | tf_op jit(solution)/shard_map/ppermute | solution.py:600
  12.1 16.9 %collective-permute-start = (bf16[608,384]{1,0:T(8,128)(2,1)}, bf16[608,384]{1,0:T(8,128)(2,1)}, u32[]{:S(2)}, u32[]{:S(2)}) collective-permute-start(bf16[608,384]{1,0:T(8,128)(2,1)} %pad_maximum_fusion.refs_9_), channel_id=1, source_target_pairs={{0,8},{1,17},{8,0},{9,25},{16,24},{17,1},{24,16},{25,9},{2,10},{3,... | collective-permute-start | bytes 1400840 | tf_op jit(solution)/shard_map/ppermute | solution.py:600
  12.7 24.4 %collective-permute-start.11 = (bf16[608,384]{1,0:T(8,128)(2,1)S(1)}, bf16[608,384]{1,0:T(8,128)(2,1)S(1)}, u32[]{:S(2)}, u32[]{:S(2)}) collective-permute-start(bf16[608,384]{1,0:T(8,128)(2,1)S(1)} %pad_maximum_fusion.1.refs_13_.refs_15_), channel_id=1, source_target_pairs={{0,16},{1,9},{8,24},{9,1},{16,0},{17,25},{24,8},{25,17},{2,18},{3,... | collective-permute-start | bytes 1400840 | tf_op jit(solution)/shard_map/ppermute | solution.py:601
  16.1 13.0 %copy-start.8 = (bf16[64,2560]{1,0:T(8,128)(2,1)}, bf16[64,2560]{1,0:T(8,128)(2,1)S(1)}, u32[]{:S(2)}) copy-start(bf16[64,2560]{1,0:T(8,128)(2,1)S(1)} %collective-permute-done.3.following.refs_3_) | copy-start | bytes 983044
  16.1 13.0 %collective-permute-start.4 = (bf16[32,2560]{1,0:T(8,128)(2,1)S(1)}, bf16[32,2560]{1,0:T(8,128)(2,1)S(1)}, u32[]{:S(2)}, u32[]{:S(2)}) collective-permute-start(bf16[32,2560]{1,0:T(8,128)(2,1)S(1)} %slice.8), channel_id=1, source_target_pairs={{2,0},{6,2},{4,6},{0,4},{3,1},{7,3},{5,7},{1,5},{10,8},{14,10},{12... | collective-permute-start | bytes 491528 | tf_op jit(solution)/shard_map/ppermute | solution.py:579
  24.8 4.3 %copy-start.10 = (bf16[64,2560]{1,0:T(8,128)(2,1)}, bf16[64,2560]{1,0:T(8,128)(2,1)S(1)}, u32[]{:S(2)}) copy-start(bf16[64,2560]{1,0:T(8,128)(2,1)S(1)} %collective-permute-done.2.previous.refs_1_) | copy-start | bytes 983044
  25.5 7.1 %collective-permute-start.7 = (bf16[32,2560]{1,0:T(8,128)(2,1)}, bf16[32,2560]{1,0:T(8,128)(2,1)S(1)}, u32[]{:S(2)}, u32[]{:S(2)}) collective-permute-start(bf16[32,2560]{1,0:T(8,128)(2,1)} %slice.9), channel_id=1, source_target_pairs={{0,2},{2,6},{6,4},{4,0},{1,3},{3,7},{7,5},{5,1},{8,10},{10,14},{14... | collective-permute-start | bytes 491528 | tf_op jit(solution)/shard_map/ppermute | solution.py:573
  26.2 21.2 %copy-start.12 = (bf16[608,384]{1,0:T(8,128)(2,1)}, bf16[608,384]{1,0:T(8,128)(2,1)S(1)}, u32[]{:S(2)}) copy-start(bf16[608,384]{1,0:T(8,128)(2,1)S(1)} %collective-permute-done.1.refs_14_.refs_16_) | copy-start | bytes 1400836
  26.2 21.2 %collective-permute-start.10 = (bf16[608,384]{1,0:T(8,128)(2,1)}, bf16[608,384]{1,0:T(8,128)(2,1)}, u32[]{:S(2)}, u32[]{:S(2)}) collective-permute-start(bf16[608,384]{1,0:T(8,128)(2,1)} %pad_maximum_fusion.refs_9_), channel_id=1, source_target_pairs={{0,16},{1,9},{8,24},{9,1},{16,0},{17,25},{24,8},{25,17},{2,18},{3,... | collective-permute-start | bytes 1400840 | tf_op jit(solution)/shard_map/ppermute | solution.py:601
  29.1 0.7 copy-start.14
  32.5 14.9 %copy-start.15 = (bf16[32,2560]{1,0:T(8,128)(2,1)S(1)}, bf16[32,2560]{1,0:T(8,128)(2,1)}, u32[]{:S(2)}) copy-start(bf16[32,2560]{1,0:T(8,128)(2,1)} %copy-done.14) | copy-start | bytes 491524
  32.5 19.1 %copy-start.11 = (bf16[64,2560]{1,0:T(8,128)(2,1)S(1)}, bf16[64,2560]{1,0:T(8,128)(2,1)}, u32[]{:S(2)}) copy-start(bf16[64,2560]{1,0:T(8,128)(2,1)} %copy-done.10) | copy-start | bytes 983044
  32.5 19.6 %copy-start.9 = (bf16[64,2560]{1,0:T(8,128)(2,1)S(1)}, bf16[64,2560]{1,0:T(8,128)(2,1)}, u32[]{:S(2)}) copy-start(bf16[64,2560]{1,0:T(8,128)(2,1)} %copy-done.8) | copy-start | bytes 983044
  32.7 22.2 %copy-start.23 = (bf16[32,2560]{1,0:T(8,128)(2,1)}, bf16[32,2560]{1,0:T(8,128)(2,1)S(1)}, u32[]{:S(2)}) copy-start(bf16[32,2560]{1,0:T(8,128)(2,1)S(1)} %collective-permute-done.7.refs_5_) | copy-start | bytes 491524
  32.7 11.0 %collective-permute-start.15 = (bf16[64,2560]{1,0:T(8,128)(2,1)}, bf16[64,2560]{1,0:T(8,128)(2,1)S(1)}, u32[]{:S(2)}, u32[]{:S(2)}) collective-permute-start(bf16[64,2560]{1,0:T(8,128)(2,1)} %get-tuple-element.78), channel_id=1, source_target_pairs={{2,0},{6,2},{4,6},{0,4},{3,1},{7,3},{5,7},{1,5},{10,8},{14,10},{12... | collective-permute-start | bytes 983048 | tf_op jit(solution)/shard_map/ppermute | solution.py:579
  35.1 16.4 %collective-permute-start.12 = (bf16[608,384]{1,0:T(8,128)(2,1)}, bf16[608,384]{1,0:T(8,128)(2,1)}, u32[]{:S(2)}, u32[]{:S(2)}) collective-permute-start(bf16[608,384]{1,0:T(8,128)(2,1)} %collective-permute-done.refs_10_), channel_id=1, source_target_pairs={{0,16},{1,9},{8,24},{9,1},{16,0},{17,25},{24,8},{25,17},{2,18},{3,... | collective-permute-start | bytes 1400840 | tf_op jit(solution)/shard_map/ppermute | solution.py:636
  36.6 14.9 %collective-permute-start.13 = (bf16[608,384]{1,0:T(8,128)(2,1)S(1)}, bf16[608,384]{1,0:T(8,128)(2,1)}, u32[]{:S(2)}, u32[]{:S(2)}) collective-permute-start(bf16[608,384]{1,0:T(8,128)(2,1)S(1)} %collective-permute-done.1.refs_14_.refs_16_), channel_id=1, source_target_pairs={{0,16},{1,9},{8,24},{9,1},{16,0},{17,25},{24,8},{25,17},{2,18},{3,... | collective-permute-start | bytes 1400840 | tf_op jit(solution)/shard_map/ppermute | solution.py:636
  37.1 17.8 %copy-start.13 = (bf16[608,384]{1,0:T(8,128)(2,1)}, bf16[608,384]{1,0:T(8,128)(2,1)S(1)}, u32[]{:S(2)}) copy-start(bf16[608,384]{1,0:T(8,128)(2,1)S(1)} %collective-permute-done.11.refs_15_.refs_17_) | copy-start | bytes 1400836
  37.1 14.3 %collective-permute-start.9 = (bf16[64,2560]{1,0:T(8,128)(2,1)}, bf16[64,2560]{1,0:T(8,128)(2,1)S(1)}, u32[]{:S(2)}, u32[]{:S(2)}) collective-permute-start(bf16[64,2560]{1,0:T(8,128)(2,1)} %get-tuple-element.78), channel_id=1, source_target_pairs={{0,2},{2,6},{6,4},{4,0},{1,3},{3,7},{7,5},{5,1},{8,10},{10,14},{14... | collective-permute-start | bytes 983048 | tf_op jit(solution)/shard_map/ppermute | solution.py:573
  43.6 19.4 %copy-start.16 = (bf16[64,2560]{1,0:T(8,128)(2,1)}, bf16[64,2560]{1,0:T(8,128)(2,1)S(1)}, u32[]{:S(2)}) copy-start(bf16[64,2560]{1,0:T(8,128)(2,1)S(1)} %collective-permute-done.15.refs_11_) | copy-start | bytes 983044
  43.6 8.7 %collective-permute-start.16 = (bf16[64,2560]{1,0:T(8,128)(2,1)S(1)}, bf16[64,2560]{1,0:T(8,128)(2,1)S(1)}, u32[]{:S(2)}, u32[]{:S(2)}) collective-permute-start(bf16[64,2560]{1,0:T(8,128)(2,1)S(1)} %collective-permute-done.15.refs_11_), channel_id=1, source_target_pairs={{0,1},{1,0},{2,3},{3,2},{4,5},{5,4},{6,7},{7,6},{8,9},{9,8},{10,11... | collective-permute-start | bytes 983048 | tf_op jit(solution)/shard_map/ppermute | solution.py:576
  47.4 4.7 %collective-permute-start.17 = (bf16[32,2560]{1,0:T(8,128)(2,1)S(1)}, bf16[32,2560]{1,0:T(8,128)(2,1)S(1)}, u32[]{:S(2)}, u32[]{:S(2)}) collective-permute-start(bf16[32,2560]{1,0:T(8,128)(2,1)S(1)} %copy-done.15), channel_id=1, source_target_pairs={{0,1},{1,0},{2,3},{3,2},{4,5},{5,4},{6,7},{7,6},{8,9},{9,8},{10,11... | collective-permute-start | bytes 491528 | tf_op jit(solution)/shard_map/ppermute | solution.py:576
  51.5 11.5 %copy-start.17 = (bf16[64,2560]{1,0:T(8,128)(2,1)}, bf16[64,2560]{1,0:T(8,128)(2,1)S(1)}, u32[]{:S(2)}) copy-start(bf16[64,2560]{1,0:T(8,128)(2,1)S(1)} %collective-permute-done.9.refs_9_) | copy-start | bytes 983044
  51.5 1.7 %collective-permute-start.14 = (bf16[64,2560]{1,0:T(8,128)(2,1)S(1)}, bf16[64,2560]{1,0:T(8,128)(2,1)S(1)}, u32[]{:S(2)}, u32[]{:S(2)}) collective-permute-start(bf16[64,2560]{1,0:T(8,128)(2,1)S(1)} %collective-permute-done.9.refs_9_), channel_id=1, source_target_pairs={{0,1},{1,0},{2,3},{3,2},{4,5},{5,4},{6,7},{7,6},{8,9},{9,8},{10,11... | collective-permute-start | bytes 983048 | tf_op jit(solution)/shard_map/ppermute | solution.py:576
  51.6 2.5 %collective-permute-start.5 = (bf16[64,2560]{1,0:T(8,128)(2,1)S(1)}, bf16[64,2560]{1,0:T(8,128)(2,1)S(1)}, u32[]{:S(2)}, u32[]{:S(2)}) collective-permute-start(bf16[64,2560]{1,0:T(8,128)(2,1)S(1)} %copy-done.11), channel_id=1, source_target_pairs={{0,1},{1,0},{2,3},{3,2},{4,5},{5,4},{6,7},{7,6},{8,9},{9,8},{10,11... | collective-permute-start | bytes 983048 | tf_op jit(solution)/shard_map/ppermute | solution.py:576
  52.1 2.8 %collective-permute-start.6 = (bf16[64,2560]{1,0:T(8,128)(2,1)S(1)}, bf16[64,2560]{1,0:T(8,128)(2,1)}, u32[]{:S(2)}, u32[]{:S(2)}) collective-permute-start(bf16[64,2560]{1,0:T(8,128)(2,1)S(1)} %copy-done.9), channel_id=1, source_target_pairs={{0,1},{1,0},{2,3},{3,2},{4,5},{5,4},{6,7},{7,6},{8,9},{9,8},{10,11... | collective-permute-start | bytes 983048 | tf_op jit(solution)/shard_map/ppermute | solution.py:576
  52.1 2.0 %copy-start.24 = (bf16[32,2560]{1,0:T(8,128)(2,1)}, bf16[32,2560]{1,0:T(8,128)(2,1)S(1)}, u32[]{:S(2)}) copy-start(bf16[32,2560]{1,0:T(8,128)(2,1)S(1)} %collective-permute-done.17.refs_8_) | copy-start | bytes 491524
  52.1 10.9 %collective-permute-start.18 = (bf16[64,2560]{1,0:T(8,128)(2,1)S(1)}, bf16[64,2560]{1,0:T(8,128)(2,1)S(1)}, u32[]{:S(2)}, u32[]{:S(2)}) collective-permute-start(bf16[64,2560]{1,0:T(8,128)(2,1)S(1)} %collective-permute-done.9.refs_9_), channel_id=1, source_target_pairs={{0,2},{2,6},{6,4},{4,0},{1,3},{3,7},{7,5},{5,1},{8,10},{10,14},{14... | collective-permute-start | bytes 983048 | tf_op jit(solution)/shard_map/ppermute | solution.py:573
  52.3 10.7 %copy-start.18 = (bf16[64,2560]{1,0:T(8,128)(2,1)}, bf16[64,2560]{1,0:T(8,128)(2,1)S(1)}, u32[]{:S(2)}) copy-start(bf16[64,2560]{1,0:T(8,128)(2,1)S(1)} %collective-permute-done.16.refs_12_) | copy-start | bytes 983044
  52.3 1.8 %collective-permute-start.8 = (bf16[32,2560]{1,0:T(8,128)(2,1)S(1)}, bf16[32,2560]{1,0:T(8,128)(2,1)S(1)}, u32[]{:S(2)}, u32[]{:S(2)}) collective-permute-start(bf16[32,2560]{1,0:T(8,128)(2,1)S(1)} %collective-permute-done.7.refs_5_), channel_id=1, source_target_pairs={{0,1},{1,0},{2,3},{3,2},{4,5},{5,4},{6,7},{7,6},{8,9},{9,8},{10,11... | collective-permute-start | bytes 491528 | tf_op jit(solution)/shard_map/ppermute | solution.py:576
  53.2 9.9 %copy-start.19 = (bf16[64,2560]{1,0:T(8,128)(2,1)}, bf16[64,2560]{1,0:T(8,128)(2,1)S(1)}, u32[]{:S(2)}) copy-start(bf16[64,2560]{1,0:T(8,128)(2,1)S(1)} %collective-permute-done.14.refs_10_) | copy-start | bytes 983044
  54.1 0.8 copy-start.25
  54.1 0.8 copy-start.21
  63.1 1.9 %copy-start.20 = (bf16[64,2560]{1,0:T(8,128)(2,1)}, bf16[64,2560]{1,0:T(8,128)(2,1)S(1)}, u32[]{:S(2)}) copy-start(bf16[64,2560]{1,0:T(8,128)(2,1)S(1)} %collective-permute-done.18.refs_13_) | copy-start | bytes 983044
  63.1 1.7 %collective-permute-start.19 = (bf16[64,2560]{1,0:T(8,128)(2,1)S(1)}, bf16[64,2560]{1,0:T(8,128)(2,1)S(1)}, u32[]{:S(2)}, u32[]{:S(2)}) collective-permute-start(bf16[64,2560]{1,0:T(8,128)(2,1)S(1)} %collective-permute-done.18.refs_13_), channel_id=1, source_target_pairs={{0,1},{1,0},{2,3},{3,2},{4,5},{5,4},{6,7},{7,6},{8,9},{9,8},{10,11... | collective-permute-start | bytes 983048 | tf_op jit(solution)/shard_map/ppermute | solution.py:576
  64.7 0.7 copy-start.22
  64.7 17.3 %collective-permute-start.23 = (bf16[1216,640]{1,0:T(8,128)(2,1)}, bf16[1216,640]{1,0:T(8,128)(2,1)}, u32[]{:S(2)}, u32[]{:S(2)}) collective-permute-start(bf16[1216,640]{1,0:T(8,128)(2,1)} %get-tuple-element.112.refs_7_), channel_id=1, source_target_pairs={{0,1},{1,0},{2,3},{3,2},{4,5},{5,4},{6,7},{7,6},{8,9},{9,8},{10,11... | collective-permute-start | bytes 4669448 | tf_op jit(solution)/shard_map/ppermute | solution.py:576
  65.5 16.5 %copy-start.2 = (bf16[1216,640]{1,0:T(8,128)(2,1)S(1)}, bf16[1216,640]{1,0:T(8,128)(2,1)}, u32[]{:S(2)}) copy-start(bf16[1216,640]{1,0:T(8,128)(2,1)} %get-tuple-element.89.refs_6_.w_own) | copy-start | bytes 4669444
  76.0 1.7 %collective-permute-start.22 = (bf16[64,1216]{1,0:T(8,128)(2,1)}, bf16[64,1216]{1,0:T(8,128)(2,1)S(1)}, u32[]{:S(2)}, u32[]{:S(2)}) collective-permute-start(bf16[64,1216]{1,0:T(8,128)(2,1)} %get-tuple-element.109), channel_id=1, source_target_pairs={{0,1},{1,0},{2,3},{3,2},{4,5},{5,4},{6,7},{7,6},{8,9},{9,8},{10,11... | collective-permute-start | bytes 466952 | tf_op jit(solution)/shard_map/ppermute | solution.py:576
  76.3 3.9 %collective-permute-start.21 = (bf16[64,1216]{1,0:T(8,128)(2,1)}, bf16[64,1216]{1,0:T(8,128)(2,1)S(1)}, u32[]{:S(2)}, u32[]{:S(2)}) collective-permute-start(bf16[64,1216]{1,0:T(8,128)(2,1)} %get-tuple-element.107), channel_id=1, source_target_pairs={{0,1},{1,0},{2,3},{3,2},{4,5},{5,4},{6,7},{7,6},{8,9},{9,8},{10,11... | collective-permute-start | bytes 466952 | tf_op jit(solution)/shard_map/ppermute | solution.py:576
  76.6 5.4 %collective-permute-start.20 = (bf16[384,640]{1,0:T(8,128)(2,1)}, bf16[384,640]{1,0:T(8,128)(2,1)S(1)}, u32[]{:S(2)}, u32[]{:S(2)}) collective-permute-start(bf16[384,640]{1,0:T(8,128)(2,1)} %get-tuple-element.110.own), channel_id=1, source_target_pairs={{0,1},{1,0},{2,3},{3,2},{4,5},{5,4},{6,7},{7,6},{8,9},{9,8},{10,11... | collective-permute-start | bytes 1474568 | tf_op jit(solution)/shard_map/ppermute | solution.py:576
  78.7 8.0 %collective-permute-start.27 = (bf16[64,1216]{1,0:T(8,128)(2,1)S(1)}, bf16[64,1216]{1,0:T(8,128)(2,1)S(1)}, u32[]{:S(2)}, u32[]{:S(2)}) collective-permute-start(bf16[64,1216]{1,0:T(8,128)(2,1)S(1)} %add_convert_fusion.4), channel_id=1, source_target_pairs={{0,2},{2,6},{6,4},{4,0},{1,3},{3,7},{7,5},{5,1},{8,10},{10,14},{14... | collective-permute-start | bytes 466952 | tf_op jit(solution)/shard_map/ppermute | solution.py:573
  81.2 8.3 %collective-permute-start.24 = (bf16[64,1216]{1,0:T(8,128)(2,1)S(1)}, bf16[64,1216]{1,0:T(8,128)(2,1)S(1)}, u32[]{:S(2)}, u32[]{:S(2)}) collective-permute-start(bf16[64,1216]{1,0:T(8,128)(2,1)S(1)} %add_convert_fusion.5), channel_id=1, source_target_pairs={{0,2},{2,6},{6,4},{4,0},{1,3},{3,7},{7,5},{5,1},{8,10},{10,14},{14... | collective-permute-start | bytes 466952 | tf_op jit(solution)/shard_map/ppermute | solution.py:573
  82.0 1.0 copy-start.6
  86.2 17.9 %copy-start.1 = (f32[128,1216]{1,0:T(8,128)S(1)}, f32[128,1216]{1,0:T(8,128)}, u32[]{:S(2)}) copy-start(f32[128,1216]{1,0:T(8,128)} %get-tuple-element.120.normed) | copy-start | bytes 1867780
  86.2 17.9 %copy-start.5 = (f32[1,1216]{1,0:T(1,128)S(1)}, f32[1,1216]{1,0:T(1,128)}, u32[]{:S(2)}) copy-start(f32[1,1216]{1,0:T(1,128)} %get-tuple-element.119.scale) | copy-start | bytes 14596
  86.7 6.7 %collective-permute-start.28 = (bf16[64,1216]{1,0:T(8,128)(2,1)S(1)}, bf16[64,1216]{1,0:T(8,128)(2,1)S(1)}, u32[]{:S(2)}, u32[]{:S(2)}) collective-permute-start(bf16[64,1216]{1,0:T(8,128)(2,1)S(1)} %add_convert_fusion.1), channel_id=1, source_target_pairs={{0,2},{2,6},{6,4},{4,0},{1,3},{3,7},{7,5},{5,1},{8,10},{10,14},{14... | collective-permute-start | bytes 466952 | tf_op jit(solution)/shard_map/ppermute | solution.py:573
  89.6 16.0 %copy-start.3 = (f32[128,1216]{1,0:T(8,128)S(1)}, f32[128,1216]{1,0:T(8,128)}, u32[]{:S(2)}) copy-start(f32[128,1216]{1,0:T(8,128)} %get-tuple-element.123.base) | copy-start | bytes 1867780
  89.6 16.0 %copy-start.4 = (f32[128,128]{1,0:T(8,128)S(1)}, f32[128,128]{1,0:T(8,128)}, u32[]{:S(2)}) copy-start(f32[128,128]{1,0:T(8,128)} %get-tuple-element.124.inv_std) | copy-start | bytes 196612
  89.6 8.1 %collective-permute-start.25 = (bf16[64,1216]{1,0:T(8,128)(2,1)S(1)}, bf16[64,1216]{1,0:T(8,128)(2,1)S(1)}, u32[]{:S(2)}, u32[]{:S(2)}) collective-permute-start(bf16[64,1216]{1,0:T(8,128)(2,1)S(1)} %add_convert_fusion.3), channel_id=1, source_target_pairs={{0,2},{2,6},{6,4},{4,0},{1,3},{3,7},{7,5},{5,1},{8,10},{10,14},{14... | collective-permute-start | bytes 466952 | tf_op jit(solution)/shard_map/ppermute | solution.py:573
  93.4 7.6 %collective-permute-start.29 = (bf16[64,1216]{1,0:T(8,128)(2,1)S(1)}, bf16[64,1216]{1,0:T(8,128)(2,1)S(1)}, u32[]{:S(2)}, u32[]{:S(2)}) collective-permute-start(bf16[64,1216]{1,0:T(8,128)(2,1)S(1)} %add_convert_fusion), channel_id=1, source_target_pairs={{0,2},{2,6},{6,4},{4,0},{1,3},{3,7},{7,5},{5,1},{8,10},{10,14},{14... | collective-permute-start | bytes 466952 | tf_op jit(solution)/shard_map/ppermute | solution.py:573
  97.7 6.3 %collective-permute-start.26 = (bf16[64,1216]{1,0:T(8,128)(2,1)S(1)}, bf16[64,1216]{1,0:T(8,128)(2,1)S(1)}, u32[]{:S(2)}, u32[]{:S(2)}) collective-permute-start(bf16[64,1216]{1,0:T(8,128)(2,1)S(1)} %add_convert_fusion.2), channel_id=1, source_target_pairs={{0,2},{2,6},{6,4},{4,0},{1,3},{3,7},{7,5},{5,1},{8,10},{10,14},{14... | collective-permute-start | bytes 466952 | tf_op jit(solution)/shard_map/ppermute | solution.py:573
  104.3 1.3 %collective-permute-start.30 = (f32[128,128]{1,0:T(8,128)S(1)}, f32[128,128]{1,0:T(8,128)S(1)}, u32[]{:S(2)}, u32[]{:S(2)}) collective-permute-start(f32[128,128]{1,0:T(8,128)S(1)} %get-tuple-element.122.sums), channel_id=1, source_target_pairs={{0,1},{1,0},{2,3},{3,2},{4,5},{5,4},{6,7},{7,6},{8,9},{9,8},{10,11... | collective-permute-start | bytes 196616 | tf_op jit(solution)/shard_map/ppermute | solution.py:576

commit v7 on v6

--- a/solution.py
+++ b/solution.py
@@ -167,7 +167,8 @@
             grid=(1,),
             in_specs=[pl.BlockSpec((half, width), lambda i, core: (core[0], 0))]
             + [whole(table_rows), whole(text), whole(extra)]
-            + [tail(one) for one in (previous, following, opposite)],
+            + [tail(one) for one in (previous, following)]
+            + [whole(opposite)],
             out_specs=tuple(whole(one) for one in outs),
         ),
         compiler_params=pltpu.CompilerParams(vmem_limit_bytes=GRANT),
@@ -605,7 +606,7 @@
     clip_limit = 0.5 * (tok_count * seq_count * model_width) ** 0.5
     extra, *w_first = pin((extra, *w_first))
     cot_half, clip = cotangent_call(
-        clip_limit, scalars, adjoint_rows, table_rows, text_kv[0], extra, *mod_near, mod_far[1]
+        clip_limit, scalars, adjoint_rows, table_rows, text_kv[0], extra, *mod_near, mod_far[1][:, model_width:]
     )
     cot_half, mod_far[0] = pin((cot_half, mod_far[0]))
     cot_near = spread(cot_half)

time: 107 us -> 107 us (level)
  waiting for transfers between devices: 33.7 us -> 32.6 us
    ppermute x10, waiting for transfers between devices: 20.5 us -> 18.9 us  [step(): return lax.ppermute(moving, 'seq', seq_next)]
  transfers between devices with their start and end apart: 31 -> 31, of which waited for: 17 -> 15; matrix products, arithmetic and copies ran while one was open for 6% -> 7% of each run, Pallas kernels for 26% -> 27%
where the time goes in v7:
time: 107 us; the launch traced here: 106 us
  waiting for transfers between devices  32.6 us (30%)
  Pallas kernels  32.5 us (30%)
  starting transfers between devices  30 us (28%)
  local copies, waits for them, and re-layouts  6.17 us (6%)
  other arithmetic  3.24 us (3%)
  between operations  1.72 us (2%)
    ppermute x10, waiting for transfers between devices, step(): return lax.ppermute(moving, 'seq', seq_next)  18.9 us
    ppermute x3, starting transfers between devices, step_back(): return lax.ppermute(moving, 'seq', [(b, a) for a, b in seq_next])  10.7 us
    pallas_call x1, Pallas kernels, attend_call(): pl.pallas_call(functools.partial(attend_kernel, slots, count, rows, shard...  10.5 us
    ppermute x10, starting transfers between devices, step(): return lax.ppermute(moving, 'seq', seq_next)  9.23 us
    ppermute x3, waiting for transfers between devices, step_back(): return lax.ppermute(moving, 'seq', [(b, a) for a, b in seq_next])  8.31 us
    pallas_call x1, Pallas kernels, project_call(): pl.pallas_call(functools.partial(project_kernel, slots, count, rows, shar...  8.09 us
    pallas_call x3, Pallas kernels, local_call(): pl.pallas_call(kernel, out_shape=tuple((jax.ShapeDtypeStruct(*one) for on...  5.22 us
    ppermute x4, starting transfers between devices, shards_by_head(): lax.ppermute(part, ('dp', 'head'), second_way)  5.07 us
  transfers between devices with their start and end apart: 31, of which 15 were waited for; matrix products, arithmetic and copies ran while one was open for 7% of the time, Pallas kernels for 27%

profile of v7, /device:TPU:0, one launch (start us, length us, event | category | flops | bytes accessed | tf_op | source)
XLA Modules:
  0.0 106.3 jit_solution(3756754521180290634)
XLA Ops:
  0.7 2.9 %shard_map.91 = (bf16[64,2560]{1,0:T(8,128)(2,1)}, f32[8,2432]{1,0:T(8,128)}, bf16[64,128]{1,0:T(8,128)(2,1)}) custom-call(s32[1]{0:T(128)S(6)} %copy.11.step, s32[1]{0:T(128)} %bitcast.core, bf16[128,2432]{1,0:T(8,128)(2,1)} %bitcast.31, f32[3,28,2432]{2,1,0:T(8,128)} %bitcast.33, f32[128,2432]{1,0:T(8,128)} %bitcast.28, bf16[8,2,640]{2,1,0:T(2,128)(2,1)} %bitcast.34), custom_call_target="tpu_custom_call" | custom-call | flops 1245184 | bytes 2490368 | tf_op jit(solution)/shard_map/pallas_call | solution.py:110
  3.6 4.0 %collective-permute-start.3 = (bf16[64,2560]{1,0:T(8,128)(2,1)}, bf16[64,2560]{1,0:T(8,128)(2,1)S(1)}, u32[]{:S(2)}, u32[]{:S(2)}) collective-permute-start(bf16[64,2560]{1,0:T(8,128)(2,1)} %get-tuple-element.67), channel_id=1, source_target_pairs={{2,0},{6,2},{4,6},{0,4},{3,1},{7,3},{5,7},{1,5},{10,8},{14,10},{12... | collective-permute-start | bytes 983048 | tf_op jit(solution)/shard_map/ppermute | solution.py:580
  7.6 1.7 %dynamic-slice_bitcast_fusion.1 = (bf16[608,192]{1,0:T(8,128)(2,1)S(1)}, bf16[608,192]{1,0:T(8,128)(2,1)S(1)}, bf16[608,192]{1,0:T(8,128)(2,1)S(1)}) fusion(bf16[608,3,640]{2,0,1:T(8,128)(2,1)} %param.15, s32[]{:T(128)S(6)} %select_n.103), kind=kLoop, calls=%fused_computation.9 | loop fusion | bytes 1400836 | tf_op jit(solution)/shard_map/squeeze | solution.py:596
  9.3 0.2 dynamic-slice_bitcast_fusion
  9.5 0.2 pad_maximum_fusion.1.refs_13_.refs_15_
  9.7 1.6 %collective-permute-start.1 = (bf16[608,384]{1,0:T(8,128)(2,1)S(1)}, bf16[608,384]{1,0:T(8,128)(2,1)S(1)}, u32[]{:S(2)}, u32[]{:S(2)}) collective-permute-start(bf16[608,384]{1,0:T(8,128)(2,1)S(1)} %pad_maximum_fusion.1.refs_13_.refs_15_), channel_id=1, source_target_pairs={{0,8},{1,17},{8,0},{9,25},{16,24},{17,1},{24,16},{25,9},{2,10},{3,... | collective-permute-start | bytes 1400840 | tf_op jit(solution)/shard_map/ppermute | solution.py:601
  11.2 0.9 pad_maximum_fusion.refs_9_
  12.2 0.5 collective-permute-start
  12.7 1.5 %collective-permute-start.11 = (bf16[608,384]{1,0:T(8,128)(2,1)S(1)}, bf16[608,384]{1,0:T(8,128)(2,1)S(1)}, u32[]{:S(2)}, u32[]{:S(2)}) collective-permute-start(bf16[608,384]{1,0:T(8,128)(2,1)S(1)} %pad_maximum_fusion.1.refs_13_.refs_15_), channel_id=1, source_target_pairs={{0,16},{1,9},{8,24},{9,1},{16,0},{17,25},{24,8},{25,17},{2,18},{3,... | collective-permute-start | bytes 1400840 | tf_op jit(solution)/shard_map/ppermute | solution.py:602
  14.2 1.9 %collective-permute-done.3.following.refs_3_ = bf16[64,2560]{1,0:T(8,128)(2,1)S(1)} collective-permute-done((bf16[64,2560]{1,0:T(8,128)(2,1)}, bf16[64,2560]{1,0:T(8,128)(2,1)S(1)}, u32[]{:S(2)}, u32[]{:S(2)}) %collective-permute-start.3) | collective-permute-done | bytes 327712 | tf_op jit(solution)/shard_map/ppermute | solution.py:580
  16.1 0.7 slice.12
  16.8 3.3 %collective-permute-start.4 = (bf16[32,2560]{1,0:T(8,128)(2,1)}, bf16[32,2560]{1,0:T(8,128)(2,1)S(1)}, u32[]{:S(2)}, u32[]{:S(2)}) collective-permute-start(bf16[32,2560]{1,0:T(8,128)(2,1)} %slice.12), channel_id=1, source_target_pairs={{2,0},{6,2},{4,6},{0,4},{3,1},{7,3},{5,7},{1,5},{10,8},{14,10},{12... | collective-permute-start | bytes 491528 | tf_op jit(solution)/shard_map/ppermute | solution.py:580
  20.1 4.7 %collective-permute-done.2.previous.refs_1_ = bf16[64,2560]{1,0:T(8,128)(2,1)S(1)} collective-permute-done((bf16[64,2560]{1,0:T(8,128)(2,1)}, bf16[64,2560]{1,0:T(8,128)(2,1)S(1)}, u32[]{:S(2)}, u32[]{:S(2)}) %collective-permute-start.2) | collective-permute-done | bytes 327712 | tf_op jit(solution)/shard_map/ppermute | solution.py:574
  24.8 0.7 collective-permute-start.7
  25.6 1.5 %collective-permute-start.10 = (bf16[608,384]{1,0:T(8,128)(2,1)}, bf16[608,384]{1,0:T(8,128)(2,1)}, u32[]{:S(2)}, u32[]{:S(2)}) collective-permute-start(bf16[608,384]{1,0:T(8,128)(2,1)} %pad_maximum_fusion.refs_9_), channel_id=1, source_target_pairs={{0,16},{1,9},{8,24},{9,1},{16,0},{17,25},{24,8},{25,17},{2,18},{3,... | collective-permute-start | bytes 1400840 | tf_op jit(solution)/shard_map/ppermute | solution.py:602
  27.8 0.7 stack.67.core.scalars
  28.4 0.5 collective-permute-done.refs_10_
  28.9 0.6 slice.13.opposite
  29.5 2.8 %shard_map.92 = (bf16[64,2560]{1,0:T(8,128)(2,1)}, f32[8,128]{1,0:T(8,128)}) custom-call(s32[14]{0:T(128)} %stack.67.core.scalars, f32[128,2432]{1,0:T(8,128)} %bitcast.29, f32[8,2432]{1,0:T(8,128)} %get-tuple-element.65.table_rows, bf16[8,2,640]{2,1,0:T(2,128)(2,1)} %bitcast.35, bf16[64,128]{1,0:T(8,128)(2,1)} %get-tuple-element.70.extra, ...), custom_call_target="tpu_custom_call" | custom-call | flops 622592 | bytes 933888 | tf_op jit(solution)/shard_map/pallas_call | solution.py:162
  32.3 3.4 %collective-permute-start.15 = (bf16[64,2560]{1,0:T(8,128)(2,1)}, bf16[64,2560]{1,0:T(8,128)(2,1)S(1)}, u32[]{:S(2)}, u32[]{:S(2)}) collective-permute-start(bf16[64,2560]{1,0:T(8,128)(2,1)} %get-tuple-element.78), channel_id=1, source_target_pairs={{2,0},{6,2},{4,6},{0,4},{3,1},{7,3},{5,7},{1,5},{10,8},{14,10},{12... | collective-permute-start | bytes 983048 | tf_op jit(solution)/shard_map/ppermute | solution.py:580
  35.7 1.5 %collective-permute-start.12 = (bf16[608,384]{1,0:T(8,128)(2,1)}, bf16[608,384]{1,0:T(8,128)(2,1)}, u32[]{:S(2)}, u32[]{:S(2)}) collective-permute-start(bf16[608,384]{1,0:T(8,128)(2,1)} %collective-permute-done.refs_10_), channel_id=1, source_target_pairs={{0,16},{1,9},{8,24},{9,1},{16,0},{17,25},{24,8},{25,17},{2,18},{3,... | collective-permute-start | bytes 1400840 | tf_op jit(solution)/shard_map/ppermute | solution.py:637
  37.3 0.5 collective-permute-start.13
  37.8 6.4 %collective-permute-done.15.refs_11_ = bf16[64,2560]{1,0:T(8,128)(2,1)S(1)} collective-permute-done((bf16[64,2560]{1,0:T(8,128)(2,1)}, bf16[64,2560]{1,0:T(8,128)(2,1)S(1)}, u32[]{:S(2)}, u32[]{:S(2)}) %collective-permute-start.15) | collective-permute-done | bytes 327712 | tf_op jit(solution)/shard_map/ppermute | solution.py:580
  44.2 3.8 %shard_map.93 = (bf16[128,2560]{1,0:T(8,128)(2,1)}, bf16[128,2560]{1,0:T(8,128)(2,1)}, f32[128,1216]{1,0:T(8,128)}, f32[1,1216]{1,0:T(1,128)}, f32[128,128]{1,0:T(8,128)}, /*index=5*/f32[128,1216]{1,0:T(8,128)}) custom-call(s32[1]{0:T(128)} %bitcast.core, bf16[128,2432]{1,0:T(8,128)(2,1)} %bitcast.32, f32[128,2432]{1,0:T(8,128)} %bitcast.30, ...), custom_call_target="tpu_custom_call" | custom-call | flops 661505 | bytes 1986564 | tf_op jit(solution)/shard_map/pallas_call | solution.py:525
  48.1 0.4 collective-permute-start.17
  48.5 2.3 %collective-permute-done.9.refs_9_ = bf16[64,2560]{1,0:T(8,128)(2,1)S(1)} collective-permute-done((bf16[64,2560]{1,0:T(8,128)(2,1)}, bf16[64,2560]{1,0:T(8,128)(2,1)S(1)}, u32[]{:S(2)}, u32[]{:S(2)}) %collective-permute-start.9) | collective-permute-done | bytes 327712 | tf_op jit(solution)/shard_map/ppermute | solution.py:574
  50.8 0.1 collective-permute-start.14
  50.9 0.5 collective-permute-start.5
  51.4 0.1 collective-permute-start.6
  51.5 0.2 collective-permute-start.18
  51.7 0.3 collective-permute-start.8
  52.0 0.5 collective-permute-done.14.refs_10_
  52.5 0.9 collective-permute-done.8.refs_6_
  53.5 0.8 copy-done.19
  54.3 8.1 %shard_map.94 = (bf16[512,576]{1,0:T(8,128)(2,1)}, bf16[192,512]{1,0:T(8,128)(2,1)}, f32[512,384]{1,0:T(8,128)}, f32[512,384]{1,0:T(8,128)}, bf16[3,32,64]{2,1,0...) custom-call(s32[14]{0:T(128)} %stack.67.core.scalars, ...), custom_call_target="tpu_custom_call" | custom-call | flops 1434451968 | bytes 6914048 | tf_op jit(solution)/shard_map/pallas_call | solution.py:420
  62.4 0.0 collective-permute-done.18.refs_13_
  62.4 0.3 collective-permute-start.19
  62.8 1.3 %collective-permute-done.19.refs_14_ = bf16[64,2560]{1,0:T(8,128)(2,1)S(1)} collective-permute-done((bf16[64,2560]{1,0:T(8,128)(2,1)S(1)}, bf16[64,2560]{1,0:T(8,128)(2,1)S(1)}, u32[]{:S(2)}, u32[]{:S(2)}) %collective-permute-start.19) | collective-permute-done | bytes 327712 | tf_op jit(solution)/shard_map/ppermute | solution.py:577
  64.1 0.3 collective-permute-start.23
  64.4 0.4 copy-done.20
  64.8 10.5 %shard_map.95 = (f32[64,1216]{1,0:T(8,128)}, f32[64,1216]{1,0:T(8,128)}, bf16[64,1216]{1,0:T(8,128)(2,1)}, bf16[64,1216]{1,0:T(8,128)(2,1)}, bf16[384,640]{1,0:T(8,128)(2,1)}) custom-call(s32[14]{0:T(128)} %stack.67.core.scalars, f32[2,64]{1,0:T(2,128)} %gain.3, bf16[512,576]{1,0:T(8,128)(2,1)} %get-tuple-element.83.refs_0_, ...), custom_call_target="tpu_custom_call" | custom-call | flops 981467136 | bytes 4358144 | tf_op jit(solution)/shard_map/pallas_call | solution.py:453
  75.3 0.3 collective-permute-start.22
  75.7 0.2 collective-permute-start.21
  75.9 0.3 collective-permute-start.20
  76.2 0.8 collective-permute-done.22
  77.0 1.0 add_convert_fusion.4
  78.0 1.6 %collective-permute-start.27 = (bf16[64,1216]{1,0:T(8,128)(2,1)S(1)}, bf16[64,1216]{1,0:T(8,128)(2,1)S(1)}, u32[]{:S(2)}, u32[]{:S(2)}) collective-permute-start(bf16[64,1216]{1,0:T(8,128)(2,1)S(1)} %add_convert_fusion.4), channel_id=1, source_target_pairs={{0,2},{2,6},{6,4},{4,0},{1,3},{3,7},{7,5},{5,1},{8,10},{10,14},{14... | collective-permute-start | bytes 466952 | tf_op jit(solution)/shard_map/ppermute | solution.py:574
  79.7 1.0 add_convert_fusion.5
  80.7 1.3 %collective-permute-start.24 = (bf16[64,1216]{1,0:T(8,128)(2,1)S(1)}, bf16[64,1216]{1,0:T(8,128)(2,1)S(1)}, u32[]{:S(2)}, u32[]{:S(2)}) collective-permute-start(bf16[64,1216]{1,0:T(8,128)(2,1)S(1)} %add_convert_fusion.5), channel_id=1, source_target_pairs={{0,2},{2,6},{6,4},{4,0},{1,3},{3,7},{7,5},{5,1},{8,10},{10,14},{14... | collective-permute-start | bytes 466952 | tf_op jit(solution)/shard_map/ppermute | solution.py:574
  82.0 1.0 copy-done.6
  83.0 3.1 %shard_map.96 = (f32[64,1216]{1,0:T(8,128)S(1)}, f32[64,1216]{1,0:T(8,128)S(1)}, f32[64,1216]{1,0:T(8,128)S(1)}, f32[64,1216]{1,0:T(8,128)S(1)}, f32[64,1216]{1,0:T(8,128)S(1)}, /*index=5*/f32[64,1216]{1,0:T(8,128)S(1)}) custom-call(bf16[384,640]{1,0:T(8,128)(2,1)S(1)} %copy-done.6, bf16[384,640]{1,0:T(8,128)(2,1)S(1)} %collective-permute-done.20.other, ...), custom_call_target="tpu_custom_call" | custom-call | flops 1195376640 | bytes 5963776 | tf_op jit(solution)/shard_map/pallas_call | solution.py:489
  86.2 1.8 %collective-permute-start.28 = (bf16[64,1216]{1,0:T(8,128)(2,1)S(1)}, bf16[64,1216]{1,0:T(8,128)(2,1)S(1)}, u32[]{:S(2)}, u32[]{:S(2)}) collective-permute-start(bf16[64,1216]{1,0:T(8,128)(2,1)S(1)} %add_convert_fusion.1), channel_id=1, source_target_pairs={{0,2},{2,6},{6,4},{4,0},{1,3},{3,7},{7,5},{5,1},{8,10},{10,14},{14... | collective-permute-start | bytes 466952 | tf_op jit(solution)/shard_map/ppermute | solution.py:574
  88.0 0.8 collective-permute-done.24
  88.9 0.6 collective-permute-start.25
  89.5 4.2 %collective-permute-done.28 = bf16[64,1216]{1,0:T(8,128)(2,1)S(1)} collective-permute-done((bf16[64,1216]{1,0:T(8,128)(2,1)S(1)}, bf16[64,1216]{1,0:T(8,128)(2,1)S(1)}, u32[]{:S(2)}, u32[]{:S(2)}) %collective-permute-start.28) | collective-permute-done | bytes 155680 | tf_op jit(solution)/shard_map/ppermute | solution.py:574
  93.8 1.5 %collective-permute-start.29 = (bf16[64,1216]{1,0:T(8,128)(2,1)S(1)}, bf16[64,1216]{1,0:T(8,128)(2,1)S(1)}, u32[]{:S(2)}, u32[]{:S(2)}) collective-permute-start(bf16[64,1216]{1,0:T(8,128)(2,1)S(1)} %add_convert_fusion), channel_id=1, source_target_pairs={{0,2},{2,6},{6,4},{4,0},{1,3},{3,7},{7,5},{5,1},{8,10},{10,14},{14... | collective-permute-start | bytes 466952 | tf_op jit(solution)/shard_map/ppermute | solution.py:574
  95.2 2.0 %collective-permute-done.25 = bf16[64,1216]{1,0:T(8,128)(2,1)S(1)} collective-permute-done((bf16[64,1216]{1,0:T(8,128)(2,1)S(1)}, bf16[64,1216]{1,0:T(8,128)(2,1)S(1)}, u32[]{:S(2)}, u32[]{:S(2)}) %collective-permute-start.25) | collective-permute-done | bytes 155680 | tf_op jit(solution)/shard_map/ppermute | solution.py:574
  97.3 1.5 %collective-permute-start.26 = (bf16[64,1216]{1,0:T(8,128)(2,1)S(1)}, bf16[64,1216]{1,0:T(8,128)(2,1)S(1)}, u32[]{:S(2)}, u32[]{:S(2)}) collective-permute-start(bf16[64,1216]{1,0:T(8,128)(2,1)S(1)} %add_convert_fusion.2), channel_id=1, source_target_pairs={{0,2},{2,6},{6,4},{4,0},{1,3},{3,7},{7,5},{5,1},{8,10},{10,14},{14... | collective-permute-start | bytes 466952 | tf_op jit(solution)/shard_map/ppermute | solution.py:574
  98.8 2.1 %collective-permute-done.29.far = bf16[64,1216]{1,0:T(8,128)(2,1)S(1)} collective-permute-done((bf16[64,1216]{1,0:T(8,128)(2,1)S(1)}, bf16[64,1216]{1,0:T(8,128)(2,1)S(1)}, u32[]{:S(2)}, u32[]{:S(2)}) %collective-permute-start.29) | collective-permute-done | bytes 155680 | tf_op jit(solution)/shard_map/ppermute | solution.py:574
  100.9 2.6 %collective-permute-done.26.near = bf16[64,1216]{1,0:T(8,128)(2,1)S(1)} collective-permute-done((bf16[64,1216]{1,0:T(8,128)(2,1)S(1)}, bf16[64,1216]{1,0:T(8,128)(2,1)S(1)}, u32[]{:S(2)}, u32[]{:S(2)}) %collective-permute-start.26) | collective-permute-done | bytes 155680 | tf_op jit(solution)/shard_map/ppermute | solution.py:574
  103.5 0.2 shard_map.97
  103.8 0.1 collective-permute-start.30
  103.9 1.2 %collective-permute-done.30.other = f32[128,128]{1,0:T(8,128)S(1)} collective-permute-done((f32[128,128]{1,0:T(8,128)S(1)}, f32[128,128]{1,0:T(8,128)S(1)}, u32[]{:S(2)}, u32[]{:S(2)}) %collective-permute-start.30) | collective-permute-done | bytes 65568 | tf_op jit(solution)/shard_map/ppermute | solution.py:577
  105.1 1.2 %shard_map.98 = f32[1216,128]{1,0:T(8,128)} custom-call(f32[128,1216]{1,0:T(8,128)S(1)} %get-tuple-element.121.grad, f32[128,128]{1,0:T(8,128)S(1)} %get-tuple-element.122.sums, f32[128,128]{1,0:T(8,128)S(1)} %collective-permute-done.30.other, f32[128,1216]{1,0:T(8,128)S(1)} %copy-done.1, f32[128,1216]{1,0:T(8,128)S(1)} %copy-done.3, f32[128,128]{1,0:T(8,128)S(1)} %copy-done.4), custom_call_target="tpu_custom_call" | custom-call | flops 516096 | bytes 2064384 | tf_op jit(solution)/shard_map/pallas_call | solution.py:525
  (72 shorter events, 0.3 us)
Async XLA Ops:
  0.0 9.3 %copy-start = (bf16[640,608]{0,1:T(8,128)(2,1)S(1)}, bf16[640,608]{0,1:T(8,128)(2,1)}, u32[]{:S(2)}) copy-start(bf16[640,608]{0,1:T(8,128)(2,1)} %param.17) | copy-start | bytes 2334724
  3.6 12.5 %collective-permute-start.3 = (bf16[64,2560]{1,0:T(8,128)(2,1)}, bf16[64,2560]{1,0:T(8,128)(2,1)S(1)}, u32[]{:S(2)}, u32[]{:S(2)}) collective-permute-start(bf16[64,2560]{1,0:T(8,128)(2,1)} %get-tuple-element.67), channel_id=1, source_target_pairs={{2,0},{6,2},{4,6},{0,4},{3,1},{7,3},{5,7},{1,5},{10,8},{14,10},{12... | collective-permute-start | bytes 983048 | tf_op jit(solution)/shard_map/ppermute | solution.py:580
  7.6 17.2 %collective-permute-start.2 = (bf16[64,2560]{1,0:T(8,128)(2,1)}, bf16[64,2560]{1,0:T(8,128)(2,1)S(1)}, u32[]{:S(2)}, u32[]{:S(2)}) collective-permute-start(bf16[64,2560]{1,0:T(8,128)(2,1)} %get-tuple-element.67), channel_id=1, source_target_pairs={{0,2},{2,6},{6,4},{4,0},{1,3},{3,7},{7,5},{5,1},{8,10},{10,14},{14... | collective-permute-start | bytes 983048 | tf_op jit(solution)/shard_map/ppermute | solution.py:574
  9.7 22.6 %copy-start.7 = (bf16[608,384]{1,0:T(8,128)(2,1)}, bf16[608,384]{1,0:T(8,128)(2,1)S(1)}, u32[]{:S(2)}) copy-start(bf16[608,384]{1,0:T(8,128)(2,1)S(1)} %pad_maximum_fusion.1.refs_13_.refs_15_) | copy-start | bytes 1400836
  9.7 15.9 %collective-permute-start.1 = (bf16[608,384]{1,0:T(8,128)(2,1)S(1)}, bf16[608,384]{1,0:T(8,128)(2,1)S(1)}, u32[]{:S(2)}, u32[]{:S(2)}) collective-permute-start(bf16[608,384]{1,0:T(8,128)(2,1)S(1)} %pad_maximum_fusion.1.refs_13_.refs_15_), channel_id=1, source_target_pairs={{0,8},{1,17},{8,0},{9,25},{16,24},{17,1},{24,16},{25,9},{2,10},{3,... | collective-permute-start | bytes 1400840 | tf_op jit(solution)/shard_map/ppermute | solution.py:601
  12.2 16.7 %collective-permute-start = (bf16[608,384]{1,0:T(8,128)(2,1)}, bf16[608,384]{1,0:T(8,128)(2,1)}, u32[]{:S(2)}, u32[]{:S(2)}) collective-permute-start(bf16[608,384]{1,0:T(8,128)(2,1)} %pad_maximum_fusion.refs_9_), channel_id=1, source_target_pairs={{0,8},{1,17},{8,0},{9,25},{16,24},{17,1},{24,16},{25,9},{2,10},{3,... | collective-permute-start | bytes 1400840 | tf_op jit(solution)/shard_map/ppermute | solution.py:601
  12.7 25.1 %collective-permute-start.11 = (bf16[608,384]{1,0:T(8,128)(2,1)S(1)}, bf16[608,384]{1,0:T(8,128)(2,1)S(1)}, u32[]{:S(2)}, u32[]{:S(2)}) collective-permute-start(bf16[608,384]{1,0:T(8,128)(2,1)S(1)} %pad_maximum_fusion.1.refs_13_.refs_15_), channel_id=1, source_target_pairs={{0,16},{1,9},{8,24},{9,1},{16,0},{17,25},{24,8},{25,17},{2,18},{3,... | collective-permute-start | bytes 1400840 | tf_op jit(solution)/shard_map/ppermute | solution.py:602
  16.1 13.4 %copy-start.8 = (bf16[64,2560]{1,0:T(8,128)(2,1)}, bf16[64,2560]{1,0:T(8,128)(2,1)S(1)}, u32[]{:S(2)}) copy-start(bf16[64,2560]{1,0:T(8,128)(2,1)S(1)} %collective-permute-done.3.following.refs_3_) | copy-start | bytes 983044
  16.8 12.1 %collective-permute-start.4 = (bf16[32,2560]{1,0:T(8,128)(2,1)}, bf16[32,2560]{1,0:T(8,128)(2,1)S(1)}, u32[]{:S(2)}, u32[]{:S(2)}) collective-permute-start(bf16[32,2560]{1,0:T(8,128)(2,1)} %slice.12), channel_id=1, source_target_pairs={{2,0},{6,2},{4,6},{0,4},{3,1},{7,3},{5,7},{1,5},{10,8},{14,10},{12... | collective-permute-start | bytes 491528 | tf_op jit(solution)/shard_map/ppermute | solution.py:580
  24.8 4.7 %copy-start.10 = (bf16[64,2560]{1,0:T(8,128)(2,1)}, bf16[64,2560]{1,0:T(8,128)(2,1)S(1)}, u32[]{:S(2)}) copy-start(bf16[64,2560]{1,0:T(8,128)(2,1)S(1)} %collective-permute-done.2.previous.refs_1_) | copy-start | bytes 983044
  24.8 7.5 %collective-permute-start.7 = (bf16[32,2560]{1,0:T(8,128)(2,1)S(1)}, bf16[32,2560]{1,0:T(8,128)(2,1)S(1)}, u32[]{:S(2)}, u32[]{:S(2)}) collective-permute-start(bf16[32,2560]{1,0:T(8,128)(2,1)S(1)} %slice.14), channel_id=1, source_target_pairs={{0,2},{2,6},{6,4},{4,0},{1,3},{3,7},{7,5},{5,1},{8,10},{10,14},{14... | collective-permute-start | bytes 491528 | tf_op jit(solution)/shard_map/ppermute | solution.py:574
  25.6 22.5 %copy-start.12 = (bf16[608,384]{1,0:T(8,128)(2,1)}, bf16[608,384]{1,0:T(8,128)(2,1)S(1)}, u32[]{:S(2)}) copy-start(bf16[608,384]{1,0:T(8,128)(2,1)S(1)} %collective-permute-done.1.refs_14_.refs_16_) | copy-start | bytes 1400836
  25.6 22.5 %collective-permute-start.10 = (bf16[608,384]{1,0:T(8,128)(2,1)}, bf16[608,384]{1,0:T(8,128)(2,1)}, u32[]{:S(2)}, u32[]{:S(2)}) collective-permute-start(bf16[608,384]{1,0:T(8,128)(2,1)} %pad_maximum_fusion.refs_9_), channel_id=1, source_target_pairs={{0,16},{1,9},{8,24},{9,1},{16,0},{17,25},{24,8},{25,17},{2,18},{3,... | collective-permute-start | bytes 1400840 | tf_op jit(solution)/shard_map/ppermute | solution.py:602
  28.9 19.1 %copy-start.21 = (bf16[32,2560]{1,0:T(8,128)(2,1)}, bf16[32,2560]{1,0:T(8,128)(2,1)S(1)}, u32[]{:S(2)}) copy-start(bf16[32,2560]{1,0:T(8,128)(2,1)S(1)} %collective-permute-done.4.refs_7_) | copy-start | bytes 491524
  32.3 18.6 %copy-start.11 = (bf16[64,2560]{1,0:T(8,128)(2,1)S(1)}, bf16[64,2560]{1,0:T(8,128)(2,1)}, u32[]{:S(2)}) copy-start(bf16[64,2560]{1,0:T(8,128)(2,1)} %copy-done.10) | copy-start | bytes 983044
  32.3 19.1 %copy-start.9 = (bf16[64,2560]{1,0:T(8,128)(2,1)S(1)}, bf16[64,2560]{1,0:T(8,128)(2,1)}, u32[]{:S(2)}) copy-start(bf16[64,2560]{1,0:T(8,128)(2,1)} %copy-done.8) | copy-start | bytes 983044
  32.3 5.4 %copy-start.22 = (bf16[32,2560]{1,0:T(8,128)(2,1)}, bf16[32,2560]{1,0:T(8,128)(2,1)S(1)}, u32[]{:S(2)}) copy-start(bf16[32,2560]{1,0:T(8,128)(2,1)S(1)} %collective-permute-done.7.refs_5_) | copy-start | bytes 491524
  32.3 11.9 %collective-permute-start.15 = (bf16[64,2560]{1,0:T(8,128)(2,1)}, bf16[64,2560]{1,0:T(8,128)(2,1)S(1)}, u32[]{:S(2)}, u32[]{:S(2)}) collective-permute-start(bf16[64,2560]{1,0:T(8,128)(2,1)} %get-tuple-element.78), channel_id=1, source_target_pairs={{2,0},{6,2},{4,6},{0,4},{3,1},{7,3},{5,7},{1,5},{10,8},{14,10},{12... | collective-permute-start | bytes 983048 | tf_op jit(solution)/shard_map/ppermute | solution.py:580
  35.7 15.1 %collective-permute-start.12 = (bf16[608,384]{1,0:T(8,128)(2,1)}, bf16[608,384]{1,0:T(8,128)(2,1)}, u32[]{:S(2)}, u32[]{:S(2)}) collective-permute-start(bf16[608,384]{1,0:T(8,128)(2,1)} %collective-permute-done.refs_10_), channel_id=1, source_target_pairs={{0,16},{1,9},{8,24},{9,1},{16,0},{17,25},{24,8},{25,17},{2,18},{3,... | collective-permute-start | bytes 1400840 | tf_op jit(solution)/shard_map/ppermute | solution.py:637
  37.3 13.6 %collective-permute-start.13 = (bf16[608,384]{1,0:T(8,128)(2,1)S(1)}, bf16[608,384]{1,0:T(8,128)(2,1)}, u32[]{:S(2)}, u32[]{:S(2)}) collective-permute-start(bf16[608,384]{1,0:T(8,128)(2,1)S(1)} %collective-permute-done.1.refs_14_.refs_16_), channel_id=1, source_target_pairs={{0,16},{1,9},{8,24},{9,1},{16,0},{17,25},{24,8},{25,17},{2,18},{3,... | collective-permute-start | bytes 1400840 | tf_op jit(solution)/shard_map/ppermute | solution.py:637
  37.8 16.5 %copy-start.13 = (bf16[608,384]{1,0:T(8,128)(2,1)}, bf16[608,384]{1,0:T(8,128)(2,1)S(1)}, u32[]{:S(2)}) copy-start(bf16[608,384]{1,0:T(8,128)(2,1)S(1)} %collective-permute-done.11.refs_15_.refs_17_) | copy-start | bytes 1400836
  37.8 13.0 %collective-permute-start.9 = (bf16[64,2560]{1,0:T(8,128)(2,1)}, bf16[64,2560]{1,0:T(8,128)(2,1)S(1)}, u32[]{:S(2)}, u32[]{:S(2)}) collective-permute-start(bf16[64,2560]{1,0:T(8,128)(2,1)} %get-tuple-element.78), channel_id=1, source_target_pairs={{0,2},{2,6},{6,4},{4,0},{1,3},{3,7},{7,5},{5,1},{8,10},{10,14},{14... | collective-permute-start | bytes 983048 | tf_op jit(solution)/shard_map/ppermute | solution.py:574
  44.2 18.1 %copy-start.14 = (bf16[64,2560]{1,0:T(8,128)(2,1)}, bf16[64,2560]{1,0:T(8,128)(2,1)S(1)}, u32[]{:S(2)}) copy-start(bf16[64,2560]{1,0:T(8,128)(2,1)S(1)} %collective-permute-done.15.refs_11_) | copy-start | bytes 983044
  44.2 7.5 %copy-start.23 = (bf16[32,2560]{1,0:T(8,128)(2,1)S(1)}, bf16[32,2560]{1,0:T(8,128)(2,1)}, u32[]{:S(2)}) copy-start(bf16[32,2560]{1,0:T(8,128)(2,1)} %copy-done.22) | copy-start | bytes 491524
  44.2 7.5 %collective-permute-start.16 = (bf16[64,2560]{1,0:T(8,128)(2,1)S(1)}, bf16[64,2560]{1,0:T(8,128)(2,1)S(1)}, u32[]{:S(2)}, u32[]{:S(2)}) collective-permute-start(bf16[64,2560]{1,0:T(8,128)(2,1)S(1)} %collective-permute-done.15.refs_11_), channel_id=1, source_target_pairs={{0,1},{1,0},{2,3},{3,2},{4,5},{5,4},{6,7},{7,6},{8,9},{9,8},{10,11... | collective-permute-start | bytes 983048 | tf_op jit(solution)/shard_map/ppermute | solution.py:577
  48.1 3.4 %collective-permute-start.17 = (bf16[32,2560]{1,0:T(8,128)(2,1)S(1)}, bf16[32,2560]{1,0:T(8,128)(2,1)S(1)}, u32[]{:S(2)}, u32[]{:S(2)}) collective-permute-start(bf16[32,2560]{1,0:T(8,128)(2,1)S(1)} %collective-permute-done.4.refs_7_), channel_id=1, source_target_pairs={{0,1},{1,0},{2,3},{3,2},{4,5},{5,4},{6,7},{7,6},{8,9},{9,8},{10,11... | collective-permute-start | bytes 491528 | tf_op jit(solution)/shard_map/ppermute | solution.py:577
  50.8 11.5 %copy-start.15 = (bf16[64,2560]{1,0:T(8,128)(2,1)}, bf16[64,2560]{1,0:T(8,128)(2,1)S(1)}, u32[]{:S(2)}) copy-start(bf16[64,2560]{1,0:T(8,128)(2,1)S(1)} %collective-permute-done.9.refs_9_) | copy-start | bytes 983044
  50.8 1.7 %collective-permute-start.14 = (bf16[64,2560]{1,0:T(8,128)(2,1)S(1)}, bf16[64,2560]{1,0:T(8,128)(2,1)S(1)}, u32[]{:S(2)}, u32[]{:S(2)}) collective-permute-start(bf16[64,2560]{1,0:T(8,128)(2,1)S(1)} %collective-permute-done.9.refs_9_), channel_id=1, source_target_pairs={{0,1},{1,0},{2,3},{3,2},{4,5},{5,4},{6,7},{7,6},{8,9},{9,8},{10,11... | collective-permute-start | bytes 983048 | tf_op jit(solution)/shard_map/ppermute | solution.py:577
  50.9 2.5 %collective-permute-start.5 = (bf16[64,2560]{1,0:T(8,128)(2,1)S(1)}, bf16[64,2560]{1,0:T(8,128)(2,1)S(1)}, u32[]{:S(2)}, u32[]{:S(2)}) collective-permute-start(bf16[64,2560]{1,0:T(8,128)(2,1)S(1)} %copy-done.11), channel_id=1, source_target_pairs={{0,1},{1,0},{2,3},{3,2},{4,5},{5,4},{6,7},{7,6},{8,9},{9,8},{10,11... | collective-permute-start | bytes 983048 | tf_op jit(solution)/shard_map/ppermute | solution.py:577
  51.4 2.8 %collective-permute-start.6 = (bf16[64,2560]{1,0:T(8,128)(2,1)S(1)}, bf16[64,2560]{1,0:T(8,128)(2,1)}, u32[]{:S(2)}, u32[]{:S(2)}) collective-permute-start(bf16[64,2560]{1,0:T(8,128)(2,1)S(1)} %copy-done.9), channel_id=1, source_target_pairs={{0,1},{1,0},{2,3},{3,2},{4,5},{5,4},{6,7},{7,6},{8,9},{9,8},{10,11... | collective-permute-start | bytes 983048 | tf_op jit(solution)/shard_map/ppermute | solution.py:577
  51.5 2.0 %copy-start.24 = (bf16[32,2560]{1,0:T(8,128)(2,1)}, bf16[32,2560]{1,0:T(8,128)(2,1)S(1)}, u32[]{:S(2)}) copy-start(bf16[32,2560]{1,0:T(8,128)(2,1)S(1)} %collective-permute-done.17.refs_8_) | copy-start | bytes 491524
  51.5 10.9 %collective-permute-start.18 = (bf16[64,2560]{1,0:T(8,128)(2,1)S(1)}, bf16[64,2560]{1,0:T(8,128)(2,1)S(1)}, u32[]{:S(2)}, u32[]{:S(2)}) collective-permute-start(bf16[64,2560]{1,0:T(8,128)(2,1)S(1)} %collective-permute-done.9.refs_9_), channel_id=1, source_target_pairs={{0,2},{2,6},{6,4},{4,0},{1,3},{3,7},{7,5},{5,1},{8,10},{10,14},{14... | collective-permute-start | bytes 983048 | tf_op jit(solution)/shard_map/ppermute | solution.py:574
  51.7 10.7 %copy-start.16 = (bf16[64,2560]{1,0:T(8,128)(2,1)}, bf16[64,2560]{1,0:T(8,128)(2,1)S(1)}, u32[]{:S(2)}) copy-start(bf16[64,2560]{1,0:T(8,128)(2,1)S(1)} %collective-permute-done.16.refs_12_) | copy-start | bytes 983044
  51.7 1.8 %collective-permute-start.8 = (bf16[32,2560]{1,0:T(8,128)(2,1)S(1)}, bf16[32,2560]{1,0:T(8,128)(2,1)S(1)}, u32[]{:S(2)}, u32[]{:S(2)}) collective-permute-start(bf16[32,2560]{1,0:T(8,128)(2,1)S(1)} %copy-done.23), channel_id=1, source_target_pairs={{0,1},{1,0},{2,3},{3,2},{4,5},{5,4},{6,7},{7,6},{8,9},{9,8},{10,11... | collective-permute-start | bytes 491528 | tf_op jit(solution)/shard_map/ppermute | solution.py:577
  52.5 9.9 %copy-start.17 = (bf16[64,2560]{1,0:T(8,128)(2,1)}, bf16[64,2560]{1,0:T(8,128)(2,1)S(1)}, u32[]{:S(2)}) copy-start(bf16[64,2560]{1,0:T(8,128)(2,1)S(1)} %collective-permute-done.14.refs_10_) | copy-start | bytes 983044
  53.5 0.8 copy-start.25
  53.5 0.8 copy-start.19
  62.4 2.0 %copy-start.18 = (bf16[64,2560]{1,0:T(8,128)(2,1)}, bf16[64,2560]{1,0:T(8,128)(2,1)S(1)}, u32[]{:S(2)}) copy-start(bf16[64,2560]{1,0:T(8,128)(2,1)S(1)} %collective-permute-done.18.refs_13_) | copy-start | bytes 983044
  62.4 1.7 %collective-permute-start.19 = (bf16[64,2560]{1,0:T(8,128)(2,1)S(1)}, bf16[64,2560]{1,0:T(8,128)(2,1)S(1)}, u32[]{:S(2)}, u32[]{:S(2)}) collective-permute-start(bf16[64,2560]{1,0:T(8,128)(2,1)S(1)} %collective-permute-done.18.refs_13_), channel_id=1, source_target_pairs={{0,1},{1,0},{2,3},{3,2},{4,5},{5,4},{6,7},{7,6},{8,9},{9,8},{10,11... | collective-permute-start | bytes 983048 | tf_op jit(solution)/shard_map/ppermute | solution.py:577
  64.1 0.7 copy-start.20
  64.1 17.9 %collective-permute-start.23 = (bf16[1216,640]{1,0:T(8,128)(2,1)}, bf16[1216,640]{1,0:T(8,128)(2,1)}, u32[]{:S(2)}, u32[]{:S(2)}) collective-permute-start(bf16[1216,640]{1,0:T(8,128)(2,1)} %get-tuple-element.112.refs_7_), channel_id=1, source_target_pairs={{0,1},{1,0},{2,3},{3,2},{4,5},{5,4},{6,7},{7,6},{8,9},{9,8},{10,11... | collective-permute-start | bytes 4669448 | tf_op jit(solution)/shard_map/ppermute | solution.py:577
  64.8 17.2 %copy-start.2 = (bf16[1216,640]{1,0:T(8,128)(2,1)S(1)}, bf16[1216,640]{1,0:T(8,128)(2,1)}, u32[]{:S(2)}) copy-start(bf16[1216,640]{1,0:T(8,128)(2,1)} %get-tuple-element.89.refs_6_.w_own) | copy-start | bytes 4669444
  75.3 1.7 %collective-permute-start.22 = (bf16[64,1216]{1,0:T(8,128)(2,1)}, bf16[64,1216]{1,0:T(8,128)(2,1)S(1)}, u32[]{:S(2)}, u32[]{:S(2)}) collective-permute-start(bf16[64,1216]{1,0:T(8,128)(2,1)} %get-tuple-element.109), channel_id=1, source_target_pairs={{0,1},{1,0},{2,3},{3,2},{4,5},{5,4},{6,7},{7,6},{8,9},{9,8},{10,11... | collective-permute-start | bytes 466952 | tf_op jit(solution)/shard_map/ppermute | solution.py:577
  75.7 4.0 %collective-permute-start.21 = (bf16[64,1216]{1,0:T(8,128)(2,1)}, bf16[64,1216]{1,0:T(8,128)(2,1)S(1)}, u32[]{:S(2)}, u32[]{:S(2)}) collective-permute-start(bf16[64,1216]{1,0:T(8,128)(2,1)} %get-tuple-element.107), channel_id=1, source_target_pairs={{0,1},{1,0},{2,3},{3,2},{4,5},{5,4},{6,7},{7,6},{8,9},{9,8},{10,11... | collective-permute-start | bytes 466952 | tf_op jit(solution)/shard_map/ppermute | solution.py:577
  75.9 6.1 %collective-permute-start.20 = (bf16[384,640]{1,0:T(8,128)(2,1)}, bf16[384,640]{1,0:T(8,128)(2,1)S(1)}, u32[]{:S(2)}, u32[]{:S(2)}) collective-permute-start(bf16[384,640]{1,0:T(8,128)(2,1)} %get-tuple-element.110.own), channel_id=1, source_target_pairs={{0,1},{1,0},{2,3},{3,2},{4,5},{5,4},{6,7},{7,6},{8,9},{9,8},{10,11... | collective-permute-start | bytes 1474568 | tf_op jit(solution)/shard_map/ppermute | solution.py:577
  78.0 8.1 %collective-permute-start.27 = (bf16[64,1216]{1,0:T(8,128)(2,1)S(1)}, bf16[64,1216]{1,0:T(8,128)(2,1)S(1)}, u32[]{:S(2)}, u32[]{:S(2)}) collective-permute-start(bf16[64,1216]{1,0:T(8,128)(2,1)S(1)} %add_convert_fusion.4), channel_id=1, source_target_pairs={{0,2},{2,6},{6,4},{4,0},{1,3},{3,7},{7,5},{5,1},{8,10},{10,14},{14... | collective-permute-start | bytes 466952 | tf_op jit(solution)/shard_map/ppermute | solution.py:574
  80.7 8.2 %collective-permute-start.24 = (bf16[64,1216]{1,0:T(8,128)(2,1)S(1)}, bf16[64,1216]{1,0:T(8,128)(2,1)S(1)}, u32[]{:S(2)}, u32[]{:S(2)}) collective-permute-start(bf16[64,1216]{1,0:T(8,128)(2,1)S(1)} %add_convert_fusion.5), channel_id=1, source_target_pairs={{0,2},{2,6},{6,4},{4,0},{1,3},{3,7},{7,5},{5,1},{8,10},{10,14},{14... | collective-permute-start | bytes 466952 | tf_op jit(solution)/shard_map/ppermute | solution.py:574
  82.0 1.0 copy-start.6
  86.1 17.4 %copy-start.1 = (f32[128,1216]{1,0:T(8,128)S(1)}, f32[128,1216]{1,0:T(8,128)}, u32[]{:S(2)}) copy-start(f32[128,1216]{1,0:T(8,128)} %get-tuple-element.120.normed) | copy-start | bytes 1867780
  86.1 17.4 %copy-start.5 = (f32[1,1216]{1,0:T(1,128)S(1)}, f32[1,1216]{1,0:T(1,128)}, u32[]{:S(2)}) copy-start(f32[1,1216]{1,0:T(1,128)} %get-tuple-element.119.scale) | copy-start | bytes 14596
  86.2 7.5 %collective-permute-start.28 = (bf16[64,1216]{1,0:T(8,128)(2,1)S(1)}, bf16[64,1216]{1,0:T(8,128)(2,1)S(1)}, u32[]{:S(2)}, u32[]{:S(2)}) collective-permute-start(bf16[64,1216]{1,0:T(8,128)(2,1)S(1)} %add_convert_fusion.1), channel_id=1, source_target_pairs={{0,2},{2,6},{6,4},{4,0},{1,3},{3,7},{7,5},{5,1},{8,10},{10,14},{14... | collective-permute-start | bytes 466952 | tf_op jit(solution)/shard_map/ppermute | solution.py:574
  88.9 16.2 %copy-start.3 = (f32[128,1216]{1,0:T(8,128)S(1)}, f32[128,1216]{1,0:T(8,128)}, u32[]{:S(2)}) copy-start(f32[128,1216]{1,0:T(8,128)} %get-tuple-element.123.base) | copy-start | bytes 1867780
  88.9 16.2 %copy-start.4 = (f32[128,128]{1,0:T(8,128)S(1)}, f32[128,128]{1,0:T(8,128)}, u32[]{:S(2)}) copy-start(f32[128,128]{1,0:T(8,128)} %get-tuple-element.124.inv_std) | copy-start | bytes 196612
  88.9 8.3 %collective-permute-start.25 = (bf16[64,1216]{1,0:T(8,128)(2,1)S(1)}, bf16[64,1216]{1,0:T(8,128)(2,1)S(1)}, u32[]{:S(2)}, u32[]{:S(2)}) collective-permute-start(bf16[64,1216]{1,0:T(8,128)(2,1)S(1)} %add_convert_fusion.3), channel_id=1, source_target_pairs={{0,2},{2,6},{6,4},{4,0},{1,3},{3,7},{7,5},{5,1},{8,10},{10,14},{14... | collective-permute-start | bytes 466952 | tf_op jit(solution)/shard_map/ppermute | solution.py:574
  93.8 7.1 %collective-permute-start.29 = (bf16[64,1216]{1,0:T(8,128)(2,1)S(1)}, bf16[64,1216]{1,0:T(8,128)(2,1)S(1)}, u32[]{:S(2)}, u32[]{:S(2)}) collective-permute-start(bf16[64,1216]{1,0:T(8,128)(2,1)S(1)} %add_convert_fusion), channel_id=1, source_target_pairs={{0,2},{2,6},{6,4},{4,0},{1,3},{3,7},{7,5},{5,1},{8,10},{10,14},{14... | collective-permute-start | bytes 466952 | tf_op jit(solution)/shard_map/ppermute | solution.py:574
  97.3 6.3 %collective-permute-start.26 = (bf16[64,1216]{1,0:T(8,128)(2,1)S(1)}, bf16[64,1216]{1,0:T(8,128)(2,1)S(1)}, u32[]{:S(2)}, u32[]{:S(2)}) collective-permute-start(bf16[64,1216]{1,0:T(8,128)(2,1)S(1)} %add_convert_fusion.2), channel_id=1, source_target_pairs={{0,2},{2,6},{6,4},{4,0},{1,3},{3,7},{7,5},{5,1},{8,10},{10,14},{14... | collective-permute-start | bytes 466952 | tf_op jit(solution)/shard_map/ppermute | solution.py:574
  103.8 1.3 %collective-permute-start.30 = (f32[128,128]{1,0:T(8,128)S(1)}, f32[128,128]{1,0:T(8,128)S(1)}, u32[]{:S(2)}, u32[]{:S(2)}) collective-permute-start(f32[128,128]{1,0:T(8,128)S(1)} %get-tuple-element.122.sums), channel_id=1, source_target_pairs={{0,1},{1,0},{2,3},{3,2},{4,5},{5,4},{6,7},{7,6},{8,9},{9,8},{10,11... | collective-permute-start | bytes 196616 | tf_op jit(solution)/shard_map/ppermute | solution.py:577
